TPU v7x, 32 devices: a whole 2x2x4 slice. The times are simulated.
32 devices in a mesh: hours: 2 (over x), chan: 2 (over core), freq: 8 (over z, y).
Axes of the slice: x: 2, y: 2, z: 4, core: 2. Of those that a mesh axis runs over, the one named last changes fastest.
Arguments:
- samples: bfloat16 [1152, 32, 1024], P('chan', ('hours', 'freq')), parts along dimension 1, may hold values from -18 to 18
Outputs:
- cross_spectra: bfloat16 [2, 256, 1152, 1152], P(None, ('hours', 'freq'), None, 'chan'), parts along dimension 1
There are 2 independent parts, one for each index of `hours`. A program takes and returns all parts, laid end to end along the dimension named above; each array names one. Nothing has to cross between parts.
All inputs are finite; a program needn't handle non-finite values.
Results may differ from a plain program's by a relative error of at most 0.008.
Values may be sent and summed in bfloat16 or wider, within the bound.
No kernel may reach another device: no remote copies, remote signals or barrier semaphores. Data moves between devices by JAX's collectives and lax.ppermute only.
A program may use at most 192 MiB of HBM per device.

v0:
```python
import math

import jax
import jax.numpy as jnp
from jax import lax
from jax.sharding import PartitionSpec as P

BINS = 128


def padded_2(cells, sides, width):
    for axis, dim in sides:
        count = lax.axis_size(axis)
        ends = count - 1
        head = lax.slice_in_dim(cells, 0, width, axis=dim)
        tail = lax.slice_in_dim(cells, cells.shape[dim] - width, cells.shape[dim], axis=dim)
        cells = jnp.concatenate(
            [
                lax.ppermute(tail, axis, [(i, (i + 1) % count) for i in range(ends)]),
                cells,
                lax.ppermute(head, axis, [((i + 1) % count, i) for i in range(ends)]),
            ],
            axis=dim,
        )
    return cells


def from_behind(value, axis, steps):
    count = lax.axis_size(axis)
    pairs = [(source, (source + steps) % count) for source in range(count)]
    return lax.ppermute(value, axis, pairs)


def bin_table(length, bins):
    position = lax.broadcasted_iota(jnp.int32, (length, bins), 0)
    number = lax.broadcasted_iota(jnp.int32, (length, bins), 1) + 1
    phase = (position * number % length).astype(jnp.float32) * (2.0 * math.pi / length)
    taper = 0.5 - 0.5 * jnp.cos(position.astype(jnp.float32) * (2.0 * math.pi / length))
    factor = math.sqrt(8.0 / (3.0 * length))
    table = jnp.concatenate([taper * jnp.cos(phase), -(taper * jnp.sin(phase))], axis=1) * factor
    return table.astype(jnp.bfloat16)


def whiten(padded, first_bin, total_bins):
    count_bins = padded.shape[1] - 4
    values = padded.astype(jnp.float32)
    power = values[0] * values[0] + values[1] * values[1]
    summed = power[0:count_bins] + power[1 : count_bins + 1]
    summed = summed + power[2 : count_bins + 2]
    summed = summed + power[3 : count_bins + 3]
    summed = summed + power[4 : count_bins + 4]
    which = first_bin + jnp.arange(count_bins, dtype=jnp.int32)
    upper = jnp.minimum(which + 2, total_bins - 1)
    lower = jnp.maximum(which - 2, 0)
    count = (upper - lower + 1).astype(jnp.float32)
    level = jnp.maximum(summed / count[:, None, None], 0.1)
    return (values[:, 2 : count_bins + 2] / jnp.sqrt(level)[None]).astype(jnp.bfloat16)


def local(samples):
    local_channels, local_windows, length = samples.shape
    table = bin_table(length, BINS)
    spectrum = jnp.einsum("cws,sj->jwc", samples, table, preferred_element_type=jnp.float32)
    spectrum = spectrum.reshape(2, BINS, local_windows, local_channels).astype(jnp.bfloat16)
    arrived = lax.all_to_all(spectrum, "freq", split_axis=1, concat_axis=2, tiled=True)
    rimmed = padded_2(arrived, (("freq", 1),), 2)
    whitened = whiten(rimmed, lax.axis_index("freq") * arrived.shape[1], BINS)
    local_bins = whitened.shape[1]
    windows = whitened.shape[2]
    blocks = lax.axis_size("chan")
    own_block = lax.axis_index("chan")
    scale = 1.0 / windows
    visitors = [whitened]
    visiting = whitened
    visiting = from_behind(visiting, "chan", 1)
    visitors.append(visiting)
    stacked = jnp.stack(visitors)
    order = (own_block - jnp.arange(blocks, dtype=jnp.int32)) % blocks
    ordered = jnp.take(stacked, order, axis=0)
    every = jnp.transpose(ordered, (1, 2, 3, 0, 4)).reshape(
        2, local_bins, windows, blocks * local_channels
    )
    real_part = jnp.einsum("pkwb,pkwa->kba", every, whitened, preferred_element_type=jnp.float32)
    imag_part = jnp.einsum(
        "kwb,kwa->kba", every[0], whitened[1], preferred_element_type=jnp.float32
    )
    imag_part = imag_part - jnp.einsum(
        "kwb,kwa->kba", every[1], whitened[0], preferred_element_type=jnp.float32
    )
    return (jnp.stack([real_part, imag_part]) * scale).astype(jnp.bfloat16)


def solution(mesh):
    placed = (P("chan", ("hours", "freq"), None),)
    return jax.shard_map(
        local,
        mesh=mesh,
        in_specs=placed,
        out_specs=P(None, ("hours", "freq"), None, "chan"),
        check_vma=False,
    )
```

profile of v0, /device:TPU:0, one launch (start us, length us, event | category | flops | bytes accessed | tf_op | source)
XLA Modules:
  0.0 168.4 jit_solution(10404083622506896489)
XLA Ops:
  0.1 2.1 %cosine_multiply_fusion = (f32[1024,128]{1,0:T(8,128)S(1)}, f32[1024,128]{1,0:T(8,128)S(1)}) fusion(s32[128]{0:T(128)S(1)} %iota_add_fusion, f32[1024]{0:T(1024)S(1)} %multiply_subtract_fusion), kind=kLoop, calls=%fused_computation.36 | loop fusion | flops 2228224 | bytes 1053184 | tf_op jit(solution)/shard_map/mul | solution.py:40
  2.2 0.8 fusion.7
  3.0 0.1 convert_element_type.44
  3.1 2.7 %copy.14 = bf16[2,128,2,576]{3,2,0,1:T(2,128)(2,1)} copy(bf16[2,128,2,576]{1,0,3,2:T(2,128)(2,1)S(1)} %convert_element_type.44) | data formatting | bytes 1179648 | tf_op jit(solution)/shard_map/convert_element_type | solution.py:64
  5.8 7.3 %all-to-all-start = ((bf16[2,128,2,576]{3,2,0,1:T(2,128)(2,1)}), bf16[2,128,2,576]{3,2,0,1:T(2,128)(2,1)S(1)}, u32[]{:S(2)}, u32[]{:S(2)}) async-start(bf16[2,128,2,576]{3,2,0,1:T(2,128)(2,1)} %copy.14), calls=%async_computation | async-start | bytes 1310720 | tf_op jit(solution)/shard_map/all_to_all | solution.py:65
  13.1 17.3 %all-to-all-done = bf16[2,128,2,576]{3,2,0,1:T(2,128)(2,1)S(1)} async-done(((bf16[2,128,2,576]{3,2,0,1:T(2,128)(2,1)}), bf16[2,128,2,576]{3,2,0,1:T(2,128)(2,1)S(1)}, u32[]{:S(2)}, u32[]{:S(2)}) %all-to-all-start) | async-done | bytes 589856 | tf_op jit(solution)/shard_map/all_to_all | solution.py:65
  30.5 0.7 copy.16
  31.1 0.5 all_to_all.16
  31.7 3.4 %collective-permute-start = (bf16[2,2,16,576]{3,2,1,0:T(8,128)(2,1)S(1)}, bf16[2,2,16,576]{3,2,1,0:T(8,128)(2,1)S(1)}, u32[]{:S(2)}, u32[]{:S(2)}) collective-permute-start(bf16[2,2,16,576]{3,2,1,0:T(8,128)(2,1)S(1)} %get-tuple-element.7), channel_id=1, source_target_pairs={{0,1},{1,2},{2,3},{3,4},{4,5},{5,6},{6,7},{8,9},{9,10},{10,11},{11... | collective-permute-start | bytes 221192 | tf_op jit(solution)/shard_map/ppermute | solution.py:19
  35.1 1.3 collective-permute-start.1
  36.4 0.7 collective-permute-done
  37.1 4.3 %collective-permute-done.1 = bf16[2,2,16,576]{3,2,1,0:T(8,128)(2,1)S(1)} collective-permute-done((bf16[2,2,16,576]{3,2,1,0:T(8,128)(2,1)S(1)}, bf16[2,2,16,576]{3,2,1,0:T(8,128)(2,1)S(1)}, u32[]{:S(2)}, u32[]{:S(2)}) %collective-permute-start.1) | collective-permute-done | bytes 73760 | tf_op jit(solution)/shard_map/ppermute | solution.py:21
  41.4 0.2 maximum_convert_fusion
  41.6 0.1 fusion.11
  41.7 0.3 fusion.15
  42.0 0.1 fusion.6
  42.3 0.1 fusion.37
  42.4 1.9 %collective-permute-done.2 = bf16[2,16,16,576]{3,2,1,0:T(8,128)(2,1)S(1)} collective-permute-done((bf16[2,16,16,576]{3,2,1,0:T(8,128)(2,1)S(1)}, bf16[2,16,16,576]{3,2,1,0:T(8,128)(2,1)S(1)}, u32[]{:S(2)}, u32[]{:S(2)}) %collective-permute-start.2) | collective-permute-done | bytes 589856 | tf_op jit(solution)/shard_map/ppermute | solution.py:31
  44.3 0.2 pad_maximum_fusion
  44.5 1.8 %gather_fusion = bf16[2,2,16,16,576]{4,3,2,1,0:T(8,128)(2,1)} fusion(bf16[2,2,16,16,576]{4,3,2,1,0:T(8,128)(2,1)S(1)} %pad_maximum_fusion, s32[1024]{0:T(1024)S(1)} %pad_clamp_fusion), kind=kCustom, calls=%fused_computation | custom fusion | bytes 2359304 | tf_op jit(solution)/shard_map/jit(_take)/gather | solution.py:79
  46.3 1.5 select_bitcast_fusion
  47.8 2.4 %copy.17 = bf16[2,16,16,2,576]{4,3,2,1,0:T(2,128)(2,1)} copy(bf16[2,16,16,2,576]{4,2,1,0,3:T(8,128)(2,1)S(1)} %select_bitcast_fusion) | data formatting | bytes 2359296 | tf_op jit(solution)/shard_map/jit(_take)/select_n | solution.py:79
  50.2 1.0 fusion.31
  51.2 3.1 %reshape.85 = bf16[2,16,16,1152]{3,2,1,0:T(8,128)(2,1)S(1)} reshape(bf16[2,16,16,2,576]{4,3,2,1,0:T(2,128)(2,1)} %copy.17) | data formatting | bytes 2359296 | tf_op jit(solution)/shard_map/reshape | solution.py:80
  54.2 1.5 copy.19
  55.7 2.0 %squeeze.18 = bf16[16,16,1152]{2,1,0:T(8,128)(2,1)S(1)} reshape(bf16[1,16,16,2,576]{4,3,2,1,0:T(2,128)(2,1)} %copy.19) | data formatting | bytes 1179648 | tf_op jit(solution)/shard_map/squeeze | solution.py:88
  57.8 2.6 %copy.18 = bf16[1,16,16,2,576]{4,3,2,1,0:T(2,128)(2,1)} copy(bf16[1,16,16,2,576]{4,2,1,0,3:T(8,128)(2,1)} %get-tuple-element.6) | data formatting | bytes 1179648 | tf_op jit(solution)/shard_map/slice | solution.py:85
  60.4 2.0 %squeeze.16 = bf16[16,16,1152]{2,1,0:T(8,128)(2,1)S(1)} reshape(bf16[1,16,16,2,576]{4,3,2,1,0:T(2,128)(2,1)} %copy.18) | data formatting | bytes 1179648 | tf_op jit(solution)/shard_map/squeeze | solution.py:85
  62.4 16.5 %convolution_bitcast_fusion = f32[1,16,1152,576]{2,3,1,0:T(8,128)} fusion(bf16[2,16,16,1152]{3,2,1,0:T(8,128)(2,1)S(1)} %reshape.85, bf16[2,16,16,576]{3,2,1,0:T(8,128)(2,1)S(1)} %fusion.6), kind=kOutput, calls=%fused_computation.4 | convolution fusion | flops 679477248 | bytes 44236800 | tf_op jit(solution)/shard_map/pkwb,pkwa->kba/dot_general | solution.py:83
  78.9 17.6 %fusion.25 = f32[16,1152,576]{1,2,0:T(8,128)} fusion(bf16[16,16,1152]{2,1,0:T(8,128)(2,1)S(1)} %squeeze.16, bf16[2,16,16,576]{3,2,1,0:T(8,128)(2,1)S(1)} %fusion.6), kind=kOutput, calls=%fused_computation.42 | convolution fusion | flops 339738624 | bytes 43384832 | tf_op jit(solution)/shard_map/kwb,kwa->kba/dot_general | solution.py:84
  96.5 30.7 %subtract_bitcast_fusion = f32[1,16,1152,576]{2,3,1,0:T(8,128)} fusion(f32[16,1152,576]{1,2,0:T(8,128)} %fusion.25, bf16[16,16,1152]{2,1,0:T(8,128)(2,1)S(1)} %squeeze.18, bf16[2,16,16,576]{3,2,1,0:T(8,128)(2,1)S(1)} %fusion.6), kind=kOutput, calls=%fused_computation.3 | convolution fusion | flops 350355456 | bytes 85852160 | tf_op jit(solution)/shard_map/kwb,kwa->kba/dot_general | solution.py:87
  127.2 41.0 %fusion = bf16[2,16,1152,576]{2,3,1,0:T(8,128)(2,1)} fusion(f32[1,16,1152,576]{2,3,1,0:T(8,128)} %subtract_bitcast_fusion, f32[1,16,1152,576]{2,3,1,0:T(8,128)} %convolution_bitcast_fusion), kind=kLoop, calls=%fused_computation.2 | loop fusion | flops 63700992 | bytes 127401984 | tf_op jit(solution)/shard_map/convert_element_type | solution.py:90
  (13 shorter events, 0.3 us)
Async XLA Ops:
  0.0 2.2 %copy-start = (bf16[576,2,1024]{2,1,0:T(2,128)(2,1)S(1)}, bf16[576,2,1024]{2,1,0:T(2,128)(2,1)}, u32[]{:S(2)}) copy-start(bf16[576,2,1024]{2,1,0:T(2,128)(2,1)} %param.1) | copy-start | bytes 7077892
  5.8 24.6 %all-to-all-start = ((bf16[2,128,2,576]{3,2,0,1:T(2,128)(2,1)}), bf16[2,128,2,576]{3,2,0,1:T(2,128)(2,1)S(1)}, u32[]{:S(2)}, u32[]{:S(2)}) async-start(bf16[2,128,2,576]{3,2,0,1:T(2,128)(2,1)} %copy.14), calls=%async_computation | async-start | bytes 1310720 | tf_op jit(solution)/shard_map/all_to_all | solution.py:65
  31.7 5.4 %collective-permute-start = (bf16[2,2,16,576]{3,2,1,0:T(8,128)(2,1)S(1)}, bf16[2,2,16,576]{3,2,1,0:T(8,128)(2,1)S(1)}, u32[]{:S(2)}, u32[]{:S(2)}) collective-permute-start(bf16[2,2,16,576]{3,2,1,0:T(8,128)(2,1)S(1)} %get-tuple-element.7), channel_id=1, source_target_pairs={{0,1},{1,2},{2,3},{3,4},{4,5},{5,6},{6,7},{8,9},{9,10},{10,11},{11... | collective-permute-start | bytes 221192 | tf_op jit(solution)/shard_map/ppermute | solution.py:19
  35.1 6.3 %collective-permute-start.1 = (bf16[2,2,16,576]{3,2,1,0:T(8,128)(2,1)S(1)}, bf16[2,2,16,576]{3,2,1,0:T(8,128)(2,1)S(1)}, u32[]{:S(2)}, u32[]{:S(2)}) collective-permute-start(bf16[2,2,16,576]{3,2,1,0:T(8,128)(2,1)S(1)} %get-tuple-element.8), channel_id=1, source_target_pairs={{1,0},{2,1},{3,2},{4,3},{5,4},{6,5},{7,6},{9,8},{10,9},{11,10},{12... | collective-permute-start | bytes 221192 | tf_op jit(solution)/shard_map/ppermute | solution.py:21
  42.1 2.2 %collective-permute-start.2 = (bf16[2,16,16,576]{3,2,1,0:T(8,128)(2,1)S(1)}, bf16[2,16,16,576]{3,2,1,0:T(8,128)(2,1)S(1)}, u32[]{:S(2)}, u32[]{:S(2)}) collective-permute-start(bf16[2,16,16,576]{3,2,1,0:T(8,128)(2,1)S(1)} %fusion.6), channel_id=1, source_target_pairs={{0,8},{8,0},{1,9},{9,1},{2,10},{10,2},{3,11},{11,3},{4,12},{12,4},... | collective-permute-start | bytes 1769480 | tf_op jit(solution)/shard_map/ppermute | solution.py:31
  127.2 41.0 %copy-start.1 = (bf16[576,2,1024]{2,1,0:T(2,128)(2,1)S(1)}, bf16[576,2,1024]{2,1,0:T(2,128)(2,1)}, u32[]{:S(2)}) copy-start(bf16[576,2,1024]{2,1,0:T(2,128)(2,1)} %param.1) | copy-start | bytes 7077892
where the time goes:
time: 169 us; the launch traced here: 168 us
  matrix products  65.5 us (39%)
  other arithmetic  45.8 us (27%)
  waiting for transfers between devices  24.2 us (14%)
  local copies, waits for them, and re-layouts  20.4 us (12%)
  starting transfers between devices  12 us (7%)
    convert_element_type x1, other arithmetic, local(): return (jnp.stack([real_part, imag_part]) * scale).astype(jnp.bfloat16)  41 us
    dot_general x1, matrix products, local(): jnp.einsum('kwb,kwa->kba', every[1], whitened[0], preferred_element_type=...  30.7 us
    dot_general x1, matrix products, local(): jnp.einsum('kwb,kwa->kba', every[0], whitened[1], preferred_element_type=...  17.6 us
    all_to_all x1, waiting for transfers between devices, local(): lax.all_to_all(spectrum, 'freq', split_axis=1, concat_axis=2, tiled=True)  17.3 us
    dot_general x1, matrix products, local(): jnp.einsum('pkwb,pkwa->kba', every, whitened, preferred_element_type=jnp....  16.5 us
    all_to_all x1, starting transfers between devices, local(): lax.all_to_all(spectrum, 'freq', split_axis=1, concat_axis=2, tiled=True)  7.28 us
    ppermute x1, waiting for transfers between devices, padded_2(): lax.ppermute(head, axis, [((i + 1) % count, i) for i in range(ends)])  4.3 us
  transfers between devices with their start and end apart: 4, of which 4 were waited for; matrix products, arithmetic and copies ran while one was open for 0% of the time, Pallas kernels for 0%

commit v1 on v0

v1 whole, which is shorter than its diff:
```python
import functools
import math

import jax
import jax.numpy as jnp
import ml_dtypes
import numpy as np
from jax import lax
from jax.experimental import pallas as pl
from jax.experimental.pallas import tpu as pltpu
from jax.sharding import PartitionSpec as P

BINS = 128
LANES = 128
VMEM_BYTES = 56 * 1024 * 1024


def bin_table(length, bins, group):
    position = np.arange(length)[None, :]
    number = np.arange(1, bins + 1)[:, None]
    phase = (position * number % length).astype(np.float32) * np.float32(2.0 * math.pi / length)
    taper = np.float32(0.5) - np.float32(0.5) * np.cos(
        position.astype(np.float32) * np.float32(2.0 * math.pi / length)
    )
    factor = np.float32(math.sqrt(8.0 / (3.0 * length)))
    table = np.stack([taper * np.cos(phase), -(taper * np.sin(phase))]) * factor
    table = table.reshape(2, bins // group, group, length).transpose(1, 0, 2, 3)
    return table.reshape(2 * bins, length).astype(ml_dtypes.bfloat16)


def channel_blocks(channels):
    return [
        (first, min(LANES, channels - first), 2 * first) for first in range(0, channels, LANES)
    ]


def whiten_kernel(group, samples_ref, table_ref, out_ref):
    channels, windows, _ = samples_ref.shape
    bins = table_ref.shape[0] // 2
    table = table_ref[...]
    row = lax.broadcasted_iota(jnp.int32, (bins, 1), 0)
    count = jnp.minimum(row + 2, bins - 1) - jnp.maximum(row - 2, 0) + 1
    share = 1.0 / count.astype(jnp.float32)

    for first, width, lane in channel_blocks(channels):
        blocks = [
            lax.dot_general(
                table,
                samples_ref[first : first + width, w, :],
                (((1,), (1,)), ((), ())),
                preferred_element_type=jnp.float32,
            )
            for w in range(windows)
        ]
        spectrum = jnp.concatenate(blocks, axis=1).astype(jnp.bfloat16).astype(jnp.float32)
        cols = windows * width
        parts = spectrum.reshape(bins // group, 2, group, cols)
        power = (parts[:, 0] * parts[:, 0] + parts[:, 1] * parts[:, 1]).reshape(bins, cols)
        summed = power
        for step in (1, 2):
            summed = summed + jnp.where(row >= step, pltpu.roll(power, step, axis=0), 0.0)
            summed = summed + jnp.where(
                row < bins - step, pltpu.roll(power, bins - step, axis=0), 0.0
            )
        level = jnp.maximum(summed * share, 0.1)
        inverse = lax.rsqrt(level).reshape(bins // group, 1, group, cols)
        whitened = (parts * inverse).reshape(2 * bins, cols).astype(jnp.bfloat16)
        out_ref[:, lane : lane + cols] = whitened


def swap_halves(tile):
    return pltpu.roll(tile, LANES // 2, axis=1)


def outer_kernel(bins, scale, own_ref, other_ref, out_ref, right, left):
    half = LANES // 2
    channels = out_ref.shape[2]
    full = channels // LANES
    step = pl.program_id(1)

    @pl.when(step == 0)
    def _():
        me = lax.axis_index("chan")
        which = pl.program_id(0)
        own = own_ref[:, which].astype(jnp.float32)
        other = other_ref[:, which].astype(jnp.float32)
        rows = own.shape[0] * own.shape[1]
        own = own.reshape(rows, own.shape[2])
        other = other.reshape(rows, other.shape[2])
        block0 = jnp.where(me == 0, own, other)
        block1 = jnp.where(me == 0, other, own)
        row = lax.broadcasted_iota(jnp.int32, (rows, 1), 0)
        first_part = (row // bins) % 2 == 0
        low = lax.broadcasted_iota(jnp.int32, (rows, LANES), 1) < half

        def tiles_of(block, w):
            tiles = [
                block[:, (2 * j + w) * LANES : (2 * j + w + 1) * LANES] for j in range(full)
            ]
            last = block[:, 2 * full * LANES :]
            turned = swap_halves(last)
            both = jnp.where(low, last, turned) if w == 0 else jnp.where(low, turned, last)
            return tiles, both

        for w in range(2):
            at = pl.ds(w * rows, rows)
            tiles, last0 = tiles_of(block0, w)
            tiles1, last1 = tiles_of(block1, w)
            turned = [swap_halves(tile) for tile in tiles1]
            chain = [last0] + turned + [last1]
            tiles = tiles + [
                jnp.where(low, chain[j], chain[j + 1]) for j in range(len(chain) - 1)
            ]
            for j, tile in enumerate(tiles):
                rotated = jnp.where(
                    first_part,
                    -pltpu.roll(tile, rows - bins, axis=0),
                    pltpu.roll(tile, bins, axis=0),
                )
                right[at, j * LANES : (j + 1) * LANES] = tile.astype(jnp.bfloat16)
                right[at, 2 * channels + j * LANES : 2 * channels + (j + 1) * LANES] = (
                    rotated.astype(jnp.bfloat16)
                )
        scaled = own * scale
        for j in range(full):
            for w in range(2):
                lanes = (2 * j + w) * LANES
                left[j * LANES : (j + 1) * LANES, w * rows : (w + 1) * rows] = scaled[
                    :, lanes : lanes + LANES
                ].T
        last = scaled[:, 2 * full * LANES :].T
        for w in range(2):
            left[full * LANES :, w * rows : (w + 1) * rows] = last[w * half : (w + 1) * half]

    depth = left.shape[1]
    lane = lax.broadcasted_iota(jnp.int32, (channels, depth), 1)
    chosen = jnp.where(lane % bins == step, left[...], 0.0).astype(jnp.bfloat16)
    width = 2 * LANES
    for tile in range(4 * channels // width):
        product = jnp.dot(
            chosen,
            right[:, tile * width : (tile + 1) * width],
            preferred_element_type=jnp.float32,
        ).astype(jnp.bfloat16)
        for piece in range(2):
            lanes = tile * width + piece * LANES
            part, lanes = lanes // (2 * channels), lanes % (2 * channels)
            out_ref[part, 0, :, lanes : lanes + LANES] = product[
                :, piece * LANES : (piece + 1) * LANES
            ]


def local(samples):
    local_channels, local_windows, length = samples.shape
    devices = lax.axis_size("freq")
    local_bins = BINS // devices
    windows = local_windows * devices
    bins = min(local_bins, 128 // (2 * devices))
    groups = local_bins // bins
    aligned = bins % 8 == 0
    group = bins if aligned else BINS
    table = jnp.asarray(bin_table(length, BINS, group))
    lanes = local_windows * local_channels
    vmem = pl.BlockSpec(memory_space=pltpu.VMEM)
    params = pltpu.CompilerParams(vmem_limit_bytes=VMEM_BYTES)

    with jax.named_scope("whiten"):
        whitened = pl.pallas_call(
            functools.partial(whiten_kernel, group),
            out_shape=jax.ShapeDtypeStruct((2 * BINS, lanes), jnp.bfloat16),
            in_specs=[vmem, vmem],
            out_specs=vmem,
            compiler_params=params,
            cost_estimate=pl.CostEstimate(
                flops=4 * BINS * lanes * length, bytes_accessed=3 << 20, transcendentals=BINS * lanes
            ),
        )(samples, table)
    if aligned:
        whitened = whitened.reshape(devices, groups, 2 * bins, lanes)
    else:
        whitened = whitened.reshape(2, devices, groups, bins, lanes).transpose(1, 2, 0, 3, 4)
        whitened = whitened.reshape(devices, groups, 2 * bins, lanes)
    own = lax.all_to_all(whitened, "freq", split_axis=0, concat_axis=0, tiled=True)
    if not aligned:
        own = own.transpose(1, 0, 2, 3).reshape(1, groups, devices * 2 * bins, lanes)
    other = lax.ppermute(own, "chan", [(0, 1), (1, 0)])
    depth = local_windows * devices * 2 * bins
    with jax.named_scope("outer_products"):
        out = pl.pallas_call(
            functools.partial(outer_kernel, bins, 1.0 / windows),
            out_shape=jax.ShapeDtypeStruct(
                (2, local_bins, local_channels, 2 * local_channels), jnp.bfloat16
            ),
            grid=(groups, bins),
            in_specs=[vmem, vmem],
            out_specs=pl.BlockSpec(
                (2, 1, local_channels, 2 * local_channels),
                lambda g, k: (0, g * bins + k, 0, 0),
            ),
            scratch_shapes=[
                pltpu.VMEM((depth, 4 * local_channels), jnp.bfloat16),
                pltpu.VMEM((local_channels, depth), jnp.float32),
            ],
            compiler_params=params,
            cost_estimate=pl.CostEstimate(
                flops=8 * local_bins * depth * local_channels * local_channels,
                bytes_accessed=8 * local_bins * local_channels * local_channels,
                transcendentals=0,
            ),
        )(own, other)
    return jnp.transpose(out, (0, 1, 3, 2))


def solution(mesh):
    placed = (P("chan", ("hours", "freq"), None),)
    return jax.shard_map(
        local,
        mesh=mesh,
        in_specs=placed,
        out_specs=P(None, ("hours", "freq"), None, "chan"),
        check_vma=False,
    )
```

time: 169 us -> 57.5 us (0.34)
  matrix products: 65.5 us -> 0 us
  other arithmetic: 45.8 us -> 0 us
  Pallas kernels: 0 us -> 30.6 us
  blocking collectives: 0 us -> 23.8 us
  waiting for transfers between devices: 24.2 us -> 2 us
  local copies, waits for them, and re-layouts: 20.4 us -> 0.81 us
  starting transfers between devices: 12 us -> 0.01 us
    dot_general x4 -> x0, matrix products: 65.5 us -> none  [the longest x1 30.7 us: local(): jnp.einsum('kwb,kwa->kba', every[1], whitened[0], preferred_element_type=...]
    convert_element_type x4 -> x0, other arithmetic: 41.3 us -> none  [the longest x1 41 us: local(): return (jnp.stack([real_part, imag_part]) * scale).astype(jnp.bfloat16)]
    pallas_call x0 -> x2, Pallas kernels: none -> 30.6 us  [the longest x1 21.8 us: local(): pl.pallas_call(functools.partial(outer_kernel, bins, 1.0 / windows), out_...]
    all_to_all x0 -> x1, blocking collectives: none -> 23.8 us  [local(): lax.all_to_all(whitened, 'freq', split_axis=0, concat_axis=0, tiled=True)]
    all_to_all x1 -> x0, waiting for transfers between devices: 17.3 us -> none  [local(): lax.all_to_all(spectrum, 'freq', split_axis=1, concat_axis=2, tiled=True)]
    all_to_all x1 -> x0, starting transfers between devices: 7.28 us -> none  [local(): lax.all_to_all(spectrum, 'freq', split_axis=1, concat_axis=2, tiled=True)]
    slice x4 -> x0, local copies, waits for them, and re-layouts: 5.08 us -> none  [the longest x1 2.6 us: local(): every[0]]
    ppermute x3 -> x1, waiting for transfers between devices: 6.9 us -> 2 us  [local(): other = lax.ppermute(own, 'chan', [(0, 1), (1, 0)])]
  transfers between devices with their start and end apart: 4 -> 1, of which waited for: 4 -> 1; matrix products, arithmetic and copies ran while one was open for 0% -> 0% of each run, Pallas kernels for 0% -> 0%
where the time goes in v1:
time: 57.5 us; the launch traced here: 57.3 us
  Pallas kernels  30.6 us (53%)
  blocking collectives  23.8 us (41%)
  waiting for transfers between devices  2 us (3%)
  local copies, waits for them, and re-layouts  0.81 us (1%)
    all_to_all x1, blocking collectives, local(): lax.all_to_all(whitened, 'freq', split_axis=0, concat_axis=0, tiled=True)  23.8 us
    pallas_call x1, Pallas kernels, local(): pl.pallas_call(functools.partial(outer_kernel, bins, 1.0 / windows), out_...  21.8 us
    pallas_call x1, Pallas kernels, local(): pl.pallas_call(functools.partial(whiten_kernel, group), out_shape=jax.Sha...  8.75 us
    ppermute x1, waiting for transfers between devices, local(): other = lax.ppermute(own, 'chan', [(0, 1), (1, 0)])  2 us
  transfers between devices with their start and end apart: 1, of which 1 were waited for; matrix products, arithmetic and copies ran while one was open for 0% of the time, Pallas kernels for 0%

profile of v1, /device:TPU:0, one launch (start us, length us, event | category | flops | bytes accessed | tf_op | source)
XLA Modules:
  0.0 57.3 jit_solution(3200396085442730953)
XLA Ops:
  0.0 8.7 %whiten.1 = bf16[256,1152]{1,0:T(8,128)(2,1)} custom-call(bf16[576,2,1024]{2,1,0:T(2,128)(2,1)} %samples_ref.1, bf16[256,1024]{1,0:T(8,128)(2,1)} %constant.2.clone.table_ref), custom_call_target="tpu_custom_call" | custom-call | flops 603979776 | bytes 3145728 | tf_op jit(solution)/shard_map/whiten/pallas_call | solution.py:168
  8.7 23.8 %all_to_all.5.own_ref = bf16[8,2,16,1152]{3,2,1,0:T(8,128)(2,1)S(1)} all-to-all(bf16[8,2,16,1152]{3,2,1,0:T(8,128)(2,1)} %bitcast.2), channel_id=1, replica_groups=mesh['hours'=2,'chan'=2,'freq'=8] {'freq'}, dimensions={0} | all-to-all | bytes 1179648 | tf_op jit(solution)/shard_map/all_to_all | solution.py:183
  32.6 0.0 copy-start
  32.6 0.0 collective-permute-start
  32.6 2.0 %collective-permute-done.other_ref = bf16[8,2,16,1152]{3,2,1,0:T(8,128)(2,1)S(1)} collective-permute-done((bf16[8,2,16,1152]{3,2,1,0:T(8,128)(2,1)S(1)}, bf16[8,2,16,1152]{3,2,1,0:T(8,128)(2,1)S(1)}, u32[]{:S(2)}, u32[]{:S(2)}) %collective-permute-start) | collective-permute-done | bytes 589856 | tf_op jit(solution)/shard_map/ppermute | solution.py:186
  34.6 0.0 copy-done
  34.6 0.0 copy-start.1
  34.6 0.8 %copy-done.1 = bf16[8,2,16,1152]{3,2,1,0:T(8,128)(2,1)} copy-done((bf16[8,2,16,1152]{3,2,1,0:T(8,128)(2,1)}, bf16[8,2,16,1152]{3,2,1,0:T(8,128)(2,1)S(1)}, u32[]{:S(2)}) %copy-start.1) | copy-done | bytes 589848
  35.4 21.8 %outer_products.1 = bf16[2,16,576,1152]{3,2,1,0:T(8,128)(2,1)} custom-call(bf16[8,2,16,1152]{3,2,1,0:T(8,128)(2,1)} %copy-done, bf16[8,2,16,1152]{3,2,1,0:T(8,128)(2,1)} %copy-done.1), custom_call_target="tpu_custom_call" | custom-call | flops 10871635968 | bytes 42467328 | tf_op jit(solution)/shard_map/outer_products/pallas_call | solution.py:189
Async XLA Ops:
  32.6 2.0 %copy-start = (bf16[8,2,16,1152]{3,2,1,0:T(8,128)(2,1)}, bf16[8,2,16,1152]{3,2,1,0:T(8,128)(2,1)S(1)}, u32[]{:S(2)}) copy-start(bf16[8,2,16,1152]{3,2,1,0:T(8,128)(2,1)S(1)} %all_to_all.5.own_ref) | copy-start | bytes 1769476
  32.6 2.0 %collective-permute-start = (bf16[8,2,16,1152]{3,2,1,0:T(8,128)(2,1)S(1)}, bf16[8,2,16,1152]{3,2,1,0:T(8,128)(2,1)S(1)}, u32[]{:S(2)}, u32[]{:S(2)}) collective-permute-start(bf16[8,2,16,1152]{3,2,1,0:T(8,128)(2,1)S(1)} %all_to_all.5.own_ref), channel_id=1, source_target_pairs={{0,8},{8,0},{1,9},{9,1},{2,10},{10,2},{3,11},{11,3},{4,12},{12,4},... | collective-permute-start | bytes 1769480 | tf_op jit(solution)/shard_map/ppermute | solution.py:186
  34.6 0.8 %copy-start.1 = (bf16[8,2,16,1152]{3,2,1,0:T(8,128)(2,1)}, bf16[8,2,16,1152]{3,2,1,0:T(8,128)(2,1)S(1)}, u32[]{:S(2)}) copy-start(bf16[8,2,16,1152]{3,2,1,0:T(8,128)(2,1)S(1)} %collective-permute-done.other_ref) | copy-start | bytes 1769476

commit v2 on v1

--- a/solution.py
+++ b/solution.py
@@ -12,7 +12,7 @@
 
 BINS = 128
 LANES = 128
-VMEM_BYTES = 56 * 1024 * 1024
+MIB = 1024 * 1024
 
 
 def bin_table(length, bins, group):
@@ -24,8 +24,8 @@
     )
     factor = np.float32(math.sqrt(8.0 / (3.0 * length)))
     table = np.stack([taper * np.cos(phase), -(taper * np.sin(phase))]) * factor
-    table = table.reshape(2, bins // group, group, length).transpose(1, 0, 2, 3)
-    return table.reshape(2 * bins, length).astype(ml_dtypes.bfloat16)
+    table = table.reshape(2, bins // group, group, length).transpose(3, 1, 0, 2)
+    return table.reshape(length, 2 * bins).astype(ml_dtypes.bfloat16)
 
 
 def channel_blocks(channels):
@@ -34,25 +34,20 @@
     ]
 
 
-def whiten_kernel(group, samples_ref, table_ref, out_ref):
-    channels, windows, _ = samples_ref.shape
-    bins = table_ref.shape[0] // 2
-    table = table_ref[...]
+def whiten_kernel(group, spectrum_ref, *refs):
+    pieces, rows_ref = refs[:-1], refs[-1]
+    windows, channels, columns = spectrum_ref.shape
+    bins = columns // 2
     row = lax.broadcasted_iota(jnp.int32, (bins, 1), 0)
     count = jnp.minimum(row + 2, bins - 1) - jnp.maximum(row - 2, 0) + 1
     share = 1.0 / count.astype(jnp.float32)
 
     for first, width, lane in channel_blocks(channels):
         blocks = [
-            lax.dot_general(
-                table,
-                samples_ref[first : first + width, w, :],
-                (((1,), (1,)), ((), ())),
-                preferred_element_type=jnp.float32,
-            )
+            spectrum_ref[w, first : first + width, :].astype(jnp.float32).T
             for w in range(windows)
         ]
-        spectrum = jnp.concatenate(blocks, axis=1).astype(jnp.bfloat16).astype(jnp.float32)
+        spectrum = jnp.concatenate(blocks, axis=1)
         cols = windows * width
         parts = spectrum.reshape(bins // group, 2, group, cols)
         power = (parts[:, 0] * parts[:, 0] + parts[:, 1] * parts[:, 1]).reshape(bins, cols)
@@ -64,15 +59,25 @@
             )
         level = jnp.maximum(summed * share, 0.1)
         inverse = lax.rsqrt(level).reshape(bins // group, 1, group, cols)
-        whitened = (parts * inverse).reshape(2 * bins, cols).astype(jnp.bfloat16)
-        out_ref[:, lane : lane + cols] = whitened
+        whitened = (parts * inverse).astype(jnp.bfloat16)
+        rows_ref[..., lane : lane + cols] = whitened.reshape(rows_ref.shape[:-1] + (cols,))
+
+    if len(pieces) == 1:
+        pieces[0][...] = rows_ref[...]
+    else:
+        me = lax.axis_index("freq")
+        for m, piece in enumerate(pieces):
+            piece[...] = rows_ref[me ^ m]
 
 
 def swap_halves(tile):
     return pltpu.roll(tile, LANES // 2, axis=1)
 
 
-def outer_kernel(bins, scale, own_ref, other_ref, out_ref, right, left):
+def outer_kernel(bins, scale, *refs):
+    out_ref, right, left = refs[-3:]
+    count = (len(refs) - 3) // 2
+    own_refs, other_refs = refs[:count], refs[count:-3]
     half = LANES // 2
     channels = out_ref.shape[2]
     full = channels // LANES
@@ -82,11 +87,9 @@
     def _():
         me = lax.axis_index("chan")
         which = pl.program_id(0)
-        own = own_ref[:, which].astype(jnp.float32)
-        other = other_ref[:, which].astype(jnp.float32)
-        rows = own.shape[0] * own.shape[1]
-        own = own.reshape(rows, own.shape[2])
-        other = other.reshape(rows, other.shape[2])
+        own = jnp.concatenate([ref[which].astype(jnp.float32) for ref in own_refs])
+        other = jnp.concatenate([ref[which].astype(jnp.float32) for ref in other_refs])
+        rows = own.shape[0]
         block0 = jnp.where(me == 0, own, other)
         block1 = jnp.where(me == 0, other, own)
         row = lax.broadcasted_iota(jnp.int32, (rows, 1), 0)
@@ -133,21 +136,12 @@
             left[full * LANES :, w * rows : (w + 1) * rows] = last[w * half : (w + 1) * half]
 
     depth = left.shape[1]
-    lane = lax.broadcasted_iota(jnp.int32, (channels, depth), 1)
-    chosen = jnp.where(lane % bins == step, left[...], 0.0).astype(jnp.bfloat16)
-    width = 2 * LANES
-    for tile in range(4 * channels // width):
-        product = jnp.dot(
-            chosen,
-            right[:, tile * width : (tile + 1) * width],
-            preferred_element_type=jnp.float32,
-        ).astype(jnp.bfloat16)
-        for piece in range(2):
-            lanes = tile * width + piece * LANES
-            part, lanes = lanes // (2 * channels), lanes % (2 * channels)
-            out_ref[part, 0, :, lanes : lanes + LANES] = product[
-                :, piece * LANES : (piece + 1) * LANES
-            ]
+    lane = lax.broadcasted_iota(jnp.int32, (1, depth), 1)
+    chosen = jnp.where((lane & (bins - 1)) == step, left[...], 0.0).astype(jnp.bfloat16)
+    product = jnp.dot(chosen, right[...], preferred_element_type=jnp.float32)
+    for part in range(2):
+        lanes = part * 2 * channels
+        out_ref[part, 0] = product[:, lanes : lanes + 2 * channels].astype(jnp.bfloat16)
 
 
 def local(samples):
@@ -162,28 +156,35 @@
     table = jnp.asarray(bin_table(length, BINS, group))
     lanes = local_windows * local_channels
     vmem = pl.BlockSpec(memory_space=pltpu.VMEM)
-    params = pltpu.CompilerParams(vmem_limit_bytes=VMEM_BYTES)
-
+
+    spectrum = jnp.einsum("cws,sj->wcj", samples, table, preferred_element_type=jnp.float32)
+    spectrum = spectrum.astype(jnp.bfloat16)
+    pieces = devices if aligned else 1
+    rows = (devices, groups, 2 * bins, lanes) if aligned else (2 * BINS, lanes)
+    piece = rows[1:] if aligned else rows
     with jax.named_scope("whiten"):
         whitened = pl.pallas_call(
             functools.partial(whiten_kernel, group),
-            out_shape=jax.ShapeDtypeStruct((2 * BINS, lanes), jnp.bfloat16),
-            in_specs=[vmem, vmem],
-            out_specs=vmem,
-            compiler_params=params,
+            out_shape=[jax.ShapeDtypeStruct(piece, jnp.bfloat16)] * pieces,
+            in_specs=[vmem],
+            out_specs=[vmem] * pieces,
+            scratch_shapes=[pltpu.VMEM(rows, jnp.bfloat16)],
+            compiler_params=pltpu.CompilerParams(vmem_limit_bytes=16 * MIB),
             cost_estimate=pl.CostEstimate(
-                flops=4 * BINS * lanes * length, bytes_accessed=3 << 20, transcendentals=BINS * lanes
-            ),
-        )(samples, table)
+                flops=40 * BINS * lanes, bytes_accessed=12 * BINS * lanes, transcendentals=BINS * lanes
+            ),
+        )(spectrum)
     if aligned:
-        whitened = whitened.reshape(devices, groups, 2 * bins, lanes)
+        own = [whitened[0]] + [None] * (devices - 1)
+        for m in reversed(range(1, devices)):
+            pairs = [(source, source ^ m) for source in range(devices)]
+            own[m] = lax.ppermute(whitened[m], "freq", pairs)
     else:
-        whitened = whitened.reshape(2, devices, groups, bins, lanes).transpose(1, 2, 0, 3, 4)
-        whitened = whitened.reshape(devices, groups, 2 * bins, lanes)
-    own = lax.all_to_all(whitened, "freq", split_axis=0, concat_axis=0, tiled=True)
-    if not aligned:
-        own = own.transpose(1, 0, 2, 3).reshape(1, groups, devices * 2 * bins, lanes)
-    other = lax.ppermute(own, "chan", [(0, 1), (1, 0)])
+        rows = whitened[0].reshape(2, devices, groups, bins, lanes).transpose(1, 2, 0, 3, 4)
+        rows = rows.reshape(devices, groups, 2 * bins, lanes)
+        rows = lax.all_to_all(rows, "freq", split_axis=0, concat_axis=0, tiled=True)
+        own = [rows.transpose(1, 0, 2, 3).reshape(groups, devices * 2 * bins, lanes)]
+    other = [lax.ppermute(value, "chan", [(0, 1), (1, 0)]) for value in own]
     depth = local_windows * devices * 2 * bins
     with jax.named_scope("outer_products"):
         out = pl.pallas_call(
@@ -192,7 +193,7 @@
                 (2, local_bins, local_channels, 2 * local_channels), jnp.bfloat16
             ),
             grid=(groups, bins),
-            in_specs=[vmem, vmem],
+            in_specs=[vmem] * (2 * pieces),
             out_specs=pl.BlockSpec(
                 (2, 1, local_channels, 2 * local_channels),
                 lambda g, k: (0, g * bins + k, 0, 0),
@@ -201,13 +202,13 @@
                 pltpu.VMEM((depth, 4 * local_channels), jnp.bfloat16),
                 pltpu.VMEM((local_channels, depth), jnp.float32),
             ],
-            compiler_params=params,
+            compiler_params=pltpu.CompilerParams(vmem_limit_bytes=32 * MIB),
             cost_estimate=pl.CostEstimate(
                 flops=8 * local_bins * depth * local_channels * local_channels,
                 bytes_accessed=8 * local_bins * local_channels * local_channels,
                 transcendentals=0,
             ),
-        )(own, other)
+        )(*own, *other)
     return jnp.transpose(out, (0, 1, 3, 2))
 
 

time: 57.5 us -> 47.3 us (0.82)
  blocking collectives: 23.8 us -> 0 us
  starting transfers between devices: 0.01 us -> 14.4 us
  Pallas kernels: 30.6 us -> 21.4 us
  waiting for transfers between devices: 2 us -> 7.73 us
  matrix products: 0 us -> 1.83 us
  local copies, waits for them, and re-layouts: 0.81 us -> 1.67 us
    all_to_all x1 -> x0, blocking collectives: 23.8 us -> none  [local(): lax.all_to_all(whitened, 'freq', split_axis=0, concat_axis=0, tiled=True)]
    ppermute x1 -> x15, starting transfers between devices: 0.01 us -> 14.4 us  [the longest x7 12.5 us: local(): own[m] = lax.ppermute(whitened[m], 'freq', pairs)]
    pallas_call x1, Pallas kernels: 8.75 us -> 0.75 us  [local(): pl.pallas_call(functools.partial(whiten_kernel, group), out_shape=[jax.Sh...]
    ppermute x1 -> x15, waiting for transfers between devices: 2 us -> 7.73 us  [the longest x7 6.58 us: local(): own[m] = lax.ppermute(whitened[m], 'freq', pairs)]
    dot_general x0 -> x1, matrix products: none -> 1.83 us  [local(): jnp.einsum('cws,sj->wcj', samples, table, preferred_element_type=jnp.floa...]
    pallas_call x1, Pallas kernels: 21.8 us -> 20.6 us  [local(): pl.pallas_call(functools.partial(outer_kernel, bins, 1.0 / windows), out_...]
    unnamed x4 -> x2, local copies, waits for them, and re-layouts: 0.81 us -> 1.67 us
  transfers between devices with their start and end apart: 1 -> 15, of which waited for: 1 -> 6; matrix products, arithmetic and copies ran while one was open for 0% -> 0% of each run, Pallas kernels for 0% -> 0%
where the time goes in v2:
time: 47.3 us; the launch traced here: 47.1 us
  Pallas kernels  21.4 us (45%)
  starting transfers between devices  14.4 us (30%)
  waiting for transfers between devices  7.73 us (16%)
  matrix products  1.83 us (4%)
  local copies, waits for them, and re-layouts  1.67 us (4%)
    pallas_call x1, Pallas kernels, local(): pl.pallas_call(functools.partial(outer_kernel, bins, 1.0 / windows), out_...  20.6 us
    ppermute x7, starting transfers between devices, local(): own[m] = lax.ppermute(whitened[m], 'freq', pairs)  12.5 us
    ppermute x7, waiting for transfers between devices, local(): own[m] = lax.ppermute(whitened[m], 'freq', pairs)  6.58 us
    ppermute x8, starting transfers between devices, local(): other = [lax.ppermute(value, 'chan', [(0, 1), (1, 0)]) for value in own]  1.93 us
    dot_general x1, matrix products, local(): jnp.einsum('cws,sj->wcj', samples, table, preferred_element_type=jnp.floa...  1.83 us
    unnamed x2, local copies, waits for them, and re-layouts  1.67 us
    ppermute x8, waiting for transfers between devices, local(): other = [lax.ppermute(value, 'chan', [(0, 1), (1, 0)]) for value in own]  1.14 us
  transfers between devices with their start and end apart: 15, of which 6 were waited for; matrix products, arithmetic and copies ran while one was open for 0% of the time, Pallas kernels for 0%

profile of v2, /device:TPU:0, one launch (start us, length us, event | category | flops | bytes accessed | tf_op | source)
XLA Modules:
  0.0 47.1 jit_solution(7863937298709569409)
XLA Ops:
  0.0 1.7 %copy-done = bf16[576,2,1024]{2,1,0:T(2,128)(2,1)S(1)} copy-done((bf16[576,2,1024]{2,1,0:T(2,128)(2,1)S(1)}, bf16[576,2,1024]{2,1,0:T(2,128)(2,1)}, u32[]{:S(2)}) %copy-start) | copy-done | bytes 2359320
  1.7 1.8 %fusion.5.spectrum_ref = bf16[2,576,256]{2,1,0:T(8,128)(2,1)S(1)} fusion(bf16[1024,256,1]{1,0,2:T(8,128)(2,1)} %constant.4, bf16[576,2,1024]{2,1,0:T(2,128)(2,1)S(1)} %copy-done), kind=kOutput, calls=%fused_computation.3 | convolution fusion | flops 604274688 | bytes 3473408 | tf_op jit(solution)/shard_map/cws,sj->wcj/dot_general | solution.py:160
  3.5 0.7 %whiten.1 = (bf16[2,16,1152]{2,1,0:T(8,128)(2,1)S(1)}, bf16[2,16,1152]{2,1,0:T(8,128)(2,1)S(1)}, bf16[2,16,1152]{2,1,0:T(8,128)(2,1)S(1)}, bf16[2,16,1152]{2,1,0...) custom-call(bf16[2,576,256]{2,1,0:T(8,128)(2,1)S(1)} %fusion.5.spect, ...), custom_call_target="tpu_custom_call" | custom-call | flops 5898240 | bytes 1769472 | tf_op jit(solution)/shard_map/whiten/pallas_call | solution.py:166
  4.3 3.0 %collective-permute-start = (bf16[2,16,1152]{2,1,0:T(8,128)(2,1)S(1)}, bf16[2,16,1152]{2,1,0:T(8,128)(2,1)S(1)}, u32[]{:S(2)}, u32[]{:S(2)}) collective-permute-start(bf16[2,16,1152]{2,1,0:T(8,128)(2,1)S(1)} %get-tuple-element.14), channel_id=1, source_target_pairs={{0,1},{1,0},{2,3},{3,2},{4,5},{5,4},{6,7},{7,6},{8,9},{9,8},{10,11... | collective-permute-start | bytes 221192 | tf_op jit(solution)/shard_map/ppermute | solution.py:181
  7.3 1.6 %collective-permute-start.1 = (bf16[2,16,1152]{2,1,0:T(8,128)(2,1)S(1)}, bf16[2,16,1152]{2,1,0:T(8,128)(2,1)S(1)}, u32[]{:S(2)}, u32[]{:S(2)}) collective-permute-start(bf16[2,16,1152]{2,1,0:T(8,128)(2,1)S(1)} %get-tuple-element.15), channel_id=1, source_target_pairs={{0,2},{1,3},{2,0},{3,1},{4,6},{5,7},{6,4},{7,5},{8,10},{9,11},{10,... | collective-permute-start | bytes 221192 | tf_op jit(solution)/shard_map/ppermute | solution.py:181
  8.9 0.0 collective-permute-start.2
  8.9 3.0 %collective-permute-start.3 = (bf16[2,16,1152]{2,1,0:T(8,128)(2,1)S(1)}, bf16[2,16,1152]{2,1,0:T(8,128)(2,1)S(1)}, u32[]{:S(2)}, u32[]{:S(2)}) collective-permute-start(bf16[2,16,1152]{2,1,0:T(8,128)(2,1)S(1)} %get-tuple-element.17), channel_id=1, source_target_pairs={{0,4},{1,5},{2,6},{3,7},{4,0},{5,1},{6,2},{7,3},{8,12},{9,13},{10,... | collective-permute-start | bytes 221192 | tf_op jit(solution)/shard_map/ppermute | solution.py:181
  11.8 1.3 %collective-permute-start.4 = (bf16[2,16,1152]{2,1,0:T(8,128)(2,1)S(1)}, bf16[2,16,1152]{2,1,0:T(8,128)(2,1)S(1)}, u32[]{:S(2)}, u32[]{:S(2)}) collective-permute-start(bf16[2,16,1152]{2,1,0:T(8,128)(2,1)S(1)} %get-tuple-element.18), channel_id=1, source_target_pairs={{0,5},{1,4},{2,7},{3,6},{4,1},{5,0},{6,3},{7,2},{8,13},{9,12},{10,... | collective-permute-start | bytes 221192 | tf_op jit(solution)/shard_map/ppermute | solution.py:181
  13.1 0.0 collective-permute-done.refs_1_
  13.1 3.6 %collective-permute-start.5 = (bf16[2,16,1152]{2,1,0:T(8,128)(2,1)S(1)}, bf16[2,16,1152]{2,1,0:T(8,128)(2,1)S(1)}, u32[]{:S(2)}, u32[]{:S(2)}) collective-permute-start(bf16[2,16,1152]{2,1,0:T(8,128)(2,1)S(1)} %get-tuple-element.19), channel_id=1, source_target_pairs={{0,6},{1,7},{2,4},{3,5},{4,2},{5,3},{6,0},{7,1},{8,14},{9,15},{10,... | collective-permute-start | bytes 221192 | tf_op jit(solution)/shard_map/ppermute | solution.py:181
  16.7 0.0 collective-permute-done.1.refs_2_
  16.7 0.0 collective-permute-start.6
  16.8 0.0 collective-permute-done.2.refs_3_
  16.8 0.1 collective-permute-start.7
  16.8 0.0 collective-permute-done.3.refs_4_
  16.8 0.5 %collective-permute-start.8 = (bf16[2,16,1152]{2,1,0:T(8,128)(2,1)S(1)}, bf16[2,16,1152]{2,1,0:T(8,128)(2,1)S(1)}, u32[]{:S(2)}, u32[]{:S(2)}) collective-permute-start(bf16[2,16,1152]{2,1,0:T(8,128)(2,1)S(1)} %collective-permute-done.refs_1_), channel_id=1, source_target_pairs={{0,8},{8,0},{1,9},{9,1},{2,10},{10,2},{3,11},{11,3},{4,12},{12,4},... | collective-permute-start | bytes 221192 | tf_op jit(solution)/shard_map/ppermute | solution.py:187
  17.3 6.6 %collective-permute-done.4.refs_5_ = bf16[2,16,1152]{2,1,0:T(8,128)(2,1)S(1)} collective-permute-done((bf16[2,16,1152]{2,1,0:T(8,128)(2,1)S(1)}, bf16[2,16,1152]{2,1,0:T(8,128)(2,1)S(1)}, u32[]{:S(2)}, u32[]{:S(2)}) %collective-permute-start.4) | collective-permute-done | bytes 73760 | tf_op jit(solution)/shard_map/ppermute | solution.py:181
  23.9 0.0 collective-permute-start.9
  23.9 0.0 collective-permute-done.5.refs_6_
  23.9 0.5 %collective-permute-start.10 = (bf16[2,16,1152]{2,1,0:T(8,128)(2,1)S(1)}, bf16[2,16,1152]{2,1,0:T(8,128)(2,1)S(1)}, u32[]{:S(2)}, u32[]{:S(2)}) collective-permute-start(bf16[2,16,1152]{2,1,0:T(8,128)(2,1)S(1)} %collective-permute-done.2.refs_3_), channel_id=1, source_target_pairs={{0,8},{8,0},{1,9},{9,1},{2,10},{10,2},{3,11},{11,3},{4,12},{12,4},... | collective-permute-start | bytes 221192 | tf_op jit(solution)/shard_map/ppermute | solution.py:187
  24.4 0.0 collective-permute-done.6.refs_7_
  24.4 0.1 collective-permute-start.11
  24.5 0.4 collective-permute-start.12
  24.9 0.0 collective-permute-done.8.refs_9_
  24.9 0.1 collective-permute-start.13
  25.0 0.2 collective-permute-done.9.refs_10_
  25.2 0.3 collective-permute-start.14
  25.5 0.2 collective-permute-done.11.refs_12_
  25.7 0.2 collective-permute-done.12.refs_13_
  25.9 0.4 collective-permute-done.13.refs_14_
  26.2 0.2 collective-permute-done.14.refs_15_
  26.4 20.6 %outer_products.1 = bf16[2,16,576,1152]{3,2,1,0:T(8,128)(2,1)} custom-call(bf16[2,16,1152]{2,1,0:T(8,128)(2,1)S(1)} %get-tuple-element.13.refs_0_, bf16[2,16,1152]{2,1,0:T(8,128)(2,1)S(1)} %collective-permute-done.refs_1_, bf16[2,16,1152]{2,1,0:T(8,128)(2,1)S(1)} %collective-permute-done.1.refs_2_, bf16[2,16,1152]{2,1,0:T(8,128)(2,1)S(1)} %collective-permute-done.2.refs_3_, ...), custom_call_target="tpu_custom_call" | custom-call | flops 10871635968 | bytes 42467328 | tf_op jit(solution)/shard_map/outer_products/pallas_call | solution.py:190
  (3 shorter events, 0.0 us)
Async XLA Ops:
  0.0 1.7 %copy-start = (bf16[576,2,1024]{2,1,0:T(2,128)(2,1)S(1)}, bf16[576,2,1024]{2,1,0:T(2,128)(2,1)}, u32[]{:S(2)}) copy-start(bf16[576,2,1024]{2,1,0:T(2,128)(2,1)} %param.2) | copy-start | bytes 7077892
  4.3 8.9 %collective-permute-start = (bf16[2,16,1152]{2,1,0:T(8,128)(2,1)S(1)}, bf16[2,16,1152]{2,1,0:T(8,128)(2,1)S(1)}, u32[]{:S(2)}, u32[]{:S(2)}) collective-permute-start(bf16[2,16,1152]{2,1,0:T(8,128)(2,1)S(1)} %get-tuple-element.14), channel_id=1, source_target_pairs={{0,1},{1,0},{2,3},{3,2},{4,5},{5,4},{6,7},{7,6},{8,9},{9,8},{10,11... | collective-permute-start | bytes 221192 | tf_op jit(solution)/shard_map/ppermute | solution.py:181
  7.3 9.5 %collective-permute-start.1 = (bf16[2,16,1152]{2,1,0:T(8,128)(2,1)S(1)}, bf16[2,16,1152]{2,1,0:T(8,128)(2,1)S(1)}, u32[]{:S(2)}, u32[]{:S(2)}) collective-permute-start(bf16[2,16,1152]{2,1,0:T(8,128)(2,1)S(1)} %get-tuple-element.15), channel_id=1, source_target_pairs={{0,2},{1,3},{2,0},{3,1},{4,6},{5,7},{6,4},{7,5},{8,10},{9,11},{10,... | collective-permute-start | bytes 221192 | tf_op jit(solution)/shard_map/ppermute | solution.py:181
  8.9 7.9 %collective-permute-start.2 = (bf16[2,16,1152]{2,1,0:T(8,128)(2,1)S(1)}, bf16[2,16,1152]{2,1,0:T(8,128)(2,1)S(1)}, u32[]{:S(2)}, u32[]{:S(2)}) collective-permute-start(bf16[2,16,1152]{2,1,0:T(8,128)(2,1)S(1)} %get-tuple-element.16), channel_id=1, source_target_pairs={{0,3},{1,2},{2,1},{3,0},{4,7},{5,6},{6,5},{7,4},{8,11},{9,10},{10,... | collective-permute-start | bytes 221192 | tf_op jit(solution)/shard_map/ppermute | solution.py:181
  8.9 8.0 %collective-permute-start.3 = (bf16[2,16,1152]{2,1,0:T(8,128)(2,1)S(1)}, bf16[2,16,1152]{2,1,0:T(8,128)(2,1)S(1)}, u32[]{:S(2)}, u32[]{:S(2)}) collective-permute-start(bf16[2,16,1152]{2,1,0:T(8,128)(2,1)S(1)} %get-tuple-element.17), channel_id=1, source_target_pairs={{0,4},{1,5},{2,6},{3,7},{4,0},{5,1},{6,2},{7,3},{8,12},{9,13},{10,... | collective-permute-start | bytes 221192 | tf_op jit(solution)/shard_map/ppermute | solution.py:181
  11.8 12.1 %collective-permute-start.4 = (bf16[2,16,1152]{2,1,0:T(8,128)(2,1)S(1)}, bf16[2,16,1152]{2,1,0:T(8,128)(2,1)S(1)}, u32[]{:S(2)}, u32[]{:S(2)}) collective-permute-start(bf16[2,16,1152]{2,1,0:T(8,128)(2,1)S(1)} %get-tuple-element.18), channel_id=1, source_target_pairs={{0,5},{1,4},{2,7},{3,6},{4,1},{5,0},{6,3},{7,2},{8,13},{9,12},{10,... | collective-permute-start | bytes 221192 | tf_op jit(solution)/shard_map/ppermute | solution.py:181
  13.1 10.8 %collective-permute-start.5 = (bf16[2,16,1152]{2,1,0:T(8,128)(2,1)S(1)}, bf16[2,16,1152]{2,1,0:T(8,128)(2,1)S(1)}, u32[]{:S(2)}, u32[]{:S(2)}) collective-permute-start(bf16[2,16,1152]{2,1,0:T(8,128)(2,1)S(1)} %get-tuple-element.19), channel_id=1, source_target_pairs={{0,6},{1,7},{2,4},{3,5},{4,2},{5,3},{6,0},{7,1},{8,14},{9,15},{10,... | collective-permute-start | bytes 221192 | tf_op jit(solution)/shard_map/ppermute | solution.py:181
  16.7 7.7 %collective-permute-start.6 = (bf16[2,16,1152]{2,1,0:T(8,128)(2,1)S(1)}, bf16[2,16,1152]{2,1,0:T(8,128)(2,1)S(1)}, u32[]{:S(2)}, u32[]{:S(2)}) collective-permute-start(bf16[2,16,1152]{2,1,0:T(8,128)(2,1)S(1)} %get-tuple-element.20), channel_id=1, source_target_pairs={{0,7},{1,6},{2,5},{3,4},{4,3},{5,2},{6,1},{7,0},{8,15},{9,14},{10,... | collective-permute-start | bytes 221192 | tf_op jit(solution)/shard_map/ppermute | solution.py:181
  16.8 7.7 %collective-permute-start.7 = (bf16[2,16,1152]{2,1,0:T(8,128)(2,1)S(1)}, bf16[2,16,1152]{2,1,0:T(8,128)(2,1)S(1)}, u32[]{:S(2)}, u32[]{:S(2)}) collective-permute-start(bf16[2,16,1152]{2,1,0:T(8,128)(2,1)S(1)} %get-tuple-element.13.refs_0_), channel_id=1, source_target_pairs={{0,8},{8,0},{1,9},{9,1},{2,10},{10,2},{3,11},{11,3},{4,12},{12,4},... | collective-permute-start | bytes 221192 | tf_op jit(solution)/shard_map/ppermute | solution.py:187
  16.8 8.1 %collective-permute-start.8 = (bf16[2,16,1152]{2,1,0:T(8,128)(2,1)S(1)}, bf16[2,16,1152]{2,1,0:T(8,128)(2,1)S(1)}, u32[]{:S(2)}, u32[]{:S(2)}) collective-permute-start(bf16[2,16,1152]{2,1,0:T(8,128)(2,1)S(1)} %collective-permute-done.refs_1_), channel_id=1, source_target_pairs={{0,8},{8,0},{1,9},{9,1},{2,10},{10,2},{3,11},{11,3},{4,12},{12,4},... | collective-permute-start | bytes 221192 | tf_op jit(solution)/shard_map/ppermute | solution.py:187
  23.9 1.3 %collective-permute-start.9 = (bf16[2,16,1152]{2,1,0:T(8,128)(2,1)S(1)}, bf16[2,16,1152]{2,1,0:T(8,128)(2,1)S(1)}, u32[]{:S(2)}, u32[]{:S(2)}) collective-permute-start(bf16[2,16,1152]{2,1,0:T(8,128)(2,1)S(1)} %collective-permute-done.1.refs_2_), channel_id=1, source_target_pairs={{0,8},{8,0},{1,9},{9,1},{2,10},{10,2},{3,11},{11,3},{4,12},{12,4},... | collective-permute-start | bytes 221192 | tf_op jit(solution)/shard_map/ppermute | solution.py:187
  23.9 1.5 %collective-permute-start.10 = (bf16[2,16,1152]{2,1,0:T(8,128)(2,1)S(1)}, bf16[2,16,1152]{2,1,0:T(8,128)(2,1)S(1)}, u32[]{:S(2)}, u32[]{:S(2)}) collective-permute-start(bf16[2,16,1152]{2,1,0:T(8,128)(2,1)S(1)} %collective-permute-done.2.refs_3_), channel_id=1, source_target_pairs={{0,8},{8,0},{1,9},{9,1},{2,10},{10,2},{3,11},{11,3},{4,12},{12,4},... | collective-permute-start | bytes 221192 | tf_op jit(solution)/shard_map/ppermute | solution.py:187
  24.4 1.3 %collective-permute-start.11 = (bf16[2,16,1152]{2,1,0:T(8,128)(2,1)S(1)}, bf16[2,16,1152]{2,1,0:T(8,128)(2,1)S(1)}, u32[]{:S(2)}, u32[]{:S(2)}) collective-permute-start(bf16[2,16,1152]{2,1,0:T(8,128)(2,1)S(1)} %collective-permute-done.3.refs_4_), channel_id=1, source_target_pairs={{0,8},{8,0},{1,9},{9,1},{2,10},{10,2},{3,11},{11,3},{4,12},{12,4},... | collective-permute-start | bytes 221192 | tf_op jit(solution)/shard_map/ppermute | solution.py:187
  24.5 1.4 %collective-permute-start.12 = (bf16[2,16,1152]{2,1,0:T(8,128)(2,1)S(1)}, bf16[2,16,1152]{2,1,0:T(8,128)(2,1)S(1)}, u32[]{:S(2)}, u32[]{:S(2)}) collective-permute-start(bf16[2,16,1152]{2,1,0:T(8,128)(2,1)S(1)} %collective-permute-done.4.refs_5_), channel_id=1, source_target_pairs={{0,8},{8,0},{1,9},{9,1},{2,10},{10,2},{3,11},{11,3},{4,12},{12,4},... | collective-permute-start | bytes 221192 | tf_op jit(solution)/shard_map/ppermute | solution.py:187
  24.9 1.3 %collective-permute-start.13 = (bf16[2,16,1152]{2,1,0:T(8,128)(2,1)S(1)}, bf16[2,16,1152]{2,1,0:T(8,128)(2,1)S(1)}, u32[]{:S(2)}, u32[]{:S(2)}) collective-permute-start(bf16[2,16,1152]{2,1,0:T(8,128)(2,1)S(1)} %collective-permute-done.5.refs_6_), channel_id=1, source_target_pairs={{0,8},{8,0},{1,9},{9,1},{2,10},{10,2},{3,11},{11,3},{4,12},{12,4},... | collective-permute-start | bytes 221192 | tf_op jit(solution)/shard_map/ppermute | solution.py:187
  25.2 1.3 %collective-permute-start.14 = (bf16[2,16,1152]{2,1,0:T(8,128)(2,1)S(1)}, bf16[2,16,1152]{2,1,0:T(8,128)(2,1)S(1)}, u32[]{:S(2)}, u32[]{:S(2)}) collective-permute-start(bf16[2,16,1152]{2,1,0:T(8,128)(2,1)S(1)} %collective-permute-done.6.refs_7_), channel_id=1, source_target_pairs={{0,8},{8,0},{1,9},{9,1},{2,10},{10,2},{3,11},{11,3},{4,12},{12,4},... | collective-permute-start | bytes 221192 | tf_op jit(solution)/shard_map/ppermute | solution.py:187

commit v3 on v2

--- a/solution.py
+++ b/solution.py
@@ -34,7 +34,7 @@
     ]
 
 
-def whiten_kernel(group, spectrum_ref, *refs):
+def whiten_kernel(group, masks, spectrum_ref, *refs):
     pieces, rows_ref = refs[:-1], refs[-1]
     windows, channels, columns = spectrum_ref.shape
     bins = columns // 2
@@ -66,8 +66,8 @@
         pieces[0][...] = rows_ref[...]
     else:
         me = lax.axis_index("freq")
-        for m, piece in enumerate(pieces):
-            piece[...] = rows_ref[me ^ m]
+        for mask, piece in zip(masks, pieces):
+            piece[...] = rows_ref[me ^ mask]
 
 
 def swap_halves(tile):
@@ -75,13 +75,29 @@
 
 
 def outer_kernel(bins, scale, *refs):
-    out_ref, right, left = refs[-3:]
-    count = (len(refs) - 3) // 2
-    own_refs, other_refs = refs[:count], refs[count:-3]
+    out_ref, right, left, slots, sems = refs[-5:]
+    count = (len(refs) - 5) // 2
+    own_refs, other_refs = refs[:count], refs[count:-5]
     half = LANES // 2
     channels = out_ref.shape[2]
     full = channels // LANES
     step = pl.program_id(1)
+    now = pl.program_id(0) * bins + step
+    steps = pl.num_programs(0) * bins
+    depth_of_slots, cuts = sems.shape[:2]
+    size = channels // cuts
+
+    def copy(when, cut, part):
+        slot = lax.rem(when, depth_of_slots)
+        at = pl.ds(cut * size, size)
+        return pltpu.make_async_copy(
+            slots.at[slot, part, at], out_ref.at[part, when, at], sems.at[slot, cut, part]
+        )
+
+    def wait_for(when):
+        for cut in range(cuts):
+            for part in range(2):
+                copy(when, cut, part).wait()
 
     @pl.when(step == 0)
     def _():
@@ -138,10 +154,23 @@
     depth = left.shape[1]
     lane = lax.broadcasted_iota(jnp.int32, (1, depth), 1)
     chosen = jnp.where((lane & (bins - 1)) == step, left[...], 0.0).astype(jnp.bfloat16)
-    product = jnp.dot(chosen, right[...], preferred_element_type=jnp.float32)
-    for part in range(2):
-        lanes = part * 2 * channels
-        out_ref[part, 0] = product[:, lanes : lanes + 2 * channels].astype(jnp.bfloat16)
+    @pl.when(now >= depth_of_slots)
+    def _():
+        wait_for(now - depth_of_slots)
+
+    slot = lax.rem(now, depth_of_slots)
+    for cut in range(cuts):
+        at = slice(cut * size, (cut + 1) * size)
+        product = jnp.dot(chosen[at], right[...], preferred_element_type=jnp.float32)
+        for part in range(2):
+            lanes = part * 2 * channels
+            slots[slot, part, at] = product[:, lanes : lanes + 2 * channels].astype(jnp.bfloat16)
+            copy(now, cut, part).start()
+
+    @pl.when(now == steps - 1)
+    def _():
+        for back in reversed(range(depth_of_slots)):
+            wait_for(now - back)
 
 
 def local(samples):
@@ -157,14 +186,16 @@
     lanes = local_windows * local_channels
     vmem = pl.BlockSpec(memory_space=pltpu.VMEM)
 
+    memory = pl.BlockSpec(memory_space=pl.ANY)
     spectrum = jnp.einsum("cws,sj->wcj", samples, table, preferred_element_type=jnp.float32)
     spectrum = spectrum.astype(jnp.bfloat16)
-    pieces = devices if aligned else 1
+    masks = [1, 2, *range(devices - 1, 2, -1), 0] if aligned else [0]
+    pieces = len(masks)
     rows = (devices, groups, 2 * bins, lanes) if aligned else (2 * BINS, lanes)
     piece = rows[1:] if aligned else rows
     with jax.named_scope("whiten"):
         whitened = pl.pallas_call(
-            functools.partial(whiten_kernel, group),
+            functools.partial(whiten_kernel, group, masks),
             out_shape=[jax.ShapeDtypeStruct(piece, jnp.bfloat16)] * pieces,
             in_specs=[vmem],
             out_specs=[vmem] * pieces,
@@ -175,10 +206,10 @@
             ),
         )(spectrum)
     if aligned:
-        own = [whitened[0]] + [None] * (devices - 1)
-        for m in reversed(range(1, devices)):
-            pairs = [(source, source ^ m) for source in range(devices)]
-            own[m] = lax.ppermute(whitened[m], "freq", pairs)
+        own = []
+        for mask, value in zip(masks, whitened):
+            pairs = [(source, source ^ mask) for source in range(devices)]
+            own.append(lax.ppermute(value, "freq", pairs) if mask else value)
     else:
         rows = whitened[0].reshape(2, devices, groups, bins, lanes).transpose(1, 2, 0, 3, 4)
         rows = rows.reshape(devices, groups, 2 * bins, lanes)
@@ -194,13 +225,12 @@
             ),
             grid=(groups, bins),
             in_specs=[vmem] * (2 * pieces),
-            out_specs=pl.BlockSpec(
-                (2, 1, local_channels, 2 * local_channels),
-                lambda g, k: (0, g * bins + k, 0, 0),
-            ),
+            out_specs=memory,
             scratch_shapes=[
                 pltpu.VMEM((depth, 4 * local_channels), jnp.bfloat16),
                 pltpu.VMEM((local_channels, depth), jnp.float32),
+                pltpu.VMEM((3, 2, local_channels, 2 * local_channels), jnp.bfloat16),
+                pltpu.SemaphoreType.DMA((3, 2, 2)),
             ],
             compiler_params=pltpu.CompilerParams(vmem_limit_bytes=32 * MIB),
             cost_estimate=pl.CostEstimate(

time: 47.3 us -> 43.8 us (0.926)
  Pallas kernels: 21.4 us -> 17.7 us
  waiting for transfers between devices: 7.73 us -> 8.97 us
  starting transfers between devices: 14.4 us -> 13.5 us
    pallas_call x1, Pallas kernels: 20.6 us -> 16.9 us  [local(): pl.pallas_call(functools.partial(outer_kernel, bins, 1.0 / windows), out_...]
    ppermute x7, waiting for transfers between devices: 6.58 us -> 7.77 us  [local(): own.append(lax.ppermute(value, 'freq', pairs) if mask else value)]
    ppermute x8, starting transfers between devices: 1.93 us -> 1.1 us  [local(): other = [lax.ppermute(value, 'chan', [(0, 1), (1, 0)]) for value in own]]
  transfers between devices with their start and end apart: 15 -> 15, of which waited for: 6 -> 8; matrix products, arithmetic and copies ran while one was open for 0% -> 0% of each run, Pallas kernels for 0% -> 0%
where the time goes in v3:
time: 43.8 us; the launch traced here: 43.7 us
  Pallas kernels  17.7 us (40%)
  starting transfers between devices  13.5 us (31%)
  waiting for transfers between devices  8.97 us (20%)
  matrix products  1.83 us (4%)
  local copies, waits for them, and re-layouts  1.67 us (4%)
    pallas_call x1, Pallas kernels, local(): pl.pallas_call(functools.partial(outer_kernel, bins, 1.0 / windows), out_...  16.9 us
    ppermute x7, starting transfers between devices, local(): own.append(lax.ppermute(value, 'freq', pairs) if mask else value)  12.4 us
    ppermute x7, waiting for transfers between devices, local(): own.append(lax.ppermute(value, 'freq', pairs) if mask else value)  7.77 us
    dot_general x1, matrix products, local(): jnp.einsum('cws,sj->wcj', samples, table, preferred_element_type=jnp.floa...  1.83 us
    unnamed x2, local copies, waits for them, and re-layouts  1.67 us
    ppermute x8, waiting for transfers between devices, local(): other = [lax.ppermute(value, 'chan', [(0, 1), (1, 0)]) for value in own]  1.2 us
    ppermute x8, starting transfers between devices, local(): other = [lax.ppermute(value, 'chan', [(0, 1), (1, 0)]) for value in own]  1.1 us
  transfers between devices with their start and end apart: 15, of which 8 were waited for; matrix products, arithmetic and copies ran while one was open for 0% of the time, Pallas kernels for 0%

profile of v3, /device:TPU:0, one launch (start us, length us, event | category | flops | bytes accessed | tf_op | source)
XLA Modules:
  0.0 43.7 jit_solution(960265840347919898)
XLA Ops:
  0.0 1.7 %copy-done = bf16[576,2,1024]{2,1,0:T(2,128)(2,1)S(1)} copy-done((bf16[576,2,1024]{2,1,0:T(2,128)(2,1)S(1)}, bf16[576,2,1024]{2,1,0:T(2,128)(2,1)}, u32[]{:S(2)}) %copy-start) | copy-done | bytes 2359320
  1.7 1.8 %fusion.5.spectrum_ref = bf16[2,576,256]{2,1,0:T(8,128)(2,1)S(1)} fusion(bf16[1024,256,1]{1,0,2:T(8,128)(2,1)} %constant.4, bf16[576,2,1024]{2,1,0:T(2,128)(2,1)S(1)} %copy-done), kind=kOutput, calls=%fused_computation.3 | convolution fusion | flops 604274688 | bytes 3473408 | tf_op jit(solution)/shard_map/cws,sj->wcj/dot_general | solution.py:190
  3.5 0.7 %whiten.1 = (bf16[2,16,1152]{2,1,0:T(8,128)(2,1)S(1)}, bf16[2,16,1152]{2,1,0:T(8,128)(2,1)S(1)}, bf16[2,16,1152]{2,1,0:T(8,128)(2,1)S(1)}, bf16[2,16,1152]{2,1,0...) custom-call(bf16[2,576,256]{2,1,0:T(8,128)(2,1)S(1)} %fusion.5.spect, ...), custom_call_target="tpu_custom_call" | custom-call | flops 5898240 | bytes 1769472 | tf_op jit(solution)/shard_map/whiten/pallas_call | solution.py:197
  4.3 3.0 %collective-permute-start = (bf16[2,16,1152]{2,1,0:T(8,128)(2,1)S(1)}, bf16[2,16,1152]{2,1,0:T(8,128)(2,1)S(1)}, u32[]{:S(2)}, u32[]{:S(2)}) collective-permute-start(bf16[2,16,1152]{2,1,0:T(8,128)(2,1)S(1)} %get-tuple-element.13), channel_id=1, source_target_pairs={{0,1},{1,0},{2,3},{3,2},{4,5},{5,4},{6,7},{7,6},{8,9},{9,8},{10,11... | collective-permute-start | bytes 221192 | tf_op jit(solution)/shard_map/ppermute | solution.py:212
  7.3 1.6 %collective-permute-start.1 = (bf16[2,16,1152]{2,1,0:T(8,128)(2,1)S(1)}, bf16[2,16,1152]{2,1,0:T(8,128)(2,1)S(1)}, u32[]{:S(2)}, u32[]{:S(2)}) collective-permute-start(bf16[2,16,1152]{2,1,0:T(8,128)(2,1)S(1)} %get-tuple-element.14), channel_id=1, source_target_pairs={{0,2},{1,3},{2,0},{3,1},{4,6},{5,7},{6,4},{7,5},{8,10},{9,11},{10,... | collective-permute-start | bytes 221192 | tf_op jit(solution)/shard_map/ppermute | solution.py:212
  8.9 2.4 %collective-permute-start.2 = (bf16[2,16,1152]{2,1,0:T(8,128)(2,1)S(1)}, bf16[2,16,1152]{2,1,0:T(8,128)(2,1)S(1)}, u32[]{:S(2)}, u32[]{:S(2)}) collective-permute-start(bf16[2,16,1152]{2,1,0:T(8,128)(2,1)S(1)} %get-tuple-element.15), channel_id=1, source_target_pairs={{0,7},{1,6},{2,5},{3,4},{4,3},{5,2},{6,1},{7,0},{8,15},{9,14},{10,... | collective-permute-start | bytes 221192 | tf_op jit(solution)/shard_map/ppermute | solution.py:212
  11.3 1.4 %collective-permute-start.3 = (bf16[2,16,1152]{2,1,0:T(8,128)(2,1)S(1)}, bf16[2,16,1152]{2,1,0:T(8,128)(2,1)S(1)}, u32[]{:S(2)}, u32[]{:S(2)}) collective-permute-start(bf16[2,16,1152]{2,1,0:T(8,128)(2,1)S(1)} %get-tuple-element.16), channel_id=1, source_target_pairs={{0,6},{1,7},{2,4},{3,5},{4,2},{5,3},{6,0},{7,1},{8,14},{9,15},{10,... | collective-permute-start | bytes 221192 | tf_op jit(solution)/shard_map/ppermute | solution.py:212
  12.6 1.7 %collective-permute-start.4 = (bf16[2,16,1152]{2,1,0:T(8,128)(2,1)S(1)}, bf16[2,16,1152]{2,1,0:T(8,128)(2,1)S(1)}, u32[]{:S(2)}, u32[]{:S(2)}) collective-permute-start(bf16[2,16,1152]{2,1,0:T(8,128)(2,1)S(1)} %get-tuple-element.17), channel_id=1, source_target_pairs={{0,5},{1,4},{2,7},{3,6},{4,1},{5,0},{6,3},{7,2},{8,13},{9,12},{10,... | collective-permute-start | bytes 221192 | tf_op jit(solution)/shard_map/ppermute | solution.py:212
  14.4 0.0 collective-permute-done.refs_0_
  14.4 2.1 %collective-permute-start.5 = (bf16[2,16,1152]{2,1,0:T(8,128)(2,1)S(1)}, bf16[2,16,1152]{2,1,0:T(8,128)(2,1)S(1)}, u32[]{:S(2)}, u32[]{:S(2)}) collective-permute-start(bf16[2,16,1152]{2,1,0:T(8,128)(2,1)S(1)} %get-tuple-element.18), channel_id=1, source_target_pairs={{0,4},{1,5},{2,6},{3,7},{4,0},{5,1},{6,2},{7,3},{8,12},{9,13},{10,... | collective-permute-start | bytes 221192 | tf_op jit(solution)/shard_map/ppermute | solution.py:212
  16.5 0.0 collective-permute-done.1.refs_1_
  16.5 0.1 collective-permute-start.6
  16.6 0.0 collective-permute-done.2.refs_2_
  16.6 0.0 collective-permute-start.14
  16.7 0.8 %collective-permute-done.3.refs_3_ = bf16[2,16,1152]{2,1,0:T(8,128)(2,1)S(1)} collective-permute-done((bf16[2,16,1152]{2,1,0:T(8,128)(2,1)S(1)}, bf16[2,16,1152]{2,1,0:T(8,128)(2,1)S(1)}, u32[]{:S(2)}, u32[]{:S(2)}) %collective-permute-start.3) | collective-permute-done | bytes 73760 | tf_op jit(solution)/shard_map/ppermute | solution.py:212
  17.5 0.0 collective-permute-start.7
  17.5 6.5 %collective-permute-done.4.refs_4_ = bf16[2,16,1152]{2,1,0:T(8,128)(2,1)S(1)} collective-permute-done((bf16[2,16,1152]{2,1,0:T(8,128)(2,1)S(1)}, bf16[2,16,1152]{2,1,0:T(8,128)(2,1)S(1)}, u32[]{:S(2)}, u32[]{:S(2)}) %collective-permute-start.4) | collective-permute-done | bytes 73760 | tf_op jit(solution)/shard_map/ppermute | solution.py:212
  24.0 0.0 collective-permute-start.8
  24.0 0.4 %collective-permute-done.5.refs_5_ = bf16[2,16,1152]{2,1,0:T(8,128)(2,1)S(1)} collective-permute-done((bf16[2,16,1152]{2,1,0:T(8,128)(2,1)S(1)}, bf16[2,16,1152]{2,1,0:T(8,128)(2,1)S(1)}, u32[]{:S(2)}, u32[]{:S(2)}) %collective-permute-start.5) | collective-permute-done | bytes 73760 | tf_op jit(solution)/shard_map/ppermute | solution.py:212
  24.4 0.1 collective-permute-start.9
  24.5 0.4 %collective-permute-start.10 = (bf16[2,16,1152]{2,1,0:T(8,128)(2,1)S(1)}, bf16[2,16,1152]{2,1,0:T(8,128)(2,1)S(1)}, u32[]{:S(2)}, u32[]{:S(2)}) collective-permute-start(bf16[2,16,1152]{2,1,0:T(8,128)(2,1)S(1)} %collective-permute-done.3.refs_3_), channel_id=1, source_target_pairs={{0,8},{8,0},{1,9},{9,1},{2,10},{10,2},{3,11},{11,3},{4,12},{12,4},... | collective-permute-start | bytes 221192 | tf_op jit(solution)/shard_map/ppermute | solution.py:218
  24.9 0.0 collective-permute-done.14.refs_15_
  24.9 0.1 collective-permute-start.11
  25.0 0.4 %collective-permute-start.12 = (bf16[2,16,1152]{2,1,0:T(8,128)(2,1)S(1)}, bf16[2,16,1152]{2,1,0:T(8,128)(2,1)S(1)}, u32[]{:S(2)}, u32[]{:S(2)}) collective-permute-start(bf16[2,16,1152]{2,1,0:T(8,128)(2,1)S(1)} %collective-permute-done.5.refs_5_), channel_id=1, source_target_pairs={{0,8},{8,0},{1,9},{9,1},{2,10},{10,2},{3,11},{11,3},{4,12},{12,4},... | collective-permute-start | bytes 221192 | tf_op jit(solution)/shard_map/ppermute | solution.py:218
  25.5 0.0 collective-permute-done.8.refs_9_
  25.5 0.1 collective-permute-start.13
  25.5 0.2 collective-permute-done.9.refs_10_
  25.7 0.2 collective-permute-done.10.refs_11_
  25.8 0.4 collective-permute-done.11.refs_12_
  26.2 0.2 collective-permute-done.12.refs_13_
  26.4 0.4 collective-permute-done.13.refs_14_
  26.7 16.9 %outer_products.1 = bf16[2,16,576,1152]{3,2,1,0:T(8,128)(2,1)} custom-call(bf16[2,16,1152]{2,1,0:T(8,128)(2,1)S(1)} %collective-permute-done.refs_0_, bf16[2,16,1152]{2,1,0:T(8,128)(2,1)S(1)} %collective-permute-done.1.refs_1_, bf16[2,16,1152]{2,1,0:T(8,128)(2,1)S(1)} %collective-permute-done.2.refs_2_, ...), custom_call_target="tpu_custom_call" | custom-call | flops 10871635968 | bytes 42467328 | tf_op jit(solution)/shard_map/outer_products/pallas_call | solution.py:221
  (3 shorter events, 0.0 us)
Async XLA Ops:
  0.0 1.7 %copy-start = (bf16[576,2,1024]{2,1,0:T(2,128)(2,1)S(1)}, bf16[576,2,1024]{2,1,0:T(2,128)(2,1)}, u32[]{:S(2)}) copy-start(bf16[576,2,1024]{2,1,0:T(2,128)(2,1)} %param.2) | copy-start | bytes 7077892
  4.3 10.1 %collective-permute-start = (bf16[2,16,1152]{2,1,0:T(8,128)(2,1)S(1)}, bf16[2,16,1152]{2,1,0:T(8,128)(2,1)S(1)}, u32[]{:S(2)}, u32[]{:S(2)}) collective-permute-start(bf16[2,16,1152]{2,1,0:T(8,128)(2,1)S(1)} %get-tuple-element.13), channel_id=1, source_target_pairs={{0,1},{1,0},{2,3},{3,2},{4,5},{5,4},{6,7},{7,6},{8,9},{9,8},{10,11... | collective-permute-start | bytes 221192 | tf_op jit(solution)/shard_map/ppermute | solution.py:212
  7.3 9.2 %collective-permute-start.1 = (bf16[2,16,1152]{2,1,0:T(8,128)(2,1)S(1)}, bf16[2,16,1152]{2,1,0:T(8,128)(2,1)S(1)}, u32[]{:S(2)}, u32[]{:S(2)}) collective-permute-start(bf16[2,16,1152]{2,1,0:T(8,128)(2,1)S(1)} %get-tuple-element.14), channel_id=1, source_target_pairs={{0,2},{1,3},{2,0},{3,1},{4,6},{5,7},{6,4},{7,5},{8,10},{9,11},{10,... | collective-permute-start | bytes 221192 | tf_op jit(solution)/shard_map/ppermute | solution.py:212
  8.9 7.8 %collective-permute-start.2 = (bf16[2,16,1152]{2,1,0:T(8,128)(2,1)S(1)}, bf16[2,16,1152]{2,1,0:T(8,128)(2,1)S(1)}, u32[]{:S(2)}, u32[]{:S(2)}) collective-permute-start(bf16[2,16,1152]{2,1,0:T(8,128)(2,1)S(1)} %get-tuple-element.15), channel_id=1, source_target_pairs={{0,7},{1,6},{2,5},{3,4},{4,3},{5,2},{6,1},{7,0},{8,15},{9,14},{10,... | collective-permute-start | bytes 221192 | tf_op jit(solution)/shard_map/ppermute | solution.py:212
  11.3 6.2 %collective-permute-start.3 = (bf16[2,16,1152]{2,1,0:T(8,128)(2,1)S(1)}, bf16[2,16,1152]{2,1,0:T(8,128)(2,1)S(1)}, u32[]{:S(2)}, u32[]{:S(2)}) collective-permute-start(bf16[2,16,1152]{2,1,0:T(8,128)(2,1)S(1)} %get-tuple-element.16), channel_id=1, source_target_pairs={{0,6},{1,7},{2,4},{3,5},{4,2},{5,3},{6,0},{7,1},{8,14},{9,15},{10,... | collective-permute-start | bytes 221192 | tf_op jit(solution)/shard_map/ppermute | solution.py:212
  12.6 11.3 %collective-permute-start.4 = (bf16[2,16,1152]{2,1,0:T(8,128)(2,1)S(1)}, bf16[2,16,1152]{2,1,0:T(8,128)(2,1)S(1)}, u32[]{:S(2)}, u32[]{:S(2)}) collective-permute-start(bf16[2,16,1152]{2,1,0:T(8,128)(2,1)S(1)} %get-tuple-element.17), channel_id=1, source_target_pairs={{0,5},{1,4},{2,7},{3,6},{4,1},{5,0},{6,3},{7,2},{8,13},{9,12},{10,... | collective-permute-start | bytes 221192 | tf_op jit(solution)/shard_map/ppermute | solution.py:212
  14.4 10.0 %collective-permute-start.5 = (bf16[2,16,1152]{2,1,0:T(8,128)(2,1)S(1)}, bf16[2,16,1152]{2,1,0:T(8,128)(2,1)S(1)}, u32[]{:S(2)}, u32[]{:S(2)}) collective-permute-start(bf16[2,16,1152]{2,1,0:T(8,128)(2,1)S(1)} %get-tuple-element.18), channel_id=1, source_target_pairs={{0,4},{1,5},{2,6},{3,7},{4,0},{5,1},{6,2},{7,3},{8,12},{9,13},{10,... | collective-permute-start | bytes 221192 | tf_op jit(solution)/shard_map/ppermute | solution.py:212
  16.5 8.0 %collective-permute-start.6 = (bf16[2,16,1152]{2,1,0:T(8,128)(2,1)S(1)}, bf16[2,16,1152]{2,1,0:T(8,128)(2,1)S(1)}, u32[]{:S(2)}, u32[]{:S(2)}) collective-permute-start(bf16[2,16,1152]{2,1,0:T(8,128)(2,1)S(1)} %get-tuple-element.19), channel_id=1, source_target_pairs={{0,3},{1,2},{2,1},{3,0},{4,7},{5,6},{6,5},{7,4},{8,11},{9,10},{10,... | collective-permute-start | bytes 221192 | tf_op jit(solution)/shard_map/ppermute | solution.py:212
  16.6 8.3 %collective-permute-start.14 = (bf16[2,16,1152]{2,1,0:T(8,128)(2,1)S(1)}, bf16[2,16,1152]{2,1,0:T(8,128)(2,1)S(1)}, u32[]{:S(2)}, u32[]{:S(2)}) collective-permute-start(bf16[2,16,1152]{2,1,0:T(8,128)(2,1)S(1)} %get-tuple-element.20.refs_7_), channel_id=1, source_target_pairs={{0,8},{8,0},{1,9},{9,1},{2,10},{10,2},{3,11},{11,3},{4,12},{12,4},... | collective-permute-start | bytes 221192 | tf_op jit(solution)/shard_map/ppermute | solution.py:218
  17.5 7.6 %collective-permute-start.7 = (bf16[2,16,1152]{2,1,0:T(8,128)(2,1)S(1)}, bf16[2,16,1152]{2,1,0:T(8,128)(2,1)S(1)}, u32[]{:S(2)}, u32[]{:S(2)}) collective-permute-start(bf16[2,16,1152]{2,1,0:T(8,128)(2,1)S(1)} %collective-permute-done.refs_0_), channel_id=1, source_target_pairs={{0,8},{8,0},{1,9},{9,1},{2,10},{10,2},{3,11},{11,3},{4,12},{12,4},... | collective-permute-start | bytes 221192 | tf_op jit(solution)/shard_map/ppermute | solution.py:218
  24.0 1.5 %collective-permute-start.8 = (bf16[2,16,1152]{2,1,0:T(8,128)(2,1)S(1)}, bf16[2,16,1152]{2,1,0:T(8,128)(2,1)S(1)}, u32[]{:S(2)}, u32[]{:S(2)}) collective-permute-start(bf16[2,16,1152]{2,1,0:T(8,128)(2,1)S(1)} %collective-permute-done.1.refs_1_), channel_id=1, source_target_pairs={{0,8},{8,0},{1,9},{9,1},{2,10},{10,2},{3,11},{11,3},{4,12},{12,4},... | collective-permute-start | bytes 221192 | tf_op jit(solution)/shard_map/ppermute | solution.py:218
  24.4 1.3 %collective-permute-start.9 = (bf16[2,16,1152]{2,1,0:T(8,128)(2,1)S(1)}, bf16[2,16,1152]{2,1,0:T(8,128)(2,1)S(1)}, u32[]{:S(2)}, u32[]{:S(2)}) collective-permute-start(bf16[2,16,1152]{2,1,0:T(8,128)(2,1)S(1)} %collective-permute-done.2.refs_2_), channel_id=1, source_target_pairs={{0,8},{8,0},{1,9},{9,1},{2,10},{10,2},{3,11},{11,3},{4,12},{12,4},... | collective-permute-start | bytes 221192 | tf_op jit(solution)/shard_map/ppermute | solution.py:218
  24.5 1.4 %collective-permute-start.10 = (bf16[2,16,1152]{2,1,0:T(8,128)(2,1)S(1)}, bf16[2,16,1152]{2,1,0:T(8,128)(2,1)S(1)}, u32[]{:S(2)}, u32[]{:S(2)}) collective-permute-start(bf16[2,16,1152]{2,1,0:T(8,128)(2,1)S(1)} %collective-permute-done.3.refs_3_), channel_id=1, source_target_pairs={{0,8},{8,0},{1,9},{9,1},{2,10},{10,2},{3,11},{11,3},{4,12},{12,4},... | collective-permute-start | bytes 221192 | tf_op jit(solution)/shard_map/ppermute | solution.py:218
  24.9 1.3 %collective-permute-start.11 = (bf16[2,16,1152]{2,1,0:T(8,128)(2,1)S(1)}, bf16[2,16,1152]{2,1,0:T(8,128)(2,1)S(1)}, u32[]{:S(2)}, u32[]{:S(2)}) collective-permute-start(bf16[2,16,1152]{2,1,0:T(8,128)(2,1)S(1)} %collective-permute-done.4.refs_4_), channel_id=1, source_target_pairs={{0,8},{8,0},{1,9},{9,1},{2,10},{10,2},{3,11},{11,3},{4,12},{12,4},... | collective-permute-start | bytes 221192 | tf_op jit(solution)/shard_map/ppermute | solution.py:218
  25.0 1.4 %collective-permute-start.12 = (bf16[2,16,1152]{2,1,0:T(8,128)(2,1)S(1)}, bf16[2,16,1152]{2,1,0:T(8,128)(2,1)S(1)}, u32[]{:S(2)}, u32[]{:S(2)}) collective-permute-start(bf16[2,16,1152]{2,1,0:T(8,128)(2,1)S(1)} %collective-permute-done.5.refs_5_), channel_id=1, source_target_pairs={{0,8},{8,0},{1,9},{9,1},{2,10},{10,2},{3,11},{11,3},{4,12},{12,4},... | collective-permute-start | bytes 221192 | tf_op jit(solution)/shard_map/ppermute | solution.py:218
  25.5 1.3 %collective-permute-start.13 = (bf16[2,16,1152]{2,1,0:T(8,128)(2,1)S(1)}, bf16[2,16,1152]{2,1,0:T(8,128)(2,1)S(1)}, u32[]{:S(2)}, u32[]{:S(2)}) collective-permute-start(bf16[2,16,1152]{2,1,0:T(8,128)(2,1)S(1)} %collective-permute-done.6.refs_6_), channel_id=1, source_target_pairs={{0,8},{8,0},{1,9},{9,1},{2,10},{10,2},{3,11},{11,3},{4,12},{12,4},... | collective-permute-start | bytes 221192 | tf_op jit(solution)/shard_map/ppermute | solution.py:218

commit v4 on v3

--- a/solution.py
+++ b/solution.py
@@ -12,6 +12,9 @@
 
 BINS = 128
 LANES = 128
+TILE = 256
+BLOCK = 96
+AHEAD = 3
 MIB = 1024 * 1024
 
 
@@ -159,18 +162,99 @@
         wait_for(now - depth_of_slots)
 
     slot = lax.rem(now, depth_of_slots)
-    for cut in range(cuts):
-        at = slice(cut * size, (cut + 1) * size)
-        product = jnp.dot(chosen[at], right[...], preferred_element_type=jnp.float32)
-        for part in range(2):
-            lanes = part * 2 * channels
-            slots[slot, part, at] = product[:, lanes : lanes + 2 * channels].astype(jnp.bfloat16)
-            copy(now, cut, part).start()
+
+    def store(tile, first, product):
+        for lane in range(tile * TILE, (tile + 1) * TILE, LANES):
+            part, at = lane // (2 * channels), lane % (2 * channels)
+            piece = product[:, lane - tile * TILE : lane - tile * TILE + LANES]
+            slots[slot, part, first : first + BLOCK, at : at + LANES] = piece.astype(jnp.bfloat16)
+
+    def multiply(*accumulators):
+        units = [accumulators[:AHEAD], accumulators[AHEAD:]]
+        blocks = channels // BLOCK
+        tiles = 4 * channels // TILE
+        middle = tiles // 2
+        work = [[], []]
+        for tile in range(tiles):
+            split = tile == middle
+            for block in range(blocks):
+                if split:
+                    unit = 0 if block < blocks // 2 else 1
+                else:
+                    unit = (tile if tile < middle else tile + 1) % 2
+                work[unit].append((tile, block))
+        pushed, issued = [0, 0], [0, 0]
+        waiting = [[], []]
+        left_to_store = [blocks * (2 * channels // LANES)] * 2
+
+        def push(unit):
+            order = list(dict.fromkeys(tile for tile, _ in work[unit]))
+            if pushed[unit] < len(order):
+                tile = order[pushed[unit]]
+                pltpu.matmul_push_rhs(
+                    right[:, tile * TILE : (tile + 1) * TILE], pushed[unit] % 2, unit
+                )
+                pushed[unit] += 1
+
+        def pop(unit):
+            tile, block, acc = waiting[unit].pop(0)
+            store(tile, block * BLOCK, pltpu.matmul_pop(acc))
+            for lane in range(tile * TILE, (tile + 1) * TILE, LANES):
+                part = lane // (2 * channels)
+                left_to_store[part] -= 1
+                if left_to_store[part] == 0:
+                    for cut in range(cuts):
+                        copy(now, cut, part).start()
+
+        for unit in range(2):
+            push(unit)
+        seen = [[], []]
+        for index in range(max(len(items) for items in work)):
+            for unit in range(2):
+                if index >= len(work[unit]):
+                    continue
+                tile, block = work[unit][index]
+                if len(waiting[unit]) == AHEAD:
+                    pop(unit)
+                acc = units[unit][index % AHEAD]
+                fresh = tile not in seen[unit]
+                staged = len(seen[unit]) % 2 if fresh else None
+                pltpu.matmul_acc_lhs(acc, chosen[block * BLOCK : (block + 1) * BLOCK], staged)
+                if fresh:
+                    seen[unit].append(tile)
+                    push(unit)
+                waiting[unit].append((tile, block, acc))
+        while waiting[0] or waiting[1]:
+            for unit in range(2):
+                if waiting[unit]:
+                    pop(unit)
+
+    pl.run_scoped(
+        multiply,
+        *[
+            pltpu.ACC(unit)((BLOCK, TILE), jnp.float32)
+            for unit in range(2)
+            for _ in range(AHEAD)
+        ],
+    )
 
     @pl.when(now == steps - 1)
     def _():
         for back in reversed(range(depth_of_slots)):
             wait_for(now - back)
+
+
+def copy_kernel(in_ref, out_ref):
+    out_ref[...] = in_ref[...]
+
+
+def exchange(value, mask):
+    pairs = [(source, source ^ mask) for source in range(lax.axis_size("freq"))]
+    return lax.ppermute(value, "freq", pairs)
+
+
+def swap(value):
+    return lax.ppermute(value, "chan", [(0, 1), (1, 0)])
 
 
 def local(samples):
@@ -187,9 +271,18 @@
     vmem = pl.BlockSpec(memory_space=pltpu.VMEM)
 
     memory = pl.BlockSpec(memory_space=pl.ANY)
+    with jax.named_scope("table"):
+        table = pl.pallas_call(
+            copy_kernel,
+            out_shape=jax.ShapeDtypeStruct(table.shape, table.dtype),
+            in_specs=[vmem],
+            out_specs=vmem,
+            compiler_params=pltpu.CompilerParams(vmem_limit_bytes=8 * MIB),
+        )(table)
     spectrum = jnp.einsum("cws,sj->wcj", samples, table, preferred_element_type=jnp.float32)
     spectrum = spectrum.astype(jnp.bfloat16)
-    masks = [1, 2, *range(devices - 1, 2, -1), 0] if aligned else [0]
+    masks = [*range(devices - 1, devices // 2 - 1, -1), *range(1, devices // 2), 0]
+    masks = masks if aligned else [0]
     pieces = len(masks)
     rows = (devices, groups, 2 * bins, lanes) if aligned else (2 * BINS, lanes)
     piece = rows[1:] if aligned else rows
@@ -206,16 +299,24 @@
             ),
         )(spectrum)
     if aligned:
-        own = []
-        for mask, value in zip(masks, whitened):
-            pairs = [(source, source ^ mask) for source in range(devices)]
-            own.append(lax.ppermute(value, "freq", pairs) if mask else value)
+        pieces_of = dict(zip(masks, whitened))
+        own, other = {0: pieces_of[0]}, {}
+        for mask in masks[: devices // 2]:
+            own[mask] = exchange(pieces_of[mask], mask)
+        latest = other[0] = swap(own[0])
+        for mask in masks[devices // 2 : -1]:
+            value, latest = lax.optimization_barrier((pieces_of[mask], latest))
+            own[mask] = exchange(value, mask)
+            latest = other[mask] = swap(own[mask])
+        for mask in masks[: devices // 2]:
+            other[mask] = swap(own[mask])
+        own, other = [own[mask] for mask in masks], [other[mask] for mask in masks]
     else:
         rows = whitened[0].reshape(2, devices, groups, bins, lanes).transpose(1, 2, 0, 3, 4)
         rows = rows.reshape(devices, groups, 2 * bins, lanes)
         rows = lax.all_to_all(rows, "freq", split_axis=0, concat_axis=0, tiled=True)
         own = [rows.transpose(1, 0, 2, 3).reshape(groups, devices * 2 * bins, lanes)]
-    other = [lax.ppermute(value, "chan", [(0, 1), (1, 0)]) for value in own]
+        other = [swap(own[0])]
     depth = local_windows * devices * 2 * bins
     with jax.named_scope("outer_products"):
         out = pl.pallas_call(

time: 43.8 us -> 57.9 us (1.32)
  waiting for transfers between devices: 8.97 us -> 16.1 us
  Pallas kernels: 17.7 us -> 23.3 us
  starting transfers between devices: 13.5 us -> 15.8 us
  matrix products: 1.83 us -> 0.79 us
    ppermute x15, waiting for transfers between devices: 8.97 us -> 16.1 us  [the longest x7 13 us: exchange(): return lax.ppermute(value, 'freq', pairs)]
    pallas_call x1, Pallas kernels: 16.9 us -> 22.5 us  [local(): pl.pallas_call(functools.partial(outer_kernel, bins, 1.0 / windows), out_...]
    ppermute x15, starting transfers between devices: 13.5 us -> 15.8 us  [the longest x7 14.7 us: exchange(): return lax.ppermute(value, 'freq', pairs)]
    dot_general x1, matrix products: 1.83 us -> 0.79 us  [local(): jnp.einsum('cws,sj->wcj', samples, table, preferred_element_type=jnp.floa...]
    unnamed x2 -> x4, local copies, waits for them, and re-layouts: 1.67 us -> 1.78 us
  transfers between devices with their start and end apart: 15 -> 15, of which waited for: 8 -> 9; matrix products, arithmetic and copies ran while one was open for 0% -> 0% of each run, Pallas kernels for 0% -> 0%
where the time goes in v4:
time: 57.9 us; the launch traced here: 57.8 us
  Pallas kernels  23.3 us (40%)
  waiting for transfers between devices  16.1 us (28%)
  starting transfers between devices  15.8 us (27%)
  local copies, waits for them, and re-layouts  1.78 us (3%)
  matrix products  0.79 us (1%)
    pallas_call x1, Pallas kernels, local(): pl.pallas_call(functools.partial(outer_kernel, bins, 1.0 / windows), out_...  22.5 us
    ppermute x7, starting transfers between devices, exchange(): return lax.ppermute(value, 'freq', pairs)  14.7 us
    ppermute x7, waiting for transfers between devices, exchange(): return lax.ppermute(value, 'freq', pairs)  13 us
    ppermute x8, waiting for transfers between devices, swap(): return lax.ppermute(value, 'chan', [(0, 1), (1, 0)])  3.09 us
    unnamed x4, local copies, waits for them, and re-layouts  1.78 us
  transfers between devices with their start and end apart: 15, of which 9 were waited for; matrix products, arithmetic and copies ran while one was open for 0% of the time, Pallas kernels for 0%

profile of v4, /device:TPU:0, one launch (start us, length us, event | category | flops | bytes accessed | tf_op | source)
XLA Modules:
  0.0 57.8 jit_solution(17542111141337701313)
XLA Ops:
  0.0 1.2 %copy-done.1 = bf16[1024,256]{1,0:T(8,128)(2,1)S(1)} copy-done((bf16[1024,256]{1,0:T(8,128)(2,1)S(1)}, bf16[1024,256]{1,0:T(8,128)(2,1)}, u32[]{:S(2)}) %copy-start.1) | copy-done | bytes 524312
  1.2 0.6 %copy-done = bf16[576,2,1024]{2,1,0:T(2,128)(2,1)S(1)} copy-done((bf16[576,2,1024]{2,1,0:T(2,128)(2,1)S(1)}, bf16[576,2,1024]{2,1,0:T(2,128)(2,1)}, u32[]{:S(2)}) %copy-start) | copy-done | bytes 2359320
  1.8 0.8 %fusion.5.spectrum_ref = bf16[2,576,256]{2,1,0:T(8,128)(2,1)S(1)} fusion(bf16[576,2,1024]{2,1,0:T(2,128)(2,1)S(1)} %copy-done, bf16[1024,256]{1,0:T(8,128)(2,1)S(1)} %table.1), kind=kOutput, calls=%fused_computation.3 | convolution fusion | flops 604274688 | bytes 3473408 | tf_op jit(solution)/shard_map/cws,sj->wcj/dot_general | solution.py:282
  2.6 0.8 %whiten.1 = (bf16[2,16,1152]{2,1,0:T(8,128)(2,1)S(1)}, bf16[2,16,1152]{2,1,0:T(8,128)(2,1)S(1)}, bf16[2,16,1152]{2,1,0:T(8,128)(2,1)S(1)}, bf16[2,16,1152]{2,1,0...) custom-call(bf16[2,576,256]{2,1,0:T(8,128)(2,1)S(1)} %fusion.5.spect, ...), custom_call_target="tpu_custom_call" | custom-call | flops 5898240 | bytes 1769472 | tf_op jit(solution)/shard_map/whiten/pallas_call | solution.py:290
  3.4 0.5 collective-permute-start.4
  3.9 0.9 %collective-permute-done.4.refs_15_ = bf16[2,16,1152]{2,1,0:T(8,128)(2,1)S(1)} collective-permute-done((bf16[2,16,1152]{2,1,0:T(8,128)(2,1)S(1)}, bf16[2,16,1152]{2,1,0:T(8,128)(2,1)S(1)}, u32[]{:S(2)}, u32[]{:S(2)}) %collective-permute-start.4) | collective-permute-done | bytes 73760 | tf_op jit(solution)/shard_map/ppermute | solution.py:257
  4.8 2.9 %collective-permute-start.5 = (bf16[2,16,1152]{2,1,0:T(8,128)(2,1)S(1)}, bf16[2,16,1152]{2,1,0:T(8,128)(2,1)S(1)}, u32[]{:S(2)}, u32[]{:S(2)}) collective-permute-start(bf16[2,16,1152]{2,1,0:T(8,128)(2,1)S(1)} %get-tuple-element.22), channel_id=1, source_target_pairs={{0,1},{1,0},{2,3},{3,2},{4,5},{5,4},{6,7},{7,6},{8,9},{9,8},{10,11... | collective-permute-start | bytes 221192 | tf_op jit(solution)/shard_map/ppermute | solution.py:253
  7.7 2.6 %collective-permute-done.5.refs_4_ = bf16[2,16,1152]{2,1,0:T(8,128)(2,1)S(1)} collective-permute-done((bf16[2,16,1152]{2,1,0:T(8,128)(2,1)S(1)}, bf16[2,16,1152]{2,1,0:T(8,128)(2,1)S(1)}, u32[]{:S(2)}, u32[]{:S(2)}) %collective-permute-start.5) | collective-permute-done | bytes 73760 | tf_op jit(solution)/shard_map/ppermute | solution.py:253
  10.3 0.0 collective-permute-start.6
  10.3 1.3 %collective-permute-done.6.refs_12_ = bf16[2,16,1152]{2,1,0:T(8,128)(2,1)S(1)} collective-permute-done((bf16[2,16,1152]{2,1,0:T(8,128)(2,1)S(1)}, bf16[2,16,1152]{2,1,0:T(8,128)(2,1)S(1)}, u32[]{:S(2)}, u32[]{:S(2)}) %collective-permute-start.6) | collective-permute-done | bytes 73760 | tf_op jit(solution)/shard_map/ppermute | solution.py:257
  11.5 1.8 %collective-permute-start.7 = (bf16[2,16,1152]{2,1,0:T(8,128)(2,1)S(1)}, bf16[2,16,1152]{2,1,0:T(8,128)(2,1)S(1)}, u32[]{:S(2)}, u32[]{:S(2)}) collective-permute-start(bf16[2,16,1152]{2,1,0:T(8,128)(2,1)S(1)} %get-tuple-element.24), channel_id=1, source_target_pairs={{0,2},{1,3},{2,0},{3,1},{4,6},{5,7},{6,4},{7,5},{8,10},{9,11},{10,... | collective-permute-start | bytes 221192 | tf_op jit(solution)/shard_map/ppermute | solution.py:253
  13.4 2.6 %collective-permute-done.7.refs_5_ = bf16[2,16,1152]{2,1,0:T(8,128)(2,1)S(1)} collective-permute-done((bf16[2,16,1152]{2,1,0:T(8,128)(2,1)S(1)}, bf16[2,16,1152]{2,1,0:T(8,128)(2,1)S(1)}, u32[]{:S(2)}, u32[]{:S(2)}) %collective-permute-start.7) | collective-permute-done | bytes 73760 | tf_op jit(solution)/shard_map/ppermute | solution.py:253
  15.9 0.0 collective-permute-start.8
  15.9 4.7 %collective-permute-start = (bf16[2,16,1152]{2,1,0:T(8,128)(2,1)S(1)}, bf16[2,16,1152]{2,1,0:T(8,128)(2,1)S(1)}, u32[]{:S(2)}, u32[]{:S(2)}) collective-permute-start(bf16[2,16,1152]{2,1,0:T(8,128)(2,1)S(1)} %get-tuple-element.16), channel_id=1, source_target_pairs={{0,7},{1,6},{2,5},{3,4},{4,3},{5,2},{6,1},{7,0},{8,15},{9,14},{10,... | collective-permute-start | bytes 221192 | tf_op jit(solution)/shard_map/ppermute | solution.py:253
  20.7 0.2 collective-permute-start.1
  20.9 0.7 %collective-permute-start.2 = (bf16[2,16,1152]{2,1,0:T(8,128)(2,1)S(1)}, bf16[2,16,1152]{2,1,0:T(8,128)(2,1)S(1)}, u32[]{:S(2)}, u32[]{:S(2)}) collective-permute-start(bf16[2,16,1152]{2,1,0:T(8,128)(2,1)S(1)} %get-tuple-element.18), channel_id=1, source_target_pairs={{0,5},{1,4},{2,7},{3,6},{4,1},{5,0},{6,3},{7,2},{8,13},{9,12},{10,... | collective-permute-start | bytes 221192 | tf_op jit(solution)/shard_map/ppermute | solution.py:253
  21.6 2.0 %collective-permute-start.3 = (bf16[2,16,1152]{2,1,0:T(8,128)(2,1)S(1)}, bf16[2,16,1152]{2,1,0:T(8,128)(2,1)S(1)}, u32[]{:S(2)}, u32[]{:S(2)}) collective-permute-start(bf16[2,16,1152]{2,1,0:T(8,128)(2,1)S(1)} %get-tuple-element.19), channel_id=1, source_target_pairs={{0,4},{1,5},{2,6},{3,7},{4,0},{5,1},{6,2},{7,3},{8,12},{9,13},{10,... | collective-permute-start | bytes 221192 | tf_op jit(solution)/shard_map/ppermute | solution.py:253
  23.6 0.0 collective-permute-done.8.refs_13_
  23.6 2.4 %collective-permute-start.9 = (bf16[2,16,1152]{2,1,0:T(8,128)(2,1)S(1)}, bf16[2,16,1152]{2,1,0:T(8,128)(2,1)S(1)}, u32[]{:S(2)}, u32[]{:S(2)}) collective-permute-start(bf16[2,16,1152]{2,1,0:T(8,128)(2,1)S(1)} %get-tuple-element.26), channel_id=1, source_target_pairs={{0,3},{1,2},{2,1},{3,0},{4,7},{5,6},{6,5},{7,4},{8,11},{9,10},{10,... | collective-permute-start | bytes 221192 | tf_op jit(solution)/shard_map/ppermute | solution.py:253
  26.0 1.7 %collective-permute-done.1.refs_1_ = bf16[2,16,1152]{2,1,0:T(8,128)(2,1)S(1)} collective-permute-done((bf16[2,16,1152]{2,1,0:T(8,128)(2,1)S(1)}, bf16[2,16,1152]{2,1,0:T(8,128)(2,1)S(1)}, u32[]{:S(2)}, u32[]{:S(2)}) %collective-permute-start.1) | collective-permute-done | bytes 73760 | tf_op jit(solution)/shard_map/ppermute | solution.py:253
  27.7 4.9 %collective-permute-done.2.refs_2_ = bf16[2,16,1152]{2,1,0:T(8,128)(2,1)S(1)} collective-permute-done((bf16[2,16,1152]{2,1,0:T(8,128)(2,1)S(1)}, bf16[2,16,1152]{2,1,0:T(8,128)(2,1)S(1)}, u32[]{:S(2)}, u32[]{:S(2)}) %collective-permute-start.2) | collective-permute-done | bytes 73760 | tf_op jit(solution)/shard_map/ppermute | solution.py:253
  32.6 0.0 collective-permute-start.12
  32.6 1.2 %collective-permute-done.3.refs_3_ = bf16[2,16,1152]{2,1,0:T(8,128)(2,1)S(1)} collective-permute-done((bf16[2,16,1152]{2,1,0:T(8,128)(2,1)S(1)}, bf16[2,16,1152]{2,1,0:T(8,128)(2,1)S(1)}, u32[]{:S(2)}, u32[]{:S(2)}) %collective-permute-start.3) | collective-permute-done | bytes 73760 | tf_op jit(solution)/shard_map/ppermute | solution.py:253
  33.8 0.0 collective-permute-start.13
  33.8 0.0 collective-permute-done.9.refs_6_
  33.8 0.5 collective-permute-start.14
  34.4 0.0 collective-permute-done.10.refs_8_
  34.4 0.0 collective-permute-done.11.refs_9_
  34.4 0.0 collective-permute-done.12.refs_10_
  34.4 0.7 %collective-permute-done.13.refs_11_ = bf16[2,16,1152]{2,1,0:T(8,128)(2,1)S(1)} collective-permute-done((bf16[2,16,1152]{2,1,0:T(8,128)(2,1)S(1)}, bf16[2,16,1152]{2,1,0:T(8,128)(2,1)S(1)}, u32[]{:S(2)}, u32[]{:S(2)}) %collective-permute-start.13) | collective-permute-done | bytes 73760 | tf_op jit(solution)/shard_map/ppermute | solution.py:257
  35.1 0.2 collective-permute-done.14.refs_14_
  35.3 22.5 %outer_products.1 = bf16[2,16,576,1152]{3,2,1,0:T(8,128)(2,1)} custom-call(bf16[2,16,1152]{2,1,0:T(8,128)(2,1)S(1)} %collective-permute-done.refs_0_, bf16[2,16,1152]{2,1,0:T(8,128)(2,1)S(1)} %collective-permute-done.1.refs_1_, bf16[2,16,1152]{2,1,0:T(8,128)(2,1)S(1)} %collective-permute-done.2.refs_2_, ...), custom_call_target="tpu_custom_call" | custom-call | flops 10871635968 | bytes 42467328 | tf_op jit(solution)/shard_map/outer_products/pallas_call | solution.py:322
  (6 shorter events, 0.0 us)
Async XLA Ops:
  0.0 1.8 %copy-start = (bf16[576,2,1024]{2,1,0:T(2,128)(2,1)S(1)}, bf16[576,2,1024]{2,1,0:T(2,128)(2,1)}, u32[]{:S(2)}) copy-start(bf16[576,2,1024]{2,1,0:T(2,128)(2,1)} %param.2) | copy-start | bytes 7077892
  0.0 1.2 %copy-start.1 = (bf16[1024,256]{1,0:T(8,128)(2,1)S(1)}, bf16[1024,256]{1,0:T(8,128)(2,1)}, u32[]{:S(2)}) copy-start(bf16[1024,256]{1,0:T(8,128)(2,1)} %constant.2.clone.in_ref) | copy-start | bytes 1572868
  3.4 1.4 %collective-permute-start.4 = (bf16[2,16,1152]{2,1,0:T(8,128)(2,1)S(1)}, bf16[2,16,1152]{2,1,0:T(8,128)(2,1)S(1)}, u32[]{:S(2)}, u32[]{:S(2)}) collective-permute-start(bf16[2,16,1152]{2,1,0:T(8,128)(2,1)S(1)} %get-tuple-element.21.refs_7_), channel_id=1, source_target_pairs={{0,8},{8,0},{1,9},{9,1},{2,10},{10,2},{3,11},{11,3},{4,12},{12,4},... | collective-permute-start | bytes 221192 | tf_op jit(solution)/shard_map/ppermute | solution.py:257
  4.8 5.5 %collective-permute-start.5 = (bf16[2,16,1152]{2,1,0:T(8,128)(2,1)S(1)}, bf16[2,16,1152]{2,1,0:T(8,128)(2,1)S(1)}, u32[]{:S(2)}, u32[]{:S(2)}) collective-permute-start(bf16[2,16,1152]{2,1,0:T(8,128)(2,1)S(1)} %get-tuple-element.22), channel_id=1, source_target_pairs={{0,1},{1,0},{2,3},{3,2},{4,5},{5,4},{6,7},{7,6},{8,9},{9,8},{10,11... | collective-permute-start | bytes 221192 | tf_op jit(solution)/shard_map/ppermute | solution.py:253
  10.3 1.3 %collective-permute-start.6 = (bf16[2,16,1152]{2,1,0:T(8,128)(2,1)S(1)}, bf16[2,16,1152]{2,1,0:T(8,128)(2,1)S(1)}, u32[]{:S(2)}, u32[]{:S(2)}) collective-permute-start(bf16[2,16,1152]{2,1,0:T(8,128)(2,1)S(1)} %collective-permute-done.5.refs_4_), channel_id=1, source_target_pairs={{0,8},{8,0},{1,9},{9,1},{2,10},{10,2},{3,11},{11,3},{4,12},{12,4},... | collective-permute-start | bytes 221192 | tf_op jit(solution)/shard_map/ppermute | solution.py:257
  11.5 4.4 %collective-permute-start.7 = (bf16[2,16,1152]{2,1,0:T(8,128)(2,1)S(1)}, bf16[2,16,1152]{2,1,0:T(8,128)(2,1)S(1)}, u32[]{:S(2)}, u32[]{:S(2)}) collective-permute-start(bf16[2,16,1152]{2,1,0:T(8,128)(2,1)S(1)} %get-tuple-element.24), channel_id=1, source_target_pairs={{0,2},{1,3},{2,0},{3,1},{4,6},{5,7},{6,4},{7,5},{8,10},{9,11},{10,... | collective-permute-start | bytes 221192 | tf_op jit(solution)/shard_map/ppermute | solution.py:253
  15.9 7.7 %collective-permute-start.8 = (bf16[2,16,1152]{2,1,0:T(8,128)(2,1)S(1)}, bf16[2,16,1152]{2,1,0:T(8,128)(2,1)S(1)}, u32[]{:S(2)}, u32[]{:S(2)}) collective-permute-start(bf16[2,16,1152]{2,1,0:T(8,128)(2,1)S(1)} %collective-permute-done.7.refs_5_), channel_id=1, source_target_pairs={{0,8},{8,0},{1,9},{9,1},{2,10},{10,2},{3,11},{11,3},{4,12},{12,4},... | collective-permute-start | bytes 221192 | tf_op jit(solution)/shard_map/ppermute | solution.py:257
  15.9 10.0 %collective-permute-start = (bf16[2,16,1152]{2,1,0:T(8,128)(2,1)S(1)}, bf16[2,16,1152]{2,1,0:T(8,128)(2,1)S(1)}, u32[]{:S(2)}, u32[]{:S(2)}) collective-permute-start(bf16[2,16,1152]{2,1,0:T(8,128)(2,1)S(1)} %get-tuple-element.16), channel_id=1, source_target_pairs={{0,7},{1,6},{2,5},{3,4},{4,3},{5,2},{6,1},{7,0},{8,15},{9,14},{10,... | collective-permute-start | bytes 221192 | tf_op jit(solution)/shard_map/ppermute | solution.py:253
  20.7 7.0 %collective-permute-start.1 = (bf16[2,16,1152]{2,1,0:T(8,128)(2,1)S(1)}, bf16[2,16,1152]{2,1,0:T(8,128)(2,1)S(1)}, u32[]{:S(2)}, u32[]{:S(2)}) collective-permute-start(bf16[2,16,1152]{2,1,0:T(8,128)(2,1)S(1)} %get-tuple-element.17), channel_id=1, source_target_pairs={{0,6},{1,7},{2,4},{3,5},{4,2},{5,3},{6,0},{7,1},{8,14},{9,15},{10,... | collective-permute-start | bytes 221192 | tf_op jit(solution)/shard_map/ppermute | solution.py:253
  20.9 11.7 %collective-permute-start.2 = (bf16[2,16,1152]{2,1,0:T(8,128)(2,1)S(1)}, bf16[2,16,1152]{2,1,0:T(8,128)(2,1)S(1)}, u32[]{:S(2)}, u32[]{:S(2)}) collective-permute-start(bf16[2,16,1152]{2,1,0:T(8,128)(2,1)S(1)} %get-tuple-element.18), channel_id=1, source_target_pairs={{0,5},{1,4},{2,7},{3,6},{4,1},{5,0},{6,3},{7,2},{8,13},{9,12},{10,... | collective-permute-start | bytes 221192 | tf_op jit(solution)/shard_map/ppermute | solution.py:253
  21.6 12.2 %collective-permute-start.3 = (bf16[2,16,1152]{2,1,0:T(8,128)(2,1)S(1)}, bf16[2,16,1152]{2,1,0:T(8,128)(2,1)S(1)}, u32[]{:S(2)}, u32[]{:S(2)}) collective-permute-start(bf16[2,16,1152]{2,1,0:T(8,128)(2,1)S(1)} %get-tuple-element.19), channel_id=1, source_target_pairs={{0,4},{1,5},{2,6},{3,7},{4,0},{5,1},{6,2},{7,3},{8,12},{9,13},{10,... | collective-permute-start | bytes 221192 | tf_op jit(solution)/shard_map/ppermute | solution.py:253
  23.6 10.2 %collective-permute-start.9 = (bf16[2,16,1152]{2,1,0:T(8,128)(2,1)S(1)}, bf16[2,16,1152]{2,1,0:T(8,128)(2,1)S(1)}, u32[]{:S(2)}, u32[]{:S(2)}) collective-permute-start(bf16[2,16,1152]{2,1,0:T(8,128)(2,1)S(1)} %get-tuple-element.26), channel_id=1, source_target_pairs={{0,3},{1,2},{2,1},{3,0},{4,7},{5,6},{6,5},{7,4},{8,11},{9,10},{10,... | collective-permute-start | bytes 221192 | tf_op jit(solution)/shard_map/ppermute | solution.py:253
  26.0 8.4 %collective-permute-start.10 = (bf16[2,16,1152]{2,1,0:T(8,128)(2,1)S(1)}, bf16[2,16,1152]{2,1,0:T(8,128)(2,1)S(1)}, u32[]{:S(2)}, u32[]{:S(2)}) collective-permute-start(bf16[2,16,1152]{2,1,0:T(8,128)(2,1)S(1)} %collective-permute-done.refs_0_), channel_id=1, source_target_pairs={{0,8},{8,0},{1,9},{9,1},{2,10},{10,2},{3,11},{11,3},{4,12},{12,4},... | collective-permute-start | bytes 221192 | tf_op jit(solution)/shard_map/ppermute | solution.py:257
  27.7 6.7 %collective-permute-start.11 = (bf16[2,16,1152]{2,1,0:T(8,128)(2,1)S(1)}, bf16[2,16,1152]{2,1,0:T(8,128)(2,1)S(1)}, u32[]{:S(2)}, u32[]{:S(2)}) collective-permute-start(bf16[2,16,1152]{2,1,0:T(8,128)(2,1)S(1)} %collective-permute-done.1.refs_1_), channel_id=1, source_target_pairs={{0,8},{8,0},{1,9},{9,1},{2,10},{10,2},{3,11},{11,3},{4,12},{12,4},... | collective-permute-start | bytes 221192 | tf_op jit(solution)/shard_map/ppermute | solution.py:257
  32.6 1.8 %collective-permute-start.12 = (bf16[2,16,1152]{2,1,0:T(8,128)(2,1)S(1)}, bf16[2,16,1152]{2,1,0:T(8,128)(2,1)S(1)}, u32[]{:S(2)}, u32[]{:S(2)}) collective-permute-start(bf16[2,16,1152]{2,1,0:T(8,128)(2,1)S(1)} %collective-permute-done.2.refs_2_), channel_id=1, source_target_pairs={{0,8},{8,0},{1,9},{9,1},{2,10},{10,2},{3,11},{11,3},{4,12},{12,4},... | collective-permute-start | bytes 221192 | tf_op jit(solution)/shard_map/ppermute | solution.py:257
  33.8 1.3 %collective-permute-start.13 = (bf16[2,16,1152]{2,1,0:T(8,128)(2,1)S(1)}, bf16[2,16,1152]{2,1,0:T(8,128)(2,1)S(1)}, u32[]{:S(2)}, u32[]{:S(2)}) collective-permute-start(bf16[2,16,1152]{2,1,0:T(8,128)(2,1)S(1)} %collective-permute-done.3.refs_3_), channel_id=1, source_target_pairs={{0,8},{8,0},{1,9},{9,1},{2,10},{10,2},{3,11},{11,3},{4,12},{12,4},... | collective-permute-start | bytes 221192 | tf_op jit(solution)/shard_map/ppermute | solution.py:257
  33.8 1.4 %collective-permute-start.14 = (bf16[2,16,1152]{2,1,0:T(8,128)(2,1)S(1)}, bf16[2,16,1152]{2,1,0:T(8,128)(2,1)S(1)}, u32[]{:S(2)}, u32[]{:S(2)}) collective-permute-start(bf16[2,16,1152]{2,1,0:T(8,128)(2,1)S(1)} %collective-permute-done.9.refs_6_), channel_id=1, source_target_pairs={{0,8},{8,0},{1,9},{9,1},{2,10},{10,2},{3,11},{11,3},{4,12},{12,4},... | collective-permute-start | bytes 221192 | tf_op jit(solution)/shard_map/ppermute | solution.py:257

commit v5 on v3

--- a/solution.py
+++ b/solution.py
@@ -34,7 +34,7 @@
     ]
 
 
-def whiten_kernel(group, masks, spectrum_ref, *refs):
+def whiten_kernel(group, near, spectrum_ref, *refs):
     pieces, rows_ref = refs[:-1], refs[-1]
     windows, channels, columns = spectrum_ref.shape
     bins = columns // 2
@@ -62,16 +62,28 @@
         whitened = (parts * inverse).astype(jnp.bfloat16)
         rows_ref[..., lane : lane + cols] = whitened.reshape(rows_ref.shape[:-1] + (cols,))
 
-    if len(pieces) == 1:
+    if near is None:
         pieces[0][...] = rows_ref[...]
     else:
         me = lax.axis_index("freq")
-        for mask, piece in zip(masks, pieces):
+        first = (me // near) * near
+        for i in range(near):
+            pieces[0][i] = rows_ref[first + i]
+        for mask, piece in enumerate(pieces[1:], near):
             piece[...] = rows_ref[me ^ mask]
 
 
 def swap_halves(tile):
     return pltpu.roll(tile, LANES // 2, axis=1)
+
+
+def rows_of(refs, which):
+    for ref in refs:
+        if len(ref.shape) == 3:
+            yield ref[which]
+        else:
+            for i in range(ref.shape[0]):
+                yield ref[i, which]
 
 
 def outer_kernel(bins, scale, *refs):
@@ -103,8 +115,8 @@
     def _():
         me = lax.axis_index("chan")
         which = pl.program_id(0)
-        own = jnp.concatenate([ref[which].astype(jnp.float32) for ref in own_refs])
-        other = jnp.concatenate([ref[which].astype(jnp.float32) for ref in other_refs])
+        own = jnp.concatenate([rows.astype(jnp.float32) for rows in rows_of(own_refs, which)])
+        other = jnp.concatenate([rows.astype(jnp.float32) for rows in rows_of(other_refs, which)])
         rows = own.shape[0]
         block0 = jnp.where(me == 0, own, other)
         block1 = jnp.where(me == 0, other, own)
@@ -159,18 +171,46 @@
         wait_for(now - depth_of_slots)
 
     slot = lax.rem(now, depth_of_slots)
-    for cut in range(cuts):
-        at = slice(cut * size, (cut + 1) * size)
-        product = jnp.dot(chosen[at], right[...], preferred_element_type=jnp.float32)
-        for part in range(2):
-            lanes = part * 2 * channels
-            slots[slot, part, at] = product[:, lanes : lanes + 2 * channels].astype(jnp.bfloat16)
+
+    whole = 2 * channels // (2 * LANES) * (2 * LANES)
+    starts = [0, whole, 4 * channels - whole, 4 * channels]
+    left_over = 2 * channels - whole
+
+    def multiply(first, last):
+        return jnp.dot(
+            chosen, right[:, first:last], preferred_element_type=jnp.float32
+        ).astype(jnp.bfloat16)
+
+    def send(part):
+        for cut in range(cuts):
             copy(now, cut, part).start()
+
+    slots[slot, 0, :, :whole] = multiply(*starts[:2])
+    if left_over:
+        both = multiply(*starts[1:3])
+        slots[slot, 0, :, whole:] = both[:, :left_over]
+        slots[slot, 1, :, :left_over] = both[:, left_over:]
+    send(0)
+    slots[slot, 1, :, left_over:] = multiply(*starts[2:])
+    send(1)
 
     @pl.when(now == steps - 1)
     def _():
         for back in reversed(range(depth_of_slots)):
             wait_for(now - back)
+
+
+def copy_kernel(in_ref, out_ref):
+    out_ref[...] = in_ref[...]
+
+
+def exchange(value, mask):
+    pairs = [(source, source ^ mask) for source in range(lax.axis_size("freq"))]
+    return lax.ppermute(value, "freq", pairs)
+
+
+def swap(value):
+    return lax.ppermute(value, "chan", [(0, 1), (1, 0)])
 
 
 def local(samples):
@@ -185,18 +225,25 @@
     table = jnp.asarray(bin_table(length, BINS, group))
     lanes = local_windows * local_channels
     vmem = pl.BlockSpec(memory_space=pltpu.VMEM)
-
     memory = pl.BlockSpec(memory_space=pl.ANY)
+    near = devices // 2 if aligned else None
+    pieces = devices - near + 1 if aligned else 1
+    rows = (devices, groups, 2 * bins, lanes) if aligned else (2 * BINS, lanes)
+    shapes = [(near,) + rows[1:]] + [rows[1:]] * (pieces - 1) if aligned else [rows]
+    with jax.named_scope("table"):
+        table = pl.pallas_call(
+            copy_kernel,
+            out_shape=jax.ShapeDtypeStruct(table.shape, table.dtype),
+            in_specs=[vmem],
+            out_specs=vmem,
+            compiler_params=pltpu.CompilerParams(vmem_limit_bytes=8 * MIB),
+        )(table)
     spectrum = jnp.einsum("cws,sj->wcj", samples, table, preferred_element_type=jnp.float32)
     spectrum = spectrum.astype(jnp.bfloat16)
-    masks = [1, 2, *range(devices - 1, 2, -1), 0] if aligned else [0]
-    pieces = len(masks)
-    rows = (devices, groups, 2 * bins, lanes) if aligned else (2 * BINS, lanes)
-    piece = rows[1:] if aligned else rows
     with jax.named_scope("whiten"):
         whitened = pl.pallas_call(
-            functools.partial(whiten_kernel, group, masks),
-            out_shape=[jax.ShapeDtypeStruct(piece, jnp.bfloat16)] * pieces,
+            functools.partial(whiten_kernel, group, near),
+            out_shape=[jax.ShapeDtypeStruct(shape, jnp.bfloat16) for shape in shapes],
             in_specs=[vmem],
             out_specs=[vmem] * pieces,
             scratch_shapes=[pltpu.VMEM(rows, jnp.bfloat16)],
@@ -206,16 +253,18 @@
             ),
         )(spectrum)
     if aligned:
-        own = []
-        for mask, value in zip(masks, whitened):
-            pairs = [(source, source ^ mask) for source in range(devices)]
-            own.append(lax.ppermute(value, "freq", pairs) if mask else value)
+        far = [exchange(value, mask) for mask, value in enumerate(whitened[1:], near)]
+        grouped = [list(range(first, first + near)) for first in range(0, devices, near)]
+        own = lax.all_to_all(
+            whitened[0], "freq", split_axis=0, concat_axis=0, tiled=True, axis_index_groups=grouped
+        )
+        own = [own] + far
     else:
         rows = whitened[0].reshape(2, devices, groups, bins, lanes).transpose(1, 2, 0, 3, 4)
         rows = rows.reshape(devices, groups, 2 * bins, lanes)
         rows = lax.all_to_all(rows, "freq", split_axis=0, concat_axis=0, tiled=True)
         own = [rows.transpose(1, 0, 2, 3).reshape(groups, devices * 2 * bins, lanes)]
-    other = [lax.ppermute(value, "chan", [(0, 1), (1, 0)]) for value in own]
+    other = [swap(value) for value in own]
     depth = local_windows * devices * 2 * bins
     with jax.named_scope("outer_products"):
         out = pl.pallas_call(

time: 43.8 us -> 47.9 us (1.094); the launches traced: 43.7 us -> 47.2 us
  blocking collectives: 0 us -> 11.4 us
  starting transfers between devices: 13.5 us -> 8.23 us
  waiting for transfers between devices: 8.97 us -> 7.26 us
  matrix products: 1.83 us -> 0.79 us
    all_to_all x0 -> x1, blocking collectives: none -> 11.4 us  [local(): lax.all_to_all(whitened[0], 'freq', split_axis=0, concat_axis=0, tiled=Tr...]
    ppermute x15 -> x9, starting transfers between devices: 13.5 us -> 8.23 us  [the longest x4 7.65 us: exchange(): return lax.ppermute(value, 'freq', pairs)]
    ppermute x15 -> x9, waiting for transfers between devices: 8.97 us -> 7.26 us  [the longest x4 6.07 us: exchange(): return lax.ppermute(value, 'freq', pairs)]
    dot_general x1, matrix products: 1.83 us -> 0.79 us  [local(): jnp.einsum('cws,sj->wcj', samples, table, preferred_element_type=jnp.floa...]
    unnamed x2 -> x4, local copies, waits for them, and re-layouts: 1.67 us -> 1.78 us
  transfers between devices with their start and end apart: 15 -> 9, of which waited for: 8 -> 5; matrix products, arithmetic and copies ran while one was open for 0% -> 0% of each run, Pallas kernels for 0% -> 0%
where the time goes in v5:
time: 47.9 us; the launch traced here: 47.2 us
  Pallas kernels  17.8 us (37%)
  blocking collectives  11.4 us (24%)
  starting transfers between devices  8.23 us (17%)
  waiting for transfers between devices  7.26 us (15%)
  local copies, waits for them, and re-layouts  1.78 us (4%)
  matrix products  0.79 us (2%)
    pallas_call x1, Pallas kernels, local(): pl.pallas_call(functools.partial(outer_kernel, bins, 1.0 / windows), out_...  17 us
    all_to_all x1, blocking collectives, local(): lax.all_to_all(whitened[0], 'freq', split_axis=0, concat_axis=0, tiled=Tr...  11.4 us
    ppermute x4, starting transfers between devices, exchange(): return lax.ppermute(value, 'freq', pairs)  7.65 us
    ppermute x4, waiting for transfers between devices, exchange(): return lax.ppermute(value, 'freq', pairs)  6.07 us
    unnamed x4, local copies, waits for them, and re-layouts  1.78 us
    ppermute x5, waiting for transfers between devices, swap(): return lax.ppermute(value, 'chan', [(0, 1), (1, 0)])  1.2 us
  transfers between devices with their start and end apart: 9, of which 5 were waited for; matrix products, arithmetic and copies ran while one was open for 0% of the time, Pallas kernels for 0%

profile of v5, /device:TPU:0, one launch (start us, length us, event | category | flops | bytes accessed | tf_op | source)
XLA Modules:
  0.0 47.2 jit_solution(232850827666041258)
XLA Ops:
  0.0 0.0 copy-start
  0.0 0.0 copy-start.1
  0.0 1.2 %copy-done.1 = bf16[1024,256]{1,0:T(8,128)(2,1)S(1)} copy-done((bf16[1024,256]{1,0:T(8,128)(2,1)S(1)}, bf16[1024,256]{1,0:T(8,128)(2,1)}, u32[]{:S(2)}) %copy-start.1) | copy-done | bytes 524312
  1.2 0.6 %copy-done = bf16[576,2,1024]{2,1,0:T(2,128)(2,1)S(1)} copy-done((bf16[576,2,1024]{2,1,0:T(2,128)(2,1)S(1)}, bf16[576,2,1024]{2,1,0:T(2,128)(2,1)}, u32[]{:S(2)}) %copy-start) | copy-done | bytes 2359320
  1.8 0.8 %fusion.5.spectrum_ref = bf16[2,576,256]{2,1,0:T(8,128)(2,1)S(1)} fusion(bf16[576,2,1024]{2,1,0:T(2,128)(2,1)S(1)} %copy-done, bf16[1024,256]{1,0:T(8,128)(2,1)S(1)} %table.1), kind=kOutput, calls=%fused_computation.3 | convolution fusion | flops 604274688 | bytes 3473408 | tf_op jit(solution)/shard_map/cws,sj->wcj/dot_general | solution.py:241
  2.6 0.7 %whiten.1 = (bf16[4,2,16,1152]{3,2,1,0:T(8,128)(2,1)S(1)}, bf16[2,16,1152]{2,1,0:T(8,128)(2,1)S(1)}, bf16[2,16,1152]{2,1,0:T(8,128)(2,1)S(1)}, bf16[2,16,1152]{2,1,0:T(8,128)(2,1)S(1)}, bf16[2,16,1152]{2,1,0:T(8,128)(2,1)S(1)}) custom-call(bf16[2,576,256]{2,1,0:T(8,128)(2,1)S(1)} %fusion.5.spectrum_ref), custom_call_target="tpu_custom_call" | custom-call | flops 5898240 | bytes 1769472 | tf_op jit(solution)/shard_map/whiten/pallas_call | solution.py:244
  3.4 11.4 %all_to_all.5.refs_0_ = bf16[4,2,16,1152]{3,2,1,0:T(8,128)(2,1)S(1)} all-to-all(bf16[4,2,16,1152]{3,2,1,0:T(8,128)(2,1)S(1)} %get-tuple-element.10), channel_id=1, replica_groups={{0,1,2,3},{4,5,6,7},{8,9,10,11},{12,13,14,15},{16,17,18,19},{20,21,22,2..., dimensions={0} | all-to-all | bytes 589824 | tf_op jit(solution)/shard_map/all_to_all | solution.py:258
  14.8 0.0 collective-permute-start.4
  14.8 2.6 %collective-permute-start = (bf16[2,16,1152]{2,1,0:T(8,128)(2,1)S(1)}, bf16[2,16,1152]{2,1,0:T(8,128)(2,1)S(1)}, u32[]{:S(2)}, u32[]{:S(2)}) collective-permute-start(bf16[2,16,1152]{2,1,0:T(8,128)(2,1)S(1)} %get-tuple-element.11), channel_id=1, source_target_pairs={{0,4},{1,5},{2,6},{3,7},{4,0},{5,1},{6,2},{7,3},{8,12},{9,13},{10,... | collective-permute-start | bytes 221192 | tf_op jit(solution)/shard_map/ppermute | solution.py:209
  17.3 0.4 collective-permute-start.1
  17.8 2.6 %collective-permute-start.2 = (bf16[2,16,1152]{2,1,0:T(8,128)(2,1)S(1)}, bf16[2,16,1152]{2,1,0:T(8,128)(2,1)S(1)}, u32[]{:S(2)}, u32[]{:S(2)}) collective-permute-start(bf16[2,16,1152]{2,1,0:T(8,128)(2,1)S(1)} %get-tuple-element.13), channel_id=1, source_target_pairs={{0,6},{1,7},{2,4},{3,5},{4,2},{5,3},{6,0},{7,1},{8,14},{9,15},{10,... | collective-permute-start | bytes 221192 | tf_op jit(solution)/shard_map/ppermute | solution.py:209
  20.4 2.0 %collective-permute-start.3 = (bf16[2,16,1152]{2,1,0:T(8,128)(2,1)S(1)}, bf16[2,16,1152]{2,1,0:T(8,128)(2,1)S(1)}, u32[]{:S(2)}, u32[]{:S(2)}) collective-permute-start(bf16[2,16,1152]{2,1,0:T(8,128)(2,1)S(1)} %get-tuple-element.14), channel_id=1, source_target_pairs={{0,7},{1,6},{2,5},{3,4},{4,3},{5,2},{6,1},{7,0},{8,15},{9,14},{10,... | collective-permute-start | bytes 221192 | tf_op jit(solution)/shard_map/ppermute | solution.py:209
  22.4 2.9 %collective-permute-done.refs_1_ = bf16[2,16,1152]{2,1,0:T(8,128)(2,1)S(1)} collective-permute-done((bf16[2,16,1152]{2,1,0:T(8,128)(2,1)S(1)}, bf16[2,16,1152]{2,1,0:T(8,128)(2,1)S(1)}, u32[]{:S(2)}, u32[]{:S(2)}) %collective-permute-start) | collective-permute-done | bytes 73760 | tf_op jit(solution)/shard_map/ppermute | solution.py:209
  25.3 0.0 collective-permute-start.5
  25.3 3.2 %collective-permute-done.1.refs_2_ = bf16[2,16,1152]{2,1,0:T(8,128)(2,1)S(1)} collective-permute-done((bf16[2,16,1152]{2,1,0:T(8,128)(2,1)S(1)}, bf16[2,16,1152]{2,1,0:T(8,128)(2,1)S(1)}, u32[]{:S(2)}, u32[]{:S(2)}) %collective-permute-start.1) | collective-permute-done | bytes 73760 | tf_op jit(solution)/shard_map/ppermute | solution.py:209
  28.5 0.0 collective-permute-start.6
  28.5 0.0 collective-permute-done.2.refs_3_
  28.5 0.5 %collective-permute-start.7 = (bf16[2,16,1152]{2,1,0:T(8,128)(2,1)S(1)}, bf16[2,16,1152]{2,1,0:T(8,128)(2,1)S(1)}, u32[]{:S(2)}, u32[]{:S(2)}) collective-permute-start(bf16[2,16,1152]{2,1,0:T(8,128)(2,1)S(1)} %collective-permute-done.2.refs_3_), channel_id=1, source_target_pairs={{0,8},{8,0},{1,9},{9,1},{2,10},{10,2},{3,11},{11,3},{4,12},{12,4},... | collective-permute-start | bytes 221192 | tf_op jit(solution)/shard_map/ppermute | solution.py:213
  29.0 0.0 collective-permute-done.3.refs_4_
  29.0 0.1 collective-permute-start.8
  29.1 0.0 collective-permute-done.5.refs_6_
  29.1 0.7 %collective-permute-done.6.refs_7_ = bf16[2,16,1152]{2,1,0:T(8,128)(2,1)S(1)} collective-permute-done((bf16[2,16,1152]{2,1,0:T(8,128)(2,1)S(1)}, bf16[2,16,1152]{2,1,0:T(8,128)(2,1)S(1)}, u32[]{:S(2)}, u32[]{:S(2)}) %collective-permute-start.6) | collective-permute-done | bytes 73760 | tf_op jit(solution)/shard_map/ppermute | solution.py:213
  29.7 0.2 collective-permute-done.7.refs_8_
  29.9 0.4 collective-permute-done.8.refs_9_
  30.3 0.0 collective-permute-done.4.refs_5_
  30.3 17.0 %outer_products.1 = bf16[2,16,576,1152]{3,2,1,0:T(8,128)(2,1)} custom-call(bf16[4,2,16,1152]{3,2,1,0:T(8,128)(2,1)S(1)} %all_to_all.5.refs_0_, bf16[2,16,1152]{2,1,0:T(8,128)(2,1)S(1)} %collective-permute-done.refs_1_, bf16[2,16,1152]{2,1,0:T(8,128)(2,1)S(1)} %collective-permute-done.1.refs_2_, bf16[2,16,1152]{2,1,0:T(8,128)(2,1)S(1)} %collective-permute-done.2.refs_3_, ...), custom_call_target="tpu_custom_call" | custom-call | flops 10871635968 | bytes 42467328 | tf_op jit(solution)/shard_map/outer_products/pallas_call | solution.py:270
  (1 shorter events, 0.0 us)
Async XLA Ops:
  0.0 1.8 %copy-start = (bf16[576,2,1024]{2,1,0:T(2,128)(2,1)S(1)}, bf16[576,2,1024]{2,1,0:T(2,128)(2,1)}, u32[]{:S(2)}) copy-start(bf16[576,2,1024]{2,1,0:T(2,128)(2,1)} %param.2) | copy-start | bytes 7077892
  0.0 1.2 %copy-start.1 = (bf16[1024,256]{1,0:T(8,128)(2,1)S(1)}, bf16[1024,256]{1,0:T(8,128)(2,1)}, u32[]{:S(2)}) copy-start(bf16[1024,256]{1,0:T(8,128)(2,1)} %constant.2.clone.in_ref) | copy-start | bytes 1572868
  14.8 15.5 %collective-permute-start.4 = (bf16[4,2,16,1152]{3,2,1,0:T(8,128)(2,1)S(1)}, bf16[4,2,16,1152]{3,2,1,0:T(8,128)(2,1)S(1)}, u32[]{:S(2)}, u32[]{:S(2)}) collective-permute-start(bf16[4,2,16,1152]{3,2,1,0:T(8,128)(2,1)S(1)} %all_to_all.5.refs_0_), channel_id=1, source_target_pairs={{0,8},{8,0},{1,9},{9,1},{2,10},{10,2},{3,11},{11,3},{4,12},{12,4},... | collective-permute-start | bytes 884744 | tf_op jit(solution)/shard_map/ppermute | solution.py:213
  14.8 10.5 %collective-permute-start = (bf16[2,16,1152]{2,1,0:T(8,128)(2,1)S(1)}, bf16[2,16,1152]{2,1,0:T(8,128)(2,1)S(1)}, u32[]{:S(2)}, u32[]{:S(2)}) collective-permute-start(bf16[2,16,1152]{2,1,0:T(8,128)(2,1)S(1)} %get-tuple-element.11), channel_id=1, source_target_pairs={{0,4},{1,5},{2,6},{3,7},{4,0},{5,1},{6,2},{7,3},{8,12},{9,13},{10,... | collective-permute-start | bytes 221192 | tf_op jit(solution)/shard_map/ppermute | solution.py:209
  17.3 11.1 %collective-permute-start.1 = (bf16[2,16,1152]{2,1,0:T(8,128)(2,1)S(1)}, bf16[2,16,1152]{2,1,0:T(8,128)(2,1)S(1)}, u32[]{:S(2)}, u32[]{:S(2)}) collective-permute-start(bf16[2,16,1152]{2,1,0:T(8,128)(2,1)S(1)} %get-tuple-element.12), channel_id=1, source_target_pairs={{0,5},{1,4},{2,7},{3,6},{4,1},{5,0},{6,3},{7,2},{8,13},{9,12},{10,... | collective-permute-start | bytes 221192 | tf_op jit(solution)/shard_map/ppermute | solution.py:209
  17.8 10.7 %collective-permute-start.2 = (bf16[2,16,1152]{2,1,0:T(8,128)(2,1)S(1)}, bf16[2,16,1152]{2,1,0:T(8,128)(2,1)S(1)}, u32[]{:S(2)}, u32[]{:S(2)}) collective-permute-start(bf16[2,16,1152]{2,1,0:T(8,128)(2,1)S(1)} %get-tuple-element.13), channel_id=1, source_target_pairs={{0,6},{1,7},{2,4},{3,5},{4,2},{5,3},{6,0},{7,1},{8,14},{9,15},{10,... | collective-permute-start | bytes 221192 | tf_op jit(solution)/shard_map/ppermute | solution.py:209
  20.4 8.6 %collective-permute-start.3 = (bf16[2,16,1152]{2,1,0:T(8,128)(2,1)S(1)}, bf16[2,16,1152]{2,1,0:T(8,128)(2,1)S(1)}, u32[]{:S(2)}, u32[]{:S(2)}) collective-permute-start(bf16[2,16,1152]{2,1,0:T(8,128)(2,1)S(1)} %get-tuple-element.14), channel_id=1, source_target_pairs={{0,7},{1,6},{2,5},{3,4},{4,3},{5,2},{6,1},{7,0},{8,15},{9,14},{10,... | collective-permute-start | bytes 221192 | tf_op jit(solution)/shard_map/ppermute | solution.py:209
  25.3 3.8 %collective-permute-start.5 = (bf16[2,16,1152]{2,1,0:T(8,128)(2,1)S(1)}, bf16[2,16,1152]{2,1,0:T(8,128)(2,1)S(1)}, u32[]{:S(2)}, u32[]{:S(2)}) collective-permute-start(bf16[2,16,1152]{2,1,0:T(8,128)(2,1)S(1)} %collective-permute-done.refs_1_), channel_id=1, source_target_pairs={{0,8},{8,0},{1,9},{9,1},{2,10},{10,2},{3,11},{11,3},{4,12},{12,4},... | collective-permute-start | bytes 221192 | tf_op jit(solution)/shard_map/ppermute | solution.py:213
  28.5 1.3 %collective-permute-start.6 = (bf16[2,16,1152]{2,1,0:T(8,128)(2,1)S(1)}, bf16[2,16,1152]{2,1,0:T(8,128)(2,1)S(1)}, u32[]{:S(2)}, u32[]{:S(2)}) collective-permute-start(bf16[2,16,1152]{2,1,0:T(8,128)(2,1)S(1)} %collective-permute-done.1.refs_2_), channel_id=1, source_target_pairs={{0,8},{8,0},{1,9},{9,1},{2,10},{10,2},{3,11},{11,3},{4,12},{12,4},... | collective-permute-start | bytes 221192 | tf_op jit(solution)/shard_map/ppermute | solution.py:213
  28.5 1.4 %collective-permute-start.7 = (bf16[2,16,1152]{2,1,0:T(8,128)(2,1)S(1)}, bf16[2,16,1152]{2,1,0:T(8,128)(2,1)S(1)}, u32[]{:S(2)}, u32[]{:S(2)}) collective-permute-start(bf16[2,16,1152]{2,1,0:T(8,128)(2,1)S(1)} %collective-permute-done.2.refs_3_), channel_id=1, source_target_pairs={{0,8},{8,0},{1,9},{9,1},{2,10},{10,2},{3,11},{11,3},{4,12},{12,4},... | collective-permute-start | bytes 221192 | tf_op jit(solution)/shard_map/ppermute | solution.py:213
  29.0 1.3 %collective-permute-start.8 = (bf16[2,16,1152]{2,1,0:T(8,128)(2,1)S(1)}, bf16[2,16,1152]{2,1,0:T(8,128)(2,1)S(1)}, u32[]{:S(2)}, u32[]{:S(2)}) collective-permute-start(bf16[2,16,1152]{2,1,0:T(8,128)(2,1)S(1)} %collective-permute-done.3.refs_4_), channel_id=1, source_target_pairs={{0,8},{8,0},{1,9},{9,1},{2,10},{10,2},{3,11},{11,3},{4,12},{12,4},... | collective-permute-start | bytes 221192 | tf_op jit(solution)/shard_map/ppermute | solution.py:213

commit v6 on v5

--- a/solution.py
+++ b/solution.py
@@ -12,6 +12,7 @@
 
 BINS = 128
 LANES = 128
+CUTS = 6
 MIB = 1024 * 1024
 
 
@@ -66,36 +67,37 @@
         pieces[0][...] = rows_ref[...]
     else:
         me = lax.axis_index("freq")
-        first = (me // near) * near
-        for i in range(near):
-            pieces[0][i] = rows_ref[first + i]
-        for mask, piece in enumerate(pieces[1:], near):
-            piece[...] = rows_ref[me ^ mask]
+        for mask in range(near):
+            pieces[mask][...] = rows_ref[me ^ mask]
+        for i, piece in enumerate(pieces[near:]):
+            mask, which = near + i % near, i // near
+            piece[0] = rows_ref[me ^ mask, which]
 
 
 def swap_halves(tile):
     return pltpu.roll(tile, LANES // 2, axis=1)
 
 
-def rows_of(refs, which):
-    for ref in refs:
-        if len(ref.shape) == 3:
+def rows_of(refs, which, kinds):
+    for ref, kind in zip(refs, kinds):
+        if kind == "groups":
             yield ref[which]
+        elif kind == "pair":
+            near = lax.axis_size("freq") // 2
+            yield ref[1 - lax.axis_index("freq") // near]
         else:
-            for i in range(ref.shape[0]):
-                yield ref[i, which]
-
-
-def outer_kernel(bins, scale, *refs):
+            yield ref[0]
+
+
+def outer_kernel(bins, scale, which, kinds, *refs):
     out_ref, right, left, slots, sems = refs[-5:]
-    count = (len(refs) - 5) // 2
-    own_refs, other_refs = refs[:count], refs[count:-5]
+    count = len(kinds)
+    own_refs, other_refs = refs[:count], refs[count : 2 * count]
     half = LANES // 2
     channels = out_ref.shape[2]
     full = channels // LANES
-    step = pl.program_id(1)
-    now = pl.program_id(0) * bins + step
-    steps = pl.num_programs(0) * bins
+    step = now = pl.program_id(0)
+    steps = bins
     depth_of_slots, cuts = sems.shape[:2]
     size = channels // cuts
 
@@ -103,7 +105,7 @@
         slot = lax.rem(when, depth_of_slots)
         at = pl.ds(cut * size, size)
         return pltpu.make_async_copy(
-            slots.at[slot, part, at], out_ref.at[part, when, at], sems.at[slot, cut, part]
+            slots.at[slot, part, at], out_ref.at[part, which * bins + when, at], sems.at[slot, cut, part]
         )
 
     def wait_for(when):
@@ -114,9 +116,10 @@
     @pl.when(step == 0)
     def _():
         me = lax.axis_index("chan")
-        which = pl.program_id(0)
-        own = jnp.concatenate([rows.astype(jnp.float32) for rows in rows_of(own_refs, which)])
-        other = jnp.concatenate([rows.astype(jnp.float32) for rows in rows_of(other_refs, which)])
+        own, other = (
+            jnp.concatenate([rows.astype(jnp.float32) for rows in rows_of(some, which, kinds)])
+            for some in (own_refs, other_refs)
+        )
         rows = own.shape[0]
         block0 = jnp.where(me == 0, own, other)
         block1 = jnp.where(me == 0, other, own)
@@ -209,6 +212,13 @@
     return lax.ppermute(value, "freq", pairs)
 
 
+def gather_pair(value, mask):
+    pairs = sorted({(min(i, i ^ mask), max(i, i ^ mask)) for i in range(lax.axis_size("freq"))})
+    return lax.all_gather(
+        value, "freq", axis_index_groups=[list(pair) for pair in pairs], tiled=True
+    )
+
+
 def swap(value):
     return lax.ppermute(value, "chan", [(0, 1), (1, 0)])
 
@@ -227,9 +237,12 @@
     vmem = pl.BlockSpec(memory_space=pltpu.VMEM)
     memory = pl.BlockSpec(memory_space=pl.ANY)
     near = devices // 2 if aligned else None
-    pieces = devices - near + 1 if aligned else 1
-    rows = (devices, groups, 2 * bins, lanes) if aligned else (2 * BINS, lanes)
-    shapes = [(near,) + rows[1:]] + [rows[1:]] * (pieces - 1) if aligned else [rows]
+    if aligned:
+        rows = (devices, groups, 2 * bins, lanes)
+        shapes = [rows[1:]] * near + [(1,) + rows[2:]] * (groups * near)
+    else:
+        rows = (2 * BINS, lanes)
+        shapes = [rows]
     with jax.named_scope("table"):
         table = pl.pallas_call(
             copy_kernel,
@@ -245,7 +258,7 @@
             functools.partial(whiten_kernel, group, near),
             out_shape=[jax.ShapeDtypeStruct(shape, jnp.bfloat16) for shape in shapes],
             in_specs=[vmem],
-            out_specs=[vmem] * pieces,
+            out_specs=[vmem] * len(shapes),
             scratch_shapes=[pltpu.VMEM(rows, jnp.bfloat16)],
             compiler_params=pltpu.CompilerParams(vmem_limit_bytes=16 * MIB),
             cost_estimate=pl.CostEstimate(
@@ -253,41 +266,65 @@
             ),
         )(spectrum)
     if aligned:
-        far = [exchange(value, mask) for mask, value in enumerate(whitened[1:], near)]
-        grouped = [list(range(first, first + near)) for first in range(0, devices, near)]
-        own = lax.all_to_all(
-            whitened[0], "freq", split_axis=0, concat_axis=0, tiled=True, axis_index_groups=grouped
-        )
-        own = [own] + far
+        own = {mask: whitened[mask] for mask in range(near)}
+        far = [whitened[near * (1 + g) : near * (2 + g)] for g in range(groups)]
+        first = {}
+        for mask in (1, 2, *range(devices - 1, near - 1, -1), *range(3, near)):
+            if mask < near:
+                own[mask] = exchange(own[mask], mask)
+            else:
+                first[mask] = exchange(far[0][mask - near], mask)
+        sources = [[*own.values(), *first.values()]]
+        kinds = [["groups"] * near + ["whole"] * near]
+        for g in range(1, groups):
+            later, held = lax.optimization_barrier((far[g], sources[-1][-2:]))
+            sources[-1][-2:] = held
+            gathered = [gather_pair(value, near + i) for i, value in enumerate(later)]
+            sources.append([*own.values(), *gathered])
+            kinds.append(["groups"] * near + ["pair"] * near)
+        near_other = [swap(value) for value in own.values()]
     else:
         rows = whitened[0].reshape(2, devices, groups, bins, lanes).transpose(1, 2, 0, 3, 4)
         rows = rows.reshape(devices, groups, 2 * bins, lanes)
         rows = lax.all_to_all(rows, "freq", split_axis=0, concat_axis=0, tiled=True)
-        own = [rows.transpose(1, 0, 2, 3).reshape(groups, devices * 2 * bins, lanes)]
-    other = [swap(value) for value in own]
+        own = rows.transpose(1, 0, 2, 3).reshape(groups, devices * 2 * bins, lanes)
+        near, near_other = 1, [swap(own)]
+        sources, kinds = [[own]] * groups, [["groups"]] * groups
     depth = local_windows * devices * 2 * bins
-    with jax.named_scope("outer_products"):
-        out = pl.pallas_call(
-            functools.partial(outer_kernel, bins, 1.0 / windows),
-            out_shape=jax.ShapeDtypeStruct(
-                (2, local_bins, local_channels, 2 * local_channels), jnp.bfloat16
-            ),
-            grid=(groups, bins),
-            in_specs=[vmem] * (2 * pieces),
-            out_specs=memory,
-            scratch_shapes=[
-                pltpu.VMEM((depth, 4 * local_channels), jnp.bfloat16),
-                pltpu.VMEM((local_channels, depth), jnp.float32),
-                pltpu.VMEM((3, 2, local_channels, 2 * local_channels), jnp.bfloat16),
-                pltpu.SemaphoreType.DMA((3, 2, 2)),
-            ],
-            compiler_params=pltpu.CompilerParams(vmem_limit_bytes=32 * MIB),
-            cost_estimate=pl.CostEstimate(
-                flops=8 * local_bins * depth * local_channels * local_channels,
-                bytes_accessed=8 * local_bins * local_channels * local_channels,
-                transcendentals=0,
-            ),
-        )(*own, *other)
+    out = None
+    for g in range(groups):
+        later = sources[g][near:]
+        if out is not None and later:
+            later, out = lax.optimization_barrier((later, out))
+        operands = [*sources[g][:near], *later, *near_other, *map(swap, later)]
+        specs = [vmem] * len(operands)
+        aliases = {}
+        if out is not None:
+            aliases = {len(operands): 0}
+            operands, specs = [*operands, out], [*specs, memory]
+        with jax.named_scope("outer_products"):
+            out = pl.pallas_call(
+                functools.partial(outer_kernel, bins, 1.0 / windows, g, kinds[g]),
+                out_shape=jax.ShapeDtypeStruct(
+                    (2, local_bins, local_channels, 2 * local_channels), jnp.bfloat16
+                ),
+                grid=(bins,),
+                in_specs=specs,
+                out_specs=memory,
+                input_output_aliases=aliases,
+                scratch_shapes=[
+                    pltpu.VMEM((depth, 4 * local_channels), jnp.bfloat16),
+                    pltpu.VMEM((local_channels, depth), jnp.float32),
+                    pltpu.VMEM((3, 2, local_channels, 2 * local_channels), jnp.bfloat16),
+                    pltpu.SemaphoreType.DMA((3, CUTS, 2)),
+                ],
+                compiler_params=pltpu.CompilerParams(vmem_limit_bytes=32 * MIB),
+                cost_estimate=pl.CostEstimate(
+                    flops=8 * bins * depth * local_channels * local_channels,
+                    bytes_accessed=8 * bins * local_channels * local_channels,
+                    transcendentals=0,
+                ),
+            )(*operands)
     return jnp.transpose(out, (0, 1, 3, 2))
 
 

time: 47.9 us -> 68.6 us (1.43)
  blocking collectives: 11.4 us -> 26.7 us
  starting transfers between devices: 8.23 us -> 14.3 us
  waiting for transfers between devices: 7.26 us -> 4.78 us
  Pallas kernels: 17.8 us -> 19.9 us
    all_gather x0 -> x4, blocking collectives: none -> 26.7 us  [gather_pair(): lax.all_gather(value, 'freq', axis_index_groups=[list(pair) for pair in p...]
    all_to_all x1 -> x0, blocking collectives: 11.4 us -> none  [local(): lax.all_to_all(whitened[0], 'freq', split_axis=0, concat_axis=0, tiled=Tr...]
    ppermute x4 -> x7, starting transfers between devices: 7.65 us -> 11.7 us  [exchange(): return lax.ppermute(value, 'freq', pairs)]
    ppermute x4 -> x7, waiting for transfers between devices: 6.07 us -> 3.16 us  [exchange(): return lax.ppermute(value, 'freq', pairs)]
    pallas_call x1 -> x2, Pallas kernels: 17 us -> 19.1 us  [local(): pl.pallas_call(functools.partial(outer_kernel, bins, 1.0 / windows, g, ki...]
    ppermute x5 -> x12, starting transfers between devices: 0.59 us -> 2.59 us  [swap(): return lax.ppermute(value, 'chan', [(0, 1), (1, 0)])]
    ppermute x5 -> x12, waiting for transfers between devices: 1.2 us -> 1.63 us  [swap(): return lax.ppermute(value, 'chan', [(0, 1), (1, 0)])]
  transfers between devices with their start and end apart: 9 -> 19, of which waited for: 5 -> 7; matrix products, arithmetic and copies ran while one was open for 0% -> 0% of each run, Pallas kernels for 0% -> 0%
where the time goes in v6:
time: 68.6 us; the launch traced here: 68.4 us
  blocking collectives  26.7 us (39%)
  Pallas kernels  19.9 us (29%)
  starting transfers between devices  14.3 us (21%)
  waiting for transfers between devices  4.78 us (7%)
  local copies, waits for them, and re-layouts  1.78 us (3%)
  matrix products  0.79 us (1%)
    all_gather x4, blocking collectives, gather_pair(): lax.all_gather(value, 'freq', axis_index_groups=[list(pair) for pair in p...  26.7 us
    pallas_call x2, Pallas kernels, local(): pl.pallas_call(functools.partial(outer_kernel, bins, 1.0 / windows, g, ki...  19.1 us
    ppermute x7, starting transfers between devices, exchange(): return lax.ppermute(value, 'freq', pairs)  11.7 us
    ppermute x7, waiting for transfers between devices, exchange(): return lax.ppermute(value, 'freq', pairs)  3.16 us
    ppermute x12, starting transfers between devices, swap(): return lax.ppermute(value, 'chan', [(0, 1), (1, 0)])  2.59 us
    unnamed x4, local copies, waits for them, and re-layouts  1.78 us
    ppermute x12, waiting for transfers between devices, swap(): return lax.ppermute(value, 'chan', [(0, 1), (1, 0)])  1.63 us
  transfers between devices with their start and end apart: 19, of which 7 were waited for; matrix products, arithmetic and copies ran while one was open for 0% of the time, Pallas kernels for 0%

profile of v6, /device:TPU:0, one launch (start us, length us, event | category | flops | bytes accessed | tf_op | source)
XLA Modules:
  0.0 68.4 jit_solution(4902034622381762125)
XLA Ops:
  0.0 1.2 %copy-done.1 = bf16[1024,256]{1,0:T(8,128)(2,1)S(1)} copy-done((bf16[1024,256]{1,0:T(8,128)(2,1)S(1)}, bf16[1024,256]{1,0:T(8,128)(2,1)}, u32[]{:S(2)}) %copy-start.1) | copy-done | bytes 524312
  1.2 0.6 copy-done
  1.8 0.8 %fusion.5.spectrum_ref = bf16[2,576,256]{2,1,0:T(8,128)(2,1)S(1)} fusion(bf16[576,2,1024]{2,1,0:T(2,128)(2,1)S(1)} %copy-done, bf16[1024,256]{1,0:T(8,128)(2,1)S(1)} %table.1), kind=kOutput, calls=%fused_computation.3 | convolution fusion | flops 604274688 | bytes 3473408 | tf_op jit(solution)/shard_map/cws,sj->wcj/dot_general | solution.py:254
  2.6 0.8 %whiten.1 = (bf16[2,16,1152]{2,1,0:T(8,128)(2,1)S(1)}, bf16[2,16,1152]{2,1,0:T(8,128)(2,1)S(1)}, bf16[2,16,1152]{2,1,0:T(8,128)(2,1)S(1)}, bf16[2,16,1152]{2,1,0...) custom-call(bf16[2,576,256]{2,1,0:T(8,128)(2,1)S(1)} %fusion.5.spect, ...), custom_call_target="tpu_custom_call" | custom-call | flops 5898240 | bytes 1769472 | tf_op jit(solution)/shard_map/whiten/pallas_call | solution.py:257
  3.4 5.1 %collective-permute-start.3 = (bf16[1,16,1152]{2,1,0:T(8,128)(2,1)S(1)}, bf16[1,16,1152]{2,1,0:T(8,128)(2,1)S(1)}, u32[]{:S(2)}, u32[]{:S(2)}) collective-permute-start(bf16[1,16,1152]{2,1,0:T(8,128)(2,1)S(1)} %get-tuple-element.36), channel_id=1, source_target_pairs={{0,5},{1,4},{2,7},{3,6},{4,1},{5,0},{6,3},{7,2},{8,13},{9,12},{10,... | collective-permute-start | bytes 110600 | tf_op jit(solution)/shard_map/ppermute | solution.py:212
  8.4 0.3 collective-permute-start.4
  8.8 3.5 %collective-permute-start.5 = (bf16[1,16,1152]{2,1,0:T(8,128)(2,1)S(1)}, bf16[1,16,1152]{2,1,0:T(8,128)(2,1)S(1)}, u32[]{:S(2)}, u32[]{:S(2)}) collective-permute-start(bf16[1,16,1152]{2,1,0:T(8,128)(2,1)S(1)} %get-tuple-element.42), channel_id=1, source_target_pairs={{0,7},{1,6},{2,5},{3,4},{4,3},{5,2},{6,1},{7,0},{8,15},{9,14},{10,... | collective-permute-start | bytes 110600 | tf_op jit(solution)/shard_map/ppermute | solution.py:212
  12.3 0.1 collective-permute-start.6
  12.4 1.7 %collective-permute-start = (bf16[2,16,1152]{2,1,0:T(8,128)(2,1)S(1)}, bf16[2,16,1152]{2,1,0:T(8,128)(2,1)S(1)}, u32[]{:S(2)}, u32[]{:S(2)}) collective-permute-start(bf16[2,16,1152]{2,1,0:T(8,128)(2,1)S(1)} %get-tuple-element.29), channel_id=1, source_target_pairs={{0,1},{1,0},{2,3},{3,2},{4,5},{5,4},{6,7},{7,6},{8,9},{9,8},{10,11... | collective-permute-start | bytes 221192 | tf_op jit(solution)/shard_map/ppermute | solution.py:212
  14.1 0.8 %collective-permute-done.4.refs_7_ = bf16[1,16,1152]{2,1,0:T(8,128)(2,1)S(1)} collective-permute-done((bf16[1,16,1152]{2,1,0:T(8,128)(2,1)S(1)}, bf16[1,16,1152]{2,1,0:T(8,128)(2,1)S(1)}, u32[]{:S(2)}, u32[]{:S(2)}) %collective-permute-start.4) | collective-permute-done | bytes 36896 | tf_op jit(solution)/shard_map/ppermute | solution.py:212
  14.9 1.0 %collective-permute-start.2 = (bf16[2,16,1152]{2,1,0:T(8,128)(2,1)S(1)}, bf16[2,16,1152]{2,1,0:T(8,128)(2,1)S(1)}, u32[]{:S(2)}, u32[]{:S(2)}) collective-permute-start(bf16[2,16,1152]{2,1,0:T(8,128)(2,1)S(1)} %get-tuple-element.31), channel_id=1, source_target_pairs={{0,3},{1,2},{2,1},{3,0},{4,7},{5,6},{6,5},{7,4},{8,11},{9,10},{10,... | collective-permute-start | bytes 221192 | tf_op jit(solution)/shard_map/ppermute | solution.py:212
  15.9 2.3 %collective-permute-done.6.refs_5_ = bf16[1,16,1152]{2,1,0:T(8,128)(2,1)S(1)} collective-permute-done((bf16[1,16,1152]{2,1,0:T(8,128)(2,1)S(1)}, bf16[1,16,1152]{2,1,0:T(8,128)(2,1)S(1)}, u32[]{:S(2)}, u32[]{:S(2)}) %collective-permute-start.6) | collective-permute-done | bytes 36896 | tf_op jit(solution)/shard_map/ppermute | solution.py:212
  18.2 0.5 collective-permute-start.7
  18.7 0.7 %collective-permute-done.14.refs_15_ = bf16[1,16,1152]{2,1,0:T(8,128)(2,1)S(1)} collective-permute-done((bf16[1,16,1152]{2,1,0:T(8,128)(2,1)S(1)}, bf16[1,16,1152]{2,1,0:T(8,128)(2,1)S(1)}, u32[]{:S(2)}, u32[]{:S(2)}) %collective-permute-start.14) | collective-permute-done | bytes 36896 | tf_op jit(solution)/shard_map/ppermute | solution.py:223
  19.4 0.2 collective-permute-start.11
  19.6 0.3 collective-permute-start.8
  19.9 0.2 collective-permute-start.9
  20.1 0.3 collective-permute-start.10
  20.4 6.6 %all_gather.12.refs_4_ = bf16[2,16,1152]{2,1,0:T(8,128)(2,1)S(1)} all-gather(bf16[1,16,1152]{2,1,0:T(8,128)(2,1)S(1)} %get-tuple-element.38), channel_id=1, replica_groups={{0,4},{1,5},{2,6},{3,7},{8,12},{9,13},{10,14},{11,15},{16,20},{17,21},{..., dimensions={0}, use_global_device_ids=true | all-gather | bytes 110592 | tf_op jit(solution)/shard_map/all_gather | solution.py:217
  27.0 6.4 %all_gather.13.refs_5_ = bf16[2,16,1152]{2,1,0:T(8,128)(2,1)S(1)} all-gather(bf16[1,16,1152]{2,1,0:T(8,128)(2,1)S(1)} %get-tuple-element.39), channel_id=1, replica_groups={{0,5},{1,4},{2,7},{3,6},{8,13},{9,12},{10,15},{11,14},{16,21},{17,20},{..., dimensions={0}, use_global_device_ids=true | all-gather | bytes 110592 | tf_op jit(solution)/shard_map/all_gather | solution.py:217
  33.5 6.4 %all_gather.14.refs_6_ = bf16[2,16,1152]{2,1,0:T(8,128)(2,1)S(1)} all-gather(bf16[1,16,1152]{2,1,0:T(8,128)(2,1)S(1)} %get-tuple-element.40), channel_id=1, replica_groups={{0,6},{1,7},{2,4},{3,5},{8,14},{9,15},{10,12},{11,13},{16,22},{17,23},{..., dimensions={0}, use_global_device_ids=true | all-gather | bytes 110592 | tf_op jit(solution)/shard_map/all_gather | solution.py:217
  39.9 7.3 %all_gather.15.refs_7_ = bf16[2,16,1152]{2,1,0:T(8,128)(2,1)S(1)} all-gather(bf16[1,16,1152]{2,1,0:T(8,128)(2,1)S(1)} %get-tuple-element.41), channel_id=1, replica_groups={{0,7},{1,6},{2,5},{3,4},{8,15},{9,14},{10,13},{11,12},{16,23},{17,22},{..., dimensions={0}, use_global_device_ids=true | all-gather | bytes 110592 | tf_op jit(solution)/shard_map/all_gather | solution.py:217
  47.2 9.6 %outer_products.2.refs_16_ = bf16[2,16,576,1152]{3,2,1,0:T(8,128)(2,1)} custom-call(bf16[2,16,1152]{2,1,0:T(8,128)(2,1)S(1)} %get-tuple-element.28.refs_0_, bf16[2,16,1152]{2,1,0:T(8,128)(2,1)S(1)} %collective-permute-done.refs_1_, bf16[2,16,1152]{2,1,0:T(8,128)(2,1)S(1)} %collective-permute-done.1.refs_2_, ...), custom_call_target="tpu_custom_call" | custom-call | flops 5435817984 | bytes 21233664 | tf_op jit(solution)/shard_map/outer_products/pallas_call | solution.py:306
  56.8 0.1 collective-permute-start.15
  56.9 0.5 collective-permute-start.16
  57.4 0.1 collective-permute-start.17
  57.5 0.4 collective-permute-start.18
  57.9 0.2 collective-permute-done.15.refs_12_
  58.2 0.2 collective-permute-done.16.refs_13_
  58.3 0.4 collective-permute-done.17.refs_14_
  58.7 0.2 collective-permute-done.18.refs_15_
  58.8 9.5 %outer_products.3 = bf16[2,16,576,1152]{3,2,1,0:T(8,128)(2,1)} custom-call(bf16[2,16,1152]{2,1,0:T(8,128)(2,1)S(1)} %get-tuple-element.28.refs_0_, bf16[2,16,1152]{2,1,0:T(8,128)(2,1)S(1)} %collective-permute-done.refs_1_, bf16[2,16,1152]{2,1,0:T(8,128)(2,1)S(1)} %collective-permute-done.1.refs_2_, ...), custom_call_target="tpu_custom_call", output_to_operand_aliasing={{}: (16, {})} | custom-call | flops 5435817984 | bytes 21233664 | tf_op jit(solution)/shard_map/outer_products/pallas_call | solution.py:306
  (19 shorter events, 0.1 us)
Async XLA Ops:
  0.0 1.8 %copy-start = (bf16[576,2,1024]{2,1,0:T(2,128)(2,1)S(1)}, bf16[576,2,1024]{2,1,0:T(2,128)(2,1)}, u32[]{:S(2)}) copy-start(bf16[576,2,1024]{2,1,0:T(2,128)(2,1)} %param.2) | copy-start | bytes 7077892
  0.0 1.2 %copy-start.1 = (bf16[1024,256]{1,0:T(8,128)(2,1)S(1)}, bf16[1024,256]{1,0:T(8,128)(2,1)}, u32[]{:S(2)}) copy-start(bf16[1024,256]{1,0:T(8,128)(2,1)} %constant.2.clone.in_ref) | copy-start | bytes 1572868
  3.4 10.7 %collective-permute-start.3 = (bf16[1,16,1152]{2,1,0:T(8,128)(2,1)S(1)}, bf16[1,16,1152]{2,1,0:T(8,128)(2,1)S(1)}, u32[]{:S(2)}, u32[]{:S(2)}) collective-permute-start(bf16[1,16,1152]{2,1,0:T(8,128)(2,1)S(1)} %get-tuple-element.36), channel_id=1, source_target_pairs={{0,5},{1,4},{2,7},{3,6},{4,1},{5,0},{6,3},{7,2},{8,13},{9,12},{10,... | collective-permute-start | bytes 110600 | tf_op jit(solution)/shard_map/ppermute | solution.py:212
  8.4 6.4 %collective-permute-start.4 = (bf16[1,16,1152]{2,1,0:T(8,128)(2,1)S(1)}, bf16[1,16,1152]{2,1,0:T(8,128)(2,1)S(1)}, u32[]{:S(2)}, u32[]{:S(2)}) collective-permute-start(bf16[1,16,1152]{2,1,0:T(8,128)(2,1)S(1)} %get-tuple-element.37), channel_id=1, source_target_pairs={{0,4},{1,5},{2,6},{3,7},{4,0},{5,1},{6,2},{7,3},{8,12},{9,13},{10,... | collective-permute-start | bytes 110600 | tf_op jit(solution)/shard_map/ppermute | solution.py:212
  8.8 7.1 %collective-permute-start.5 = (bf16[1,16,1152]{2,1,0:T(8,128)(2,1)S(1)}, bf16[1,16,1152]{2,1,0:T(8,128)(2,1)S(1)}, u32[]{:S(2)}, u32[]{:S(2)}) collective-permute-start(bf16[1,16,1152]{2,1,0:T(8,128)(2,1)S(1)} %get-tuple-element.42), channel_id=1, source_target_pairs={{0,7},{1,6},{2,5},{3,4},{4,3},{5,2},{6,1},{7,0},{8,15},{9,14},{10,... | collective-permute-start | bytes 110600 | tf_op jit(solution)/shard_map/ppermute | solution.py:212
  12.3 5.9 %collective-permute-start.6 = (bf16[1,16,1152]{2,1,0:T(8,128)(2,1)S(1)}, bf16[1,16,1152]{2,1,0:T(8,128)(2,1)S(1)}, u32[]{:S(2)}, u32[]{:S(2)}) collective-permute-start(bf16[1,16,1152]{2,1,0:T(8,128)(2,1)S(1)} %get-tuple-element.43), channel_id=1, source_target_pairs={{0,6},{1,7},{2,4},{3,5},{4,2},{5,3},{6,0},{7,1},{8,14},{9,15},{10,... | collective-permute-start | bytes 110600 | tf_op jit(solution)/shard_map/ppermute | solution.py:212
  12.4 7.2 %collective-permute-start = (bf16[2,16,1152]{2,1,0:T(8,128)(2,1)S(1)}, bf16[2,16,1152]{2,1,0:T(8,128)(2,1)S(1)}, u32[]{:S(2)}, u32[]{:S(2)}) collective-permute-start(bf16[2,16,1152]{2,1,0:T(8,128)(2,1)S(1)} %get-tuple-element.29), channel_id=1, source_target_pairs={{0,1},{1,0},{2,3},{3,2},{4,5},{5,4},{6,7},{7,6},{8,9},{9,8},{10,11... | collective-permute-start | bytes 221192 | tf_op jit(solution)/shard_map/ppermute | solution.py:212
  14.1 5.9 %collective-permute-start.1 = (bf16[2,16,1152]{2,1,0:T(8,128)(2,1)S(1)}, bf16[2,16,1152]{2,1,0:T(8,128)(2,1)S(1)}, u32[]{:S(2)}, u32[]{:S(2)}) collective-permute-start(bf16[2,16,1152]{2,1,0:T(8,128)(2,1)S(1)} %get-tuple-element.30), channel_id=1, source_target_pairs={{0,2},{1,3},{2,0},{3,1},{4,6},{5,7},{6,4},{7,5},{8,10},{9,11},{10,... | collective-permute-start | bytes 221192 | tf_op jit(solution)/shard_map/ppermute | solution.py:212
  14.9 5.3 %collective-permute-start.2 = (bf16[2,16,1152]{2,1,0:T(8,128)(2,1)S(1)}, bf16[2,16,1152]{2,1,0:T(8,128)(2,1)S(1)}, u32[]{:S(2)}, u32[]{:S(2)}) collective-permute-start(bf16[2,16,1152]{2,1,0:T(8,128)(2,1)S(1)} %get-tuple-element.31), channel_id=1, source_target_pairs={{0,3},{1,2},{2,1},{3,0},{4,7},{5,6},{6,5},{7,4},{8,11},{9,10},{10,... | collective-permute-start | bytes 221192 | tf_op jit(solution)/shard_map/ppermute | solution.py:212
  15.9 2.3 %collective-permute-start.13 = (bf16[1,16,1152]{2,1,0:T(8,128)(2,1)S(1)}, bf16[1,16,1152]{2,1,0:T(8,128)(2,1)S(1)}, u32[]{:S(2)}, u32[]{:S(2)}) collective-permute-start(bf16[1,16,1152]{2,1,0:T(8,128)(2,1)S(1)} %collective-permute-done.3.refs_6_), channel_id=1, source_target_pairs={{0,8},{8,0},{1,9},{9,1},{2,10},{10,2},{3,11},{11,3},{4,12},{12,4},... | collective-permute-start | bytes 110600 | tf_op jit(solution)/shard_map/ppermute | solution.py:223
  18.2 1.2 %collective-permute-start.14 = (bf16[1,16,1152]{2,1,0:T(8,128)(2,1)S(1)}, bf16[1,16,1152]{2,1,0:T(8,128)(2,1)S(1)}, u32[]{:S(2)}, u32[]{:S(2)}) collective-permute-start(bf16[1,16,1152]{2,1,0:T(8,128)(2,1)S(1)} %collective-permute-done.4.refs_7_), channel_id=1, source_target_pairs={{0,8},{8,0},{1,9},{9,1},{2,10},{10,2},{3,11},{11,3},{4,12},{12,4},... | collective-permute-start | bytes 110600 | tf_op jit(solution)/shard_map/ppermute | solution.py:223
  18.2 29.0 %collective-permute-start.7 = (bf16[2,16,1152]{2,1,0:T(8,128)(2,1)S(1)}, bf16[2,16,1152]{2,1,0:T(8,128)(2,1)S(1)}, u32[]{:S(2)}, u32[]{:S(2)}) collective-permute-start(bf16[2,16,1152]{2,1,0:T(8,128)(2,1)S(1)} %get-tuple-element.28.refs_0_), channel_id=1, source_target_pairs={{0,8},{8,0},{1,9},{9,1},{2,10},{10,2},{3,11},{11,3},{4,12},{12,4},... | collective-permute-start | bytes 221192 | tf_op jit(solution)/shard_map/ppermute | solution.py:223
  19.4 14.0 %collective-permute-start.11 = (bf16[1,16,1152]{2,1,0:T(8,128)(2,1)S(1)}, bf16[1,16,1152]{2,1,0:T(8,128)(2,1)S(1)}, u32[]{:S(2)}, u32[]{:S(2)}) collective-permute-start(bf16[1,16,1152]{2,1,0:T(8,128)(2,1)S(1)} %collective-permute-done.5.refs_4_), channel_id=1, source_target_pairs={{0,8},{8,0},{1,9},{9,1},{2,10},{10,2},{3,11},{11,3},{4,12},{12,4},... | collective-permute-start | bytes 110600 | tf_op jit(solution)/shard_map/ppermute | solution.py:223
  19.6 27.6 %collective-permute-start.8 = (bf16[2,16,1152]{2,1,0:T(8,128)(2,1)S(1)}, bf16[2,16,1152]{2,1,0:T(8,128)(2,1)S(1)}, u32[]{:S(2)}, u32[]{:S(2)}) collective-permute-start(bf16[2,16,1152]{2,1,0:T(8,128)(2,1)S(1)} %collective-permute-done.refs_1_), channel_id=1, source_target_pairs={{0,8},{8,0},{1,9},{9,1},{2,10},{10,2},{3,11},{11,3},{4,12},{12,4},... | collective-permute-start | bytes 221192 | tf_op jit(solution)/shard_map/ppermute | solution.py:223
  19.9 27.3 %collective-permute-start.9 = (bf16[2,16,1152]{2,1,0:T(8,128)(2,1)S(1)}, bf16[2,16,1152]{2,1,0:T(8,128)(2,1)S(1)}, u32[]{:S(2)}, u32[]{:S(2)}) collective-permute-start(bf16[2,16,1152]{2,1,0:T(8,128)(2,1)S(1)} %collective-permute-done.1.refs_2_), channel_id=1, source_target_pairs={{0,8},{8,0},{1,9},{9,1},{2,10},{10,2},{3,11},{11,3},{4,12},{12,4},... | collective-permute-start | bytes 221192 | tf_op jit(solution)/shard_map/ppermute | solution.py:223
  20.1 27.1 %collective-permute-start.10 = (bf16[2,16,1152]{2,1,0:T(8,128)(2,1)S(1)}, bf16[2,16,1152]{2,1,0:T(8,128)(2,1)S(1)}, u32[]{:S(2)}, u32[]{:S(2)}) collective-permute-start(bf16[2,16,1152]{2,1,0:T(8,128)(2,1)S(1)} %collective-permute-done.2.refs_3_), channel_id=1, source_target_pairs={{0,8},{8,0},{1,9},{9,1},{2,10},{10,2},{3,11},{11,3},{4,12},{12,4},... | collective-permute-start | bytes 221192 | tf_op jit(solution)/shard_map/ppermute | solution.py:223
  33.5 13.7 %collective-permute-start.12 = (bf16[1,16,1152]{2,1,0:T(8,128)(2,1)S(1)}, bf16[1,16,1152]{2,1,0:T(8,128)(2,1)S(1)}, u32[]{:S(2)}, u32[]{:S(2)}) collective-permute-start(bf16[1,16,1152]{2,1,0:T(8,128)(2,1)S(1)} %collective-permute-done.6.refs_5_), channel_id=1, source_target_pairs={{0,8},{8,0},{1,9},{9,1},{2,10},{10,2},{3,11},{11,3},{4,12},{12,4},... | collective-permute-start | bytes 110600 | tf_op jit(solution)/shard_map/ppermute | solution.py:223
  56.8 1.3 %collective-permute-start.15 = (bf16[2,16,1152]{2,1,0:T(8,128)(2,1)S(1)}, bf16[2,16,1152]{2,1,0:T(8,128)(2,1)S(1)}, u32[]{:S(2)}, u32[]{:S(2)}) collective-permute-start(bf16[2,16,1152]{2,1,0:T(8,128)(2,1)S(1)} %all_gather.12.refs_4_), channel_id=1, source_target_pairs={{0,8},{8,0},{1,9},{9,1},{2,10},{10,2},{3,11},{11,3},{4,12},{12,4},... | collective-permute-start | bytes 221192 | tf_op jit(solution)/shard_map/ppermute | solution.py:223
  56.9 1.4 %collective-permute-start.16 = (bf16[2,16,1152]{2,1,0:T(8,128)(2,1)S(1)}, bf16[2,16,1152]{2,1,0:T(8,128)(2,1)S(1)}, u32[]{:S(2)}, u32[]{:S(2)}) collective-permute-start(bf16[2,16,1152]{2,1,0:T(8,128)(2,1)S(1)} %all_gather.13.refs_5_), channel_id=1, source_target_pairs={{0,8},{8,0},{1,9},{9,1},{2,10},{10,2},{3,11},{11,3},{4,12},{12,4},... | collective-permute-start | bytes 221192 | tf_op jit(solution)/shard_map/ppermute | solution.py:223
  57.4 1.3 %collective-permute-start.17 = (bf16[2,16,1152]{2,1,0:T(8,128)(2,1)S(1)}, bf16[2,16,1152]{2,1,0:T(8,128)(2,1)S(1)}, u32[]{:S(2)}, u32[]{:S(2)}) collective-permute-start(bf16[2,16,1152]{2,1,0:T(8,128)(2,1)S(1)} %all_gather.14.refs_6_), channel_id=1, source_target_pairs={{0,8},{8,0},{1,9},{9,1},{2,10},{10,2},{3,11},{11,3},{4,12},{12,4},... | collective-permute-start | bytes 221192 | tf_op jit(solution)/shard_map/ppermute | solution.py:223
  57.5 1.3 %collective-permute-start.18 = (bf16[2,16,1152]{2,1,0:T(8,128)(2,1)S(1)}, bf16[2,16,1152]{2,1,0:T(8,128)(2,1)S(1)}, u32[]{:S(2)}, u32[]{:S(2)}) collective-permute-start(bf16[2,16,1152]{2,1,0:T(8,128)(2,1)S(1)} %all_gather.15.refs_7_), channel_id=1, source_target_pairs={{0,8},{8,0},{1,9},{9,1},{2,10},{10,2},{3,11},{11,3},{4,12},{12,4},... | collective-permute-start | bytes 221192 | tf_op jit(solution)/shard_map/ppermute | solution.py:223

commit v7 on v6

--- a/solution.py
+++ b/solution.py
@@ -12,7 +12,7 @@
 
 BINS = 128
 LANES = 128
-CUTS = 6
+CUTS = 2
 MIB = 1024 * 1024
 
 
@@ -35,7 +35,7 @@
     ]
 
 
-def whiten_kernel(group, near, spectrum_ref, *refs):
+def whiten_kernel(group, spectrum_ref, *refs):
     pieces, rows_ref = refs[:-1], refs[-1]
     windows, channels, columns = spectrum_ref.shape
     bins = columns // 2
@@ -63,36 +63,19 @@
         whitened = (parts * inverse).astype(jnp.bfloat16)
         rows_ref[..., lane : lane + cols] = whitened.reshape(rows_ref.shape[:-1] + (cols,))
 
-    if near is None:
+    if len(pieces) == 1:
         pieces[0][...] = rows_ref[...]
     else:
-        me = lax.axis_index("freq")
-        for mask in range(near):
-            pieces[mask][...] = rows_ref[me ^ mask]
-        for i, piece in enumerate(pieces[near:]):
-            mask, which = near + i % near, i // near
-            piece[0] = rows_ref[me ^ mask, which]
+        for which, piece in enumerate(pieces):
+            piece[...] = rows_ref[:, which]
 
 
 def swap_halves(tile):
     return pltpu.roll(tile, LANES // 2, axis=1)
 
 
-def rows_of(refs, which, kinds):
-    for ref, kind in zip(refs, kinds):
-        if kind == "groups":
-            yield ref[which]
-        elif kind == "pair":
-            near = lax.axis_size("freq") // 2
-            yield ref[1 - lax.axis_index("freq") // near]
-        else:
-            yield ref[0]
-
-
-def outer_kernel(bins, scale, which, kinds, *refs):
+def outer_kernel(bins, scale, which, own_ref, other_ref, *refs):
     out_ref, right, left, slots, sems = refs[-5:]
-    count = len(kinds)
-    own_refs, other_refs = refs[:count], refs[count : 2 * count]
     half = LANES // 2
     channels = out_ref.shape[2]
     full = channels // LANES
@@ -116,11 +99,10 @@
     @pl.when(step == 0)
     def _():
         me = lax.axis_index("chan")
+        rows = own_ref.shape[0] * own_ref.shape[1]
         own, other = (
-            jnp.concatenate([rows.astype(jnp.float32) for rows in rows_of(some, which, kinds)])
-            for some in (own_refs, other_refs)
+            ref[...].astype(jnp.float32).reshape(rows, ref.shape[2]) for ref in (own_ref, other_ref)
         )
-        rows = own.shape[0]
         block0 = jnp.where(me == 0, own, other)
         block1 = jnp.where(me == 0, other, own)
         row = lax.broadcasted_iota(jnp.int32, (rows, 1), 0)
@@ -207,18 +189,6 @@
     out_ref[...] = in_ref[...]
 
 
-def exchange(value, mask):
-    pairs = [(source, source ^ mask) for source in range(lax.axis_size("freq"))]
-    return lax.ppermute(value, "freq", pairs)
-
-
-def gather_pair(value, mask):
-    pairs = sorted({(min(i, i ^ mask), max(i, i ^ mask)) for i in range(lax.axis_size("freq"))})
-    return lax.all_gather(
-        value, "freq", axis_index_groups=[list(pair) for pair in pairs], tiled=True
-    )
-
-
 def swap(value):
     return lax.ppermute(value, "chan", [(0, 1), (1, 0)])
 
@@ -236,10 +206,9 @@
     lanes = local_windows * local_channels
     vmem = pl.BlockSpec(memory_space=pltpu.VMEM)
     memory = pl.BlockSpec(memory_space=pl.ANY)
-    near = devices // 2 if aligned else None
     if aligned:
         rows = (devices, groups, 2 * bins, lanes)
-        shapes = [rows[1:]] * near + [(1,) + rows[2:]] * (groups * near)
+        shapes = [(devices, 2 * bins, lanes)] * groups
     else:
         rows = (2 * BINS, lanes)
         shapes = [rows]
@@ -255,7 +224,7 @@
     spectrum = spectrum.astype(jnp.bfloat16)
     with jax.named_scope("whiten"):
         whitened = pl.pallas_call(
-            functools.partial(whiten_kernel, group, near),
+            functools.partial(whiten_kernel, group),
             out_shape=[jax.ShapeDtypeStruct(shape, jnp.bfloat16) for shape in shapes],
             in_specs=[vmem],
             out_specs=[vmem] * len(shapes),
@@ -265,38 +234,22 @@
                 flops=40 * BINS * lanes, bytes_accessed=12 * BINS * lanes, transcendentals=BINS * lanes
             ),
         )(spectrum)
-    if aligned:
-        own = {mask: whitened[mask] for mask in range(near)}
-        far = [whitened[near * (1 + g) : near * (2 + g)] for g in range(groups)]
-        first = {}
-        for mask in (1, 2, *range(devices - 1, near - 1, -1), *range(3, near)):
-            if mask < near:
-                own[mask] = exchange(own[mask], mask)
-            else:
-                first[mask] = exchange(far[0][mask - near], mask)
-        sources = [[*own.values(), *first.values()]]
-        kinds = [["groups"] * near + ["whole"] * near]
-        for g in range(1, groups):
-            later, held = lax.optimization_barrier((far[g], sources[-1][-2:]))
-            sources[-1][-2:] = held
-            gathered = [gather_pair(value, near + i) for i, value in enumerate(later)]
-            sources.append([*own.values(), *gathered])
-            kinds.append(["groups"] * near + ["pair"] * near)
-        near_other = [swap(value) for value in own.values()]
-    else:
-        rows = whitened[0].reshape(2, devices, groups, bins, lanes).transpose(1, 2, 0, 3, 4)
-        rows = rows.reshape(devices, groups, 2 * bins, lanes)
-        rows = lax.all_to_all(rows, "freq", split_axis=0, concat_axis=0, tiled=True)
-        own = rows.transpose(1, 0, 2, 3).reshape(groups, devices * 2 * bins, lanes)
-        near, near_other = 1, [swap(own)]
-        sources, kinds = [[own]] * groups, [["groups"]] * groups
+    if not aligned:
+        rows = whitened[0].reshape(2, devices, groups, bins, lanes).transpose(2, 1, 0, 3, 4)
+        whitened = rows.reshape(groups, devices, 2 * bins, lanes)
+    sources = [
+        lax.all_to_all(whitened[g], "freq", split_axis=0, concat_axis=0, tiled=True)
+        for g in range(groups)
+    ]
+    if not aligned:
+        sources = [own.reshape(1, devices * 2 * bins, lanes) for own in sources]
     depth = local_windows * devices * 2 * bins
     out = None
     for g in range(groups):
-        later = sources[g][near:]
-        if out is not None and later:
-            later, out = lax.optimization_barrier((later, out))
-        operands = [*sources[g][:near], *later, *near_other, *map(swap, later)]
+        own = sources[g]
+        if out is not None:
+            own, out = lax.optimization_barrier((own, out))
+        operands = [own, swap(own)]
         specs = [vmem] * len(operands)
         aliases = {}
         if out is not None:
@@ -304,7 +257,7 @@
             operands, specs = [*operands, out], [*specs, memory]
         with jax.named_scope("outer_products"):
             out = pl.pallas_call(
-                functools.partial(outer_kernel, bins, 1.0 / windows, g, kinds[g]),
+                functools.partial(outer_kernel, bins, 1.0 / windows, g),
                 out_shape=jax.ShapeDtypeStruct(
                     (2, local_bins, local_channels, 2 * local_channels), jnp.bfloat16
                 ),

time: 68.6 us -> 46.2 us (0.67)
  starting transfers between devices: 14.3 us -> 3.43 us
  blocking collectives: 26.7 us -> 17.4 us
  waiting for transfers between devices: 4.78 us -> 2.93 us
    all_gather x4 -> x0, blocking collectives: 26.7 us -> none  [gather_pair(): lax.all_gather(value, 'freq', axis_index_groups=[list(pair) for pair in p...]
    all_to_all x0 -> x1, blocking collectives: none -> 17.4 us  [local(): lax.all_to_all(whitened[g], 'freq', split_axis=0, concat_axis=0, tiled=True)]
    ppermute x7 -> x0, starting transfers between devices: 11.7 us -> none  [exchange(): return lax.ppermute(value, 'freq', pairs)]
    all_to_all x0 -> x1, starting transfers between devices: none -> 3.42 us  [local(): lax.all_to_all(whitened[g], 'freq', split_axis=0, concat_axis=0, tiled=True)]
    ppermute x7 -> x0, waiting for transfers between devices: 3.16 us -> none  [exchange(): return lax.ppermute(value, 'freq', pairs)]
    ppermute x12 -> x2, starting transfers between devices: 2.59 us -> 0.01 us  [swap(): return lax.ppermute(value, 'chan', [(0, 1), (1, 0)])]
    all_to_all x0 -> x1, waiting for transfers between devices: none -> 1.34 us  [local(): lax.all_to_all(whitened[g], 'freq', split_axis=0, concat_axis=0, tiled=True)]
    ppermute x12 -> x2, waiting for transfers between devices: 1.63 us -> 1.58 us  [swap(): return lax.ppermute(value, 'chan', [(0, 1), (1, 0)])]
  transfers between devices with their start and end apart: 19 -> 3, of which waited for: 7 -> 2; matrix products, arithmetic and copies ran while one was open for 0% -> 0% of each run, Pallas kernels for 0% -> 20%
where the time goes in v7:
time: 46.2 us; the launch traced here: 45.9 us
  Pallas kernels  19.6 us (42%)
  blocking collectives  17.4 us (38%)
  starting transfers between devices  3.43 us (7%)
  waiting for transfers between devices  2.93 us (6%)
  local copies, waits for them, and re-layouts  1.78 us (4%)
  matrix products  0.79 us (2%)
    pallas_call x2, Pallas kernels, local(): pl.pallas_call(functools.partial(outer_kernel, bins, 1.0 / windows, g), o...  18.1 us
    all_to_all x1, blocking collectives, local(): lax.all_to_all(whitened[g], 'freq', split_axis=0, concat_axis=0, tiled=True)  17.4 us
    all_to_all x1, starting transfers between devices, local(): lax.all_to_all(whitened[g], 'freq', split_axis=0, concat_axis=0, tiled=True)  3.42 us
    unnamed x4, local copies, waits for them, and re-layouts  1.78 us
    ppermute x2, waiting for transfers between devices, swap(): return lax.ppermute(value, 'chan', [(0, 1), (1, 0)])  1.58 us
    pallas_call x1, Pallas kernels, local(): pl.pallas_call(functools.partial(whiten_kernel, group), out_shape=[jax.Sh...  1.42 us
    all_to_all x1, waiting for transfers between devices, local(): lax.all_to_all(whitened[g], 'freq', split_axis=0, concat_axis=0, tiled=True)  1.34 us
  transfers between devices with their start and end apart: 3, of which 2 were waited for; matrix products, arithmetic and copies ran while one was open for 0% of the time, Pallas kernels for 20%

profile of v7, /device:TPU:0, one launch (start us, length us, event | category | flops | bytes accessed | tf_op | source)
XLA Modules:
  0.0 45.9 jit_solution(16409896752616329253)
XLA Ops:
  0.0 0.0 copy-start
  0.0 0.0 copy-start.1
  0.0 1.2 %copy-done.1 = bf16[1024,256]{1,0:T(8,128)(2,1)S(1)} copy-done((bf16[1024,256]{1,0:T(8,128)(2,1)S(1)}, bf16[1024,256]{1,0:T(8,128)(2,1)}, u32[]{:S(2)}) %copy-start.1) | copy-done | bytes 524312
  1.2 0.6 %copy-done = bf16[576,2,1024]{2,1,0:T(2,128)(2,1)S(1)} copy-done((bf16[576,2,1024]{2,1,0:T(2,128)(2,1)S(1)}, bf16[576,2,1024]{2,1,0:T(2,128)(2,1)}, u32[]{:S(2)}) %copy-start) | copy-done | bytes 2359320
  1.8 0.8 %fusion.5.spectrum_ref = bf16[2,576,256]{2,1,0:T(8,128)(2,1)S(1)} fusion(bf16[576,2,1024]{2,1,0:T(2,128)(2,1)S(1)} %copy-done, bf16[1024,256]{1,0:T(8,128)(2,1)S(1)} %table.1), kind=kOutput, calls=%fused_computation.3 | convolution fusion | flops 604274688 | bytes 3473408 | tf_op jit(solution)/shard_map/cws,sj->wcj/dot_general | solution.py:223
  2.6 1.4 %whiten.1 = (bf16[8,16,1152]{2,1,0:T(8,128)(2,1)S(1)}, bf16[8,16,1152]{2,1,0:T(8,128)(2,1)}) custom-call(bf16[2,576,256]{2,1,0:T(8,128)(2,1)S(1)} %fusion.5.spectrum_ref), custom_call_target="tpu_custom_call" | custom-call | flops 5898240 | bytes 1769472 | tf_op jit(solution)/shard_map/whiten/pallas_call | solution.py:226
  4.0 17.4 %all_to_all.10.own_ref = bf16[8,16,1152]{2,1,0:T(8,128)(2,1)S(1)} all-to-all(bf16[8,16,1152]{2,1,0:T(8,128)(2,1)S(1)} %get-tuple-element.10), channel_id=1, replica_groups=mesh['hours'=2,'chan'=2,'freq'=8] {'freq'}, dimensions={0} | all-to-all | bytes 589824 | tf_op jit(solution)/shard_map/all_to_all | solution.py:241
  21.4 0.0 collective-permute-start
  21.4 3.4 %all-to-all-start = ((bf16[8,16,1152]{2,1,0:T(8,128)(2,1)}), bf16[8,16,1152]{2,1,0:T(8,128)(2,1)S(1)}, u32[]{:S(2)}, u32[]{:S(2)}) async-start(bf16[8,16,1152]{2,1,0:T(8,128)(2,1)} %get-tuple-element.9), calls=%async_computation | async-start | bytes 589824 | tf_op jit(solution)/shard_map/all_to_all | solution.py:241
  24.9 0.0 collective-permute-done.other_ref
  24.9 9.1 %outer_products.2.refs_0_ = bf16[2,16,576,1152]{3,2,1,0:T(8,128)(2,1)} custom-call(bf16[8,16,1152]{2,1,0:T(8,128)(2,1)S(1)} %all_to_all.10.own_ref, bf16[8,16,1152]{2,1,0:T(8,128)(2,1)S(1)} %collective-permute-done.other_ref), custom_call_target="tpu_custom_call" | custom-call | flops 5435817984 | bytes 21233664 | tf_op jit(solution)/shard_map/outer_products/pallas_call | solution.py:259
  34.0 1.3 %all-to-all-done.own_ref = bf16[8,16,1152]{2,1,0:T(8,128)(2,1)S(1)} async-done(((bf16[8,16,1152]{2,1,0:T(8,128)(2,1)}), bf16[8,16,1152]{2,1,0:T(8,128)(2,1)S(1)}, u32[]{:S(2)}, u32[]{:S(2)}) %all-to-all-start) | async-done | bytes 294944 | tf_op jit(solution)/shard_map/all_to_all | solution.py:241
  35.3 0.0 collective-permute-start.1
  35.3 1.6 %collective-permute-done.1.other_ref = bf16[8,16,1152]{2,1,0:T(8,128)(2,1)S(1)} collective-permute-done((bf16[8,16,1152]{2,1,0:T(8,128)(2,1)S(1)}, bf16[8,16,1152]{2,1,0:T(8,128)(2,1)S(1)}, u32[]{:S(2)}, u32[]{:S(2)}) %collective-permute-start.1) | collective-permute-done | bytes 294944 | tf_op jit(solution)/shard_map/ppermute | solution.py:193
  36.9 9.0 %outer_products.3 = bf16[2,16,576,1152]{3,2,1,0:T(8,128)(2,1)} custom-call(bf16[8,16,1152]{2,1,0:T(8,128)(2,1)S(1)} %all-to-all-done.own_ref, bf16[8,16,1152]{2,1,0:T(8,128)(2,1)S(1)} %collective-permute-done.1.other_ref, bf16[2,16,576,1152]{3,2,1,0:T(8,128)(2,1)} %outer_products.2.refs_0_), custom_call_target="tpu_custom_call", output_to_operand_aliasing={{}: (2, {})} | custom-call | flops 5435817984 | bytes 21233664 | tf_op jit(solution)/shard_map/outer_products/pallas_call | solution.py:259
  (1 shorter events, 0.0 us)
Async XLA Ops:
  0.0 1.8 %copy-start = (bf16[576,2,1024]{2,1,0:T(2,128)(2,1)S(1)}, bf16[576,2,1024]{2,1,0:T(2,128)(2,1)}, u32[]{:S(2)}) copy-start(bf16[576,2,1024]{2,1,0:T(2,128)(2,1)} %param.2) | copy-start | bytes 7077892
  0.0 1.2 %copy-start.1 = (bf16[1024,256]{1,0:T(8,128)(2,1)S(1)}, bf16[1024,256]{1,0:T(8,128)(2,1)}, u32[]{:S(2)}) copy-start(bf16[1024,256]{1,0:T(8,128)(2,1)} %constant.2.clone.in_ref) | copy-start | bytes 1572868
  21.4 3.4 %collective-permute-start = (bf16[8,16,1152]{2,1,0:T(8,128)(2,1)S(1)}, bf16[8,16,1152]{2,1,0:T(8,128)(2,1)S(1)}, u32[]{:S(2)}, u32[]{:S(2)}) collective-permute-start(bf16[8,16,1152]{2,1,0:T(8,128)(2,1)S(1)} %all_to_all.10.own_ref), channel_id=1, source_target_pairs={{0,8},{8,0},{1,9},{9,1},{2,10},{10,2},{3,11},{11,3},{4,12},{12,4},... | collective-permute-start | bytes 884744 | tf_op jit(solution)/shard_map/ppermute | solution.py:193
  21.4 13.9 %all-to-all-start = ((bf16[8,16,1152]{2,1,0:T(8,128)(2,1)}), bf16[8,16,1152]{2,1,0:T(8,128)(2,1)S(1)}, u32[]{:S(2)}, u32[]{:S(2)}) async-start(bf16[8,16,1152]{2,1,0:T(8,128)(2,1)} %get-tuple-element.9), calls=%async_computation | async-start | bytes 589824 | tf_op jit(solution)/shard_map/all_to_all | solution.py:241
  35.3 1.6 %collective-permute-start.1 = (bf16[8,16,1152]{2,1,0:T(8,128)(2,1)S(1)}, bf16[8,16,1152]{2,1,0:T(8,128)(2,1)S(1)}, u32[]{:S(2)}, u32[]{:S(2)}) collective-permute-start(bf16[8,16,1152]{2,1,0:T(8,128)(2,1)S(1)} %all-to-all-done.own_ref), channel_id=1, source_target_pairs={{0,8},{8,0},{1,9},{9,1},{2,10},{10,2},{3,11},{11,3},{4,12},{12,4},... | collective-permute-start | bytes 884744 | tf_op jit(solution)/shard_map/ppermute | solution.py:193

commit v8 on v5

--- a/solution.py
+++ b/solution.py
@@ -34,7 +34,7 @@
     ]
 
 
-def whiten_kernel(group, near, spectrum_ref, *refs):
+def whiten_kernel(group, masks, spectrum_ref, *refs):
     pieces, rows_ref = refs[:-1], refs[-1]
     windows, channels, columns = spectrum_ref.shape
     bins = columns // 2
@@ -62,14 +62,11 @@
         whitened = (parts * inverse).astype(jnp.bfloat16)
         rows_ref[..., lane : lane + cols] = whitened.reshape(rows_ref.shape[:-1] + (cols,))
 
-    if near is None:
+    if len(pieces) == 1:
         pieces[0][...] = rows_ref[...]
     else:
         me = lax.axis_index("freq")
-        first = (me // near) * near
-        for i in range(near):
-            pieces[0][i] = rows_ref[first + i]
-        for mask, piece in enumerate(pieces[1:], near):
+        for mask, piece in zip(masks, pieces):
             piece[...] = rows_ref[me ^ mask]
 
 
@@ -77,16 +74,27 @@
     return pltpu.roll(tile, LANES // 2, axis=1)
 
 
-def rows_of(refs, which):
-    for ref in refs:
-        if len(ref.shape) == 3:
-            yield ref[which]
-        else:
-            for i in range(ref.shape[0]):
-                yield ref[i, which]
-
-
-def outer_kernel(bins, scale, *refs):
+def split_rows(tile, bins, sets):
+    rows, lanes = tile.shape
+    if sets == 1:
+        first_part = (lax.broadcasted_iota(jnp.int32, (rows, 1), 0) // bins) % 2 == 0
+        rotated = jnp.where(
+            first_part, -pltpu.roll(tile, rows - bins, axis=0), pltpu.roll(tile, bins, axis=0)
+        )
+        return [(tile, rotated)]
+    parts = tile.reshape(rows // (2 * bins), 2, bins, lanes)
+    real, imag = parts[:, 0], parts[:, 1]
+    within = bins // sets
+    low = lax.broadcasted_iota(jnp.int32, real.shape, 1) < within
+    turned_real, turned_imag = (pltpu.roll(part, within, axis=1) for part in (real, imag))
+    found = [
+        (jnp.where(low, real, turned_imag), jnp.where(low, -imag, turned_real)),
+        (jnp.where(low, turned_real, imag), jnp.where(low, -turned_imag, real)),
+    ]
+    return [tuple(part.reshape(rows // sets, lanes) for part in pair) for pair in found]
+
+
+def outer_kernel(bins, sets, scale, *refs):
     out_ref, right, left, slots, sems = refs[-5:]
     count = (len(refs) - 5) // 2
     own_refs, other_refs = refs[:count], refs[count:-5]
@@ -115,13 +123,11 @@
     def _():
         me = lax.axis_index("chan")
         which = pl.program_id(0)
-        own = jnp.concatenate([rows.astype(jnp.float32) for rows in rows_of(own_refs, which)])
-        other = jnp.concatenate([rows.astype(jnp.float32) for rows in rows_of(other_refs, which)])
+        own = jnp.concatenate([ref[which].astype(jnp.float32) for ref in own_refs])
+        other = jnp.concatenate([ref[which].astype(jnp.float32) for ref in other_refs])
         rows = own.shape[0]
         block0 = jnp.where(me == 0, own, other)
         block1 = jnp.where(me == 0, other, own)
-        row = lax.broadcasted_iota(jnp.int32, (rows, 1), 0)
-        first_part = (row // bins) % 2 == 0
         low = lax.broadcasted_iota(jnp.int32, (rows, LANES), 1) < half
 
         def tiles_of(block, w):
@@ -133,8 +139,9 @@
             both = jnp.where(low, last, turned) if w == 0 else jnp.where(low, turned, last)
             return tiles, both
 
+        share = rows // sets
         for w in range(2):
-            at = pl.ds(w * rows, rows)
+            at = pl.ds(w * share, share)
             tiles, last0 = tiles_of(block0, w)
             tiles1, last1 = tiles_of(block1, w)
             turned = [swap_halves(tile) for tile in tiles1]
@@ -143,29 +150,31 @@
                 jnp.where(low, chain[j], chain[j + 1]) for j in range(len(chain) - 1)
             ]
             for j, tile in enumerate(tiles):
-                rotated = jnp.where(
-                    first_part,
-                    -pltpu.roll(tile, rows - bins, axis=0),
-                    pltpu.roll(tile, bins, axis=0),
-                )
-                right[at, j * LANES : (j + 1) * LANES] = tile.astype(jnp.bfloat16)
-                right[at, 2 * channels + j * LANES : 2 * channels + (j + 1) * LANES] = (
-                    rotated.astype(jnp.bfloat16)
-                )
+                lanes = slice(j * LANES, (j + 1) * LANES)
+                lanes_imag = slice(2 * channels + j * LANES, 2 * channels + (j + 1) * LANES)
+                for q, (plain, rotated) in enumerate(split_rows(tile, bins, sets)):
+                    right[q, at, lanes] = plain.astype(jnp.bfloat16)
+                    right[q, at, lanes_imag] = rotated.astype(jnp.bfloat16)
         scaled = own * scale
-        for j in range(full):
-            for w in range(2):
-                lanes = (2 * j + w) * LANES
-                left[j * LANES : (j + 1) * LANES, w * rows : (w + 1) * rows] = scaled[
-                    :, lanes : lanes + LANES
-                ].T
-        last = scaled[:, 2 * full * LANES :].T
-        for w in range(2):
-            left[full * LANES :, w * rows : (w + 1) * rows] = last[w * half : (w + 1) * half]
-
-    depth = left.shape[1]
+        for j in range(full + 1):
+            block = scaled[:, 2 * j * LANES : (2 * j + 2) * LANES]
+            if j < full:
+                windows = [block[:, :LANES], block[:, LANES:]]
+            else:
+                windows = [block, swap_halves(block)]
+            kept = min(LANES, channels - j * LANES)
+            pieces = [split_rows(window, bins, sets) for window in windows]
+            for q in range(sets):
+                turned = jnp.concatenate([piece[q][0] for piece in pieces]).T
+                left[q, j * LANES : j * LANES + kept] = turned[:kept]
+
+    depth = left.shape[2]
+    within = bins // sets
     lane = lax.broadcasted_iota(jnp.int32, (1, depth), 1)
-    chosen = jnp.where((lane & (bins - 1)) == step, left[...], 0.0).astype(jnp.bfloat16)
+    taken = (lane & (within - 1)) == (step & (within - 1))
+    chosen = jnp.where(taken, left[step // within], 0.0).astype(jnp.bfloat16)
+    weights = right.at[step // within]
+
     @pl.when(now >= depth_of_slots)
     def _():
         wait_for(now - depth_of_slots)
@@ -178,7 +187,7 @@
 
     def multiply(first, last):
         return jnp.dot(
-            chosen, right[:, first:last], preferred_element_type=jnp.float32
+            chosen, weights[:, first:last], preferred_element_type=jnp.float32
         ).astype(jnp.bfloat16)
 
     def send(part):
@@ -206,7 +215,7 @@
 
 def exchange(value, mask):
     pairs = [(source, source ^ mask) for source in range(lax.axis_size("freq"))]
-    return lax.ppermute(value, "freq", pairs)
+    return lax.ppermute(value, "freq", pairs) if mask else value
 
 
 def swap(value):
@@ -220,16 +229,16 @@
     windows = local_windows * devices
     bins = min(local_bins, 128 // (2 * devices))
     groups = local_bins // bins
-    aligned = bins % 8 == 0
+    aligned = bins == 8
     group = bins if aligned else BINS
     table = jnp.asarray(bin_table(length, BINS, group))
     lanes = local_windows * local_channels
     vmem = pl.BlockSpec(memory_space=pltpu.VMEM)
     memory = pl.BlockSpec(memory_space=pl.ANY)
-    near = devices // 2 if aligned else None
-    pieces = devices - near + 1 if aligned else 1
+    masks = [1, 2, *range(devices - 1, 2, -1), 0] if aligned else [0]
+    pieces = len(masks)
     rows = (devices, groups, 2 * bins, lanes) if aligned else (2 * BINS, lanes)
-    shapes = [(near,) + rows[1:]] + [rows[1:]] * (pieces - 1) if aligned else [rows]
+    piece = rows[1:] if aligned else rows
     with jax.named_scope("table"):
         table = pl.pallas_call(
             copy_kernel,
@@ -242,8 +251,8 @@
     spectrum = spectrum.astype(jnp.bfloat16)
     with jax.named_scope("whiten"):
         whitened = pl.pallas_call(
-            functools.partial(whiten_kernel, group, near),
-            out_shape=[jax.ShapeDtypeStruct(shape, jnp.bfloat16) for shape in shapes],
+            functools.partial(whiten_kernel, group, masks),
+            out_shape=[jax.ShapeDtypeStruct(piece, jnp.bfloat16)] * pieces,
             in_specs=[vmem],
             out_specs=[vmem] * pieces,
             scratch_shapes=[pltpu.VMEM(rows, jnp.bfloat16)],
@@ -253,22 +262,18 @@
             ),
         )(spectrum)
     if aligned:
-        far = [exchange(value, mask) for mask, value in enumerate(whitened[1:], near)]
-        grouped = [list(range(first, first + near)) for first in range(0, devices, near)]
-        own = lax.all_to_all(
-            whitened[0], "freq", split_axis=0, concat_axis=0, tiled=True, axis_index_groups=grouped
-        )
-        own = [own] + far
+        own = [exchange(value, mask) for mask, value in zip(masks, whitened)]
     else:
         rows = whitened[0].reshape(2, devices, groups, bins, lanes).transpose(1, 2, 0, 3, 4)
         rows = rows.reshape(devices, groups, 2 * bins, lanes)
         rows = lax.all_to_all(rows, "freq", split_axis=0, concat_axis=0, tiled=True)
         own = [rows.transpose(1, 0, 2, 3).reshape(groups, devices * 2 * bins, lanes)]
     other = [swap(value) for value in own]
-    depth = local_windows * devices * 2 * bins
+    sets = 2 if aligned else 1
+    depth = local_windows * devices * 2 * bins // sets
     with jax.named_scope("outer_products"):
         out = pl.pallas_call(
-            functools.partial(outer_kernel, bins, 1.0 / windows),
+            functools.partial(outer_kernel, bins, sets, 1.0 / windows),
             out_shape=jax.ShapeDtypeStruct(
                 (2, local_bins, local_channels, 2 * local_channels), jnp.bfloat16
             ),
@@ -276,8 +281,8 @@
             in_specs=[vmem] * (2 * pieces),
             out_specs=memory,
             scratch_shapes=[
-                pltpu.VMEM((depth, 4 * local_channels), jnp.bfloat16),
-                pltpu.VMEM((local_channels, depth), jnp.float32),
+                pltpu.VMEM((sets, depth, 4 * local_channels), jnp.bfloat16),
+                pltpu.VMEM((sets, local_channels, depth), jnp.float32),
                 pltpu.VMEM((3, 2, local_channels, 2 * local_channels), jnp.bfloat16),
                 pltpu.SemaphoreType.DMA((3, 2, 2)),
             ],

time: 47.9 us -> 42.8 us (0.89); the launches traced: 47.2 us -> 42.7 us
  blocking collectives: 11.4 us -> 0 us
  starting transfers between devices: 8.23 us -> 13.5 us
  waiting for transfers between devices: 7.26 us -> 8.97 us
    all_to_all x1 -> x0, blocking collectives: 11.4 us -> none  [local(): lax.all_to_all(whitened[0], 'freq', split_axis=0, concat_axis=0, tiled=Tr...]
    ppermute x4 -> x7, starting transfers between devices: 7.65 us -> 12.4 us  [exchange(): return lax.ppermute(value, 'freq', pairs) if mask else value]
    ppermute x4 -> x7, waiting for transfers between devices: 6.07 us -> 7.77 us  [exchange(): return lax.ppermute(value, 'freq', pairs) if mask else value]
    ppermute x5 -> x8, starting transfers between devices: 0.59 us -> 1.1 us  [swap(): return lax.ppermute(value, 'chan', [(0, 1), (1, 0)])]
    ppermute x5 -> x8, waiting for transfers between devices: 1.2 us -> 1.2 us  [swap(): return lax.ppermute(value, 'chan', [(0, 1), (1, 0)])]
  transfers between devices with their start and end apart: 9 -> 15, of which waited for: 5 -> 8; matrix products, arithmetic and copies ran while one was open for 0% -> 0% of each run, Pallas kernels for 0% -> 0%
where the time goes in v8:
time: 42.8 us; the launch traced here: 42.7 us
  Pallas kernels  17.6 us (41%)
  starting transfers between devices  13.5 us (32%)
  waiting for transfers between devices  8.97 us (21%)
  local copies, waits for them, and re-layouts  1.78 us (4%)
  matrix products  0.79 us (2%)
    pallas_call x1, Pallas kernels, local(): pl.pallas_call(functools.partial(outer_kernel, bins, sets, 1.0 / windows)...  16.9 us
    ppermute x7, starting transfers between devices, exchange(): return lax.ppermute(value, 'freq', pairs) if mask else value  12.4 us
    ppermute x7, waiting for transfers between devices, exchange(): return lax.ppermute(value, 'freq', pairs) if mask else value  7.77 us
    unnamed x4, local copies, waits for them, and re-layouts  1.78 us
    ppermute x8, waiting for transfers between devices, swap(): return lax.ppermute(value, 'chan', [(0, 1), (1, 0)])  1.2 us
    ppermute x8, starting transfers between devices, swap(): return lax.ppermute(value, 'chan', [(0, 1), (1, 0)])  1.1 us
  transfers between devices with their start and end apart: 15, of which 8 were waited for; matrix products, arithmetic and copies ran while one was open for 0% of the time, Pallas kernels for 0%

profile of v8, /device:TPU:0, one launch (start us, length us, event | category | flops | bytes accessed | tf_op | source)
XLA Modules:
  0.0 42.7 jit_solution(8089318393754034581)
XLA Ops:
  0.0 1.2 %copy-done.1 = bf16[1024,256]{1,0:T(8,128)(2,1)S(1)} copy-done((bf16[1024,256]{1,0:T(8,128)(2,1)S(1)}, bf16[1024,256]{1,0:T(8,128)(2,1)}, u32[]{:S(2)}) %copy-start.1) | copy-done | bytes 524312
  1.2 0.6 %copy-done = bf16[576,2,1024]{2,1,0:T(2,128)(2,1)S(1)} copy-done((bf16[576,2,1024]{2,1,0:T(2,128)(2,1)S(1)}, bf16[576,2,1024]{2,1,0:T(2,128)(2,1)}, u32[]{:S(2)}) %copy-start) | copy-done | bytes 2359320
  1.8 0.8 %fusion.5.spectrum_ref = bf16[2,576,256]{2,1,0:T(8,128)(2,1)S(1)} fusion(bf16[576,2,1024]{2,1,0:T(2,128)(2,1)S(1)} %copy-done, bf16[1024,256]{1,0:T(8,128)(2,1)S(1)} %table.1), kind=kOutput, calls=%fused_computation.3 | convolution fusion | flops 604274688 | bytes 3473408 | tf_op jit(solution)/shard_map/cws,sj->wcj/dot_general | solution.py:250
  2.6 0.7 %whiten.1 = (bf16[2,16,1152]{2,1,0:T(8,128)(2,1)S(1)}, bf16[2,16,1152]{2,1,0:T(8,128)(2,1)S(1)}, bf16[2,16,1152]{2,1,0:T(8,128)(2,1)S(1)}, bf16[2,16,1152]{2,1,0...) custom-call(bf16[2,576,256]{2,1,0:T(8,128)(2,1)S(1)} %fusion.5.spect, ...), custom_call_target="tpu_custom_call" | custom-call | flops 5898240 | bytes 1769472 | tf_op jit(solution)/shard_map/whiten/pallas_call | solution.py:253
  3.4 3.0 %collective-permute-start = (bf16[2,16,1152]{2,1,0:T(8,128)(2,1)S(1)}, bf16[2,16,1152]{2,1,0:T(8,128)(2,1)S(1)}, u32[]{:S(2)}, u32[]{:S(2)}) collective-permute-start(bf16[2,16,1152]{2,1,0:T(8,128)(2,1)S(1)} %get-tuple-element.13), channel_id=1, source_target_pairs={{0,1},{1,0},{2,3},{3,2},{4,5},{5,4},{6,7},{7,6},{8,9},{9,8},{10,11... | collective-permute-start | bytes 221192 | tf_op jit(solution)/shard_map/ppermute | solution.py:218
  6.4 1.6 %collective-permute-start.1 = (bf16[2,16,1152]{2,1,0:T(8,128)(2,1)S(1)}, bf16[2,16,1152]{2,1,0:T(8,128)(2,1)S(1)}, u32[]{:S(2)}, u32[]{:S(2)}) collective-permute-start(bf16[2,16,1152]{2,1,0:T(8,128)(2,1)S(1)} %get-tuple-element.14), channel_id=1, source_target_pairs={{0,2},{1,3},{2,0},{3,1},{4,6},{5,7},{6,4},{7,5},{8,10},{9,11},{10,... | collective-permute-start | bytes 221192 | tf_op jit(solution)/shard_map/ppermute | solution.py:218
  8.0 2.4 %collective-permute-start.2 = (bf16[2,16,1152]{2,1,0:T(8,128)(2,1)S(1)}, bf16[2,16,1152]{2,1,0:T(8,128)(2,1)S(1)}, u32[]{:S(2)}, u32[]{:S(2)}) collective-permute-start(bf16[2,16,1152]{2,1,0:T(8,128)(2,1)S(1)} %get-tuple-element.15), channel_id=1, source_target_pairs={{0,7},{1,6},{2,5},{3,4},{4,3},{5,2},{6,1},{7,0},{8,15},{9,14},{10,... | collective-permute-start | bytes 221192 | tf_op jit(solution)/shard_map/ppermute | solution.py:218
  10.4 1.3 %collective-permute-start.3 = (bf16[2,16,1152]{2,1,0:T(8,128)(2,1)S(1)}, bf16[2,16,1152]{2,1,0:T(8,128)(2,1)S(1)}, u32[]{:S(2)}, u32[]{:S(2)}) collective-permute-start(bf16[2,16,1152]{2,1,0:T(8,128)(2,1)S(1)} %get-tuple-element.16), channel_id=1, source_target_pairs={{0,6},{1,7},{2,4},{3,5},{4,2},{5,3},{6,0},{7,1},{8,14},{9,15},{10,... | collective-permute-start | bytes 221192 | tf_op jit(solution)/shard_map/ppermute | solution.py:218
  11.8 1.8 %collective-permute-start.4 = (bf16[2,16,1152]{2,1,0:T(8,128)(2,1)S(1)}, bf16[2,16,1152]{2,1,0:T(8,128)(2,1)S(1)}, u32[]{:S(2)}, u32[]{:S(2)}) collective-permute-start(bf16[2,16,1152]{2,1,0:T(8,128)(2,1)S(1)} %get-tuple-element.17), channel_id=1, source_target_pairs={{0,5},{1,4},{2,7},{3,6},{4,1},{5,0},{6,3},{7,2},{8,13},{9,12},{10,... | collective-permute-start | bytes 221192 | tf_op jit(solution)/shard_map/ppermute | solution.py:218
  13.5 0.0 collective-permute-done.refs_0_
  13.5 2.1 %collective-permute-start.5 = (bf16[2,16,1152]{2,1,0:T(8,128)(2,1)S(1)}, bf16[2,16,1152]{2,1,0:T(8,128)(2,1)S(1)}, u32[]{:S(2)}, u32[]{:S(2)}) collective-permute-start(bf16[2,16,1152]{2,1,0:T(8,128)(2,1)S(1)} %get-tuple-element.18), channel_id=1, source_target_pairs={{0,4},{1,5},{2,6},{3,7},{4,0},{5,1},{6,2},{7,3},{8,12},{9,13},{10,... | collective-permute-start | bytes 221192 | tf_op jit(solution)/shard_map/ppermute | solution.py:218
  15.6 0.0 collective-permute-done.1.refs_1_
  15.6 0.1 collective-permute-start.6
  15.8 0.0 collective-permute-done.2.refs_2_
  15.8 0.0 collective-permute-start.14
  15.8 0.8 %collective-permute-done.3.refs_3_ = bf16[2,16,1152]{2,1,0:T(8,128)(2,1)S(1)} collective-permute-done((bf16[2,16,1152]{2,1,0:T(8,128)(2,1)S(1)}, bf16[2,16,1152]{2,1,0:T(8,128)(2,1)S(1)}, u32[]{:S(2)}, u32[]{:S(2)}) %collective-permute-start.3) | collective-permute-done | bytes 73760 | tf_op jit(solution)/shard_map/ppermute | solution.py:218
  16.6 0.0 collective-permute-start.7
  16.6 6.5 %collective-permute-done.4.refs_4_ = bf16[2,16,1152]{2,1,0:T(8,128)(2,1)S(1)} collective-permute-done((bf16[2,16,1152]{2,1,0:T(8,128)(2,1)S(1)}, bf16[2,16,1152]{2,1,0:T(8,128)(2,1)S(1)}, u32[]{:S(2)}, u32[]{:S(2)}) %collective-permute-start.4) | collective-permute-done | bytes 73760 | tf_op jit(solution)/shard_map/ppermute | solution.py:218
  23.1 0.0 collective-permute-start.8
  23.1 0.4 %collective-permute-done.5.refs_5_ = bf16[2,16,1152]{2,1,0:T(8,128)(2,1)S(1)} collective-permute-done((bf16[2,16,1152]{2,1,0:T(8,128)(2,1)S(1)}, bf16[2,16,1152]{2,1,0:T(8,128)(2,1)S(1)}, u32[]{:S(2)}, u32[]{:S(2)}) %collective-permute-start.5) | collective-permute-done | bytes 73760 | tf_op jit(solution)/shard_map/ppermute | solution.py:218
  23.5 0.1 collective-permute-start.9
  23.6 0.0 collective-permute-done.6.refs_6_
  23.6 0.4 %collective-permute-start.10 = (bf16[2,16,1152]{2,1,0:T(8,128)(2,1)S(1)}, bf16[2,16,1152]{2,1,0:T(8,128)(2,1)S(1)}, u32[]{:S(2)}, u32[]{:S(2)}) collective-permute-start(bf16[2,16,1152]{2,1,0:T(8,128)(2,1)S(1)} %collective-permute-done.3.refs_3_), channel_id=1, source_target_pairs={{0,8},{8,0},{1,9},{9,1},{2,10},{10,2},{3,11},{11,3},{4,12},{12,4},... | collective-permute-start | bytes 221192 | tf_op jit(solution)/shard_map/ppermute | solution.py:222
  24.1 0.1 collective-permute-start.11
  24.1 0.4 %collective-permute-start.12 = (bf16[2,16,1152]{2,1,0:T(8,128)(2,1)S(1)}, bf16[2,16,1152]{2,1,0:T(8,128)(2,1)S(1)}, u32[]{:S(2)}, u32[]{:S(2)}) collective-permute-start(bf16[2,16,1152]{2,1,0:T(8,128)(2,1)S(1)} %collective-permute-done.5.refs_5_), channel_id=1, source_target_pairs={{0,8},{8,0},{1,9},{9,1},{2,10},{10,2},{3,11},{11,3},{4,12},{12,4},... | collective-permute-start | bytes 221192 | tf_op jit(solution)/shard_map/ppermute | solution.py:222
  24.6 0.1 collective-permute-start.13
  24.6 0.2 collective-permute-done.9.refs_10_
  24.8 0.2 collective-permute-done.10.refs_11_
  25.0 0.4 collective-permute-done.11.refs_12_
  25.3 0.2 collective-permute-done.12.refs_13_
  25.5 0.4 collective-permute-done.13.refs_14_
  25.8 16.9 %outer_products.1 = bf16[2,16,576,1152]{3,2,1,0:T(8,128)(2,1)} custom-call(bf16[2,16,1152]{2,1,0:T(8,128)(2,1)S(1)} %collective-permute-done.refs_0_, bf16[2,16,1152]{2,1,0:T(8,128)(2,1)S(1)} %collective-permute-done.1.refs_1_, bf16[2,16,1152]{2,1,0:T(8,128)(2,1)S(1)} %collective-permute-done.2.refs_2_, ...), custom_call_target="tpu_custom_call" | custom-call | flops 5435817984 | bytes 42467328 | tf_op jit(solution)/shard_map/outer_products/pallas_call | solution.py:275
  (6 shorter events, 0.0 us)
Async XLA Ops:
  0.0 1.8 %copy-start = (bf16[576,2,1024]{2,1,0:T(2,128)(2,1)S(1)}, bf16[576,2,1024]{2,1,0:T(2,128)(2,1)}, u32[]{:S(2)}) copy-start(bf16[576,2,1024]{2,1,0:T(2,128)(2,1)} %param.2) | copy-start | bytes 7077892
  0.0 1.2 %copy-start.1 = (bf16[1024,256]{1,0:T(8,128)(2,1)S(1)}, bf16[1024,256]{1,0:T(8,128)(2,1)}, u32[]{:S(2)}) copy-start(bf16[1024,256]{1,0:T(8,128)(2,1)} %constant.2.clone.in_ref) | copy-start | bytes 1572868
  3.4 10.1 %collective-permute-start = (bf16[2,16,1152]{2,1,0:T(8,128)(2,1)S(1)}, bf16[2,16,1152]{2,1,0:T(8,128)(2,1)S(1)}, u32[]{:S(2)}, u32[]{:S(2)}) collective-permute-start(bf16[2,16,1152]{2,1,0:T(8,128)(2,1)S(1)} %get-tuple-element.13), channel_id=1, source_target_pairs={{0,1},{1,0},{2,3},{3,2},{4,5},{5,4},{6,7},{7,6},{8,9},{9,8},{10,11... | collective-permute-start | bytes 221192 | tf_op jit(solution)/shard_map/ppermute | solution.py:218
  6.4 9.2 %collective-permute-start.1 = (bf16[2,16,1152]{2,1,0:T(8,128)(2,1)S(1)}, bf16[2,16,1152]{2,1,0:T(8,128)(2,1)S(1)}, u32[]{:S(2)}, u32[]{:S(2)}) collective-permute-start(bf16[2,16,1152]{2,1,0:T(8,128)(2,1)S(1)} %get-tuple-element.14), channel_id=1, source_target_pairs={{0,2},{1,3},{2,0},{3,1},{4,6},{5,7},{6,4},{7,5},{8,10},{9,11},{10,... | collective-permute-start | bytes 221192 | tf_op jit(solution)/shard_map/ppermute | solution.py:218
  8.0 7.8 %collective-permute-start.2 = (bf16[2,16,1152]{2,1,0:T(8,128)(2,1)S(1)}, bf16[2,16,1152]{2,1,0:T(8,128)(2,1)S(1)}, u32[]{:S(2)}, u32[]{:S(2)}) collective-permute-start(bf16[2,16,1152]{2,1,0:T(8,128)(2,1)S(1)} %get-tuple-element.15), channel_id=1, source_target_pairs={{0,7},{1,6},{2,5},{3,4},{4,3},{5,2},{6,1},{7,0},{8,15},{9,14},{10,... | collective-permute-start | bytes 221192 | tf_op jit(solution)/shard_map/ppermute | solution.py:218
  10.4 6.2 %collective-permute-start.3 = (bf16[2,16,1152]{2,1,0:T(8,128)(2,1)S(1)}, bf16[2,16,1152]{2,1,0:T(8,128)(2,1)S(1)}, u32[]{:S(2)}, u32[]{:S(2)}) collective-permute-start(bf16[2,16,1152]{2,1,0:T(8,128)(2,1)S(1)} %get-tuple-element.16), channel_id=1, source_target_pairs={{0,6},{1,7},{2,4},{3,5},{4,2},{5,3},{6,0},{7,1},{8,14},{9,15},{10,... | collective-permute-start | bytes 221192 | tf_op jit(solution)/shard_map/ppermute | solution.py:218
  11.8 11.3 %collective-permute-start.4 = (bf16[2,16,1152]{2,1,0:T(8,128)(2,1)S(1)}, bf16[2,16,1152]{2,1,0:T(8,128)(2,1)S(1)}, u32[]{:S(2)}, u32[]{:S(2)}) collective-permute-start(bf16[2,16,1152]{2,1,0:T(8,128)(2,1)S(1)} %get-tuple-element.17), channel_id=1, source_target_pairs={{0,5},{1,4},{2,7},{3,6},{4,1},{5,0},{6,3},{7,2},{8,13},{9,12},{10,... | collective-permute-start | bytes 221192 | tf_op jit(solution)/shard_map/ppermute | solution.py:218
  13.5 10.0 %collective-permute-start.5 = (bf16[2,16,1152]{2,1,0:T(8,128)(2,1)S(1)}, bf16[2,16,1152]{2,1,0:T(8,128)(2,1)S(1)}, u32[]{:S(2)}, u32[]{:S(2)}) collective-permute-start(bf16[2,16,1152]{2,1,0:T(8,128)(2,1)S(1)} %get-tuple-element.18), channel_id=1, source_target_pairs={{0,4},{1,5},{2,6},{3,7},{4,0},{5,1},{6,2},{7,3},{8,12},{9,13},{10,... | collective-permute-start | bytes 221192 | tf_op jit(solution)/shard_map/ppermute | solution.py:218
  15.6 8.0 %collective-permute-start.6 = (bf16[2,16,1152]{2,1,0:T(8,128)(2,1)S(1)}, bf16[2,16,1152]{2,1,0:T(8,128)(2,1)S(1)}, u32[]{:S(2)}, u32[]{:S(2)}) collective-permute-start(bf16[2,16,1152]{2,1,0:T(8,128)(2,1)S(1)} %get-tuple-element.19), channel_id=1, source_target_pairs={{0,3},{1,2},{2,1},{3,0},{4,7},{5,6},{6,5},{7,4},{8,11},{9,10},{10,... | collective-permute-start | bytes 221192 | tf_op jit(solution)/shard_map/ppermute | solution.py:218
  15.8 8.3 %collective-permute-start.14 = (bf16[2,16,1152]{2,1,0:T(8,128)(2,1)S(1)}, bf16[2,16,1152]{2,1,0:T(8,128)(2,1)S(1)}, u32[]{:S(2)}, u32[]{:S(2)}) collective-permute-start(bf16[2,16,1152]{2,1,0:T(8,128)(2,1)S(1)} %get-tuple-element.20.refs_7_), channel_id=1, source_target_pairs={{0,8},{8,0},{1,9},{9,1},{2,10},{10,2},{3,11},{11,3},{4,12},{12,4},... | collective-permute-start | bytes 221192 | tf_op jit(solution)/shard_map/ppermute | solution.py:222
  16.6 7.6 %collective-permute-start.7 = (bf16[2,16,1152]{2,1,0:T(8,128)(2,1)S(1)}, bf16[2,16,1152]{2,1,0:T(8,128)(2,1)S(1)}, u32[]{:S(2)}, u32[]{:S(2)}) collective-permute-start(bf16[2,16,1152]{2,1,0:T(8,128)(2,1)S(1)} %collective-permute-done.refs_0_), channel_id=1, source_target_pairs={{0,8},{8,0},{1,9},{9,1},{2,10},{10,2},{3,11},{11,3},{4,12},{12,4},... | collective-permute-start | bytes 221192 | tf_op jit(solution)/shard_map/ppermute | solution.py:222
  23.1 1.5 %collective-permute-start.8 = (bf16[2,16,1152]{2,1,0:T(8,128)(2,1)S(1)}, bf16[2,16,1152]{2,1,0:T(8,128)(2,1)S(1)}, u32[]{:S(2)}, u32[]{:S(2)}) collective-permute-start(bf16[2,16,1152]{2,1,0:T(8,128)(2,1)S(1)} %collective-permute-done.1.refs_1_), channel_id=1, source_target_pairs={{0,8},{8,0},{1,9},{9,1},{2,10},{10,2},{3,11},{11,3},{4,12},{12,4},... | collective-permute-start | bytes 221192 | tf_op jit(solution)/shard_map/ppermute | solution.py:222
  23.5 1.3 %collective-permute-start.9 = (bf16[2,16,1152]{2,1,0:T(8,128)(2,1)S(1)}, bf16[2,16,1152]{2,1,0:T(8,128)(2,1)S(1)}, u32[]{:S(2)}, u32[]{:S(2)}) collective-permute-start(bf16[2,16,1152]{2,1,0:T(8,128)(2,1)S(1)} %collective-permute-done.2.refs_2_), channel_id=1, source_target_pairs={{0,8},{8,0},{1,9},{9,1},{2,10},{10,2},{3,11},{11,3},{4,12},{12,4},... | collective-permute-start | bytes 221192 | tf_op jit(solution)/shard_map/ppermute | solution.py:222
  23.6 1.4 %collective-permute-start.10 = (bf16[2,16,1152]{2,1,0:T(8,128)(2,1)S(1)}, bf16[2,16,1152]{2,1,0:T(8,128)(2,1)S(1)}, u32[]{:S(2)}, u32[]{:S(2)}) collective-permute-start(bf16[2,16,1152]{2,1,0:T(8,128)(2,1)S(1)} %collective-permute-done.3.refs_3_), channel_id=1, source_target_pairs={{0,8},{8,0},{1,9},{9,1},{2,10},{10,2},{3,11},{11,3},{4,12},{12,4},... | collective-permute-start | bytes 221192 | tf_op jit(solution)/shard_map/ppermute | solution.py:222
  24.1 1.3 %collective-permute-start.11 = (bf16[2,16,1152]{2,1,0:T(8,128)(2,1)S(1)}, bf16[2,16,1152]{2,1,0:T(8,128)(2,1)S(1)}, u32[]{:S(2)}, u32[]{:S(2)}) collective-permute-start(bf16[2,16,1152]{2,1,0:T(8,128)(2,1)S(1)} %collective-permute-done.4.refs_4_), channel_id=1, source_target_pairs={{0,8},{8,0},{1,9},{9,1},{2,10},{10,2},{3,11},{11,3},{4,12},{12,4},... | collective-permute-start | bytes 221192 | tf_op jit(solution)/shard_map/ppermute | solution.py:222
  24.1 1.4 %collective-permute-start.12 = (bf16[2,16,1152]{2,1,0:T(8,128)(2,1)S(1)}, bf16[2,16,1152]{2,1,0:T(8,128)(2,1)S(1)}, u32[]{:S(2)}, u32[]{:S(2)}) collective-permute-start(bf16[2,16,1152]{2,1,0:T(8,128)(2,1)S(1)} %collective-permute-done.5.refs_5_), channel_id=1, source_target_pairs={{0,8},{8,0},{1,9},{9,1},{2,10},{10,2},{3,11},{11,3},{4,12},{12,4},... | collective-permute-start | bytes 221192 | tf_op jit(solution)/shard_map/ppermute | solution.py:222
  24.6 1.3 %collective-permute-start.13 = (bf16[2,16,1152]{2,1,0:T(8,128)(2,1)S(1)}, bf16[2,16,1152]{2,1,0:T(8,128)(2,1)S(1)}, u32[]{:S(2)}, u32[]{:S(2)}) collective-permute-start(bf16[2,16,1152]{2,1,0:T(8,128)(2,1)S(1)} %collective-permute-done.6.refs_6_), channel_id=1, source_target_pairs={{0,8},{8,0},{1,9},{9,1},{2,10},{10,2},{3,11},{11,3},{4,12},{12,4},... | collective-permute-start | bytes 221192 | tf_op jit(solution)/shard_map/ppermute | solution.py:222

commit v9 on v8

--- a/solution.py
+++ b/solution.py
@@ -74,24 +74,24 @@
     return pltpu.roll(tile, LANES // 2, axis=1)
 
 
-def split_rows(tile, bins, sets):
+def rows_of_set(tile, bins, sets, q):
     rows, lanes = tile.shape
     if sets == 1:
         first_part = (lax.broadcasted_iota(jnp.int32, (rows, 1), 0) // bins) % 2 == 0
         rotated = jnp.where(
             first_part, -pltpu.roll(tile, rows - bins, axis=0), pltpu.roll(tile, bins, axis=0)
         )
-        return [(tile, rotated)]
+        return tile, rotated
     parts = tile.reshape(rows // (2 * bins), 2, bins, lanes)
     real, imag = parts[:, 0], parts[:, 1]
     within = bins // sets
     low = lax.broadcasted_iota(jnp.int32, real.shape, 1) < within
     turned_real, turned_imag = (pltpu.roll(part, within, axis=1) for part in (real, imag))
-    found = [
-        (jnp.where(low, real, turned_imag), jnp.where(low, -imag, turned_real)),
-        (jnp.where(low, turned_real, imag), jnp.where(low, -turned_imag, real)),
-    ]
-    return [tuple(part.reshape(rows // sets, lanes) for part in pair) for pair in found]
+    if q == 0:
+        found = jnp.where(low, real, turned_imag), jnp.where(low, -imag, turned_real)
+    else:
+        found = jnp.where(low, turned_real, imag), jnp.where(low, -turned_imag, real)
+    return tuple(part.reshape(rows // sets, lanes) for part in found)
 
 
 def outer_kernel(bins, sets, scale, *refs):
@@ -119,8 +119,7 @@
             for part in range(2):
                 copy(when, cut, part).wait()
 
-    @pl.when(step == 0)
-    def _():
+    def prepare(q):
         me = lax.axis_index("chan")
         which = pl.program_id(0)
         own = jnp.concatenate([ref[which].astype(jnp.float32) for ref in own_refs])
@@ -152,9 +151,9 @@
             for j, tile in enumerate(tiles):
                 lanes = slice(j * LANES, (j + 1) * LANES)
                 lanes_imag = slice(2 * channels + j * LANES, 2 * channels + (j + 1) * LANES)
-                for q, (plain, rotated) in enumerate(split_rows(tile, bins, sets)):
-                    right[q, at, lanes] = plain.astype(jnp.bfloat16)
-                    right[q, at, lanes_imag] = rotated.astype(jnp.bfloat16)
+                plain, rotated = rows_of_set(tile, bins, sets, q)
+                right[q, at, lanes] = plain.astype(jnp.bfloat16)
+                right[q, at, lanes_imag] = rotated.astype(jnp.bfloat16)
         scaled = own * scale
         for j in range(full + 1):
             block = scaled[:, 2 * j * LANES : (2 * j + 2) * LANES]
@@ -163,10 +162,11 @@
             else:
                 windows = [block, swap_halves(block)]
             kept = min(LANES, channels - j * LANES)
-            pieces = [split_rows(window, bins, sets) for window in windows]
-            for q in range(sets):
-                turned = jnp.concatenate([piece[q][0] for piece in pieces]).T
-                left[q, j * LANES : j * LANES + kept] = turned[:kept]
+            pieces = [rows_of_set(window, bins, sets, q)[0] for window in windows]
+            left[q, j * LANES : j * LANES + kept] = jnp.concatenate(pieces).T[:kept]
+
+    for q in range(sets):
+        pl.when(step == q * (bins // sets))(functools.partial(prepare, q))
 
     depth = left.shape[2]
     within = bins // sets
@@ -235,7 +235,8 @@
     lanes = local_windows * local_channels
     vmem = pl.BlockSpec(memory_space=pltpu.VMEM)
     memory = pl.BlockSpec(memory_space=pl.ANY)
-    masks = [1, 2, *range(devices - 1, 2, -1), 0] if aligned else [0]
+    masks = [*range(devices - 1, devices // 2 - 1, -1), *range(1, devices // 2), 0]
+    masks = masks if aligned else [0]
     pieces = len(masks)
     rows = (devices, groups, 2 * bins, lanes) if aligned else (2 * BINS, lanes)
     piece = rows[1:] if aligned else rows
@@ -284,7 +285,7 @@
                 pltpu.VMEM((sets, depth, 4 * local_channels), jnp.bfloat16),
                 pltpu.VMEM((sets, local_channels, depth), jnp.float32),
                 pltpu.VMEM((3, 2, local_channels, 2 * local_channels), jnp.bfloat16),
-                pltpu.SemaphoreType.DMA((3, 2, 2)),
+                pltpu.SemaphoreType.DMA((3, 1, 2)),
             ],
             compiler_params=pltpu.CompilerParams(vmem_limit_bytes=32 * MIB),
             cost_estimate=pl.CostEstimate(

time: 42.8 us -> 42.5 us (level)
  waiting for transfers between devices: 8.97 us -> 3.91 us
  starting transfers between devices: 13.5 us -> 17.7 us
    ppermute x7, waiting for transfers between devices: 7.77 us -> 3 us  [exchange(): return lax.ppermute(value, 'freq', pairs) if mask else value]
    ppermute x7, starting transfers between devices: 12.4 us -> 16.1 us  [exchange(): return lax.ppermute(value, 'freq', pairs) if mask else value]
    ppermute x8, starting transfers between devices: 1.1 us -> 1.6 us  [swap(): return lax.ppermute(value, 'chan', [(0, 1), (1, 0)])]
  transfers between devices with their start and end apart: 15 -> 15, of which waited for: 8 -> 7; matrix products, arithmetic and copies ran while one was open for 0% -> 0% of each run, Pallas kernels for 0% -> 0%
where the time goes in v9:
time: 42.5 us; the launch traced here: 42.2 us
  Pallas kernels  18 us (42%)
  starting transfers between devices  17.7 us (42%)
  waiting for transfers between devices  3.91 us (9%)
  local copies, waits for them, and re-layouts  1.78 us (4%)
  matrix products  0.79 us (2%)
    pallas_call x1, Pallas kernels, local(): pl.pallas_call(functools.partial(outer_kernel, bins, sets, 1.0 / windows)...  17.2 us
    ppermute x7, starting transfers between devices, exchange(): return lax.ppermute(value, 'freq', pairs) if mask else value  16.1 us
    ppermute x7, waiting for transfers between devices, exchange(): return lax.ppermute(value, 'freq', pairs) if mask else value  3 us
    unnamed x4, local copies, waits for them, and re-layouts  1.78 us
    ppermute x8, starting transfers between devices, swap(): return lax.ppermute(value, 'chan', [(0, 1), (1, 0)])  1.6 us
    ppermute x8, waiting for transfers between devices, swap(): return lax.ppermute(value, 'chan', [(0, 1), (1, 0)])  0.92 us
  transfers between devices with their start and end apart: 15, of which 7 were waited for; matrix products, arithmetic and copies ran while one was open for 0% of the time, Pallas kernels for 0%

profile of v9, /device:TPU:0, one launch (start us, length us, event | category | flops | bytes accessed | tf_op | source)
XLA Modules:
  0.0 42.2 jit_solution(16194391485398065448)
XLA Ops:
  0.0 1.2 %copy-done.1 = bf16[1024,256]{1,0:T(8,128)(2,1)S(1)} copy-done((bf16[1024,256]{1,0:T(8,128)(2,1)S(1)}, bf16[1024,256]{1,0:T(8,128)(2,1)}, u32[]{:S(2)}) %copy-start.1) | copy-done | bytes 524312
  1.2 0.6 %copy-done = bf16[576,2,1024]{2,1,0:T(2,128)(2,1)S(1)} copy-done((bf16[576,2,1024]{2,1,0:T(2,128)(2,1)S(1)}, bf16[576,2,1024]{2,1,0:T(2,128)(2,1)}, u32[]{:S(2)}) %copy-start) | copy-done | bytes 2359320
  1.8 0.8 %fusion.5.spectrum_ref = bf16[2,576,256]{2,1,0:T(8,128)(2,1)S(1)} fusion(bf16[576,2,1024]{2,1,0:T(2,128)(2,1)S(1)} %copy-done, bf16[1024,256]{1,0:T(8,128)(2,1)S(1)} %table.1), kind=kOutput, calls=%fused_computation.3 | convolution fusion | flops 604274688 | bytes 3473408 | tf_op jit(solution)/shard_map/cws,sj->wcj/dot_general | solution.py:251
  2.6 0.8 %whiten.1 = (bf16[2,16,1152]{2,1,0:T(8,128)(2,1)S(1)}, bf16[2,16,1152]{2,1,0:T(8,128)(2,1)S(1)}, bf16[2,16,1152]{2,1,0:T(8,128)(2,1)S(1)}, bf16[2,16,1152]{2,1,0...) custom-call(bf16[2,576,256]{2,1,0:T(8,128)(2,1)S(1)} %fusion.5.spect, ...), custom_call_target="tpu_custom_call" | custom-call | flops 5898240 | bytes 1769472 | tf_op jit(solution)/shard_map/whiten/pallas_call | solution.py:254
  3.4 6.1 %collective-permute-start = (bf16[2,16,1152]{2,1,0:T(8,128)(2,1)S(1)}, bf16[2,16,1152]{2,1,0:T(8,128)(2,1)S(1)}, u32[]{:S(2)}, u32[]{:S(2)}) collective-permute-start(bf16[2,16,1152]{2,1,0:T(8,128)(2,1)S(1)} %get-tuple-element.13), channel_id=1, source_target_pairs={{0,7},{1,6},{2,5},{3,4},{4,3},{5,2},{6,1},{7,0},{8,15},{9,14},{10,... | collective-permute-start | bytes 221192 | tf_op jit(solution)/shard_map/ppermute | solution.py:218
  9.4 0.2 collective-permute-start.1
  9.7 0.7 %collective-permute-start.2 = (bf16[2,16,1152]{2,1,0:T(8,128)(2,1)S(1)}, bf16[2,16,1152]{2,1,0:T(8,128)(2,1)S(1)}, u32[]{:S(2)}, u32[]{:S(2)}) collective-permute-start(bf16[2,16,1152]{2,1,0:T(8,128)(2,1)S(1)} %get-tuple-element.15), channel_id=1, source_target_pairs={{0,5},{1,4},{2,7},{3,6},{4,1},{5,0},{6,3},{7,2},{8,13},{9,12},{10,... | collective-permute-start | bytes 221192 | tf_op jit(solution)/shard_map/ppermute | solution.py:218
  10.4 2.0 %collective-permute-start.3 = (bf16[2,16,1152]{2,1,0:T(8,128)(2,1)S(1)}, bf16[2,16,1152]{2,1,0:T(8,128)(2,1)S(1)}, u32[]{:S(2)}, u32[]{:S(2)}) collective-permute-start(bf16[2,16,1152]{2,1,0:T(8,128)(2,1)S(1)} %get-tuple-element.16), channel_id=1, source_target_pairs={{0,4},{1,5},{2,6},{3,7},{4,0},{5,1},{6,2},{7,3},{8,12},{9,13},{10,... | collective-permute-start | bytes 221192 | tf_op jit(solution)/shard_map/ppermute | solution.py:218
  12.4 1.6 %collective-permute-start.4 = (bf16[2,16,1152]{2,1,0:T(8,128)(2,1)S(1)}, bf16[2,16,1152]{2,1,0:T(8,128)(2,1)S(1)}, u32[]{:S(2)}, u32[]{:S(2)}) collective-permute-start(bf16[2,16,1152]{2,1,0:T(8,128)(2,1)S(1)} %get-tuple-element.17), channel_id=1, source_target_pairs={{0,1},{1,0},{2,3},{3,2},{4,5},{5,4},{6,7},{7,6},{8,9},{9,8},{10,11... | collective-permute-start | bytes 221192 | tf_op jit(solution)/shard_map/ppermute | solution.py:218
  14.1 0.0 collective-permute-done.refs_0_
  14.1 3.0 %collective-permute-start.5 = (bf16[2,16,1152]{2,1,0:T(8,128)(2,1)S(1)}, bf16[2,16,1152]{2,1,0:T(8,128)(2,1)S(1)}, u32[]{:S(2)}, u32[]{:S(2)}) collective-permute-start(bf16[2,16,1152]{2,1,0:T(8,128)(2,1)S(1)} %get-tuple-element.18), channel_id=1, source_target_pairs={{0,2},{1,3},{2,0},{3,1},{4,6},{5,7},{6,4},{7,5},{8,10},{9,11},{10,... | collective-permute-start | bytes 221192 | tf_op jit(solution)/shard_map/ppermute | solution.py:218
  17.0 0.0 collective-permute-done.1.refs_1_
  17.0 2.4 %collective-permute-start.6 = (bf16[2,16,1152]{2,1,0:T(8,128)(2,1)S(1)}, bf16[2,16,1152]{2,1,0:T(8,128)(2,1)S(1)}, u32[]{:S(2)}, u32[]{:S(2)}) collective-permute-start(bf16[2,16,1152]{2,1,0:T(8,128)(2,1)S(1)} %get-tuple-element.19), channel_id=1, source_target_pairs={{0,3},{1,2},{2,1},{3,0},{4,7},{5,6},{6,5},{7,4},{8,11},{9,10},{10,... | collective-permute-start | bytes 221192 | tf_op jit(solution)/shard_map/ppermute | solution.py:218
  19.4 1.7 %collective-permute-done.2.refs_2_ = bf16[2,16,1152]{2,1,0:T(8,128)(2,1)S(1)} collective-permute-done((bf16[2,16,1152]{2,1,0:T(8,128)(2,1)S(1)}, bf16[2,16,1152]{2,1,0:T(8,128)(2,1)S(1)}, u32[]{:S(2)}, u32[]{:S(2)}) %collective-permute-start.2) | collective-permute-done | bytes 73760 | tf_op jit(solution)/shard_map/ppermute | solution.py:218
  21.1 0.0 collective-permute-start.14
  21.1 0.9 %collective-permute-done.3.refs_3_ = bf16[2,16,1152]{2,1,0:T(8,128)(2,1)S(1)} collective-permute-done((bf16[2,16,1152]{2,1,0:T(8,128)(2,1)S(1)}, bf16[2,16,1152]{2,1,0:T(8,128)(2,1)S(1)}, u32[]{:S(2)}, u32[]{:S(2)}) %collective-permute-start.3) | collective-permute-done | bytes 73760 | tf_op jit(solution)/shard_map/ppermute | solution.py:218
  22.0 0.0 collective-permute-start.7
  22.0 0.0 collective-permute-done.4.refs_4_
  22.0 0.5 %collective-permute-start.8 = (bf16[2,16,1152]{2,1,0:T(8,128)(2,1)S(1)}, bf16[2,16,1152]{2,1,0:T(8,128)(2,1)S(1)}, u32[]{:S(2)}, u32[]{:S(2)}) collective-permute-start(bf16[2,16,1152]{2,1,0:T(8,128)(2,1)S(1)} %collective-permute-done.1.refs_1_), channel_id=1, source_target_pairs={{0,8},{8,0},{1,9},{9,1},{2,10},{10,2},{3,11},{11,3},{4,12},{12,4},... | collective-permute-start | bytes 221192 | tf_op jit(solution)/shard_map/ppermute | solution.py:222
  22.5 0.0 collective-permute-done.5.refs_5_
  22.5 0.1 collective-permute-start.9
  22.6 0.4 collective-permute-done.6.refs_6_
  23.0 0.0 collective-permute-start.10
  23.1 0.0 collective-permute-done.14.refs_15_
  23.1 0.5 %collective-permute-start.11 = (bf16[2,16,1152]{2,1,0:T(8,128)(2,1)S(1)}, bf16[2,16,1152]{2,1,0:T(8,128)(2,1)S(1)}, u32[]{:S(2)}, u32[]{:S(2)}) collective-permute-start(bf16[2,16,1152]{2,1,0:T(8,128)(2,1)S(1)} %collective-permute-done.4.refs_4_), channel_id=1, source_target_pairs={{0,8},{8,0},{1,9},{9,1},{2,10},{10,2},{3,11},{11,3},{4,12},{12,4},... | collective-permute-start | bytes 221192 | tf_op jit(solution)/shard_map/ppermute | solution.py:222
  23.5 0.1 collective-permute-start.12
  23.6 0.4 %collective-permute-start.13 = (bf16[2,16,1152]{2,1,0:T(8,128)(2,1)S(1)}, bf16[2,16,1152]{2,1,0:T(8,128)(2,1)S(1)}, u32[]{:S(2)}, u32[]{:S(2)}) collective-permute-start(bf16[2,16,1152]{2,1,0:T(8,128)(2,1)S(1)} %collective-permute-done.6.refs_6_), channel_id=1, source_target_pairs={{0,8},{8,0},{1,9},{9,1},{2,10},{10,2},{3,11},{11,3},{4,12},{12,4},... | collective-permute-start | bytes 221192 | tf_op jit(solution)/shard_map/ppermute | solution.py:222
  24.1 0.2 collective-permute-done.10.refs_11_
  24.3 0.2 collective-permute-done.11.refs_12_
  24.5 0.4 collective-permute-done.12.refs_13_
  24.8 0.2 collective-permute-done.13.refs_14_
  25.0 17.2 %outer_products.1 = bf16[2,16,576,1152]{3,2,1,0:T(8,128)(2,1)} custom-call(bf16[2,16,1152]{2,1,0:T(8,128)(2,1)S(1)} %collective-permute-done.refs_0_, bf16[2,16,1152]{2,1,0:T(8,128)(2,1)S(1)} %collective-permute-done.1.refs_1_, bf16[2,16,1152]{2,1,0:T(8,128)(2,1)S(1)} %collective-permute-done.2.refs_2_, ...), custom_call_target="tpu_custom_call" | custom-call | flops 5435817984 | bytes 42467328 | tf_op jit(solution)/shard_map/outer_products/pallas_call | solution.py:276
  (6 shorter events, 0.0 us)
Async XLA Ops:
  0.0 1.8 %copy-start = (bf16[576,2,1024]{2,1,0:T(2,128)(2,1)S(1)}, bf16[576,2,1024]{2,1,0:T(2,128)(2,1)}, u32[]{:S(2)}) copy-start(bf16[576,2,1024]{2,1,0:T(2,128)(2,1)} %param.2) | copy-start | bytes 7077892
  0.0 1.2 %copy-start.1 = (bf16[1024,256]{1,0:T(8,128)(2,1)S(1)}, bf16[1024,256]{1,0:T(8,128)(2,1)}, u32[]{:S(2)}) copy-start(bf16[1024,256]{1,0:T(8,128)(2,1)} %constant.2.clone.in_ref) | copy-start | bytes 1572868
  3.4 10.7 %collective-permute-start = (bf16[2,16,1152]{2,1,0:T(8,128)(2,1)S(1)}, bf16[2,16,1152]{2,1,0:T(8,128)(2,1)S(1)}, u32[]{:S(2)}, u32[]{:S(2)}) collective-permute-start(bf16[2,16,1152]{2,1,0:T(8,128)(2,1)S(1)} %get-tuple-element.13), channel_id=1, source_target_pairs={{0,7},{1,6},{2,5},{3,4},{4,3},{5,2},{6,1},{7,0},{8,15},{9,14},{10,... | collective-permute-start | bytes 221192 | tf_op jit(solution)/shard_map/ppermute | solution.py:218
  9.4 7.6 %collective-permute-start.1 = (bf16[2,16,1152]{2,1,0:T(8,128)(2,1)S(1)}, bf16[2,16,1152]{2,1,0:T(8,128)(2,1)S(1)}, u32[]{:S(2)}, u32[]{:S(2)}) collective-permute-start(bf16[2,16,1152]{2,1,0:T(8,128)(2,1)S(1)} %get-tuple-element.14), channel_id=1, source_target_pairs={{0,6},{1,7},{2,4},{3,5},{4,2},{5,3},{6,0},{7,1},{8,14},{9,15},{10,... | collective-permute-start | bytes 221192 | tf_op jit(solution)/shard_map/ppermute | solution.py:218
  9.7 11.5 %collective-permute-start.2 = (bf16[2,16,1152]{2,1,0:T(8,128)(2,1)S(1)}, bf16[2,16,1152]{2,1,0:T(8,128)(2,1)S(1)}, u32[]{:S(2)}, u32[]{:S(2)}) collective-permute-start(bf16[2,16,1152]{2,1,0:T(8,128)(2,1)S(1)} %get-tuple-element.15), channel_id=1, source_target_pairs={{0,5},{1,4},{2,7},{3,6},{4,1},{5,0},{6,3},{7,2},{8,13},{9,12},{10,... | collective-permute-start | bytes 221192 | tf_op jit(solution)/shard_map/ppermute | solution.py:218
  10.4 11.6 %collective-permute-start.3 = (bf16[2,16,1152]{2,1,0:T(8,128)(2,1)S(1)}, bf16[2,16,1152]{2,1,0:T(8,128)(2,1)S(1)}, u32[]{:S(2)}, u32[]{:S(2)}) collective-permute-start(bf16[2,16,1152]{2,1,0:T(8,128)(2,1)S(1)} %get-tuple-element.16), channel_id=1, source_target_pairs={{0,4},{1,5},{2,6},{3,7},{4,0},{5,1},{6,2},{7,3},{8,12},{9,13},{10,... | collective-permute-start | bytes 221192 | tf_op jit(solution)/shard_map/ppermute | solution.py:218
  12.4 9.6 %collective-permute-start.4 = (bf16[2,16,1152]{2,1,0:T(8,128)(2,1)S(1)}, bf16[2,16,1152]{2,1,0:T(8,128)(2,1)S(1)}, u32[]{:S(2)}, u32[]{:S(2)}) collective-permute-start(bf16[2,16,1152]{2,1,0:T(8,128)(2,1)S(1)} %get-tuple-element.17), channel_id=1, source_target_pairs={{0,1},{1,0},{2,3},{3,2},{4,5},{5,4},{6,7},{7,6},{8,9},{9,8},{10,11... | collective-permute-start | bytes 221192 | tf_op jit(solution)/shard_map/ppermute | solution.py:218
  14.1 8.5 %collective-permute-start.5 = (bf16[2,16,1152]{2,1,0:T(8,128)(2,1)S(1)}, bf16[2,16,1152]{2,1,0:T(8,128)(2,1)S(1)}, u32[]{:S(2)}, u32[]{:S(2)}) collective-permute-start(bf16[2,16,1152]{2,1,0:T(8,128)(2,1)S(1)} %get-tuple-element.18), channel_id=1, source_target_pairs={{0,2},{1,3},{2,0},{3,1},{4,6},{5,7},{6,4},{7,5},{8,10},{9,11},{10,... | collective-permute-start | bytes 221192 | tf_op jit(solution)/shard_map/ppermute | solution.py:218
  17.0 6.0 %collective-permute-start.6 = (bf16[2,16,1152]{2,1,0:T(8,128)(2,1)S(1)}, bf16[2,16,1152]{2,1,0:T(8,128)(2,1)S(1)}, u32[]{:S(2)}, u32[]{:S(2)}) collective-permute-start(bf16[2,16,1152]{2,1,0:T(8,128)(2,1)S(1)} %get-tuple-element.19), channel_id=1, source_target_pairs={{0,3},{1,2},{2,1},{3,0},{4,7},{5,6},{6,5},{7,4},{8,11},{9,10},{10,... | collective-permute-start | bytes 221192 | tf_op jit(solution)/shard_map/ppermute | solution.py:218
  21.1 1.9 %collective-permute-start.14 = (bf16[2,16,1152]{2,1,0:T(8,128)(2,1)S(1)}, bf16[2,16,1152]{2,1,0:T(8,128)(2,1)S(1)}, u32[]{:S(2)}, u32[]{:S(2)}) collective-permute-start(bf16[2,16,1152]{2,1,0:T(8,128)(2,1)S(1)} %get-tuple-element.20.refs_7_), channel_id=1, source_target_pairs={{0,8},{8,0},{1,9},{9,1},{2,10},{10,2},{3,11},{11,3},{4,12},{12,4},... | collective-permute-start | bytes 221192 | tf_op jit(solution)/shard_map/ppermute | solution.py:222
  22.0 1.5 %collective-permute-start.7 = (bf16[2,16,1152]{2,1,0:T(8,128)(2,1)S(1)}, bf16[2,16,1152]{2,1,0:T(8,128)(2,1)S(1)}, u32[]{:S(2)}, u32[]{:S(2)}) collective-permute-start(bf16[2,16,1152]{2,1,0:T(8,128)(2,1)S(1)} %collective-permute-done.refs_0_), channel_id=1, source_target_pairs={{0,8},{8,0},{1,9},{9,1},{2,10},{10,2},{3,11},{11,3},{4,12},{12,4},... | collective-permute-start | bytes 221192 | tf_op jit(solution)/shard_map/ppermute | solution.py:222
  22.0 1.6 %collective-permute-start.8 = (bf16[2,16,1152]{2,1,0:T(8,128)(2,1)S(1)}, bf16[2,16,1152]{2,1,0:T(8,128)(2,1)S(1)}, u32[]{:S(2)}, u32[]{:S(2)}) collective-permute-start(bf16[2,16,1152]{2,1,0:T(8,128)(2,1)S(1)} %collective-permute-done.1.refs_1_), channel_id=1, source_target_pairs={{0,8},{8,0},{1,9},{9,1},{2,10},{10,2},{3,11},{11,3},{4,12},{12,4},... | collective-permute-start | bytes 221192 | tf_op jit(solution)/shard_map/ppermute | solution.py:222
  22.5 1.5 %collective-permute-start.9 = (bf16[2,16,1152]{2,1,0:T(8,128)(2,1)S(1)}, bf16[2,16,1152]{2,1,0:T(8,128)(2,1)S(1)}, u32[]{:S(2)}, u32[]{:S(2)}) collective-permute-start(bf16[2,16,1152]{2,1,0:T(8,128)(2,1)S(1)} %collective-permute-done.2.refs_2_), channel_id=1, source_target_pairs={{0,8},{8,0},{1,9},{9,1},{2,10},{10,2},{3,11},{11,3},{4,12},{12,4},... | collective-permute-start | bytes 221192 | tf_op jit(solution)/shard_map/ppermute | solution.py:222
  23.0 1.3 %collective-permute-start.10 = (bf16[2,16,1152]{2,1,0:T(8,128)(2,1)S(1)}, bf16[2,16,1152]{2,1,0:T(8,128)(2,1)S(1)}, u32[]{:S(2)}, u32[]{:S(2)}) collective-permute-start(bf16[2,16,1152]{2,1,0:T(8,128)(2,1)S(1)} %collective-permute-done.3.refs_3_), channel_id=1, source_target_pairs={{0,8},{8,0},{1,9},{9,1},{2,10},{10,2},{3,11},{11,3},{4,12},{12,4},... | collective-permute-start | bytes 221192 | tf_op jit(solution)/shard_map/ppermute | solution.py:222
  23.1 1.4 %collective-permute-start.11 = (bf16[2,16,1152]{2,1,0:T(8,128)(2,1)S(1)}, bf16[2,16,1152]{2,1,0:T(8,128)(2,1)S(1)}, u32[]{:S(2)}, u32[]{:S(2)}) collective-permute-start(bf16[2,16,1152]{2,1,0:T(8,128)(2,1)S(1)} %collective-permute-done.4.refs_4_), channel_id=1, source_target_pairs={{0,8},{8,0},{1,9},{9,1},{2,10},{10,2},{3,11},{11,3},{4,12},{12,4},... | collective-permute-start | bytes 221192 | tf_op jit(solution)/shard_map/ppermute | solution.py:222
  23.5 1.3 %collective-permute-start.12 = (bf16[2,16,1152]{2,1,0:T(8,128)(2,1)S(1)}, bf16[2,16,1152]{2,1,0:T(8,128)(2,1)S(1)}, u32[]{:S(2)}, u32[]{:S(2)}) collective-permute-start(bf16[2,16,1152]{2,1,0:T(8,128)(2,1)S(1)} %collective-permute-done.5.refs_5_), channel_id=1, source_target_pairs={{0,8},{8,0},{1,9},{9,1},{2,10},{10,2},{3,11},{11,3},{4,12},{12,4},... | collective-permute-start | bytes 221192 | tf_op jit(solution)/shard_map/ppermute | solution.py:222
  23.6 1.4 %collective-permute-start.13 = (bf16[2,16,1152]{2,1,0:T(8,128)(2,1)S(1)}, bf16[2,16,1152]{2,1,0:T(8,128)(2,1)S(1)}, u32[]{:S(2)}, u32[]{:S(2)}) collective-permute-start(bf16[2,16,1152]{2,1,0:T(8,128)(2,1)S(1)} %collective-permute-done.6.refs_6_), channel_id=1, source_target_pairs={{0,8},{8,0},{1,9},{9,1},{2,10},{10,2},{3,11},{11,3},{4,12},{12,4},... | collective-permute-start | bytes 221192 | tf_op jit(solution)/shard_map/ppermute | solution.py:222

commit v10 on v9

--- a/solution.py
+++ b/solution.py
@@ -101,23 +101,25 @@
     half = LANES // 2
     channels = out_ref.shape[2]
     full = channels // LANES
-    step = pl.program_id(1)
-    now = pl.program_id(0) * bins + step
-    steps = pl.num_programs(0) * bins
-    depth_of_slots, cuts = sems.shape[:2]
+    part, step = pl.program_id(1), pl.program_id(2)
+    now = (pl.program_id(0) * 2 + part) * bins + step
+    steps = pl.num_programs(0) * 2 * bins
+    depth_of_slots, cuts = sems.shape
     size = channels // cuts
 
-    def copy(when, cut, part):
+    def copy(when, cut):
         slot = lax.rem(when, depth_of_slots)
         at = pl.ds(cut * size, size)
+        into, run = lax.rem(when // bins, 2), when // (2 * bins)
         return pltpu.make_async_copy(
-            slots.at[slot, part, at], out_ref.at[part, when, at], sems.at[slot, cut, part]
+            slots.at[slot, at],
+            out_ref.at[into, run * bins + lax.rem(when, bins), at],
+            sems.at[slot, cut],
         )
 
     def wait_for(when):
         for cut in range(cuts):
-            for part in range(2):
-                copy(when, cut, part).wait()
+            copy(when, cut).wait()
 
     def prepare(q):
         me = lax.axis_index("chan")
@@ -150,10 +152,9 @@
             ]
             for j, tile in enumerate(tiles):
                 lanes = slice(j * LANES, (j + 1) * LANES)
-                lanes_imag = slice(2 * channels + j * LANES, 2 * channels + (j + 1) * LANES)
                 plain, rotated = rows_of_set(tile, bins, sets, q)
-                right[q, at, lanes] = plain.astype(jnp.bfloat16)
-                right[q, at, lanes_imag] = rotated.astype(jnp.bfloat16)
+                right[0, q, at, lanes] = plain.astype(jnp.bfloat16)
+                right[1, q, at, lanes] = rotated.astype(jnp.bfloat16)
         scaled = own * scale
         for j in range(full + 1):
             block = scaled[:, 2 * j * LANES : (2 * j + 2) * LANES]
@@ -166,14 +167,14 @@
             left[q, j * LANES : j * LANES + kept] = jnp.concatenate(pieces).T[:kept]
 
     for q in range(sets):
-        pl.when(step == q * (bins // sets))(functools.partial(prepare, q))
+        pl.when((part == 0) & (step == q * (bins // sets)))(functools.partial(prepare, q))
 
     depth = left.shape[2]
     within = bins // sets
     lane = lax.broadcasted_iota(jnp.int32, (1, depth), 1)
     taken = (lane & (within - 1)) == (step & (within - 1))
     chosen = jnp.where(taken, left[step // within], 0.0).astype(jnp.bfloat16)
-    weights = right.at[step // within]
+    weights = right.at[part, step // within]
 
     @pl.when(now >= depth_of_slots)
     def _():
@@ -181,27 +182,11 @@
 
     slot = lax.rem(now, depth_of_slots)
 
-    whole = 2 * channels // (2 * LANES) * (2 * LANES)
-    starts = [0, whole, 4 * channels - whole, 4 * channels]
-    left_over = 2 * channels - whole
-
-    def multiply(first, last):
-        return jnp.dot(
-            chosen, weights[:, first:last], preferred_element_type=jnp.float32
-        ).astype(jnp.bfloat16)
-
-    def send(part):
-        for cut in range(cuts):
-            copy(now, cut, part).start()
-
-    slots[slot, 0, :, :whole] = multiply(*starts[:2])
-    if left_over:
-        both = multiply(*starts[1:3])
-        slots[slot, 0, :, whole:] = both[:, :left_over]
-        slots[slot, 1, :, :left_over] = both[:, left_over:]
-    send(0)
-    slots[slot, 1, :, left_over:] = multiply(*starts[2:])
-    send(1)
+    for cut in range(cuts):
+        at = slice(cut * size, (cut + 1) * size)
+        product = jnp.dot(chosen[at], weights[...], preferred_element_type=jnp.float32)
+        slots[slot, at] = product.astype(jnp.bfloat16)
+        copy(now, cut).start()
 
     @pl.when(now == steps - 1)
     def _():
@@ -235,8 +220,7 @@
     lanes = local_windows * local_channels
     vmem = pl.BlockSpec(memory_space=pltpu.VMEM)
     memory = pl.BlockSpec(memory_space=pl.ANY)
-    masks = [*range(devices - 1, devices // 2 - 1, -1), *range(1, devices // 2), 0]
-    masks = masks if aligned else [0]
+    masks = [devices - 1, 1, 2, *range(devices - 2, 2, -1), 0] if aligned else [0]
     pieces = len(masks)
     rows = (devices, groups, 2 * bins, lanes) if aligned else (2 * BINS, lanes)
     piece = rows[1:] if aligned else rows
@@ -278,14 +262,14 @@
             out_shape=jax.ShapeDtypeStruct(
                 (2, local_bins, local_channels, 2 * local_channels), jnp.bfloat16
             ),
-            grid=(groups, bins),
+            grid=(groups, 2, bins),
             in_specs=[vmem] * (2 * pieces),
             out_specs=memory,
             scratch_shapes=[
-                pltpu.VMEM((sets, depth, 4 * local_channels), jnp.bfloat16),
+                pltpu.VMEM((2, sets, depth, 2 * local_channels), jnp.bfloat16),
                 pltpu.VMEM((sets, local_channels, depth), jnp.float32),
-                pltpu.VMEM((3, 2, local_channels, 2 * local_channels), jnp.bfloat16),
-                pltpu.SemaphoreType.DMA((3, 1, 2)),
+                pltpu.VMEM((4, local_channels, 2 * local_channels), jnp.bfloat16),
+                pltpu.SemaphoreType.DMA((4, 2)),
             ],
             compiler_params=pltpu.CompilerParams(vmem_limit_bytes=32 * MIB),
             cost_estimate=pl.CostEstimate(

time: 42.5 us -> 45.8 us (1.078)
  Pallas kernels: 18 us -> 21.2 us
  waiting for transfers between devices: 3.91 us -> 5.36 us
  starting transfers between devices: 17.7 us -> 16.4 us
    pallas_call x1, Pallas kernels: 17.2 us -> 20.5 us  [local(): pl.pallas_call(functools.partial(outer_kernel, bins, sets, 1.0 / windows)...]
    ppermute x7, starting transfers between devices: 16.1 us -> 14.5 us  [exchange(): return lax.ppermute(value, 'freq', pairs) if mask else value]
    ppermute x7, waiting for transfers between devices: 3 us -> 4.22 us  [exchange(): return lax.ppermute(value, 'freq', pairs) if mask else value]
  transfers between devices with their start and end apart: 15 -> 15, of which waited for: 7 -> 6; matrix products, arithmetic and copies ran while one was open for 0% -> 0% of each run, Pallas kernels for 0% -> 0%
where the time goes in v10:
time: 45.8 us; the launch traced here: 45.6 us
  Pallas kernels  21.2 us (46%)
  starting transfers between devices  16.4 us (36%)
  waiting for transfers between devices  5.36 us (12%)
  local copies, waits for them, and re-layouts  1.78 us (4%)
  matrix products  0.79 us (2%)
    pallas_call x1, Pallas kernels, local(): pl.pallas_call(functools.partial(outer_kernel, bins, sets, 1.0 / windows)...  20.5 us
    ppermute x7, starting transfers between devices, exchange(): return lax.ppermute(value, 'freq', pairs) if mask else value  14.5 us
    ppermute x7, waiting for transfers between devices, exchange(): return lax.ppermute(value, 'freq', pairs) if mask else value  4.22 us
    ppermute x8, starting transfers between devices, swap(): return lax.ppermute(value, 'chan', [(0, 1), (1, 0)])  1.88 us
    unnamed x4, local copies, waits for them, and re-layouts  1.78 us
    ppermute x8, waiting for transfers between devices, swap(): return lax.ppermute(value, 'chan', [(0, 1), (1, 0)])  1.14 us
  transfers between devices with their start and end apart: 15, of which 6 were waited for; matrix products, arithmetic and copies ran while one was open for 0% of the time, Pallas kernels for 0%

profile of v10, /device:TPU:0, one launch (start us, length us, event | category | flops | bytes accessed | tf_op | source)
XLA Modules:
  0.0 45.6 jit_solution(163008601041894056)
XLA Ops:
  0.0 1.2 %copy-done.1 = bf16[1024,256]{1,0:T(8,128)(2,1)S(1)} copy-done((bf16[1024,256]{1,0:T(8,128)(2,1)S(1)}, bf16[1024,256]{1,0:T(8,128)(2,1)}, u32[]{:S(2)}) %copy-start.1) | copy-done | bytes 524312
  1.2 0.6 %copy-done = bf16[576,2,1024]{2,1,0:T(2,128)(2,1)S(1)} copy-done((bf16[576,2,1024]{2,1,0:T(2,128)(2,1)S(1)}, bf16[576,2,1024]{2,1,0:T(2,128)(2,1)}, u32[]{:S(2)}) %copy-start) | copy-done | bytes 2359320
  1.8 0.8 %fusion.5.spectrum_ref = bf16[2,576,256]{2,1,0:T(8,128)(2,1)S(1)} fusion(bf16[576,2,1024]{2,1,0:T(2,128)(2,1)S(1)} %copy-done, bf16[1024,256]{1,0:T(8,128)(2,1)S(1)} %table.1), kind=kOutput, calls=%fused_computation.3 | convolution fusion | flops 604274688 | bytes 3473408 | tf_op jit(solution)/shard_map/cws,sj->wcj/dot_general | solution.py:235
  2.6 0.8 %whiten.1 = (bf16[2,16,1152]{2,1,0:T(8,128)(2,1)S(1)}, bf16[2,16,1152]{2,1,0:T(8,128)(2,1)S(1)}, bf16[2,16,1152]{2,1,0:T(8,128)(2,1)S(1)}, bf16[2,16,1152]{2,1,0...) custom-call(bf16[2,576,256]{2,1,0:T(8,128)(2,1)S(1)} %fusion.5.spect, ...), custom_call_target="tpu_custom_call" | custom-call | flops 5898240 | bytes 1769472 | tf_op jit(solution)/shard_map/whiten/pallas_call | solution.py:238
  3.4 6.1 %collective-permute-start = (bf16[2,16,1152]{2,1,0:T(8,128)(2,1)S(1)}, bf16[2,16,1152]{2,1,0:T(8,128)(2,1)S(1)}, u32[]{:S(2)}, u32[]{:S(2)}) collective-permute-start(bf16[2,16,1152]{2,1,0:T(8,128)(2,1)S(1)} %get-tuple-element.13), channel_id=1, source_target_pairs={{0,7},{1,6},{2,5},{3,4},{4,3},{5,2},{6,1},{7,0},{8,15},{9,14},{10,... | collective-permute-start | bytes 221192 | tf_op jit(solution)/shard_map/ppermute | solution.py:203
  9.4 0.5 %collective-permute-start.1 = (bf16[2,16,1152]{2,1,0:T(8,128)(2,1)S(1)}, bf16[2,16,1152]{2,1,0:T(8,128)(2,1)S(1)}, u32[]{:S(2)}, u32[]{:S(2)}) collective-permute-start(bf16[2,16,1152]{2,1,0:T(8,128)(2,1)S(1)} %get-tuple-element.14), channel_id=1, source_target_pairs={{0,1},{1,0},{2,3},{3,2},{4,5},{5,4},{6,7},{7,6},{8,9},{9,8},{10,11... | collective-permute-start | bytes 221192 | tf_op jit(solution)/shard_map/ppermute | solution.py:203
  10.0 0.0 collective-permute-start.2
  10.0 0.9 %collective-permute-start.3 = (bf16[2,16,1152]{2,1,0:T(8,128)(2,1)S(1)}, bf16[2,16,1152]{2,1,0:T(8,128)(2,1)S(1)}, u32[]{:S(2)}, u32[]{:S(2)}) collective-permute-start(bf16[2,16,1152]{2,1,0:T(8,128)(2,1)S(1)} %get-tuple-element.16), channel_id=1, source_target_pairs={{0,6},{1,7},{2,4},{3,5},{4,2},{5,3},{6,0},{7,1},{8,14},{9,15},{10,... | collective-permute-start | bytes 221192 | tf_op jit(solution)/shard_map/ppermute | solution.py:203
  10.9 3.5 %collective-permute-start.4 = (bf16[2,16,1152]{2,1,0:T(8,128)(2,1)S(1)}, bf16[2,16,1152]{2,1,0:T(8,128)(2,1)S(1)}, u32[]{:S(2)}, u32[]{:S(2)}) collective-permute-start(bf16[2,16,1152]{2,1,0:T(8,128)(2,1)S(1)} %get-tuple-element.17), channel_id=1, source_target_pairs={{0,5},{1,4},{2,7},{3,6},{4,1},{5,0},{6,3},{7,2},{8,13},{9,12},{10,... | collective-permute-start | bytes 221192 | tf_op jit(solution)/shard_map/ppermute | solution.py:203
  14.4 0.0 collective-permute-done.refs_0_
  14.4 0.3 collective-permute-start.5
  14.7 0.0 collective-permute-done.1.refs_1_
  14.7 3.2 %collective-permute-start.6 = (bf16[2,16,1152]{2,1,0:T(8,128)(2,1)S(1)}, bf16[2,16,1152]{2,1,0:T(8,128)(2,1)S(1)}, u32[]{:S(2)}, u32[]{:S(2)}) collective-permute-start(bf16[2,16,1152]{2,1,0:T(8,128)(2,1)S(1)} %get-tuple-element.19), channel_id=1, source_target_pairs={{0,3},{1,2},{2,1},{3,0},{4,7},{5,6},{6,5},{7,4},{8,11},{9,10},{10,... | collective-permute-start | bytes 221192 | tf_op jit(solution)/shard_map/ppermute | solution.py:203
  17.9 0.0 collective-permute-done.2.refs_2_
  17.9 0.0 collective-permute-start.14
  17.9 0.0 collective-permute-done.3.refs_3_
  17.9 0.5 %collective-permute-start.7 = (bf16[2,16,1152]{2,1,0:T(8,128)(2,1)S(1)}, bf16[2,16,1152]{2,1,0:T(8,128)(2,1)S(1)}, u32[]{:S(2)}, u32[]{:S(2)}) collective-permute-start(bf16[2,16,1152]{2,1,0:T(8,128)(2,1)S(1)} %collective-permute-done.refs_0_), channel_id=1, source_target_pairs={{0,8},{8,0},{1,9},{9,1},{2,10},{10,2},{3,11},{11,3},{4,12},{12,4},... | collective-permute-start | bytes 221192 | tf_op jit(solution)/shard_map/ppermute | solution.py:207
  18.4 4.2 %collective-permute-done.4.refs_4_ = bf16[2,16,1152]{2,1,0:T(8,128)(2,1)S(1)} collective-permute-done((bf16[2,16,1152]{2,1,0:T(8,128)(2,1)S(1)}, bf16[2,16,1152]{2,1,0:T(8,128)(2,1)S(1)}, u32[]{:S(2)}, u32[]{:S(2)}) %collective-permute-start.4) | collective-permute-done | bytes 73760 | tf_op jit(solution)/shard_map/ppermute | solution.py:203
  22.6 0.0 collective-permute-start.8
  22.6 0.0 collective-permute-done.5.refs_5_
  22.6 0.5 %collective-permute-start.9 = (bf16[2,16,1152]{2,1,0:T(8,128)(2,1)S(1)}, bf16[2,16,1152]{2,1,0:T(8,128)(2,1)S(1)}, u32[]{:S(2)}, u32[]{:S(2)}) collective-permute-start(bf16[2,16,1152]{2,1,0:T(8,128)(2,1)S(1)} %collective-permute-done.2.refs_2_), channel_id=1, source_target_pairs={{0,8},{8,0},{1,9},{9,1},{2,10},{10,2},{3,11},{11,3},{4,12},{12,4},... | collective-permute-start | bytes 221192 | tf_op jit(solution)/shard_map/ppermute | solution.py:207
  23.2 0.1 collective-permute-start.10
  23.2 0.0 collective-permute-done.14.refs_15_
  23.2 0.4 collective-permute-start.11
  23.7 0.1 collective-permute-start.12
  23.7 0.2 collective-permute-done.8.refs_9_
  23.9 0.3 collective-permute-start.13
  24.2 0.2 collective-permute-done.10.refs_11_
  24.4 0.2 collective-permute-done.11.refs_12_
  24.6 0.4 collective-permute-done.12.refs_13_
  24.9 0.2 collective-permute-done.13.refs_14_
  25.2 20.5 %outer_products.1 = bf16[2,16,576,1152]{3,2,1,0:T(8,128)(2,1)} custom-call(bf16[2,16,1152]{2,1,0:T(8,128)(2,1)S(1)} %collective-permute-done.refs_0_, bf16[2,16,1152]{2,1,0:T(8,128)(2,1)S(1)} %collective-permute-done.1.refs_1_, bf16[2,16,1152]{2,1,0:T(8,128)(2,1)S(1)} %collective-permute-done.2.refs_2_, ...), custom_call_target="tpu_custom_call" | custom-call | flops 5435817984 | bytes 42467328 | tf_op jit(solution)/shard_map/outer_products/pallas_call | solution.py:260
  (6 shorter events, 0.0 us)
Async XLA Ops:
  0.0 1.8 %copy-start = (bf16[576,2,1024]{2,1,0:T(2,128)(2,1)S(1)}, bf16[576,2,1024]{2,1,0:T(2,128)(2,1)}, u32[]{:S(2)}) copy-start(bf16[576,2,1024]{2,1,0:T(2,128)(2,1)} %param.2) | copy-start | bytes 7077892
  0.0 1.2 %copy-start.1 = (bf16[1024,256]{1,0:T(8,128)(2,1)S(1)}, bf16[1024,256]{1,0:T(8,128)(2,1)}, u32[]{:S(2)}) copy-start(bf16[1024,256]{1,0:T(8,128)(2,1)} %constant.2.clone.in_ref) | copy-start | bytes 1572868
  3.4 11.0 %collective-permute-start = (bf16[2,16,1152]{2,1,0:T(8,128)(2,1)S(1)}, bf16[2,16,1152]{2,1,0:T(8,128)(2,1)S(1)}, u32[]{:S(2)}, u32[]{:S(2)}) collective-permute-start(bf16[2,16,1152]{2,1,0:T(8,128)(2,1)S(1)} %get-tuple-element.13), channel_id=1, source_target_pairs={{0,7},{1,6},{2,5},{3,4},{4,3},{5,2},{6,1},{7,0},{8,15},{9,14},{10,... | collective-permute-start | bytes 221192 | tf_op jit(solution)/shard_map/ppermute | solution.py:203
  9.4 5.3 %collective-permute-start.1 = (bf16[2,16,1152]{2,1,0:T(8,128)(2,1)S(1)}, bf16[2,16,1152]{2,1,0:T(8,128)(2,1)S(1)}, u32[]{:S(2)}, u32[]{:S(2)}) collective-permute-start(bf16[2,16,1152]{2,1,0:T(8,128)(2,1)S(1)} %get-tuple-element.14), channel_id=1, source_target_pairs={{0,1},{1,0},{2,3},{3,2},{4,5},{5,4},{6,7},{7,6},{8,9},{9,8},{10,11... | collective-permute-start | bytes 221192 | tf_op jit(solution)/shard_map/ppermute | solution.py:203
  10.0 8.0 %collective-permute-start.2 = (bf16[2,16,1152]{2,1,0:T(8,128)(2,1)S(1)}, bf16[2,16,1152]{2,1,0:T(8,128)(2,1)S(1)}, u32[]{:S(2)}, u32[]{:S(2)}) collective-permute-start(bf16[2,16,1152]{2,1,0:T(8,128)(2,1)S(1)} %get-tuple-element.15), channel_id=1, source_target_pairs={{0,2},{1,3},{2,0},{3,1},{4,6},{5,7},{6,4},{7,5},{8,10},{9,11},{10,... | collective-permute-start | bytes 221192 | tf_op jit(solution)/shard_map/ppermute | solution.py:203
  10.0 8.0 %collective-permute-start.3 = (bf16[2,16,1152]{2,1,0:T(8,128)(2,1)S(1)}, bf16[2,16,1152]{2,1,0:T(8,128)(2,1)S(1)}, u32[]{:S(2)}, u32[]{:S(2)}) collective-permute-start(bf16[2,16,1152]{2,1,0:T(8,128)(2,1)S(1)} %get-tuple-element.16), channel_id=1, source_target_pairs={{0,6},{1,7},{2,4},{3,5},{4,2},{5,3},{6,0},{7,1},{8,14},{9,15},{10,... | collective-permute-start | bytes 221192 | tf_op jit(solution)/shard_map/ppermute | solution.py:203
  10.9 11.8 %collective-permute-start.4 = (bf16[2,16,1152]{2,1,0:T(8,128)(2,1)S(1)}, bf16[2,16,1152]{2,1,0:T(8,128)(2,1)S(1)}, u32[]{:S(2)}, u32[]{:S(2)}) collective-permute-start(bf16[2,16,1152]{2,1,0:T(8,128)(2,1)S(1)} %get-tuple-element.17), channel_id=1, source_target_pairs={{0,5},{1,4},{2,7},{3,6},{4,1},{5,0},{6,3},{7,2},{8,13},{9,12},{10,... | collective-permute-start | bytes 221192 | tf_op jit(solution)/shard_map/ppermute | solution.py:203
  14.4 8.2 %collective-permute-start.5 = (bf16[2,16,1152]{2,1,0:T(8,128)(2,1)S(1)}, bf16[2,16,1152]{2,1,0:T(8,128)(2,1)S(1)}, u32[]{:S(2)}, u32[]{:S(2)}) collective-permute-start(bf16[2,16,1152]{2,1,0:T(8,128)(2,1)S(1)} %get-tuple-element.18), channel_id=1, source_target_pairs={{0,4},{1,5},{2,6},{3,7},{4,0},{5,1},{6,2},{7,3},{8,12},{9,13},{10,... | collective-permute-start | bytes 221192 | tf_op jit(solution)/shard_map/ppermute | solution.py:203
  14.7 8.4 %collective-permute-start.6 = (bf16[2,16,1152]{2,1,0:T(8,128)(2,1)S(1)}, bf16[2,16,1152]{2,1,0:T(8,128)(2,1)S(1)}, u32[]{:S(2)}, u32[]{:S(2)}) collective-permute-start(bf16[2,16,1152]{2,1,0:T(8,128)(2,1)S(1)} %get-tuple-element.19), channel_id=1, source_target_pairs={{0,3},{1,2},{2,1},{3,0},{4,7},{5,6},{6,5},{7,4},{8,11},{9,10},{10,... | collective-permute-start | bytes 221192 | tf_op jit(solution)/shard_map/ppermute | solution.py:203
  17.9 5.3 %collective-permute-start.14 = (bf16[2,16,1152]{2,1,0:T(8,128)(2,1)S(1)}, bf16[2,16,1152]{2,1,0:T(8,128)(2,1)S(1)}, u32[]{:S(2)}, u32[]{:S(2)}) collective-permute-start(bf16[2,16,1152]{2,1,0:T(8,128)(2,1)S(1)} %get-tuple-element.20.refs_7_), channel_id=1, source_target_pairs={{0,8},{8,0},{1,9},{9,1},{2,10},{10,2},{3,11},{11,3},{4,12},{12,4},... | collective-permute-start | bytes 221192 | tf_op jit(solution)/shard_map/ppermute | solution.py:207
  17.9 5.7 %collective-permute-start.7 = (bf16[2,16,1152]{2,1,0:T(8,128)(2,1)S(1)}, bf16[2,16,1152]{2,1,0:T(8,128)(2,1)S(1)}, u32[]{:S(2)}, u32[]{:S(2)}) collective-permute-start(bf16[2,16,1152]{2,1,0:T(8,128)(2,1)S(1)} %collective-permute-done.refs_0_), channel_id=1, source_target_pairs={{0,8},{8,0},{1,9},{9,1},{2,10},{10,2},{3,11},{11,3},{4,12},{12,4},... | collective-permute-start | bytes 221192 | tf_op jit(solution)/shard_map/ppermute | solution.py:207
  22.6 1.3 %collective-permute-start.8 = (bf16[2,16,1152]{2,1,0:T(8,128)(2,1)S(1)}, bf16[2,16,1152]{2,1,0:T(8,128)(2,1)S(1)}, u32[]{:S(2)}, u32[]{:S(2)}) collective-permute-start(bf16[2,16,1152]{2,1,0:T(8,128)(2,1)S(1)} %collective-permute-done.1.refs_1_), channel_id=1, source_target_pairs={{0,8},{8,0},{1,9},{9,1},{2,10},{10,2},{3,11},{11,3},{4,12},{12,4},... | collective-permute-start | bytes 221192 | tf_op jit(solution)/shard_map/ppermute | solution.py:207
  22.6 1.5 %collective-permute-start.9 = (bf16[2,16,1152]{2,1,0:T(8,128)(2,1)S(1)}, bf16[2,16,1152]{2,1,0:T(8,128)(2,1)S(1)}, u32[]{:S(2)}, u32[]{:S(2)}) collective-permute-start(bf16[2,16,1152]{2,1,0:T(8,128)(2,1)S(1)} %collective-permute-done.2.refs_2_), channel_id=1, source_target_pairs={{0,8},{8,0},{1,9},{9,1},{2,10},{10,2},{3,11},{11,3},{4,12},{12,4},... | collective-permute-start | bytes 221192 | tf_op jit(solution)/shard_map/ppermute | solution.py:207
  23.2 1.3 %collective-permute-start.10 = (bf16[2,16,1152]{2,1,0:T(8,128)(2,1)S(1)}, bf16[2,16,1152]{2,1,0:T(8,128)(2,1)S(1)}, u32[]{:S(2)}, u32[]{:S(2)}) collective-permute-start(bf16[2,16,1152]{2,1,0:T(8,128)(2,1)S(1)} %collective-permute-done.3.refs_3_), channel_id=1, source_target_pairs={{0,8},{8,0},{1,9},{9,1},{2,10},{10,2},{3,11},{11,3},{4,12},{12,4},... | collective-permute-start | bytes 221192 | tf_op jit(solution)/shard_map/ppermute | solution.py:207
  23.2 1.4 %collective-permute-start.11 = (bf16[2,16,1152]{2,1,0:T(8,128)(2,1)S(1)}, bf16[2,16,1152]{2,1,0:T(8,128)(2,1)S(1)}, u32[]{:S(2)}, u32[]{:S(2)}) collective-permute-start(bf16[2,16,1152]{2,1,0:T(8,128)(2,1)S(1)} %collective-permute-done.4.refs_4_), channel_id=1, source_target_pairs={{0,8},{8,0},{1,9},{9,1},{2,10},{10,2},{3,11},{11,3},{4,12},{12,4},... | collective-permute-start | bytes 221192 | tf_op jit(solution)/shard_map/ppermute | solution.py:207
  23.7 1.3 %collective-permute-start.12 = (bf16[2,16,1152]{2,1,0:T(8,128)(2,1)S(1)}, bf16[2,16,1152]{2,1,0:T(8,128)(2,1)S(1)}, u32[]{:S(2)}, u32[]{:S(2)}) collective-permute-start(bf16[2,16,1152]{2,1,0:T(8,128)(2,1)S(1)} %collective-permute-done.5.refs_5_), channel_id=1, source_target_pairs={{0,8},{8,0},{1,9},{9,1},{2,10},{10,2},{3,11},{11,3},{4,12},{12,4},... | collective-permute-start | bytes 221192 | tf_op jit(solution)/shard_map/ppermute | solution.py:207
  23.9 1.3 %collective-permute-start.13 = (bf16[2,16,1152]{2,1,0:T(8,128)(2,1)S(1)}, bf16[2,16,1152]{2,1,0:T(8,128)(2,1)S(1)}, u32[]{:S(2)}, u32[]{:S(2)}) collective-permute-start(bf16[2,16,1152]{2,1,0:T(8,128)(2,1)S(1)} %collective-permute-done.6.refs_6_), channel_id=1, source_target_pairs={{0,8},{8,0},{1,9},{9,1},{2,10},{10,2},{3,11},{11,3},{4,12},{12,4},... | collective-permute-start | bytes 221192 | tf_op jit(solution)/shard_map/ppermute | solution.py:207

commit v11 on v9

--- a/solution.py
+++ b/solution.py
@@ -12,6 +12,8 @@
 
 BINS = 128
 LANES = 128
+ROWS = 96
+COLUMNS = 512
 MIB = 1024 * 1024
 
 
@@ -181,27 +183,22 @@
 
     slot = lax.rem(now, depth_of_slots)
 
-    whole = 2 * channels // (2 * LANES) * (2 * LANES)
-    starts = [0, whole, 4 * channels - whole, 4 * channels]
-    left_over = 2 * channels - whole
-
-    def multiply(first, last):
-        return jnp.dot(
-            chosen, weights[:, first:last], preferred_element_type=jnp.float32
-        ).astype(jnp.bfloat16)
-
-    def send(part):
-        for cut in range(cuts):
+    for cut in range(cuts):
+        for first in range(cut * size, (cut + 1) * size, ROWS):
+            at = slice(first, first + ROWS)
+            for lane in range(0, 4 * channels, COLUMNS):
+                last = min(lane + COLUMNS, 4 * channels)
+                product = jnp.dot(
+                    chosen[at], weights[:, lane:last], preferred_element_type=jnp.float32
+                ).astype(jnp.bfloat16)
+                middle = min(max(lane, 2 * channels), last)
+                if lane < middle:
+                    slots[slot, 0, at, lane:middle] = product[:, : middle - lane]
+                if middle < last:
+                    begin, end = middle - 2 * channels, last - 2 * channels
+                    slots[slot, 1, at, begin:end] = product[:, middle - lane :]
+        for part in range(2):
             copy(now, cut, part).start()
-
-    slots[slot, 0, :, :whole] = multiply(*starts[:2])
-    if left_over:
-        both = multiply(*starts[1:3])
-        slots[slot, 0, :, whole:] = both[:, :left_over]
-        slots[slot, 1, :, :left_over] = both[:, left_over:]
-    send(0)
-    slots[slot, 1, :, left_over:] = multiply(*starts[2:])
-    send(1)
 
     @pl.when(now == steps - 1)
     def _():
@@ -235,8 +232,7 @@
     lanes = local_windows * local_channels
     vmem = pl.BlockSpec(memory_space=pltpu.VMEM)
     memory = pl.BlockSpec(memory_space=pl.ANY)
-    masks = [*range(devices - 1, devices // 2 - 1, -1), *range(1, devices // 2), 0]
-    masks = masks if aligned else [0]
+    masks = [devices - 1, 1, 2, *range(devices - 2, 2, -1), 0] if aligned else [0]
     pieces = len(masks)
     rows = (devices, groups, 2 * bins, lanes) if aligned else (2 * BINS, lanes)
     piece = rows[1:] if aligned else rows
@@ -285,7 +281,7 @@
                 pltpu.VMEM((sets, depth, 4 * local_channels), jnp.bfloat16),
                 pltpu.VMEM((sets, local_channels, depth), jnp.float32),
                 pltpu.VMEM((3, 2, local_channels, 2 * local_channels), jnp.bfloat16),
-                pltpu.SemaphoreType.DMA((3, 1, 2)),
+                pltpu.SemaphoreType.DMA((3, 2, 2)),
             ],
             compiler_params=pltpu.CompilerParams(vmem_limit_bytes=32 * MIB),
             cost_estimate=pl.CostEstimate(

time: 42.5 us -> 42.9 us (level)
  waiting for transfers between devices: 3.91 us -> 5.36 us
  starting transfers between devices: 17.7 us -> 16.4 us
    ppermute x7, starting transfers between devices: 16.1 us -> 14.5 us  [exchange(): return lax.ppermute(value, 'freq', pairs) if mask else value]
    ppermute x7, waiting for transfers between devices: 3 us -> 4.22 us  [exchange(): return lax.ppermute(value, 'freq', pairs) if mask else value]
  transfers between devices with their start and end apart: 15 -> 15, of which waited for: 7 -> 6; matrix products, arithmetic and copies ran while one was open for 0% -> 0% of each run, Pallas kernels for 0% -> 0%
where the time goes in v11:
time: 42.9 us; the launch traced here: 42.8 us
  Pallas kernels  18.4 us (43%)
  starting transfers between devices  16.4 us (38%)
  waiting for transfers between devices  5.36 us (12%)
  local copies, waits for them, and re-layouts  1.78 us (4%)
  matrix products  0.79 us (2%)
    pallas_call x1, Pallas kernels, local(): pl.pallas_call(functools.partial(outer_kernel, bins, sets, 1.0 / windows)...  17.6 us
    ppermute x7, starting transfers between devices, exchange(): return lax.ppermute(value, 'freq', pairs) if mask else value  14.5 us
    ppermute x7, waiting for transfers between devices, exchange(): return lax.ppermute(value, 'freq', pairs) if mask else value  4.22 us
    ppermute x8, starting transfers between devices, swap(): return lax.ppermute(value, 'chan', [(0, 1), (1, 0)])  1.88 us
    unnamed x4, local copies, waits for them, and re-layouts  1.78 us
    ppermute x8, waiting for transfers between devices, swap(): return lax.ppermute(value, 'chan', [(0, 1), (1, 0)])  1.14 us
  transfers between devices with their start and end apart: 15, of which 6 were waited for; matrix products, arithmetic and copies ran while one was open for 0% of the time, Pallas kernels for 0%

profile of v11, /device:TPU:0, one launch (start us, length us, event | category | flops | bytes accessed | tf_op | source)
XLA Modules:
  0.0 42.8 jit_solution(386313761396672215)
XLA Ops:
  0.0 1.2 %copy-done.1 = bf16[1024,256]{1,0:T(8,128)(2,1)S(1)} copy-done((bf16[1024,256]{1,0:T(8,128)(2,1)S(1)}, bf16[1024,256]{1,0:T(8,128)(2,1)}, u32[]{:S(2)}) %copy-start.1) | copy-done | bytes 524312
  1.2 0.6 %copy-done = bf16[576,2,1024]{2,1,0:T(2,128)(2,1)S(1)} copy-done((bf16[576,2,1024]{2,1,0:T(2,128)(2,1)S(1)}, bf16[576,2,1024]{2,1,0:T(2,128)(2,1)}, u32[]{:S(2)}) %copy-start) | copy-done | bytes 2359320
  1.8 0.8 %fusion.5.spectrum_ref = bf16[2,576,256]{2,1,0:T(8,128)(2,1)S(1)} fusion(bf16[576,2,1024]{2,1,0:T(2,128)(2,1)S(1)} %copy-done, bf16[1024,256]{1,0:T(8,128)(2,1)S(1)} %table.1), kind=kOutput, calls=%fused_computation.3 | convolution fusion | flops 604274688 | bytes 3473408 | tf_op jit(solution)/shard_map/cws,sj->wcj/dot_general | solution.py:247
  2.6 0.8 %whiten.1 = (bf16[2,16,1152]{2,1,0:T(8,128)(2,1)S(1)}, bf16[2,16,1152]{2,1,0:T(8,128)(2,1)S(1)}, bf16[2,16,1152]{2,1,0:T(8,128)(2,1)S(1)}, bf16[2,16,1152]{2,1,0...) custom-call(bf16[2,576,256]{2,1,0:T(8,128)(2,1)S(1)} %fusion.5.spect, ...), custom_call_target="tpu_custom_call" | custom-call | flops 5898240 | bytes 1769472 | tf_op jit(solution)/shard_map/whiten/pallas_call | solution.py:250
  3.4 6.1 %collective-permute-start = (bf16[2,16,1152]{2,1,0:T(8,128)(2,1)S(1)}, bf16[2,16,1152]{2,1,0:T(8,128)(2,1)S(1)}, u32[]{:S(2)}, u32[]{:S(2)}) collective-permute-start(bf16[2,16,1152]{2,1,0:T(8,128)(2,1)S(1)} %get-tuple-element.13), channel_id=1, source_target_pairs={{0,7},{1,6},{2,5},{3,4},{4,3},{5,2},{6,1},{7,0},{8,15},{9,14},{10,... | collective-permute-start | bytes 221192 | tf_op jit(solution)/shard_map/ppermute | solution.py:215
  9.4 0.5 %collective-permute-start.1 = (bf16[2,16,1152]{2,1,0:T(8,128)(2,1)S(1)}, bf16[2,16,1152]{2,1,0:T(8,128)(2,1)S(1)}, u32[]{:S(2)}, u32[]{:S(2)}) collective-permute-start(bf16[2,16,1152]{2,1,0:T(8,128)(2,1)S(1)} %get-tuple-element.14), channel_id=1, source_target_pairs={{0,1},{1,0},{2,3},{3,2},{4,5},{5,4},{6,7},{7,6},{8,9},{9,8},{10,11... | collective-permute-start | bytes 221192 | tf_op jit(solution)/shard_map/ppermute | solution.py:215
  10.0 0.0 collective-permute-start.2
  10.0 0.9 %collective-permute-start.3 = (bf16[2,16,1152]{2,1,0:T(8,128)(2,1)S(1)}, bf16[2,16,1152]{2,1,0:T(8,128)(2,1)S(1)}, u32[]{:S(2)}, u32[]{:S(2)}) collective-permute-start(bf16[2,16,1152]{2,1,0:T(8,128)(2,1)S(1)} %get-tuple-element.16), channel_id=1, source_target_pairs={{0,6},{1,7},{2,4},{3,5},{4,2},{5,3},{6,0},{7,1},{8,14},{9,15},{10,... | collective-permute-start | bytes 221192 | tf_op jit(solution)/shard_map/ppermute | solution.py:215
  10.9 3.5 %collective-permute-start.4 = (bf16[2,16,1152]{2,1,0:T(8,128)(2,1)S(1)}, bf16[2,16,1152]{2,1,0:T(8,128)(2,1)S(1)}, u32[]{:S(2)}, u32[]{:S(2)}) collective-permute-start(bf16[2,16,1152]{2,1,0:T(8,128)(2,1)S(1)} %get-tuple-element.17), channel_id=1, source_target_pairs={{0,5},{1,4},{2,7},{3,6},{4,1},{5,0},{6,3},{7,2},{8,13},{9,12},{10,... | collective-permute-start | bytes 221192 | tf_op jit(solution)/shard_map/ppermute | solution.py:215
  14.4 0.0 collective-permute-done.refs_0_
  14.4 0.3 collective-permute-start.5
  14.7 0.0 collective-permute-done.1.refs_1_
  14.7 3.2 %collective-permute-start.6 = (bf16[2,16,1152]{2,1,0:T(8,128)(2,1)S(1)}, bf16[2,16,1152]{2,1,0:T(8,128)(2,1)S(1)}, u32[]{:S(2)}, u32[]{:S(2)}) collective-permute-start(bf16[2,16,1152]{2,1,0:T(8,128)(2,1)S(1)} %get-tuple-element.19), channel_id=1, source_target_pairs={{0,3},{1,2},{2,1},{3,0},{4,7},{5,6},{6,5},{7,4},{8,11},{9,10},{10,... | collective-permute-start | bytes 221192 | tf_op jit(solution)/shard_map/ppermute | solution.py:215
  17.9 0.5 %collective-permute-start.7 = (bf16[2,16,1152]{2,1,0:T(8,128)(2,1)S(1)}, bf16[2,16,1152]{2,1,0:T(8,128)(2,1)S(1)}, u32[]{:S(2)}, u32[]{:S(2)}) collective-permute-start(bf16[2,16,1152]{2,1,0:T(8,128)(2,1)S(1)} %collective-permute-done.refs_0_), channel_id=1, source_target_pairs={{0,8},{8,0},{1,9},{9,1},{2,10},{10,2},{3,11},{11,3},{4,12},{12,4},... | collective-permute-start | bytes 221192 | tf_op jit(solution)/shard_map/ppermute | solution.py:219
  18.4 4.2 %collective-permute-done.4.refs_4_ = bf16[2,16,1152]{2,1,0:T(8,128)(2,1)S(1)} collective-permute-done((bf16[2,16,1152]{2,1,0:T(8,128)(2,1)S(1)}, bf16[2,16,1152]{2,1,0:T(8,128)(2,1)S(1)}, u32[]{:S(2)}, u32[]{:S(2)}) %collective-permute-start.4) | collective-permute-done | bytes 73760 | tf_op jit(solution)/shard_map/ppermute | solution.py:215
  22.6 0.0 collective-permute-start.8
  22.6 0.0 collective-permute-done.5.refs_5_
  22.6 0.5 %collective-permute-start.9 = (bf16[2,16,1152]{2,1,0:T(8,128)(2,1)S(1)}, bf16[2,16,1152]{2,1,0:T(8,128)(2,1)S(1)}, u32[]{:S(2)}, u32[]{:S(2)}) collective-permute-start(bf16[2,16,1152]{2,1,0:T(8,128)(2,1)S(1)} %collective-permute-done.2.refs_2_), channel_id=1, source_target_pairs={{0,8},{8,0},{1,9},{9,1},{2,10},{10,2},{3,11},{11,3},{4,12},{12,4},... | collective-permute-start | bytes 221192 | tf_op jit(solution)/shard_map/ppermute | solution.py:219
  23.2 0.0 collective-permute-done.6.refs_6_
  23.2 0.1 collective-permute-start.10
  23.2 0.0 collective-permute-done.14.refs_15_
  23.2 0.4 %collective-permute-start.11 = (bf16[2,16,1152]{2,1,0:T(8,128)(2,1)S(1)}, bf16[2,16,1152]{2,1,0:T(8,128)(2,1)S(1)}, u32[]{:S(2)}, u32[]{:S(2)}) collective-permute-start(bf16[2,16,1152]{2,1,0:T(8,128)(2,1)S(1)} %collective-permute-done.4.refs_4_), channel_id=1, source_target_pairs={{0,8},{8,0},{1,9},{9,1},{2,10},{10,2},{3,11},{11,3},{4,12},{12,4},... | collective-permute-start | bytes 221192 | tf_op jit(solution)/shard_map/ppermute | solution.py:219
  23.7 0.0 collective-permute-done.7.refs_8_
  23.7 0.1 collective-permute-start.12
  23.7 0.2 collective-permute-done.8.refs_9_
  23.9 0.3 collective-permute-start.13
  24.2 0.0 collective-permute-done.9.refs_10_
  24.2 0.2 collective-permute-done.10.refs_11_
  24.4 0.2 collective-permute-done.11.refs_12_
  24.6 0.4 collective-permute-done.12.refs_13_
  24.9 0.2 collective-permute-done.13.refs_14_
  25.2 17.6 %outer_products.1 = bf16[2,16,576,1152]{3,2,1,0:T(8,128)(2,1)} custom-call(bf16[2,16,1152]{2,1,0:T(8,128)(2,1)S(1)} %collective-permute-done.refs_0_, bf16[2,16,1152]{2,1,0:T(8,128)(2,1)S(1)} %collective-permute-done.1.refs_1_, bf16[2,16,1152]{2,1,0:T(8,128)(2,1)S(1)} %collective-permute-done.2.refs_2_, ...), custom_call_target="tpu_custom_call" | custom-call | flops 5435817984 | bytes 42467328 | tf_op jit(solution)/shard_map/outer_products/pallas_call | solution.py:272
  (6 shorter events, 0.0 us)
Async XLA Ops:
  0.0 1.8 %copy-start = (bf16[576,2,1024]{2,1,0:T(2,128)(2,1)S(1)}, bf16[576,2,1024]{2,1,0:T(2,128)(2,1)}, u32[]{:S(2)}) copy-start(bf16[576,2,1024]{2,1,0:T(2,128)(2,1)} %param.2) | copy-start | bytes 7077892
  0.0 1.2 %copy-start.1 = (bf16[1024,256]{1,0:T(8,128)(2,1)S(1)}, bf16[1024,256]{1,0:T(8,128)(2,1)}, u32[]{:S(2)}) copy-start(bf16[1024,256]{1,0:T(8,128)(2,1)} %constant.2.clone.in_ref) | copy-start | bytes 1572868
  3.4 11.0 %collective-permute-start = (bf16[2,16,1152]{2,1,0:T(8,128)(2,1)S(1)}, bf16[2,16,1152]{2,1,0:T(8,128)(2,1)S(1)}, u32[]{:S(2)}, u32[]{:S(2)}) collective-permute-start(bf16[2,16,1152]{2,1,0:T(8,128)(2,1)S(1)} %get-tuple-element.13), channel_id=1, source_target_pairs={{0,7},{1,6},{2,5},{3,4},{4,3},{5,2},{6,1},{7,0},{8,15},{9,14},{10,... | collective-permute-start | bytes 221192 | tf_op jit(solution)/shard_map/ppermute | solution.py:215
  9.4 5.3 %collective-permute-start.1 = (bf16[2,16,1152]{2,1,0:T(8,128)(2,1)S(1)}, bf16[2,16,1152]{2,1,0:T(8,128)(2,1)S(1)}, u32[]{:S(2)}, u32[]{:S(2)}) collective-permute-start(bf16[2,16,1152]{2,1,0:T(8,128)(2,1)S(1)} %get-tuple-element.14), channel_id=1, source_target_pairs={{0,1},{1,0},{2,3},{3,2},{4,5},{5,4},{6,7},{7,6},{8,9},{9,8},{10,11... | collective-permute-start | bytes 221192 | tf_op jit(solution)/shard_map/ppermute | solution.py:215
  10.0 8.0 %collective-permute-start.2 = (bf16[2,16,1152]{2,1,0:T(8,128)(2,1)S(1)}, bf16[2,16,1152]{2,1,0:T(8,128)(2,1)S(1)}, u32[]{:S(2)}, u32[]{:S(2)}) collective-permute-start(bf16[2,16,1152]{2,1,0:T(8,128)(2,1)S(1)} %get-tuple-element.15), channel_id=1, source_target_pairs={{0,2},{1,3},{2,0},{3,1},{4,6},{5,7},{6,4},{7,5},{8,10},{9,11},{10,... | collective-permute-start | bytes 221192 | tf_op jit(solution)/shard_map/ppermute | solution.py:215
  10.0 8.0 %collective-permute-start.3 = (bf16[2,16,1152]{2,1,0:T(8,128)(2,1)S(1)}, bf16[2,16,1152]{2,1,0:T(8,128)(2,1)S(1)}, u32[]{:S(2)}, u32[]{:S(2)}) collective-permute-start(bf16[2,16,1152]{2,1,0:T(8,128)(2,1)S(1)} %get-tuple-element.16), channel_id=1, source_target_pairs={{0,6},{1,7},{2,4},{3,5},{4,2},{5,3},{6,0},{7,1},{8,14},{9,15},{10,... | collective-permute-start | bytes 221192 | tf_op jit(solution)/shard_map/ppermute | solution.py:215
  10.9 11.8 %collective-permute-start.4 = (bf16[2,16,1152]{2,1,0:T(8,128)(2,1)S(1)}, bf16[2,16,1152]{2,1,0:T(8,128)(2,1)S(1)}, u32[]{:S(2)}, u32[]{:S(2)}) collective-permute-start(bf16[2,16,1152]{2,1,0:T(8,128)(2,1)S(1)} %get-tuple-element.17), channel_id=1, source_target_pairs={{0,5},{1,4},{2,7},{3,6},{4,1},{5,0},{6,3},{7,2},{8,13},{9,12},{10,... | collective-permute-start | bytes 221192 | tf_op jit(solution)/shard_map/ppermute | solution.py:215
  14.4 8.2 %collective-permute-start.5 = (bf16[2,16,1152]{2,1,0:T(8,128)(2,1)S(1)}, bf16[2,16,1152]{2,1,0:T(8,128)(2,1)S(1)}, u32[]{:S(2)}, u32[]{:S(2)}) collective-permute-start(bf16[2,16,1152]{2,1,0:T(8,128)(2,1)S(1)} %get-tuple-element.18), channel_id=1, source_target_pairs={{0,4},{1,5},{2,6},{3,7},{4,0},{5,1},{6,2},{7,3},{8,12},{9,13},{10,... | collective-permute-start | bytes 221192 | tf_op jit(solution)/shard_map/ppermute | solution.py:215
  14.7 8.4 %collective-permute-start.6 = (bf16[2,16,1152]{2,1,0:T(8,128)(2,1)S(1)}, bf16[2,16,1152]{2,1,0:T(8,128)(2,1)S(1)}, u32[]{:S(2)}, u32[]{:S(2)}) collective-permute-start(bf16[2,16,1152]{2,1,0:T(8,128)(2,1)S(1)} %get-tuple-element.19), channel_id=1, source_target_pairs={{0,3},{1,2},{2,1},{3,0},{4,7},{5,6},{6,5},{7,4},{8,11},{9,10},{10,... | collective-permute-start | bytes 221192 | tf_op jit(solution)/shard_map/ppermute | solution.py:215
  17.9 5.3 %collective-permute-start.14 = (bf16[2,16,1152]{2,1,0:T(8,128)(2,1)S(1)}, bf16[2,16,1152]{2,1,0:T(8,128)(2,1)S(1)}, u32[]{:S(2)}, u32[]{:S(2)}) collective-permute-start(bf16[2,16,1152]{2,1,0:T(8,128)(2,1)S(1)} %get-tuple-element.20.refs_7_), channel_id=1, source_target_pairs={{0,8},{8,0},{1,9},{9,1},{2,10},{10,2},{3,11},{11,3},{4,12},{12,4},... | collective-permute-start | bytes 221192 | tf_op jit(solution)/shard_map/ppermute | solution.py:219
  17.9 5.7 %collective-permute-start.7 = (bf16[2,16,1152]{2,1,0:T(8,128)(2,1)S(1)}, bf16[2,16,1152]{2,1,0:T(8,128)(2,1)S(1)}, u32[]{:S(2)}, u32[]{:S(2)}) collective-permute-start(bf16[2,16,1152]{2,1,0:T(8,128)(2,1)S(1)} %collective-permute-done.refs_0_), channel_id=1, source_target_pairs={{0,8},{8,0},{1,9},{9,1},{2,10},{10,2},{3,11},{11,3},{4,12},{12,4},... | collective-permute-start | bytes 221192 | tf_op jit(solution)/shard_map/ppermute | solution.py:219
  22.6 1.3 %collective-permute-start.8 = (bf16[2,16,1152]{2,1,0:T(8,128)(2,1)S(1)}, bf16[2,16,1152]{2,1,0:T(8,128)(2,1)S(1)}, u32[]{:S(2)}, u32[]{:S(2)}) collective-permute-start(bf16[2,16,1152]{2,1,0:T(8,128)(2,1)S(1)} %collective-permute-done.1.refs_1_), channel_id=1, source_target_pairs={{0,8},{8,0},{1,9},{9,1},{2,10},{10,2},{3,11},{11,3},{4,12},{12,4},... | collective-permute-start | bytes 221192 | tf_op jit(solution)/shard_map/ppermute | solution.py:219
  22.6 1.5 %collective-permute-start.9 = (bf16[2,16,1152]{2,1,0:T(8,128)(2,1)S(1)}, bf16[2,16,1152]{2,1,0:T(8,128)(2,1)S(1)}, u32[]{:S(2)}, u32[]{:S(2)}) collective-permute-start(bf16[2,16,1152]{2,1,0:T(8,128)(2,1)S(1)} %collective-permute-done.2.refs_2_), channel_id=1, source_target_pairs={{0,8},{8,0},{1,9},{9,1},{2,10},{10,2},{3,11},{11,3},{4,12},{12,4},... | collective-permute-start | bytes 221192 | tf_op jit(solution)/shard_map/ppermute | solution.py:219
  23.2 1.3 %collective-permute-start.10 = (bf16[2,16,1152]{2,1,0:T(8,128)(2,1)S(1)}, bf16[2,16,1152]{2,1,0:T(8,128)(2,1)S(1)}, u32[]{:S(2)}, u32[]{:S(2)}) collective-permute-start(bf16[2,16,1152]{2,1,0:T(8,128)(2,1)S(1)} %collective-permute-done.3.refs_3_), channel_id=1, source_target_pairs={{0,8},{8,0},{1,9},{9,1},{2,10},{10,2},{3,11},{11,3},{4,12},{12,4},... | collective-permute-start | bytes 221192 | tf_op jit(solution)/shard_map/ppermute | solution.py:219
  23.2 1.4 %collective-permute-start.11 = (bf16[2,16,1152]{2,1,0:T(8,128)(2,1)S(1)}, bf16[2,16,1152]{2,1,0:T(8,128)(2,1)S(1)}, u32[]{:S(2)}, u32[]{:S(2)}) collective-permute-start(bf16[2,16,1152]{2,1,0:T(8,128)(2,1)S(1)} %collective-permute-done.4.refs_4_), channel_id=1, source_target_pairs={{0,8},{8,0},{1,9},{9,1},{2,10},{10,2},{3,11},{11,3},{4,12},{12,4},... | collective-permute-start | bytes 221192 | tf_op jit(solution)/shard_map/ppermute | solution.py:219
  23.7 1.3 %collective-permute-start.12 = (bf16[2,16,1152]{2,1,0:T(8,128)(2,1)S(1)}, bf16[2,16,1152]{2,1,0:T(8,128)(2,1)S(1)}, u32[]{:S(2)}, u32[]{:S(2)}) collective-permute-start(bf16[2,16,1152]{2,1,0:T(8,128)(2,1)S(1)} %collective-permute-done.5.refs_5_), channel_id=1, source_target_pairs={{0,8},{8,0},{1,9},{9,1},{2,10},{10,2},{3,11},{11,3},{4,12},{12,4},... | collective-permute-start | bytes 221192 | tf_op jit(solution)/shard_map/ppermute | solution.py:219
  23.9 1.3 %collective-permute-start.13 = (bf16[2,16,1152]{2,1,0:T(8,128)(2,1)S(1)}, bf16[2,16,1152]{2,1,0:T(8,128)(2,1)S(1)}, u32[]{:S(2)}, u32[]{:S(2)}) collective-permute-start(bf16[2,16,1152]{2,1,0:T(8,128)(2,1)S(1)} %collective-permute-done.6.refs_6_), channel_id=1, source_target_pairs={{0,8},{8,0},{1,9},{9,1},{2,10},{10,2},{3,11},{11,3},{4,12},{12,4},... | collective-permute-start | bytes 221192 | tf_op jit(solution)/shard_map/ppermute | solution.py:219

commit v12 on v9

--- a/solution.py
+++ b/solution.py
@@ -192,7 +192,7 @@
 
     def send(part):
         for cut in range(cuts):
-            copy(now, cut, part).start()
+            copy(now, cut, part).start(priority=cut)
 
     slots[slot, 0, :, :whole] = multiply(*starts[:2])
     if left_over:
@@ -235,8 +235,7 @@
     lanes = local_windows * local_channels
     vmem = pl.BlockSpec(memory_space=pltpu.VMEM)
     memory = pl.BlockSpec(memory_space=pl.ANY)
-    masks = [*range(devices - 1, devices // 2 - 1, -1), *range(1, devices // 2), 0]
-    masks = masks if aligned else [0]
+    masks = [devices - 1, 1, 2, *range(devices - 2, 2, -1), 0] if aligned else [0]
     pieces = len(masks)
     rows = (devices, groups, 2 * bins, lanes) if aligned else (2 * BINS, lanes)
     piece = rows[1:] if aligned else rows
@@ -285,7 +284,7 @@
                 pltpu.VMEM((sets, depth, 4 * local_channels), jnp.bfloat16),
                 pltpu.VMEM((sets, local_channels, depth), jnp.float32),
                 pltpu.VMEM((3, 2, local_channels, 2 * local_channels), jnp.bfloat16),
-                pltpu.SemaphoreType.DMA((3, 1, 2)),
+                pltpu.SemaphoreType.DMA((3, 2, 2)),
             ],
             compiler_params=pltpu.CompilerParams(vmem_limit_bytes=32 * MIB),
             cost_estimate=pl.CostEstimate(

time: 42.5 us -> 42.7 us (level)
  waiting for transfers between devices: 3.91 us -> 5.36 us
  starting transfers between devices: 17.7 us -> 16.4 us
    ppermute x7, starting transfers between devices: 16.1 us -> 14.5 us  [exchange(): return lax.ppermute(value, 'freq', pairs) if mask else value]
    ppermute x7, waiting for transfers between devices: 3 us -> 4.22 us  [exchange(): return lax.ppermute(value, 'freq', pairs) if mask else value]
  transfers between devices with their start and end apart: 15 -> 15, of which waited for: 7 -> 6; matrix products, arithmetic and copies ran while one was open for 0% -> 0% of each run, Pallas kernels for 0% -> 0%
where the time goes in v12:
time: 42.7 us; the launch traced here: 42.6 us
  Pallas kernels  18.2 us (43%)
  starting transfers between devices  16.4 us (38%)
  waiting for transfers between devices  5.36 us (13%)
  local copies, waits for them, and re-layouts  1.78 us (4%)
  matrix products  0.79 us (2%)
    pallas_call x1, Pallas kernels, local(): pl.pallas_call(functools.partial(outer_kernel, bins, sets, 1.0 / windows)...  17.4 us
    ppermute x7, starting transfers between devices, exchange(): return lax.ppermute(value, 'freq', pairs) if mask else value  14.5 us
    ppermute x7, waiting for transfers between devices, exchange(): return lax.ppermute(value, 'freq', pairs) if mask else value  4.22 us
    ppermute x8, starting transfers between devices, swap(): return lax.ppermute(value, 'chan', [(0, 1), (1, 0)])  1.88 us
    unnamed x4, local copies, waits for them, and re-layouts  1.78 us
    ppermute x8, waiting for transfers between devices, swap(): return lax.ppermute(value, 'chan', [(0, 1), (1, 0)])  1.14 us
  transfers between devices with their start and end apart: 15, of which 6 were waited for; matrix products, arithmetic and copies ran while one was open for 0% of the time, Pallas kernels for 0%

profile of v12, /device:TPU:0, one launch (start us, length us, event | category | flops | bytes accessed | tf_op | source)
XLA Modules:
  0.0 42.6 jit_solution(12647998035802582532)
XLA Ops:
  0.0 1.2 %copy-done.1 = bf16[1024,256]{1,0:T(8,128)(2,1)S(1)} copy-done((bf16[1024,256]{1,0:T(8,128)(2,1)S(1)}, bf16[1024,256]{1,0:T(8,128)(2,1)}, u32[]{:S(2)}) %copy-start.1) | copy-done | bytes 524312
  1.2 0.6 %copy-done = bf16[576,2,1024]{2,1,0:T(2,128)(2,1)S(1)} copy-done((bf16[576,2,1024]{2,1,0:T(2,128)(2,1)S(1)}, bf16[576,2,1024]{2,1,0:T(2,128)(2,1)}, u32[]{:S(2)}) %copy-start) | copy-done | bytes 2359320
  1.8 0.8 %fusion.5.spectrum_ref = bf16[2,576,256]{2,1,0:T(8,128)(2,1)S(1)} fusion(bf16[576,2,1024]{2,1,0:T(2,128)(2,1)S(1)} %copy-done, bf16[1024,256]{1,0:T(8,128)(2,1)S(1)} %table.1), kind=kOutput, calls=%fused_computation.3 | convolution fusion | flops 604274688 | bytes 3473408 | tf_op jit(solution)/shard_map/cws,sj->wcj/dot_general | solution.py:250
  2.6 0.8 %whiten.1 = (bf16[2,16,1152]{2,1,0:T(8,128)(2,1)S(1)}, bf16[2,16,1152]{2,1,0:T(8,128)(2,1)S(1)}, bf16[2,16,1152]{2,1,0:T(8,128)(2,1)S(1)}, bf16[2,16,1152]{2,1,0...) custom-call(bf16[2,576,256]{2,1,0:T(8,128)(2,1)S(1)} %fusion.5.spect, ...), custom_call_target="tpu_custom_call" | custom-call | flops 5898240 | bytes 1769472 | tf_op jit(solution)/shard_map/whiten/pallas_call | solution.py:253
  3.4 6.1 %collective-permute-start = (bf16[2,16,1152]{2,1,0:T(8,128)(2,1)S(1)}, bf16[2,16,1152]{2,1,0:T(8,128)(2,1)S(1)}, u32[]{:S(2)}, u32[]{:S(2)}) collective-permute-start(bf16[2,16,1152]{2,1,0:T(8,128)(2,1)S(1)} %get-tuple-element.13), channel_id=1, source_target_pairs={{0,7},{1,6},{2,5},{3,4},{4,3},{5,2},{6,1},{7,0},{8,15},{9,14},{10,... | collective-permute-start | bytes 221192 | tf_op jit(solution)/shard_map/ppermute | solution.py:218
  9.4 0.5 %collective-permute-start.1 = (bf16[2,16,1152]{2,1,0:T(8,128)(2,1)S(1)}, bf16[2,16,1152]{2,1,0:T(8,128)(2,1)S(1)}, u32[]{:S(2)}, u32[]{:S(2)}) collective-permute-start(bf16[2,16,1152]{2,1,0:T(8,128)(2,1)S(1)} %get-tuple-element.14), channel_id=1, source_target_pairs={{0,1},{1,0},{2,3},{3,2},{4,5},{5,4},{6,7},{7,6},{8,9},{9,8},{10,11... | collective-permute-start | bytes 221192 | tf_op jit(solution)/shard_map/ppermute | solution.py:218
  10.0 0.9 %collective-permute-start.3 = (bf16[2,16,1152]{2,1,0:T(8,128)(2,1)S(1)}, bf16[2,16,1152]{2,1,0:T(8,128)(2,1)S(1)}, u32[]{:S(2)}, u32[]{:S(2)}) collective-permute-start(bf16[2,16,1152]{2,1,0:T(8,128)(2,1)S(1)} %get-tuple-element.16), channel_id=1, source_target_pairs={{0,6},{1,7},{2,4},{3,5},{4,2},{5,3},{6,0},{7,1},{8,14},{9,15},{10,... | collective-permute-start | bytes 221192 | tf_op jit(solution)/shard_map/ppermute | solution.py:218
  10.9 3.5 %collective-permute-start.4 = (bf16[2,16,1152]{2,1,0:T(8,128)(2,1)S(1)}, bf16[2,16,1152]{2,1,0:T(8,128)(2,1)S(1)}, u32[]{:S(2)}, u32[]{:S(2)}) collective-permute-start(bf16[2,16,1152]{2,1,0:T(8,128)(2,1)S(1)} %get-tuple-element.17), channel_id=1, source_target_pairs={{0,5},{1,4},{2,7},{3,6},{4,1},{5,0},{6,3},{7,2},{8,13},{9,12},{10,... | collective-permute-start | bytes 221192 | tf_op jit(solution)/shard_map/ppermute | solution.py:218
  14.4 0.0 collective-permute-done.refs_0_
  14.4 0.3 collective-permute-start.5
  14.7 0.0 collective-permute-done.1.refs_1_
  14.7 3.2 %collective-permute-start.6 = (bf16[2,16,1152]{2,1,0:T(8,128)(2,1)S(1)}, bf16[2,16,1152]{2,1,0:T(8,128)(2,1)S(1)}, u32[]{:S(2)}, u32[]{:S(2)}) collective-permute-start(bf16[2,16,1152]{2,1,0:T(8,128)(2,1)S(1)} %get-tuple-element.19), channel_id=1, source_target_pairs={{0,3},{1,2},{2,1},{3,0},{4,7},{5,6},{6,5},{7,4},{8,11},{9,10},{10,... | collective-permute-start | bytes 221192 | tf_op jit(solution)/shard_map/ppermute | solution.py:218
  17.9 0.0 collective-permute-done.2.refs_2_
  17.9 0.0 collective-permute-start.14
  17.9 0.5 %collective-permute-start.7 = (bf16[2,16,1152]{2,1,0:T(8,128)(2,1)S(1)}, bf16[2,16,1152]{2,1,0:T(8,128)(2,1)S(1)}, u32[]{:S(2)}, u32[]{:S(2)}) collective-permute-start(bf16[2,16,1152]{2,1,0:T(8,128)(2,1)S(1)} %collective-permute-done.refs_0_), channel_id=1, source_target_pairs={{0,8},{8,0},{1,9},{9,1},{2,10},{10,2},{3,11},{11,3},{4,12},{12,4},... | collective-permute-start | bytes 221192 | tf_op jit(solution)/shard_map/ppermute | solution.py:222
  18.4 4.2 %collective-permute-done.4.refs_4_ = bf16[2,16,1152]{2,1,0:T(8,128)(2,1)S(1)} collective-permute-done((bf16[2,16,1152]{2,1,0:T(8,128)(2,1)S(1)}, bf16[2,16,1152]{2,1,0:T(8,128)(2,1)S(1)}, u32[]{:S(2)}, u32[]{:S(2)}) %collective-permute-start.4) | collective-permute-done | bytes 73760 | tf_op jit(solution)/shard_map/ppermute | solution.py:218
  22.6 0.0 collective-permute-start.8
  22.6 0.0 collective-permute-done.5.refs_5_
  22.6 0.5 %collective-permute-start.9 = (bf16[2,16,1152]{2,1,0:T(8,128)(2,1)S(1)}, bf16[2,16,1152]{2,1,0:T(8,128)(2,1)S(1)}, u32[]{:S(2)}, u32[]{:S(2)}) collective-permute-start(bf16[2,16,1152]{2,1,0:T(8,128)(2,1)S(1)} %collective-permute-done.2.refs_2_), channel_id=1, source_target_pairs={{0,8},{8,0},{1,9},{9,1},{2,10},{10,2},{3,11},{11,3},{4,12},{12,4},... | collective-permute-start | bytes 221192 | tf_op jit(solution)/shard_map/ppermute | solution.py:222
  23.2 0.0 collective-permute-done.6.refs_6_
  23.2 0.1 collective-permute-start.10
  23.2 0.0 collective-permute-done.14.refs_15_
  23.2 0.4 %collective-permute-start.11 = (bf16[2,16,1152]{2,1,0:T(8,128)(2,1)S(1)}, bf16[2,16,1152]{2,1,0:T(8,128)(2,1)S(1)}, u32[]{:S(2)}, u32[]{:S(2)}) collective-permute-start(bf16[2,16,1152]{2,1,0:T(8,128)(2,1)S(1)} %collective-permute-done.4.refs_4_), channel_id=1, source_target_pairs={{0,8},{8,0},{1,9},{9,1},{2,10},{10,2},{3,11},{11,3},{4,12},{12,4},... | collective-permute-start | bytes 221192 | tf_op jit(solution)/shard_map/ppermute | solution.py:222
  23.7 0.0 collective-permute-done.7.refs_8_
  23.7 0.1 collective-permute-start.12
  23.7 0.2 collective-permute-done.8.refs_9_
  23.9 0.3 collective-permute-start.13
  24.2 0.2 collective-permute-done.10.refs_11_
  24.4 0.2 collective-permute-done.11.refs_12_
  24.6 0.4 collective-permute-done.12.refs_13_
  24.9 0.2 collective-permute-done.13.refs_14_
  25.2 17.4 %outer_products.1 = bf16[2,16,576,1152]{3,2,1,0:T(8,128)(2,1)} custom-call(bf16[2,16,1152]{2,1,0:T(8,128)(2,1)S(1)} %collective-permute-done.refs_0_, bf16[2,16,1152]{2,1,0:T(8,128)(2,1)S(1)} %collective-permute-done.1.refs_1_, bf16[2,16,1152]{2,1,0:T(8,128)(2,1)S(1)} %collective-permute-done.2.refs_2_, ...), custom_call_target="tpu_custom_call" | custom-call | flops 5435817984 | bytes 42467328 | tf_op jit(solution)/shard_map/outer_products/pallas_call | solution.py:275
  (6 shorter events, 0.0 us)
Async XLA Ops:
  0.0 1.8 %copy-start = (bf16[576,2,1024]{2,1,0:T(2,128)(2,1)S(1)}, bf16[576,2,1024]{2,1,0:T(2,128)(2,1)}, u32[]{:S(2)}) copy-start(bf16[576,2,1024]{2,1,0:T(2,128)(2,1)} %param.2) | copy-start | bytes 7077892
  0.0 1.2 %copy-start.1 = (bf16[1024,256]{1,0:T(8,128)(2,1)S(1)}, bf16[1024,256]{1,0:T(8,128)(2,1)}, u32[]{:S(2)}) copy-start(bf16[1024,256]{1,0:T(8,128)(2,1)} %constant.2.clone.in_ref) | copy-start | bytes 1572868
  3.4 11.0 %collective-permute-start = (bf16[2,16,1152]{2,1,0:T(8,128)(2,1)S(1)}, bf16[2,16,1152]{2,1,0:T(8,128)(2,1)S(1)}, u32[]{:S(2)}, u32[]{:S(2)}) collective-permute-start(bf16[2,16,1152]{2,1,0:T(8,128)(2,1)S(1)} %get-tuple-element.13), channel_id=1, source_target_pairs={{0,7},{1,6},{2,5},{3,4},{4,3},{5,2},{6,1},{7,0},{8,15},{9,14},{10,... | collective-permute-start | bytes 221192 | tf_op jit(solution)/shard_map/ppermute | solution.py:218
  9.4 5.3 %collective-permute-start.1 = (bf16[2,16,1152]{2,1,0:T(8,128)(2,1)S(1)}, bf16[2,16,1152]{2,1,0:T(8,128)(2,1)S(1)}, u32[]{:S(2)}, u32[]{:S(2)}) collective-permute-start(bf16[2,16,1152]{2,1,0:T(8,128)(2,1)S(1)} %get-tuple-element.14), channel_id=1, source_target_pairs={{0,1},{1,0},{2,3},{3,2},{4,5},{5,4},{6,7},{7,6},{8,9},{9,8},{10,11... | collective-permute-start | bytes 221192 | tf_op jit(solution)/shard_map/ppermute | solution.py:218
  10.0 8.0 %collective-permute-start.2 = (bf16[2,16,1152]{2,1,0:T(8,128)(2,1)S(1)}, bf16[2,16,1152]{2,1,0:T(8,128)(2,1)S(1)}, u32[]{:S(2)}, u32[]{:S(2)}) collective-permute-start(bf16[2,16,1152]{2,1,0:T(8,128)(2,1)S(1)} %get-tuple-element.15), channel_id=1, source_target_pairs={{0,2},{1,3},{2,0},{3,1},{4,6},{5,7},{6,4},{7,5},{8,10},{9,11},{10,... | collective-permute-start | bytes 221192 | tf_op jit(solution)/shard_map/ppermute | solution.py:218
  10.0 8.0 %collective-permute-start.3 = (bf16[2,16,1152]{2,1,0:T(8,128)(2,1)S(1)}, bf16[2,16,1152]{2,1,0:T(8,128)(2,1)S(1)}, u32[]{:S(2)}, u32[]{:S(2)}) collective-permute-start(bf16[2,16,1152]{2,1,0:T(8,128)(2,1)S(1)} %get-tuple-element.16), channel_id=1, source_target_pairs={{0,6},{1,7},{2,4},{3,5},{4,2},{5,3},{6,0},{7,1},{8,14},{9,15},{10,... | collective-permute-start | bytes 221192 | tf_op jit(solution)/shard_map/ppermute | solution.py:218
  10.9 11.8 %collective-permute-start.4 = (bf16[2,16,1152]{2,1,0:T(8,128)(2,1)S(1)}, bf16[2,16,1152]{2,1,0:T(8,128)(2,1)S(1)}, u32[]{:S(2)}, u32[]{:S(2)}) collective-permute-start(bf16[2,16,1152]{2,1,0:T(8,128)(2,1)S(1)} %get-tuple-element.17), channel_id=1, source_target_pairs={{0,5},{1,4},{2,7},{3,6},{4,1},{5,0},{6,3},{7,2},{8,13},{9,12},{10,... | collective-permute-start | bytes 221192 | tf_op jit(solution)/shard_map/ppermute | solution.py:218
  14.4 8.2 %collective-permute-start.5 = (bf16[2,16,1152]{2,1,0:T(8,128)(2,1)S(1)}, bf16[2,16,1152]{2,1,0:T(8,128)(2,1)S(1)}, u32[]{:S(2)}, u32[]{:S(2)}) collective-permute-start(bf16[2,16,1152]{2,1,0:T(8,128)(2,1)S(1)} %get-tuple-element.18), channel_id=1, source_target_pairs={{0,4},{1,5},{2,6},{3,7},{4,0},{5,1},{6,2},{7,3},{8,12},{9,13},{10,... | collective-permute-start | bytes 221192 | tf_op jit(solution)/shard_map/ppermute | solution.py:218
  14.7 8.4 %collective-permute-start.6 = (bf16[2,16,1152]{2,1,0:T(8,128)(2,1)S(1)}, bf16[2,16,1152]{2,1,0:T(8,128)(2,1)S(1)}, u32[]{:S(2)}, u32[]{:S(2)}) collective-permute-start(bf16[2,16,1152]{2,1,0:T(8,128)(2,1)S(1)} %get-tuple-element.19), channel_id=1, source_target_pairs={{0,3},{1,2},{2,1},{3,0},{4,7},{5,6},{6,5},{7,4},{8,11},{9,10},{10,... | collective-permute-start | bytes 221192 | tf_op jit(solution)/shard_map/ppermute | solution.py:218
  17.9 5.3 %collective-permute-start.14 = (bf16[2,16,1152]{2,1,0:T(8,128)(2,1)S(1)}, bf16[2,16,1152]{2,1,0:T(8,128)(2,1)S(1)}, u32[]{:S(2)}, u32[]{:S(2)}) collective-permute-start(bf16[2,16,1152]{2,1,0:T(8,128)(2,1)S(1)} %get-tuple-element.20.refs_7_), channel_id=1, source_target_pairs={{0,8},{8,0},{1,9},{9,1},{2,10},{10,2},{3,11},{11,3},{4,12},{12,4},... | collective-permute-start | bytes 221192 | tf_op jit(solution)/shard_map/ppermute | solution.py:222
  17.9 5.7 %collective-permute-start.7 = (bf16[2,16,1152]{2,1,0:T(8,128)(2,1)S(1)}, bf16[2,16,1152]{2,1,0:T(8,128)(2,1)S(1)}, u32[]{:S(2)}, u32[]{:S(2)}) collective-permute-start(bf16[2,16,1152]{2,1,0:T(8,128)(2,1)S(1)} %collective-permute-done.refs_0_), channel_id=1, source_target_pairs={{0,8},{8,0},{1,9},{9,1},{2,10},{10,2},{3,11},{11,3},{4,12},{12,4},... | collective-permute-start | bytes 221192 | tf_op jit(solution)/shard_map/ppermute | solution.py:222
  22.6 1.3 %collective-permute-start.8 = (bf16[2,16,1152]{2,1,0:T(8,128)(2,1)S(1)}, bf16[2,16,1152]{2,1,0:T(8,128)(2,1)S(1)}, u32[]{:S(2)}, u32[]{:S(2)}) collective-permute-start(bf16[2,16,1152]{2,1,0:T(8,128)(2,1)S(1)} %collective-permute-done.1.refs_1_), channel_id=1, source_target_pairs={{0,8},{8,0},{1,9},{9,1},{2,10},{10,2},{3,11},{11,3},{4,12},{12,4},... | collective-permute-start | bytes 221192 | tf_op jit(solution)/shard_map/ppermute | solution.py:222
  22.6 1.5 %collective-permute-start.9 = (bf16[2,16,1152]{2,1,0:T(8,128)(2,1)S(1)}, bf16[2,16,1152]{2,1,0:T(8,128)(2,1)S(1)}, u32[]{:S(2)}, u32[]{:S(2)}) collective-permute-start(bf16[2,16,1152]{2,1,0:T(8,128)(2,1)S(1)} %collective-permute-done.2.refs_2_), channel_id=1, source_target_pairs={{0,8},{8,0},{1,9},{9,1},{2,10},{10,2},{3,11},{11,3},{4,12},{12,4},... | collective-permute-start | bytes 221192 | tf_op jit(solution)/shard_map/ppermute | solution.py:222
  23.2 1.3 %collective-permute-start.10 = (bf16[2,16,1152]{2,1,0:T(8,128)(2,1)S(1)}, bf16[2,16,1152]{2,1,0:T(8,128)(2,1)S(1)}, u32[]{:S(2)}, u32[]{:S(2)}) collective-permute-start(bf16[2,16,1152]{2,1,0:T(8,128)(2,1)S(1)} %collective-permute-done.3.refs_3_), channel_id=1, source_target_pairs={{0,8},{8,0},{1,9},{9,1},{2,10},{10,2},{3,11},{11,3},{4,12},{12,4},... | collective-permute-start | bytes 221192 | tf_op jit(solution)/shard_map/ppermute | solution.py:222
  23.2 1.4 %collective-permute-start.11 = (bf16[2,16,1152]{2,1,0:T(8,128)(2,1)S(1)}, bf16[2,16,1152]{2,1,0:T(8,128)(2,1)S(1)}, u32[]{:S(2)}, u32[]{:S(2)}) collective-permute-start(bf16[2,16,1152]{2,1,0:T(8,128)(2,1)S(1)} %collective-permute-done.4.refs_4_), channel_id=1, source_target_pairs={{0,8},{8,0},{1,9},{9,1},{2,10},{10,2},{3,11},{11,3},{4,12},{12,4},... | collective-permute-start | bytes 221192 | tf_op jit(solution)/shard_map/ppermute | solution.py:222
  23.7 1.3 %collective-permute-start.12 = (bf16[2,16,1152]{2,1,0:T(8,128)(2,1)S(1)}, bf16[2,16,1152]{2,1,0:T(8,128)(2,1)S(1)}, u32[]{:S(2)}, u32[]{:S(2)}) collective-permute-start(bf16[2,16,1152]{2,1,0:T(8,128)(2,1)S(1)} %collective-permute-done.5.refs_5_), channel_id=1, source_target_pairs={{0,8},{8,0},{1,9},{9,1},{2,10},{10,2},{3,11},{11,3},{4,12},{12,4},... | collective-permute-start | bytes 221192 | tf_op jit(solution)/shard_map/ppermute | solution.py:222
  23.9 1.3 %collective-permute-start.13 = (bf16[2,16,1152]{2,1,0:T(8,128)(2,1)S(1)}, bf16[2,16,1152]{2,1,0:T(8,128)(2,1)S(1)}, u32[]{:S(2)}, u32[]{:S(2)}) collective-permute-start(bf16[2,16,1152]{2,1,0:T(8,128)(2,1)S(1)} %collective-permute-done.6.refs_6_), channel_id=1, source_target_pairs={{0,8},{8,0},{1,9},{9,1},{2,10},{10,2},{3,11},{11,3},{4,12},{12,4},... | collective-permute-start | bytes 221192 | tf_op jit(solution)/shard_map/ppermute | solution.py:222

commit v13 on v12

--- a/solution.py
+++ b/solution.py
@@ -101,27 +101,30 @@
     half = LANES // 2
     channels = out_ref.shape[2]
     full = channels // LANES
-    step = pl.program_id(1)
-    now = pl.program_id(0) * bins + step
-    steps = pl.num_programs(0) * bins
-    depth_of_slots, cuts = sems.shape[:2]
+    which, chosen_set = pl.program_id(0), pl.program_id(1)
+    now = which * sets + chosen_set
+    steps = pl.num_programs(0) * sets
+    within = bins // sets
+    cuts = sems.shape[2]
     size = channels // cuts
 
-    def copy(when, cut, part):
-        slot = lax.rem(when, depth_of_slots)
+    def copy(when, bin_of_set, cut, part):
+        side = lax.rem(when, 2)
         at = pl.ds(cut * size, size)
         return pltpu.make_async_copy(
-            slots.at[slot, part, at], out_ref.at[part, when, at], sems.at[slot, cut, part]
+            slots.at[side, bin_of_set, part, at],
+            out_ref.at[part, when * within + bin_of_set, at],
+            sems.at[side, bin_of_set, cut, part],
         )
 
     def wait_for(when):
-        for cut in range(cuts):
-            for part in range(2):
-                copy(when, cut, part).wait()
+        for bin_of_set in range(within):
+            for cut in range(cuts):
+                for part in range(2):
+                    copy(when, bin_of_set, cut, part).wait()
 
     def prepare(q):
         me = lax.axis_index("chan")
-        which = pl.program_id(0)
         own = jnp.concatenate([ref[which].astype(jnp.float32) for ref in own_refs])
         other = jnp.concatenate([ref[which].astype(jnp.float32) for ref in other_refs])
         rows = own.shape[0]
@@ -166,47 +169,45 @@
             left[q, j * LANES : j * LANES + kept] = jnp.concatenate(pieces).T[:kept]
 
     for q in range(sets):
-        pl.when(step == q * (bins // sets))(functools.partial(prepare, q))
+        pl.when(chosen_set == q)(functools.partial(prepare, q))
+
+    @pl.when(now >= 2)
+    def _():
+        wait_for(now - 2)
 
     depth = left.shape[2]
-    within = bins // sets
-    lane = lax.broadcasted_iota(jnp.int32, (1, depth), 1)
-    taken = (lane & (within - 1)) == (step & (within - 1))
-    chosen = jnp.where(taken, left[step // within], 0.0).astype(jnp.bfloat16)
-    weights = right.at[step // within]
-
-    @pl.when(now >= depth_of_slots)
-    def _():
-        wait_for(now - depth_of_slots)
-
-    slot = lax.rem(now, depth_of_slots)
-
+    lane = lax.broadcasted_iota(jnp.int32, (1, depth), 1) & (within - 1)
+    weights = right.at[chosen_set]
+    side = lax.rem(now, 2)
     whole = 2 * channels // (2 * LANES) * (2 * LANES)
     starts = [0, whole, 4 * channels - whole, 4 * channels]
     left_over = 2 * channels - whole
 
-    def multiply(first, last):
-        return jnp.dot(
-            chosen, weights[:, first:last], preferred_element_type=jnp.float32
-        ).astype(jnp.bfloat16)
-
-    def send(part):
-        for cut in range(cuts):
-            copy(now, cut, part).start(priority=cut)
-
-    slots[slot, 0, :, :whole] = multiply(*starts[:2])
-    if left_over:
-        both = multiply(*starts[1:3])
-        slots[slot, 0, :, whole:] = both[:, :left_over]
-        slots[slot, 1, :, :left_over] = both[:, left_over:]
-    send(0)
-    slots[slot, 1, :, left_over:] = multiply(*starts[2:])
-    send(1)
+    for k in range(within):
+        chosen = jnp.where(lane == k, left[chosen_set], 0.0).astype(jnp.bfloat16)
+
+        def multiply(first, last):
+            return jnp.dot(
+                chosen, weights[:, first:last], preferred_element_type=jnp.float32
+            ).astype(jnp.bfloat16)
+
+        def send(part):
+            for cut in range(cuts):
+                copy(now, k, cut, part).start()
+
+        slots[side, k, 0, :, :whole] = multiply(*starts[:2])
+        if left_over:
+            both = multiply(*starts[1:3])
+            slots[side, k, 0, :, whole:] = both[:, :left_over]
+            slots[side, k, 1, :, :left_over] = both[:, left_over:]
+        send(0)
+        slots[side, k, 1, :, left_over:] = multiply(*starts[2:])
+        send(1)
 
     @pl.when(now == steps - 1)
     def _():
-        for back in reversed(range(depth_of_slots)):
-            wait_for(now - back)
+        wait_for(now - 1)
+        wait_for(now)
 
 
 def copy_kernel(in_ref, out_ref):
@@ -277,16 +278,16 @@
             out_shape=jax.ShapeDtypeStruct(
                 (2, local_bins, local_channels, 2 * local_channels), jnp.bfloat16
             ),
-            grid=(groups, bins),
+            grid=(groups, sets),
             in_specs=[vmem] * (2 * pieces),
             out_specs=memory,
             scratch_shapes=[
                 pltpu.VMEM((sets, depth, 4 * local_channels), jnp.bfloat16),
                 pltpu.VMEM((sets, local_channels, depth), jnp.float32),
-                pltpu.VMEM((3, 2, local_channels, 2 * local_channels), jnp.bfloat16),
-                pltpu.SemaphoreType.DMA((3, 2, 2)),
+                pltpu.VMEM((2, bins // sets, 2, local_channels, 2 * local_channels), jnp.bfloat16),
+                pltpu.SemaphoreType.DMA((2, bins // sets, 2, 2)),
             ],
-            compiler_params=pltpu.CompilerParams(vmem_limit_bytes=32 * MIB),
+            compiler_params=pltpu.CompilerParams(vmem_limit_bytes=48 * MIB),
             cost_estimate=pl.CostEstimate(
                 flops=8 * local_bins * depth * local_channels * local_channels,
                 bytes_accessed=8 * local_bins * local_channels * local_channels,

time: 42.7 us -> 41.4 us (0.970)
  Pallas kernels: 18.2 us -> 16.8 us
    pallas_call x1, Pallas kernels: 17.4 us -> 16.1 us  [local(): pl.pallas_call(functools.partial(outer_kernel, bins, sets, 1.0 / windows)...]
where the time goes in v13:
time: 41.4 us; the launch traced here: 41.2 us
  Pallas kernels  16.8 us (41%)
  starting transfers between devices  16.4 us (40%)
  waiting for transfers between devices  5.36 us (13%)
  local copies, waits for them, and re-layouts  1.78 us (4%)
  matrix products  0.79 us (2%)
    pallas_call x1, Pallas kernels, local(): pl.pallas_call(functools.partial(outer_kernel, bins, sets, 1.0 / windows)...  16.1 us
    ppermute x7, starting transfers between devices, exchange(): return lax.ppermute(value, 'freq', pairs) if mask else value  14.5 us
    ppermute x7, waiting for transfers between devices, exchange(): return lax.ppermute(value, 'freq', pairs) if mask else value  4.22 us
    ppermute x8, starting transfers between devices, swap(): return lax.ppermute(value, 'chan', [(0, 1), (1, 0)])  1.88 us
    unnamed x4, local copies, waits for them, and re-layouts  1.78 us
    ppermute x8, waiting for transfers between devices, swap(): return lax.ppermute(value, 'chan', [(0, 1), (1, 0)])  1.14 us
  transfers between devices with their start and end apart: 15, of which 6 were waited for; matrix products, arithmetic and copies ran while one was open for 0% of the time, Pallas kernels for 0%

profile of v13, /device:TPU:0, one launch (start us, length us, event | category | flops | bytes accessed | tf_op | source)
XLA Modules:
  0.0 41.2 jit_solution(18076706618571647659)
XLA Ops:
  0.0 1.2 %copy-done.1 = bf16[1024,256]{1,0:T(8,128)(2,1)S(1)} copy-done((bf16[1024,256]{1,0:T(8,128)(2,1)S(1)}, bf16[1024,256]{1,0:T(8,128)(2,1)}, u32[]{:S(2)}) %copy-start.1) | copy-done | bytes 524312
  1.2 0.6 %copy-done = bf16[576,2,1024]{2,1,0:T(2,128)(2,1)S(1)} copy-done((bf16[576,2,1024]{2,1,0:T(2,128)(2,1)S(1)}, bf16[576,2,1024]{2,1,0:T(2,128)(2,1)}, u32[]{:S(2)}) %copy-start) | copy-done | bytes 2359320
  1.8 0.8 %fusion.5.spectrum_ref = bf16[2,576,256]{2,1,0:T(8,128)(2,1)S(1)} fusion(bf16[576,2,1024]{2,1,0:T(2,128)(2,1)S(1)} %copy-done, bf16[1024,256]{1,0:T(8,128)(2,1)S(1)} %table.1), kind=kOutput, calls=%fused_computation.3 | convolution fusion | flops 604274688 | bytes 3473408 | tf_op jit(solution)/shard_map/cws,sj->wcj/dot_general | solution.py:251
  2.6 0.8 %whiten.1 = (bf16[2,16,1152]{2,1,0:T(8,128)(2,1)S(1)}, bf16[2,16,1152]{2,1,0:T(8,128)(2,1)S(1)}, bf16[2,16,1152]{2,1,0:T(8,128)(2,1)S(1)}, bf16[2,16,1152]{2,1,0...) custom-call(bf16[2,576,256]{2,1,0:T(8,128)(2,1)S(1)} %fusion.5.spect, ...), custom_call_target="tpu_custom_call" | custom-call | flops 5898240 | bytes 1769472 | tf_op jit(solution)/shard_map/whiten/pallas_call | solution.py:254
  3.4 6.1 %collective-permute-start = (bf16[2,16,1152]{2,1,0:T(8,128)(2,1)S(1)}, bf16[2,16,1152]{2,1,0:T(8,128)(2,1)S(1)}, u32[]{:S(2)}, u32[]{:S(2)}) collective-permute-start(bf16[2,16,1152]{2,1,0:T(8,128)(2,1)S(1)} %get-tuple-element.13), channel_id=1, source_target_pairs={{0,7},{1,6},{2,5},{3,4},{4,3},{5,2},{6,1},{7,0},{8,15},{9,14},{10,... | collective-permute-start | bytes 221192 | tf_op jit(solution)/shard_map/ppermute | solution.py:219
  9.4 0.5 %collective-permute-start.1 = (bf16[2,16,1152]{2,1,0:T(8,128)(2,1)S(1)}, bf16[2,16,1152]{2,1,0:T(8,128)(2,1)S(1)}, u32[]{:S(2)}, u32[]{:S(2)}) collective-permute-start(bf16[2,16,1152]{2,1,0:T(8,128)(2,1)S(1)} %get-tuple-element.14), channel_id=1, source_target_pairs={{0,1},{1,0},{2,3},{3,2},{4,5},{5,4},{6,7},{7,6},{8,9},{9,8},{10,11... | collective-permute-start | bytes 221192 | tf_op jit(solution)/shard_map/ppermute | solution.py:219
  10.0 0.0 collective-permute-start.2
  10.0 0.9 %collective-permute-start.3 = (bf16[2,16,1152]{2,1,0:T(8,128)(2,1)S(1)}, bf16[2,16,1152]{2,1,0:T(8,128)(2,1)S(1)}, u32[]{:S(2)}, u32[]{:S(2)}) collective-permute-start(bf16[2,16,1152]{2,1,0:T(8,128)(2,1)S(1)} %get-tuple-element.16), channel_id=1, source_target_pairs={{0,6},{1,7},{2,4},{3,5},{4,2},{5,3},{6,0},{7,1},{8,14},{9,15},{10,... | collective-permute-start | bytes 221192 | tf_op jit(solution)/shard_map/ppermute | solution.py:219
  10.9 3.5 %collective-permute-start.4 = (bf16[2,16,1152]{2,1,0:T(8,128)(2,1)S(1)}, bf16[2,16,1152]{2,1,0:T(8,128)(2,1)S(1)}, u32[]{:S(2)}, u32[]{:S(2)}) collective-permute-start(bf16[2,16,1152]{2,1,0:T(8,128)(2,1)S(1)} %get-tuple-element.17), channel_id=1, source_target_pairs={{0,5},{1,4},{2,7},{3,6},{4,1},{5,0},{6,3},{7,2},{8,13},{9,12},{10,... | collective-permute-start | bytes 221192 | tf_op jit(solution)/shard_map/ppermute | solution.py:219
  14.4 0.0 collective-permute-done.refs_0_
  14.4 0.3 collective-permute-start.5
  14.7 0.0 collective-permute-done.1.refs_1_
  14.7 3.2 %collective-permute-start.6 = (bf16[2,16,1152]{2,1,0:T(8,128)(2,1)S(1)}, bf16[2,16,1152]{2,1,0:T(8,128)(2,1)S(1)}, u32[]{:S(2)}, u32[]{:S(2)}) collective-permute-start(bf16[2,16,1152]{2,1,0:T(8,128)(2,1)S(1)} %get-tuple-element.19), channel_id=1, source_target_pairs={{0,3},{1,2},{2,1},{3,0},{4,7},{5,6},{6,5},{7,4},{8,11},{9,10},{10,... | collective-permute-start | bytes 221192 | tf_op jit(solution)/shard_map/ppermute | solution.py:219
  17.9 0.0 collective-permute-done.2.refs_2_
  17.9 0.5 %collective-permute-start.7 = (bf16[2,16,1152]{2,1,0:T(8,128)(2,1)S(1)}, bf16[2,16,1152]{2,1,0:T(8,128)(2,1)S(1)}, u32[]{:S(2)}, u32[]{:S(2)}) collective-permute-start(bf16[2,16,1152]{2,1,0:T(8,128)(2,1)S(1)} %collective-permute-done.refs_0_), channel_id=1, source_target_pairs={{0,8},{8,0},{1,9},{9,1},{2,10},{10,2},{3,11},{11,3},{4,12},{12,4},... | collective-permute-start | bytes 221192 | tf_op jit(solution)/shard_map/ppermute | solution.py:223
  18.4 4.2 %collective-permute-done.4.refs_4_ = bf16[2,16,1152]{2,1,0:T(8,128)(2,1)S(1)} collective-permute-done((bf16[2,16,1152]{2,1,0:T(8,128)(2,1)S(1)}, bf16[2,16,1152]{2,1,0:T(8,128)(2,1)S(1)}, u32[]{:S(2)}, u32[]{:S(2)}) %collective-permute-start.4) | collective-permute-done | bytes 73760 | tf_op jit(solution)/shard_map/ppermute | solution.py:219
  22.6 0.0 collective-permute-start.8
  22.6 0.0 collective-permute-done.5.refs_5_
  22.6 0.5 %collective-permute-start.9 = (bf16[2,16,1152]{2,1,0:T(8,128)(2,1)S(1)}, bf16[2,16,1152]{2,1,0:T(8,128)(2,1)S(1)}, u32[]{:S(2)}, u32[]{:S(2)}) collective-permute-start(bf16[2,16,1152]{2,1,0:T(8,128)(2,1)S(1)} %collective-permute-done.2.refs_2_), channel_id=1, source_target_pairs={{0,8},{8,0},{1,9},{9,1},{2,10},{10,2},{3,11},{11,3},{4,12},{12,4},... | collective-permute-start | bytes 221192 | tf_op jit(solution)/shard_map/ppermute | solution.py:223
  23.2 0.1 collective-permute-start.10
  23.2 0.0 collective-permute-done.14.refs_15_
  23.2 0.4 %collective-permute-start.11 = (bf16[2,16,1152]{2,1,0:T(8,128)(2,1)S(1)}, bf16[2,16,1152]{2,1,0:T(8,128)(2,1)S(1)}, u32[]{:S(2)}, u32[]{:S(2)}) collective-permute-start(bf16[2,16,1152]{2,1,0:T(8,128)(2,1)S(1)} %collective-permute-done.4.refs_4_), channel_id=1, source_target_pairs={{0,8},{8,0},{1,9},{9,1},{2,10},{10,2},{3,11},{11,3},{4,12},{12,4},... | collective-permute-start | bytes 221192 | tf_op jit(solution)/shard_map/ppermute | solution.py:223
  23.7 0.0 collective-permute-done.7.refs_8_
  23.7 0.1 collective-permute-start.12
  23.7 0.2 collective-permute-done.8.refs_9_
  23.9 0.3 collective-permute-start.13
  24.2 0.0 collective-permute-done.9.refs_10_
  24.2 0.2 collective-permute-done.10.refs_11_
  24.4 0.2 collective-permute-done.11.refs_12_
  24.6 0.4 collective-permute-done.12.refs_13_
  24.9 0.2 collective-permute-done.13.refs_14_
  25.2 16.1 %outer_products.1 = bf16[2,16,576,1152]{3,2,1,0:T(8,128)(2,1)} custom-call(bf16[2,16,1152]{2,1,0:T(8,128)(2,1)S(1)} %collective-permute-done.refs_0_, bf16[2,16,1152]{2,1,0:T(8,128)(2,1)S(1)} %collective-permute-done.1.refs_1_, bf16[2,16,1152]{2,1,0:T(8,128)(2,1)S(1)} %collective-permute-done.2.refs_2_, ...), custom_call_target="tpu_custom_call" | custom-call | flops 5435817984 | bytes 42467328 | tf_op jit(solution)/shard_map/outer_products/pallas_call | solution.py:276
  (6 shorter events, 0.0 us)
Async XLA Ops:
  0.0 1.8 %copy-start = (bf16[576,2,1024]{2,1,0:T(2,128)(2,1)S(1)}, bf16[576,2,1024]{2,1,0:T(2,128)(2,1)}, u32[]{:S(2)}) copy-start(bf16[576,2,1024]{2,1,0:T(2,128)(2,1)} %param.2) | copy-start | bytes 7077892
  0.0 1.2 %copy-start.1 = (bf16[1024,256]{1,0:T(8,128)(2,1)S(1)}, bf16[1024,256]{1,0:T(8,128)(2,1)}, u32[]{:S(2)}) copy-start(bf16[1024,256]{1,0:T(8,128)(2,1)} %constant.2.clone.in_ref) | copy-start | bytes 1572868
  3.4 11.0 %collective-permute-start = (bf16[2,16,1152]{2,1,0:T(8,128)(2,1)S(1)}, bf16[2,16,1152]{2,1,0:T(8,128)(2,1)S(1)}, u32[]{:S(2)}, u32[]{:S(2)}) collective-permute-start(bf16[2,16,1152]{2,1,0:T(8,128)(2,1)S(1)} %get-tuple-element.13), channel_id=1, source_target_pairs={{0,7},{1,6},{2,5},{3,4},{4,3},{5,2},{6,1},{7,0},{8,15},{9,14},{10,... | collective-permute-start | bytes 221192 | tf_op jit(solution)/shard_map/ppermute | solution.py:219
  9.4 5.3 %collective-permute-start.1 = (bf16[2,16,1152]{2,1,0:T(8,128)(2,1)S(1)}, bf16[2,16,1152]{2,1,0:T(8,128)(2,1)S(1)}, u32[]{:S(2)}, u32[]{:S(2)}) collective-permute-start(bf16[2,16,1152]{2,1,0:T(8,128)(2,1)S(1)} %get-tuple-element.14), channel_id=1, source_target_pairs={{0,1},{1,0},{2,3},{3,2},{4,5},{5,4},{6,7},{7,6},{8,9},{9,8},{10,11... | collective-permute-start | bytes 221192 | tf_op jit(solution)/shard_map/ppermute | solution.py:219
  10.0 8.0 %collective-permute-start.2 = (bf16[2,16,1152]{2,1,0:T(8,128)(2,1)S(1)}, bf16[2,16,1152]{2,1,0:T(8,128)(2,1)S(1)}, u32[]{:S(2)}, u32[]{:S(2)}) collective-permute-start(bf16[2,16,1152]{2,1,0:T(8,128)(2,1)S(1)} %get-tuple-element.15), channel_id=1, source_target_pairs={{0,2},{1,3},{2,0},{3,1},{4,6},{5,7},{6,4},{7,5},{8,10},{9,11},{10,... | collective-permute-start | bytes 221192 | tf_op jit(solution)/shard_map/ppermute | solution.py:219
  10.0 8.0 %collective-permute-start.3 = (bf16[2,16,1152]{2,1,0:T(8,128)(2,1)S(1)}, bf16[2,16,1152]{2,1,0:T(8,128)(2,1)S(1)}, u32[]{:S(2)}, u32[]{:S(2)}) collective-permute-start(bf16[2,16,1152]{2,1,0:T(8,128)(2,1)S(1)} %get-tuple-element.16), channel_id=1, source_target_pairs={{0,6},{1,7},{2,4},{3,5},{4,2},{5,3},{6,0},{7,1},{8,14},{9,15},{10,... | collective-permute-start | bytes 221192 | tf_op jit(solution)/shard_map/ppermute | solution.py:219
  10.9 11.8 %collective-permute-start.4 = (bf16[2,16,1152]{2,1,0:T(8,128)(2,1)S(1)}, bf16[2,16,1152]{2,1,0:T(8,128)(2,1)S(1)}, u32[]{:S(2)}, u32[]{:S(2)}) collective-permute-start(bf16[2,16,1152]{2,1,0:T(8,128)(2,1)S(1)} %get-tuple-element.17), channel_id=1, source_target_pairs={{0,5},{1,4},{2,7},{3,6},{4,1},{5,0},{6,3},{7,2},{8,13},{9,12},{10,... | collective-permute-start | bytes 221192 | tf_op jit(solution)/shard_map/ppermute | solution.py:219
  14.4 8.2 %collective-permute-start.5 = (bf16[2,16,1152]{2,1,0:T(8,128)(2,1)S(1)}, bf16[2,16,1152]{2,1,0:T(8,128)(2,1)S(1)}, u32[]{:S(2)}, u32[]{:S(2)}) collective-permute-start(bf16[2,16,1152]{2,1,0:T(8,128)(2,1)S(1)} %get-tuple-element.18), channel_id=1, source_target_pairs={{0,4},{1,5},{2,6},{3,7},{4,0},{5,1},{6,2},{7,3},{8,12},{9,13},{10,... | collective-permute-start | bytes 221192 | tf_op jit(solution)/shard_map/ppermute | solution.py:219
  14.7 8.4 %collective-permute-start.6 = (bf16[2,16,1152]{2,1,0:T(8,128)(2,1)S(1)}, bf16[2,16,1152]{2,1,0:T(8,128)(2,1)S(1)}, u32[]{:S(2)}, u32[]{:S(2)}) collective-permute-start(bf16[2,16,1152]{2,1,0:T(8,128)(2,1)S(1)} %get-tuple-element.19), channel_id=1, source_target_pairs={{0,3},{1,2},{2,1},{3,0},{4,7},{5,6},{6,5},{7,4},{8,11},{9,10},{10,... | collective-permute-start | bytes 221192 | tf_op jit(solution)/shard_map/ppermute | solution.py:219
  17.9 5.3 %collective-permute-start.14 = (bf16[2,16,1152]{2,1,0:T(8,128)(2,1)S(1)}, bf16[2,16,1152]{2,1,0:T(8,128)(2,1)S(1)}, u32[]{:S(2)}, u32[]{:S(2)}) collective-permute-start(bf16[2,16,1152]{2,1,0:T(8,128)(2,1)S(1)} %get-tuple-element.20.refs_7_), channel_id=1, source_target_pairs={{0,8},{8,0},{1,9},{9,1},{2,10},{10,2},{3,11},{11,3},{4,12},{12,4},... | collective-permute-start | bytes 221192 | tf_op jit(solution)/shard_map/ppermute | solution.py:223
  17.9 5.7 %collective-permute-start.7 = (bf16[2,16,1152]{2,1,0:T(8,128)(2,1)S(1)}, bf16[2,16,1152]{2,1,0:T(8,128)(2,1)S(1)}, u32[]{:S(2)}, u32[]{:S(2)}) collective-permute-start(bf16[2,16,1152]{2,1,0:T(8,128)(2,1)S(1)} %collective-permute-done.refs_0_), channel_id=1, source_target_pairs={{0,8},{8,0},{1,9},{9,1},{2,10},{10,2},{3,11},{11,3},{4,12},{12,4},... | collective-permute-start | bytes 221192 | tf_op jit(solution)/shard_map/ppermute | solution.py:223
  22.6 1.3 %collective-permute-start.8 = (bf16[2,16,1152]{2,1,0:T(8,128)(2,1)S(1)}, bf16[2,16,1152]{2,1,0:T(8,128)(2,1)S(1)}, u32[]{:S(2)}, u32[]{:S(2)}) collective-permute-start(bf16[2,16,1152]{2,1,0:T(8,128)(2,1)S(1)} %collective-permute-done.1.refs_1_), channel_id=1, source_target_pairs={{0,8},{8,0},{1,9},{9,1},{2,10},{10,2},{3,11},{11,3},{4,12},{12,4},... | collective-permute-start | bytes 221192 | tf_op jit(solution)/shard_map/ppermute | solution.py:223
  22.6 1.5 %collective-permute-start.9 = (bf16[2,16,1152]{2,1,0:T(8,128)(2,1)S(1)}, bf16[2,16,1152]{2,1,0:T(8,128)(2,1)S(1)}, u32[]{:S(2)}, u32[]{:S(2)}) collective-permute-start(bf16[2,16,1152]{2,1,0:T(8,128)(2,1)S(1)} %collective-permute-done.2.refs_2_), channel_id=1, source_target_pairs={{0,8},{8,0},{1,9},{9,1},{2,10},{10,2},{3,11},{11,3},{4,12},{12,4},... | collective-permute-start | bytes 221192 | tf_op jit(solution)/shard_map/ppermute | solution.py:223
  23.2 1.3 %collective-permute-start.10 = (bf16[2,16,1152]{2,1,0:T(8,128)(2,1)S(1)}, bf16[2,16,1152]{2,1,0:T(8,128)(2,1)S(1)}, u32[]{:S(2)}, u32[]{:S(2)}) collective-permute-start(bf16[2,16,1152]{2,1,0:T(8,128)(2,1)S(1)} %collective-permute-done.3.refs_3_), channel_id=1, source_target_pairs={{0,8},{8,0},{1,9},{9,1},{2,10},{10,2},{3,11},{11,3},{4,12},{12,4},... | collective-permute-start | bytes 221192 | tf_op jit(solution)/shard_map/ppermute | solution.py:223
  23.2 1.4 %collective-permute-start.11 = (bf16[2,16,1152]{2,1,0:T(8,128)(2,1)S(1)}, bf16[2,16,1152]{2,1,0:T(8,128)(2,1)S(1)}, u32[]{:S(2)}, u32[]{:S(2)}) collective-permute-start(bf16[2,16,1152]{2,1,0:T(8,128)(2,1)S(1)} %collective-permute-done.4.refs_4_), channel_id=1, source_target_pairs={{0,8},{8,0},{1,9},{9,1},{2,10},{10,2},{3,11},{11,3},{4,12},{12,4},... | collective-permute-start | bytes 221192 | tf_op jit(solution)/shard_map/ppermute | solution.py:223
  23.7 1.3 %collective-permute-start.12 = (bf16[2,16,1152]{2,1,0:T(8,128)(2,1)S(1)}, bf16[2,16,1152]{2,1,0:T(8,128)(2,1)S(1)}, u32[]{:S(2)}, u32[]{:S(2)}) collective-permute-start(bf16[2,16,1152]{2,1,0:T(8,128)(2,1)S(1)} %collective-permute-done.5.refs_5_), channel_id=1, source_target_pairs={{0,8},{8,0},{1,9},{9,1},{2,10},{10,2},{3,11},{11,3},{4,12},{12,4},... | collective-permute-start | bytes 221192 | tf_op jit(solution)/shard_map/ppermute | solution.py:223
  23.9 1.3 %collective-permute-start.13 = (bf16[2,16,1152]{2,1,0:T(8,128)(2,1)S(1)}, bf16[2,16,1152]{2,1,0:T(8,128)(2,1)S(1)}, u32[]{:S(2)}, u32[]{:S(2)}) collective-permute-start(bf16[2,16,1152]{2,1,0:T(8,128)(2,1)S(1)} %collective-permute-done.6.refs_6_), channel_id=1, source_target_pairs={{0,8},{8,0},{1,9},{9,1},{2,10},{10,2},{3,11},{11,3},{4,12},{12,4},... | collective-permute-start | bytes 221192 | tf_op jit(solution)/shard_map/ppermute | solution.py:223

commit v14 on v13

--- a/solution.py
+++ b/solution.py
@@ -75,23 +75,31 @@
 
 
 def rows_of_set(tile, bins, sets, q):
+    if sets == 1:
+        return tile
     rows, lanes = tile.shape
-    if sets == 1:
-        first_part = (lax.broadcasted_iota(jnp.int32, (rows, 1), 0) // bins) % 2 == 0
-        rotated = jnp.where(
-            first_part, -pltpu.roll(tile, rows - bins, axis=0), pltpu.roll(tile, bins, axis=0)
-        )
-        return tile, rotated
     parts = tile.reshape(rows // (2 * bins), 2, bins, lanes)
     real, imag = parts[:, 0], parts[:, 1]
     within = bins // sets
     low = lax.broadcasted_iota(jnp.int32, real.shape, 1) < within
-    turned_real, turned_imag = (pltpu.roll(part, within, axis=1) for part in (real, imag))
     if q == 0:
-        found = jnp.where(low, real, turned_imag), jnp.where(low, -imag, turned_real)
+        found = jnp.where(low, real, pltpu.roll(imag, within, axis=1))
     else:
-        found = jnp.where(low, turned_real, imag), jnp.where(low, -turned_imag, real)
-    return tuple(part.reshape(rows // sets, lanes) for part in found)
+        found = jnp.where(low, pltpu.roll(real, within, axis=1), imag)
+    return found.reshape(rows // sets, lanes)
+
+
+def rotate(tile, within):
+    rows, lanes = tile.shape
+    if 2 * within == 8:
+        pairs = tile.reshape(rows // 8, 8, lanes)
+        low = lax.broadcasted_iota(jnp.int32, pairs.shape, 1) < within
+        turned = pltpu.roll(pairs, within, axis=1)
+        return jnp.where(low, -turned, turned).reshape(rows, lanes)
+    first_part = (lax.broadcasted_iota(jnp.int32, (rows, 1), 0) // within) % 2 == 0
+    return jnp.where(
+        first_part, -pltpu.roll(tile, rows - within, axis=0), pltpu.roll(tile, within, axis=0)
+    )
 
 
 def outer_kernel(bins, sets, scale, *refs):
@@ -101,27 +109,24 @@
     half = LANES // 2
     channels = out_ref.shape[2]
     full = channels // LANES
-    which, chosen_set = pl.program_id(0), pl.program_id(1)
-    now = which * sets + chosen_set
-    steps = pl.num_programs(0) * sets
+    which = pl.program_id(0)
     within = bins // sets
     cuts = sems.shape[2]
     size = channels // cuts
 
-    def copy(when, bin_of_set, cut, part):
-        side = lax.rem(when, 2)
+    def copy(group, q, k, cut, part):
         at = pl.ds(cut * size, size)
         return pltpu.make_async_copy(
-            slots.at[side, bin_of_set, part, at],
-            out_ref.at[part, when * within + bin_of_set, at],
-            sems.at[side, bin_of_set, cut, part],
+            slots.at[q, k, part, at],
+            out_ref.at[part, group * bins + q * within + k, at],
+            sems.at[q, k, cut, part],
         )
 
-    def wait_for(when):
-        for bin_of_set in range(within):
+    def wait_for(group, q):
+        for k in range(within):
             for cut in range(cuts):
                 for part in range(2):
-                    copy(when, bin_of_set, cut, part).wait()
+                    copy(group, q, k, cut, part).wait()
 
     def prepare(q):
         me = lax.axis_index("chan")
@@ -153,10 +158,7 @@
             ]
             for j, tile in enumerate(tiles):
                 lanes = slice(j * LANES, (j + 1) * LANES)
-                lanes_imag = slice(2 * channels + j * LANES, 2 * channels + (j + 1) * LANES)
-                plain, rotated = rows_of_set(tile, bins, sets, q)
-                right[q, at, lanes] = plain.astype(jnp.bfloat16)
-                right[q, at, lanes_imag] = rotated.astype(jnp.bfloat16)
+                right[q, at, lanes] = rows_of_set(tile, bins, sets, q).astype(jnp.bfloat16)
         scaled = own * scale
         for j in range(full + 1):
             block = scaled[:, 2 * j * LANES : (2 * j + 2) * LANES]
@@ -165,49 +167,52 @@
             else:
                 windows = [block, swap_halves(block)]
             kept = min(LANES, channels - j * LANES)
-            pieces = [rows_of_set(window, bins, sets, q)[0] for window in windows]
+            pieces = [rows_of_set(window, bins, sets, q) for window in windows]
             left[q, j * LANES : j * LANES + kept] = jnp.concatenate(pieces).T[:kept]
 
-    for q in range(sets):
-        pl.when(chosen_set == q)(functools.partial(prepare, q))
-
-    @pl.when(now >= 2)
-    def _():
-        wait_for(now - 2)
+    def prepare_rotated(q, first, last):
+        for lane in range(first, last, LANES):
+            plain = right[q, :, lane : lane + LANES].astype(jnp.float32)
+            at = slice(2 * channels + lane, 2 * channels + lane + LANES)
+            right[q, :, at] = rotate(plain, within).astype(jnp.bfloat16)
 
     depth = left.shape[2]
     lane = lax.broadcasted_iota(jnp.int32, (1, depth), 1) & (within - 1)
-    weights = right.at[chosen_set]
-    side = lax.rem(now, 2)
     whole = 2 * channels // (2 * LANES) * (2 * LANES)
     starts = [0, whole, 4 * channels - whole, 4 * channels]
     left_over = 2 * channels - whole
 
-    for k in range(within):
-        chosen = jnp.where(lane == k, left[chosen_set], 0.0).astype(jnp.bfloat16)
-
-        def multiply(first, last):
-            return jnp.dot(
-                chosen, weights[:, first:last], preferred_element_type=jnp.float32
-            ).astype(jnp.bfloat16)
-
-        def send(part):
-            for cut in range(cuts):
-                copy(now, k, cut, part).start()
-
-        slots[side, k, 0, :, :whole] = multiply(*starts[:2])
-        if left_over:
-            both = multiply(*starts[1:3])
-            slots[side, k, 0, :, whole:] = both[:, :left_over]
-            slots[side, k, 1, :, :left_over] = both[:, left_over:]
-        send(0)
-        slots[side, k, 1, :, left_over:] = multiply(*starts[2:])
-        send(1)
-
-    @pl.when(now == steps - 1)
+    for q in range(sets):
+        pl.when(which >= 1)(functools.partial(wait_for, which - 1, q))
+        prepare(q)
+        prepare_rotated(q, 0, left_over)
+        for k in range(within):
+            chosen = jnp.where(lane == k, left[q], 0.0).astype(jnp.bfloat16)
+
+            def multiply(first, last):
+                return jnp.dot(
+                    chosen, right[q, :, first:last], preferred_element_type=jnp.float32
+                ).astype(jnp.bfloat16)
+
+            def send(part):
+                for cut in range(cuts):
+                    copy(which, q, k, cut, part).start()
+
+            slots[q, k, 0, :, :whole] = multiply(*starts[:2])
+            if left_over:
+                both = multiply(*starts[1:3])
+                slots[q, k, 0, :, whole:] = both[:, :left_over]
+                slots[q, k, 1, :, :left_over] = both[:, left_over:]
+            send(0)
+            if k == 0:
+                prepare_rotated(q, left_over, 2 * channels)
+            slots[q, k, 1, :, left_over:] = multiply(*starts[2:])
+            send(1)
+
+    @pl.when(which == pl.num_programs(0) - 1)
     def _():
-        wait_for(now - 1)
-        wait_for(now)
+        for q in range(sets):
+            wait_for(which, q)
 
 
 def copy_kernel(in_ref, out_ref):
@@ -236,7 +241,7 @@
     lanes = local_windows * local_channels
     vmem = pl.BlockSpec(memory_space=pltpu.VMEM)
     memory = pl.BlockSpec(memory_space=pl.ANY)
-    masks = [devices - 1, 1, 2, *range(devices - 2, 2, -1), 0] if aligned else [0]
+    masks = [devices - 1, 1, 2, 3, *range(devices - 2, 3, -1), 0] if aligned else [0]
     pieces = len(masks)
     rows = (devices, groups, 2 * bins, lanes) if aligned else (2 * BINS, lanes)
     piece = rows[1:] if aligned else rows
@@ -278,14 +283,14 @@
             out_shape=jax.ShapeDtypeStruct(
                 (2, local_bins, local_channels, 2 * local_channels), jnp.bfloat16
             ),
-            grid=(groups, sets),
+            grid=(groups,),
             in_specs=[vmem] * (2 * pieces),
             out_specs=memory,
             scratch_shapes=[
                 pltpu.VMEM((sets, depth, 4 * local_channels), jnp.bfloat16),
                 pltpu.VMEM((sets, local_channels, depth), jnp.float32),
-                pltpu.VMEM((2, bins // sets, 2, local_channels, 2 * local_channels), jnp.bfloat16),
-                pltpu.SemaphoreType.DMA((2, bins // sets, 2, 2)),
+                pltpu.VMEM((sets, bins // sets, 2, local_channels, 2 * local_channels), jnp.bfloat16),
+                pltpu.SemaphoreType.DMA((sets, bins // sets, 2, 2)),
             ],
             compiler_params=pltpu.CompilerParams(vmem_limit_bytes=48 * MIB),
             cost_estimate=pl.CostEstimate(

time: 41.4 us -> 41.2 us (level)
  waiting for transfers between devices: 5.36 us -> 8.26 us
  starting transfers between devices: 16.4 us -> 14.4 us
  Pallas kernels: 16.8 us -> 15.8 us
    ppermute x7, waiting for transfers between devices: 4.22 us -> 7.17 us  [exchange(): return lax.ppermute(value, 'freq', pairs) if mask else value]
    ppermute x7, starting transfers between devices: 14.5 us -> 12.8 us  [exchange(): return lax.ppermute(value, 'freq', pairs) if mask else value]
    pallas_call x1, Pallas kernels: 16.1 us -> 15.1 us  [local(): pl.pallas_call(functools.partial(outer_kernel, bins, sets, 1.0 / windows)...]
  transfers between devices with their start and end apart: 15 -> 15, of which waited for: 6 -> 8; matrix products, arithmetic and copies ran while one was open for 0% -> 0% of each run, Pallas kernels for 0% -> 0%
where the time goes in v14:
time: 41.2 us; the launch traced here: 41.1 us
  Pallas kernels  15.8 us (38%)
  starting transfers between devices  14.4 us (35%)
  waiting for transfers between devices  8.26 us (20%)
  local copies, waits for them, and re-layouts  1.78 us (4%)
  matrix products  0.79 us (2%)
    pallas_call x1, Pallas kernels, local(): pl.pallas_call(functools.partial(outer_kernel, bins, sets, 1.0 / windows)...  15.1 us
    ppermute x7, starting transfers between devices, exchange(): return lax.ppermute(value, 'freq', pairs) if mask else value  12.8 us
    ppermute x7, waiting for transfers between devices, exchange(): return lax.ppermute(value, 'freq', pairs) if mask else value  7.17 us
    unnamed x4, local copies, waits for them, and re-layouts  1.78 us
    ppermute x8, starting transfers between devices, swap(): return lax.ppermute(value, 'chan', [(0, 1), (1, 0)])  1.54 us
    ppermute x8, waiting for transfers between devices, swap(): return lax.ppermute(value, 'chan', [(0, 1), (1, 0)])  1.09 us
  transfers between devices with their start and end apart: 15, of which 8 were waited for; matrix products, arithmetic and copies ran while one was open for 0% of the time, Pallas kernels for 0%

profile of v14, /device:TPU:0, one launch (start us, length us, event | category | flops | bytes accessed | tf_op | source)
XLA Modules:
  0.0 41.1 jit_solution(14316353875917037244)
XLA Ops:
  0.0 1.2 %copy-done.1 = bf16[1024,256]{1,0:T(8,128)(2,1)S(1)} copy-done((bf16[1024,256]{1,0:T(8,128)(2,1)S(1)}, bf16[1024,256]{1,0:T(8,128)(2,1)}, u32[]{:S(2)}) %copy-start.1) | copy-done | bytes 524312
  1.2 0.6 %copy-done = bf16[576,2,1024]{2,1,0:T(2,128)(2,1)S(1)} copy-done((bf16[576,2,1024]{2,1,0:T(2,128)(2,1)S(1)}, bf16[576,2,1024]{2,1,0:T(2,128)(2,1)}, u32[]{:S(2)}) %copy-start) | copy-done | bytes 2359320
  1.8 0.8 %fusion.5.spectrum_ref = bf16[2,576,256]{2,1,0:T(8,128)(2,1)S(1)} fusion(bf16[576,2,1024]{2,1,0:T(2,128)(2,1)S(1)} %copy-done, bf16[1024,256]{1,0:T(8,128)(2,1)S(1)} %table.1), kind=kOutput, calls=%fused_computation.3 | convolution fusion | flops 604274688 | bytes 3473408 | tf_op jit(solution)/shard_map/cws,sj->wcj/dot_general | solution.py:256
  2.6 0.8 %whiten.1 = (bf16[2,16,1152]{2,1,0:T(8,128)(2,1)S(1)}, bf16[2,16,1152]{2,1,0:T(8,128)(2,1)S(1)}, bf16[2,16,1152]{2,1,0:T(8,128)(2,1)S(1)}, bf16[2,16,1152]{2,1,0...) custom-call(bf16[2,576,256]{2,1,0:T(8,128)(2,1)S(1)} %fusion.5.spect, ...), custom_call_target="tpu_custom_call" | custom-call | flops 5898240 | bytes 1769472 | tf_op jit(solution)/shard_map/whiten/pallas_call | solution.py:259
  3.4 6.1 %collective-permute-start = (bf16[2,16,1152]{2,1,0:T(8,128)(2,1)S(1)}, bf16[2,16,1152]{2,1,0:T(8,128)(2,1)S(1)}, u32[]{:S(2)}, u32[]{:S(2)}) collective-permute-start(bf16[2,16,1152]{2,1,0:T(8,128)(2,1)S(1)} %get-tuple-element.13), channel_id=1, source_target_pairs={{0,7},{1,6},{2,5},{3,4},{4,3},{5,2},{6,1},{7,0},{8,15},{9,14},{10,... | collective-permute-start | bytes 221192 | tf_op jit(solution)/shard_map/ppermute | solution.py:224
  9.4 0.5 %collective-permute-start.1 = (bf16[2,16,1152]{2,1,0:T(8,128)(2,1)S(1)}, bf16[2,16,1152]{2,1,0:T(8,128)(2,1)S(1)}, u32[]{:S(2)}, u32[]{:S(2)}) collective-permute-start(bf16[2,16,1152]{2,1,0:T(8,128)(2,1)S(1)} %get-tuple-element.14), channel_id=1, source_target_pairs={{0,1},{1,0},{2,3},{3,2},{4,5},{5,4},{6,7},{7,6},{8,9},{9,8},{10,11... | collective-permute-start | bytes 221192 | tf_op jit(solution)/shard_map/ppermute | solution.py:224
  10.0 0.0 collective-permute-start.2
  10.0 3.0 %collective-permute-start.3 = (bf16[2,16,1152]{2,1,0:T(8,128)(2,1)S(1)}, bf16[2,16,1152]{2,1,0:T(8,128)(2,1)S(1)}, u32[]{:S(2)}, u32[]{:S(2)}) collective-permute-start(bf16[2,16,1152]{2,1,0:T(8,128)(2,1)S(1)} %get-tuple-element.16), channel_id=1, source_target_pairs={{0,3},{1,2},{2,1},{3,0},{4,7},{5,6},{6,5},{7,4},{8,11},{9,10},{10,... | collective-permute-start | bytes 221192 | tf_op jit(solution)/shard_map/ppermute | solution.py:224
  12.9 0.2 collective-permute-start.4
  13.2 0.0 collective-permute-done.refs_0_
  13.2 1.2 %collective-permute-start.5 = (bf16[2,16,1152]{2,1,0:T(8,128)(2,1)S(1)}, bf16[2,16,1152]{2,1,0:T(8,128)(2,1)S(1)}, u32[]{:S(2)}, u32[]{:S(2)}) collective-permute-start(bf16[2,16,1152]{2,1,0:T(8,128)(2,1)S(1)} %get-tuple-element.18), channel_id=1, source_target_pairs={{0,5},{1,4},{2,7},{3,6},{4,1},{5,0},{6,3},{7,2},{8,13},{9,12},{10,... | collective-permute-start | bytes 221192 | tf_op jit(solution)/shard_map/ppermute | solution.py:224
  14.4 0.2 collective-permute-done.1.refs_1_
  14.6 1.8 %collective-permute-start.6 = (bf16[2,16,1152]{2,1,0:T(8,128)(2,1)S(1)}, bf16[2,16,1152]{2,1,0:T(8,128)(2,1)S(1)}, u32[]{:S(2)}, u32[]{:S(2)}) collective-permute-start(bf16[2,16,1152]{2,1,0:T(8,128)(2,1)S(1)} %get-tuple-element.19), channel_id=1, source_target_pairs={{0,4},{1,5},{2,6},{3,7},{4,0},{5,1},{6,2},{7,3},{8,12},{9,13},{10,... | collective-permute-start | bytes 221192 | tf_op jit(solution)/shard_map/ppermute | solution.py:224
  16.4 0.0 collective-permute-done.2.refs_2_
  16.4 0.0 collective-permute-start.14
  16.4 0.0 collective-permute-done.3.refs_3_
  16.4 0.5 %collective-permute-start.7 = (bf16[2,16,1152]{2,1,0:T(8,128)(2,1)S(1)}, bf16[2,16,1152]{2,1,0:T(8,128)(2,1)S(1)}, u32[]{:S(2)}, u32[]{:S(2)}) collective-permute-start(bf16[2,16,1152]{2,1,0:T(8,128)(2,1)S(1)} %collective-permute-done.refs_0_), channel_id=1, source_target_pairs={{0,8},{8,0},{1,9},{9,1},{2,10},{10,2},{3,11},{11,3},{4,12},{12,4},... | collective-permute-start | bytes 221192 | tf_op jit(solution)/shard_map/ppermute | solution.py:228
  16.9 2.8 %collective-permute-done.4.refs_4_ = bf16[2,16,1152]{2,1,0:T(8,128)(2,1)S(1)} collective-permute-done((bf16[2,16,1152]{2,1,0:T(8,128)(2,1)S(1)}, bf16[2,16,1152]{2,1,0:T(8,128)(2,1)S(1)}, u32[]{:S(2)}, u32[]{:S(2)}) %collective-permute-start.4) | collective-permute-done | bytes 73760 | tf_op jit(solution)/shard_map/ppermute | solution.py:224
  19.8 4.0 %collective-permute-done.5.refs_5_ = bf16[2,16,1152]{2,1,0:T(8,128)(2,1)S(1)} collective-permute-done((bf16[2,16,1152]{2,1,0:T(8,128)(2,1)S(1)}, bf16[2,16,1152]{2,1,0:T(8,128)(2,1)S(1)}, u32[]{:S(2)}, u32[]{:S(2)}) %collective-permute-start.5) | collective-permute-done | bytes 73760 | tf_op jit(solution)/shard_map/ppermute | solution.py:224
  23.7 0.0 collective-permute-start.9
  23.7 0.2 collective-permute-done.6.refs_6_
  23.9 0.3 collective-permute-start.10
  24.2 0.0 collective-permute-done.14.refs_15_
  24.3 0.2 collective-permute-start.11
  24.4 0.3 collective-permute-start.12
  24.8 0.2 collective-permute-start.13
  24.9 0.1 collective-permute-done.9.refs_10_
  25.0 0.2 collective-permute-done.10.refs_11_
  25.2 0.3 collective-permute-done.11.refs_12_
  25.5 0.2 collective-permute-done.12.refs_13_
  25.7 0.3 collective-permute-done.13.refs_14_
  26.0 15.1 %outer_products.1 = bf16[2,16,576,1152]{3,2,1,0:T(8,128)(2,1)} custom-call(bf16[2,16,1152]{2,1,0:T(8,128)(2,1)S(1)} %collective-permute-done.refs_0_, bf16[2,16,1152]{2,1,0:T(8,128)(2,1)S(1)} %collective-permute-done.1.refs_1_, bf16[2,16,1152]{2,1,0:T(8,128)(2,1)S(1)} %collective-permute-done.2.refs_2_, ...), custom_call_target="tpu_custom_call" | custom-call | flops 5435817984 | bytes 42467328 | tf_op jit(solution)/shard_map/outer_products/pallas_call | solution.py:281
  (6 shorter events, 0.0 us)
Async XLA Ops:
  0.0 1.8 %copy-start = (bf16[576,2,1024]{2,1,0:T(2,128)(2,1)S(1)}, bf16[576,2,1024]{2,1,0:T(2,128)(2,1)}, u32[]{:S(2)}) copy-start(bf16[576,2,1024]{2,1,0:T(2,128)(2,1)} %param.2) | copy-start | bytes 7077892
  0.0 1.2 %copy-start.1 = (bf16[1024,256]{1,0:T(8,128)(2,1)S(1)}, bf16[1024,256]{1,0:T(8,128)(2,1)}, u32[]{:S(2)}) copy-start(bf16[1024,256]{1,0:T(8,128)(2,1)} %constant.2.clone.in_ref) | copy-start | bytes 1572868
  3.4 9.8 %collective-permute-start = (bf16[2,16,1152]{2,1,0:T(8,128)(2,1)S(1)}, bf16[2,16,1152]{2,1,0:T(8,128)(2,1)S(1)}, u32[]{:S(2)}, u32[]{:S(2)}) collective-permute-start(bf16[2,16,1152]{2,1,0:T(8,128)(2,1)S(1)} %get-tuple-element.13), channel_id=1, source_target_pairs={{0,7},{1,6},{2,5},{3,4},{4,3},{5,2},{6,1},{7,0},{8,15},{9,14},{10,... | collective-permute-start | bytes 221192 | tf_op jit(solution)/shard_map/ppermute | solution.py:224
  9.4 5.1 %collective-permute-start.1 = (bf16[2,16,1152]{2,1,0:T(8,128)(2,1)S(1)}, bf16[2,16,1152]{2,1,0:T(8,128)(2,1)S(1)}, u32[]{:S(2)}, u32[]{:S(2)}) collective-permute-start(bf16[2,16,1152]{2,1,0:T(8,128)(2,1)S(1)} %get-tuple-element.14), channel_id=1, source_target_pairs={{0,1},{1,0},{2,3},{3,2},{4,5},{5,4},{6,7},{7,6},{8,9},{9,8},{10,11... | collective-permute-start | bytes 221192 | tf_op jit(solution)/shard_map/ppermute | solution.py:224
  10.0 6.5 %collective-permute-start.2 = (bf16[2,16,1152]{2,1,0:T(8,128)(2,1)S(1)}, bf16[2,16,1152]{2,1,0:T(8,128)(2,1)S(1)}, u32[]{:S(2)}, u32[]{:S(2)}) collective-permute-start(bf16[2,16,1152]{2,1,0:T(8,128)(2,1)S(1)} %get-tuple-element.15), channel_id=1, source_target_pairs={{0,2},{1,3},{2,0},{3,1},{4,6},{5,7},{6,4},{7,5},{8,10},{9,11},{10,... | collective-permute-start | bytes 221192 | tf_op jit(solution)/shard_map/ppermute | solution.py:224
  10.0 6.5 %collective-permute-start.3 = (bf16[2,16,1152]{2,1,0:T(8,128)(2,1)S(1)}, bf16[2,16,1152]{2,1,0:T(8,128)(2,1)S(1)}, u32[]{:S(2)}, u32[]{:S(2)}) collective-permute-start(bf16[2,16,1152]{2,1,0:T(8,128)(2,1)S(1)} %get-tuple-element.16), channel_id=1, source_target_pairs={{0,3},{1,2},{2,1},{3,0},{4,7},{5,6},{6,5},{7,4},{8,11},{9,10},{10,... | collective-permute-start | bytes 221192 | tf_op jit(solution)/shard_map/ppermute | solution.py:224
  12.9 6.8 %collective-permute-start.4 = (bf16[2,16,1152]{2,1,0:T(8,128)(2,1)S(1)}, bf16[2,16,1152]{2,1,0:T(8,128)(2,1)S(1)}, u32[]{:S(2)}, u32[]{:S(2)}) collective-permute-start(bf16[2,16,1152]{2,1,0:T(8,128)(2,1)S(1)} %get-tuple-element.17), channel_id=1, source_target_pairs={{0,6},{1,7},{2,4},{3,5},{4,2},{5,3},{6,0},{7,1},{8,14},{9,15},{10,... | collective-permute-start | bytes 221192 | tf_op jit(solution)/shard_map/ppermute | solution.py:224
  13.2 10.6 %collective-permute-start.5 = (bf16[2,16,1152]{2,1,0:T(8,128)(2,1)S(1)}, bf16[2,16,1152]{2,1,0:T(8,128)(2,1)S(1)}, u32[]{:S(2)}, u32[]{:S(2)}) collective-permute-start(bf16[2,16,1152]{2,1,0:T(8,128)(2,1)S(1)} %get-tuple-element.18), channel_id=1, source_target_pairs={{0,5},{1,4},{2,7},{3,6},{4,1},{5,0},{6,3},{7,2},{8,13},{9,12},{10,... | collective-permute-start | bytes 221192 | tf_op jit(solution)/shard_map/ppermute | solution.py:224
  14.6 9.3 %collective-permute-start.6 = (bf16[2,16,1152]{2,1,0:T(8,128)(2,1)S(1)}, bf16[2,16,1152]{2,1,0:T(8,128)(2,1)S(1)}, u32[]{:S(2)}, u32[]{:S(2)}) collective-permute-start(bf16[2,16,1152]{2,1,0:T(8,128)(2,1)S(1)} %get-tuple-element.19), channel_id=1, source_target_pairs={{0,4},{1,5},{2,6},{3,7},{4,0},{5,1},{6,2},{7,3},{8,12},{9,13},{10,... | collective-permute-start | bytes 221192 | tf_op jit(solution)/shard_map/ppermute | solution.py:224
  16.4 7.8 %collective-permute-start.14 = (bf16[2,16,1152]{2,1,0:T(8,128)(2,1)S(1)}, bf16[2,16,1152]{2,1,0:T(8,128)(2,1)S(1)}, u32[]{:S(2)}, u32[]{:S(2)}) collective-permute-start(bf16[2,16,1152]{2,1,0:T(8,128)(2,1)S(1)} %get-tuple-element.20.refs_7_), channel_id=1, source_target_pairs={{0,8},{8,0},{1,9},{9,1},{2,10},{10,2},{3,11},{11,3},{4,12},{12,4},... | collective-permute-start | bytes 221192 | tf_op jit(solution)/shard_map/ppermute | solution.py:228
  16.4 8.0 %collective-permute-start.7 = (bf16[2,16,1152]{2,1,0:T(8,128)(2,1)S(1)}, bf16[2,16,1152]{2,1,0:T(8,128)(2,1)S(1)}, u32[]{:S(2)}, u32[]{:S(2)}) collective-permute-start(bf16[2,16,1152]{2,1,0:T(8,128)(2,1)S(1)} %collective-permute-done.refs_0_), channel_id=1, source_target_pairs={{0,8},{8,0},{1,9},{9,1},{2,10},{10,2},{3,11},{11,3},{4,12},{12,4},... | collective-permute-start | bytes 221192 | tf_op jit(solution)/shard_map/ppermute | solution.py:228
  19.8 5.0 %collective-permute-start.8 = (bf16[2,16,1152]{2,1,0:T(8,128)(2,1)S(1)}, bf16[2,16,1152]{2,1,0:T(8,128)(2,1)S(1)}, u32[]{:S(2)}, u32[]{:S(2)}) collective-permute-start(bf16[2,16,1152]{2,1,0:T(8,128)(2,1)S(1)} %collective-permute-done.1.refs_1_), channel_id=1, source_target_pairs={{0,8},{8,0},{1,9},{9,1},{2,10},{10,2},{3,11},{11,3},{4,12},{12,4},... | collective-permute-start | bytes 221192 | tf_op jit(solution)/shard_map/ppermute | solution.py:228
  23.7 1.3 %collective-permute-start.9 = (bf16[2,16,1152]{2,1,0:T(8,128)(2,1)S(1)}, bf16[2,16,1152]{2,1,0:T(8,128)(2,1)S(1)}, u32[]{:S(2)}, u32[]{:S(2)}) collective-permute-start(bf16[2,16,1152]{2,1,0:T(8,128)(2,1)S(1)} %collective-permute-done.2.refs_2_), channel_id=1, source_target_pairs={{0,8},{8,0},{1,9},{9,1},{2,10},{10,2},{3,11},{11,3},{4,12},{12,4},... | collective-permute-start | bytes 221192 | tf_op jit(solution)/shard_map/ppermute | solution.py:228
  23.9 1.3 %collective-permute-start.10 = (bf16[2,16,1152]{2,1,0:T(8,128)(2,1)S(1)}, bf16[2,16,1152]{2,1,0:T(8,128)(2,1)S(1)}, u32[]{:S(2)}, u32[]{:S(2)}) collective-permute-start(bf16[2,16,1152]{2,1,0:T(8,128)(2,1)S(1)} %collective-permute-done.3.refs_3_), channel_id=1, source_target_pairs={{0,8},{8,0},{1,9},{9,1},{2,10},{10,2},{3,11},{11,3},{4,12},{12,4},... | collective-permute-start | bytes 221192 | tf_op jit(solution)/shard_map/ppermute | solution.py:228
  24.3 1.3 %collective-permute-start.11 = (bf16[2,16,1152]{2,1,0:T(8,128)(2,1)S(1)}, bf16[2,16,1152]{2,1,0:T(8,128)(2,1)S(1)}, u32[]{:S(2)}, u32[]{:S(2)}) collective-permute-start(bf16[2,16,1152]{2,1,0:T(8,128)(2,1)S(1)} %collective-permute-done.4.refs_4_), channel_id=1, source_target_pairs={{0,8},{8,0},{1,9},{9,1},{2,10},{10,2},{3,11},{11,3},{4,12},{12,4},... | collective-permute-start | bytes 221192 | tf_op jit(solution)/shard_map/ppermute | solution.py:228
  24.4 1.3 %collective-permute-start.12 = (bf16[2,16,1152]{2,1,0:T(8,128)(2,1)S(1)}, bf16[2,16,1152]{2,1,0:T(8,128)(2,1)S(1)}, u32[]{:S(2)}, u32[]{:S(2)}) collective-permute-start(bf16[2,16,1152]{2,1,0:T(8,128)(2,1)S(1)} %collective-permute-done.5.refs_5_), channel_id=1, source_target_pairs={{0,8},{8,0},{1,9},{9,1},{2,10},{10,2},{3,11},{11,3},{4,12},{12,4},... | collective-permute-start | bytes 221192 | tf_op jit(solution)/shard_map/ppermute | solution.py:228
  24.8 1.3 %collective-permute-start.13 = (bf16[2,16,1152]{2,1,0:T(8,128)(2,1)S(1)}, bf16[2,16,1152]{2,1,0:T(8,128)(2,1)S(1)}, u32[]{:S(2)}, u32[]{:S(2)}) collective-permute-start(bf16[2,16,1152]{2,1,0:T(8,128)(2,1)S(1)} %collective-permute-done.6.refs_6_), channel_id=1, source_target_pairs={{0,8},{8,0},{1,9},{9,1},{2,10},{10,2},{3,11},{11,3},{4,12},{12,4},... | collective-permute-start | bytes 221192 | tf_op jit(solution)/shard_map/ppermute | solution.py:228

commit v15 on v14

--- a/solution.py
+++ b/solution.py
@@ -241,7 +241,7 @@
     lanes = local_windows * local_channels
     vmem = pl.BlockSpec(memory_space=pltpu.VMEM)
     memory = pl.BlockSpec(memory_space=pl.ANY)
-    masks = [devices - 1, 1, 2, 3, *range(devices - 2, 3, -1), 0] if aligned else [0]
+    masks = [devices - 1, 1, 2, *range(devices - 2, 2, -1), 0] if aligned else [0]
     pieces = len(masks)
     rows = (devices, groups, 2 * bins, lanes) if aligned else (2 * BINS, lanes)
     piece = rows[1:] if aligned else rows

time: 41.2 us -> 40.4 us (0.981)
  waiting for transfers between devices: 8.26 us -> 5.36 us
  starting transfers between devices: 14.4 us -> 16.4 us
    ppermute x7, waiting for transfers between devices: 7.17 us -> 4.22 us  [exchange(): return lax.ppermute(value, 'freq', pairs) if mask else value]
    ppermute x7, starting transfers between devices: 12.8 us -> 14.5 us  [exchange(): return lax.ppermute(value, 'freq', pairs) if mask else value]
  transfers between devices with their start and end apart: 15 -> 15, of which waited for: 8 -> 6; matrix products, arithmetic and copies ran while one was open for 0% -> 0% of each run, Pallas kernels for 0% -> 0%
where the time goes in v15:
time: 40.4 us; the launch traced here: 40.3 us
  starting transfers between devices  16.4 us (41%)
  Pallas kernels  15.9 us (39%)
  waiting for transfers between devices  5.36 us (13%)
  local copies, waits for them, and re-layouts  1.78 us (4%)
  matrix products  0.79 us (2%)
    pallas_call x1, Pallas kernels, local(): pl.pallas_call(functools.partial(outer_kernel, bins, sets, 1.0 / windows)...  15.1 us
    ppermute x7, starting transfers between devices, exchange(): return lax.ppermute(value, 'freq', pairs) if mask else value  14.5 us
    ppermute x7, waiting for transfers between devices, exchange(): return lax.ppermute(value, 'freq', pairs) if mask else value  4.22 us
    ppermute x8, starting transfers between devices, swap(): return lax.ppermute(value, 'chan', [(0, 1), (1, 0)])  1.88 us
    unnamed x4, local copies, waits for them, and re-layouts  1.78 us
    ppermute x8, waiting for transfers between devices, swap(): return lax.ppermute(value, 'chan', [(0, 1), (1, 0)])  1.14 us
  transfers between devices with their start and end apart: 15, of which 6 were waited for; matrix products, arithmetic and copies ran while one was open for 0% of the time, Pallas kernels for 0%

profile of v15, /device:TPU:0, one launch (start us, length us, event | category | flops | bytes accessed | tf_op | source)
XLA Modules:
  0.0 40.3 jit_solution(10790915608311272187)
XLA Ops:
  0.0 1.2 %copy-done.1 = bf16[1024,256]{1,0:T(8,128)(2,1)S(1)} copy-done((bf16[1024,256]{1,0:T(8,128)(2,1)S(1)}, bf16[1024,256]{1,0:T(8,128)(2,1)}, u32[]{:S(2)}) %copy-start.1) | copy-done | bytes 524312
  1.2 0.6 %copy-done = bf16[576,2,1024]{2,1,0:T(2,128)(2,1)S(1)} copy-done((bf16[576,2,1024]{2,1,0:T(2,128)(2,1)S(1)}, bf16[576,2,1024]{2,1,0:T(2,128)(2,1)}, u32[]{:S(2)}) %copy-start) | copy-done | bytes 2359320
  1.8 0.8 %fusion.5.spectrum_ref = bf16[2,576,256]{2,1,0:T(8,128)(2,1)S(1)} fusion(bf16[576,2,1024]{2,1,0:T(2,128)(2,1)S(1)} %copy-done, bf16[1024,256]{1,0:T(8,128)(2,1)S(1)} %table.1), kind=kOutput, calls=%fused_computation.3 | convolution fusion | flops 604274688 | bytes 3473408 | tf_op jit(solution)/shard_map/cws,sj->wcj/dot_general | solution.py:256
  2.6 0.8 %whiten.1 = (bf16[2,16,1152]{2,1,0:T(8,128)(2,1)S(1)}, bf16[2,16,1152]{2,1,0:T(8,128)(2,1)S(1)}, bf16[2,16,1152]{2,1,0:T(8,128)(2,1)S(1)}, bf16[2,16,1152]{2,1,0...) custom-call(bf16[2,576,256]{2,1,0:T(8,128)(2,1)S(1)} %fusion.5.spect, ...), custom_call_target="tpu_custom_call" | custom-call | flops 5898240 | bytes 1769472 | tf_op jit(solution)/shard_map/whiten/pallas_call | solution.py:259
  3.4 6.1 %collective-permute-start = (bf16[2,16,1152]{2,1,0:T(8,128)(2,1)S(1)}, bf16[2,16,1152]{2,1,0:T(8,128)(2,1)S(1)}, u32[]{:S(2)}, u32[]{:S(2)}) collective-permute-start(bf16[2,16,1152]{2,1,0:T(8,128)(2,1)S(1)} %get-tuple-element.13), channel_id=1, source_target_pairs={{0,7},{1,6},{2,5},{3,4},{4,3},{5,2},{6,1},{7,0},{8,15},{9,14},{10,... | collective-permute-start | bytes 221192 | tf_op jit(solution)/shard_map/ppermute | solution.py:224
  9.4 0.5 %collective-permute-start.1 = (bf16[2,16,1152]{2,1,0:T(8,128)(2,1)S(1)}, bf16[2,16,1152]{2,1,0:T(8,128)(2,1)S(1)}, u32[]{:S(2)}, u32[]{:S(2)}) collective-permute-start(bf16[2,16,1152]{2,1,0:T(8,128)(2,1)S(1)} %get-tuple-element.14), channel_id=1, source_target_pairs={{0,1},{1,0},{2,3},{3,2},{4,5},{5,4},{6,7},{7,6},{8,9},{9,8},{10,11... | collective-permute-start | bytes 221192 | tf_op jit(solution)/shard_map/ppermute | solution.py:224
  10.0 0.0 collective-permute-start.2
  10.0 0.9 %collective-permute-start.3 = (bf16[2,16,1152]{2,1,0:T(8,128)(2,1)S(1)}, bf16[2,16,1152]{2,1,0:T(8,128)(2,1)S(1)}, u32[]{:S(2)}, u32[]{:S(2)}) collective-permute-start(bf16[2,16,1152]{2,1,0:T(8,128)(2,1)S(1)} %get-tuple-element.16), channel_id=1, source_target_pairs={{0,6},{1,7},{2,4},{3,5},{4,2},{5,3},{6,0},{7,1},{8,14},{9,15},{10,... | collective-permute-start | bytes 221192 | tf_op jit(solution)/shard_map/ppermute | solution.py:224
  10.9 3.5 %collective-permute-start.4 = (bf16[2,16,1152]{2,1,0:T(8,128)(2,1)S(1)}, bf16[2,16,1152]{2,1,0:T(8,128)(2,1)S(1)}, u32[]{:S(2)}, u32[]{:S(2)}) collective-permute-start(bf16[2,16,1152]{2,1,0:T(8,128)(2,1)S(1)} %get-tuple-element.17), channel_id=1, source_target_pairs={{0,5},{1,4},{2,7},{3,6},{4,1},{5,0},{6,3},{7,2},{8,13},{9,12},{10,... | collective-permute-start | bytes 221192 | tf_op jit(solution)/shard_map/ppermute | solution.py:224
  14.4 0.0 collective-permute-done.refs_0_
  14.4 0.3 collective-permute-start.5
  14.7 3.2 %collective-permute-start.6 = (bf16[2,16,1152]{2,1,0:T(8,128)(2,1)S(1)}, bf16[2,16,1152]{2,1,0:T(8,128)(2,1)S(1)}, u32[]{:S(2)}, u32[]{:S(2)}) collective-permute-start(bf16[2,16,1152]{2,1,0:T(8,128)(2,1)S(1)} %get-tuple-element.19), channel_id=1, source_target_pairs={{0,3},{1,2},{2,1},{3,0},{4,7},{5,6},{6,5},{7,4},{8,11},{9,10},{10,... | collective-permute-start | bytes 221192 | tf_op jit(solution)/shard_map/ppermute | solution.py:224
  17.9 0.0 collective-permute-done.2.refs_2_
  17.9 0.0 collective-permute-start.14
  17.9 0.0 collective-permute-done.3.refs_3_
  17.9 0.5 %collective-permute-start.7 = (bf16[2,16,1152]{2,1,0:T(8,128)(2,1)S(1)}, bf16[2,16,1152]{2,1,0:T(8,128)(2,1)S(1)}, u32[]{:S(2)}, u32[]{:S(2)}) collective-permute-start(bf16[2,16,1152]{2,1,0:T(8,128)(2,1)S(1)} %collective-permute-done.refs_0_), channel_id=1, source_target_pairs={{0,8},{8,0},{1,9},{9,1},{2,10},{10,2},{3,11},{11,3},{4,12},{12,4},... | collective-permute-start | bytes 221192 | tf_op jit(solution)/shard_map/ppermute | solution.py:228
  18.4 4.2 %collective-permute-done.4.refs_4_ = bf16[2,16,1152]{2,1,0:T(8,128)(2,1)S(1)} collective-permute-done((bf16[2,16,1152]{2,1,0:T(8,128)(2,1)S(1)}, bf16[2,16,1152]{2,1,0:T(8,128)(2,1)S(1)}, u32[]{:S(2)}, u32[]{:S(2)}) %collective-permute-start.4) | collective-permute-done | bytes 73760 | tf_op jit(solution)/shard_map/ppermute | solution.py:224
  22.6 0.0 collective-permute-done.5.refs_5_
  22.6 0.5 %collective-permute-start.9 = (bf16[2,16,1152]{2,1,0:T(8,128)(2,1)S(1)}, bf16[2,16,1152]{2,1,0:T(8,128)(2,1)S(1)}, u32[]{:S(2)}, u32[]{:S(2)}) collective-permute-start(bf16[2,16,1152]{2,1,0:T(8,128)(2,1)S(1)} %collective-permute-done.2.refs_2_), channel_id=1, source_target_pairs={{0,8},{8,0},{1,9},{9,1},{2,10},{10,2},{3,11},{11,3},{4,12},{12,4},... | collective-permute-start | bytes 221192 | tf_op jit(solution)/shard_map/ppermute | solution.py:228
  23.2 0.0 collective-permute-done.6.refs_6_
  23.2 0.1 collective-permute-start.10
  23.2 0.4 %collective-permute-start.11 = (bf16[2,16,1152]{2,1,0:T(8,128)(2,1)S(1)}, bf16[2,16,1152]{2,1,0:T(8,128)(2,1)S(1)}, u32[]{:S(2)}, u32[]{:S(2)}) collective-permute-start(bf16[2,16,1152]{2,1,0:T(8,128)(2,1)S(1)} %collective-permute-done.4.refs_4_), channel_id=1, source_target_pairs={{0,8},{8,0},{1,9},{9,1},{2,10},{10,2},{3,11},{11,3},{4,12},{12,4},... | collective-permute-start | bytes 221192 | tf_op jit(solution)/shard_map/ppermute | solution.py:228
  23.7 0.0 collective-permute-done.7.refs_8_
  23.7 0.1 collective-permute-start.12
  23.7 0.2 collective-permute-done.8.refs_9_
  23.9 0.3 collective-permute-start.13
  24.2 0.0 collective-permute-done.9.refs_10_
  24.2 0.2 collective-permute-done.10.refs_11_
  24.4 0.2 collective-permute-done.11.refs_12_
  24.6 0.4 collective-permute-done.12.refs_13_
  24.9 0.2 collective-permute-done.13.refs_14_
  25.2 15.1 %outer_products.1 = bf16[2,16,576,1152]{3,2,1,0:T(8,128)(2,1)} custom-call(bf16[2,16,1152]{2,1,0:T(8,128)(2,1)S(1)} %collective-permute-done.refs_0_, bf16[2,16,1152]{2,1,0:T(8,128)(2,1)S(1)} %collective-permute-done.1.refs_1_, bf16[2,16,1152]{2,1,0:T(8,128)(2,1)S(1)} %collective-permute-done.2.refs_2_, ...), custom_call_target="tpu_custom_call" | custom-call | flops 5435817984 | bytes 42467328 | tf_op jit(solution)/shard_map/outer_products/pallas_call | solution.py:281
  (6 shorter events, 0.0 us)
Async XLA Ops:
  0.0 1.8 %copy-start = (bf16[576,2,1024]{2,1,0:T(2,128)(2,1)S(1)}, bf16[576,2,1024]{2,1,0:T(2,128)(2,1)}, u32[]{:S(2)}) copy-start(bf16[576,2,1024]{2,1,0:T(2,128)(2,1)} %param.2) | copy-start | bytes 7077892
  0.0 1.2 %copy-start.1 = (bf16[1024,256]{1,0:T(8,128)(2,1)S(1)}, bf16[1024,256]{1,0:T(8,128)(2,1)}, u32[]{:S(2)}) copy-start(bf16[1024,256]{1,0:T(8,128)(2,1)} %constant.2.clone.in_ref) | copy-start | bytes 1572868
  3.4 11.0 %collective-permute-start = (bf16[2,16,1152]{2,1,0:T(8,128)(2,1)S(1)}, bf16[2,16,1152]{2,1,0:T(8,128)(2,1)S(1)}, u32[]{:S(2)}, u32[]{:S(2)}) collective-permute-start(bf16[2,16,1152]{2,1,0:T(8,128)(2,1)S(1)} %get-tuple-element.13), channel_id=1, source_target_pairs={{0,7},{1,6},{2,5},{3,4},{4,3},{5,2},{6,1},{7,0},{8,15},{9,14},{10,... | collective-permute-start | bytes 221192 | tf_op jit(solution)/shard_map/ppermute | solution.py:224
  9.4 5.3 %collective-permute-start.1 = (bf16[2,16,1152]{2,1,0:T(8,128)(2,1)S(1)}, bf16[2,16,1152]{2,1,0:T(8,128)(2,1)S(1)}, u32[]{:S(2)}, u32[]{:S(2)}) collective-permute-start(bf16[2,16,1152]{2,1,0:T(8,128)(2,1)S(1)} %get-tuple-element.14), channel_id=1, source_target_pairs={{0,1},{1,0},{2,3},{3,2},{4,5},{5,4},{6,7},{7,6},{8,9},{9,8},{10,11... | collective-permute-start | bytes 221192 | tf_op jit(solution)/shard_map/ppermute | solution.py:224
  10.0 8.0 %collective-permute-start.2 = (bf16[2,16,1152]{2,1,0:T(8,128)(2,1)S(1)}, bf16[2,16,1152]{2,1,0:T(8,128)(2,1)S(1)}, u32[]{:S(2)}, u32[]{:S(2)}) collective-permute-start(bf16[2,16,1152]{2,1,0:T(8,128)(2,1)S(1)} %get-tuple-element.15), channel_id=1, source_target_pairs={{0,2},{1,3},{2,0},{3,1},{4,6},{5,7},{6,4},{7,5},{8,10},{9,11},{10,... | collective-permute-start | bytes 221192 | tf_op jit(solution)/shard_map/ppermute | solution.py:224
  10.0 8.0 %collective-permute-start.3 = (bf16[2,16,1152]{2,1,0:T(8,128)(2,1)S(1)}, bf16[2,16,1152]{2,1,0:T(8,128)(2,1)S(1)}, u32[]{:S(2)}, u32[]{:S(2)}) collective-permute-start(bf16[2,16,1152]{2,1,0:T(8,128)(2,1)S(1)} %get-tuple-element.16), channel_id=1, source_target_pairs={{0,6},{1,7},{2,4},{3,5},{4,2},{5,3},{6,0},{7,1},{8,14},{9,15},{10,... | collective-permute-start | bytes 221192 | tf_op jit(solution)/shard_map/ppermute | solution.py:224
  10.9 11.8 %collective-permute-start.4 = (bf16[2,16,1152]{2,1,0:T(8,128)(2,1)S(1)}, bf16[2,16,1152]{2,1,0:T(8,128)(2,1)S(1)}, u32[]{:S(2)}, u32[]{:S(2)}) collective-permute-start(bf16[2,16,1152]{2,1,0:T(8,128)(2,1)S(1)} %get-tuple-element.17), channel_id=1, source_target_pairs={{0,5},{1,4},{2,7},{3,6},{4,1},{5,0},{6,3},{7,2},{8,13},{9,12},{10,... | collective-permute-start | bytes 221192 | tf_op jit(solution)/shard_map/ppermute | solution.py:224
  14.4 8.2 %collective-permute-start.5 = (bf16[2,16,1152]{2,1,0:T(8,128)(2,1)S(1)}, bf16[2,16,1152]{2,1,0:T(8,128)(2,1)S(1)}, u32[]{:S(2)}, u32[]{:S(2)}) collective-permute-start(bf16[2,16,1152]{2,1,0:T(8,128)(2,1)S(1)} %get-tuple-element.18), channel_id=1, source_target_pairs={{0,4},{1,5},{2,6},{3,7},{4,0},{5,1},{6,2},{7,3},{8,12},{9,13},{10,... | collective-permute-start | bytes 221192 | tf_op jit(solution)/shard_map/ppermute | solution.py:224
  14.7 8.4 %collective-permute-start.6 = (bf16[2,16,1152]{2,1,0:T(8,128)(2,1)S(1)}, bf16[2,16,1152]{2,1,0:T(8,128)(2,1)S(1)}, u32[]{:S(2)}, u32[]{:S(2)}) collective-permute-start(bf16[2,16,1152]{2,1,0:T(8,128)(2,1)S(1)} %get-tuple-element.19), channel_id=1, source_target_pairs={{0,3},{1,2},{2,1},{3,0},{4,7},{5,6},{6,5},{7,4},{8,11},{9,10},{10,... | collective-permute-start | bytes 221192 | tf_op jit(solution)/shard_map/ppermute | solution.py:224
  17.9 5.3 %collective-permute-start.14 = (bf16[2,16,1152]{2,1,0:T(8,128)(2,1)S(1)}, bf16[2,16,1152]{2,1,0:T(8,128)(2,1)S(1)}, u32[]{:S(2)}, u32[]{:S(2)}) collective-permute-start(bf16[2,16,1152]{2,1,0:T(8,128)(2,1)S(1)} %get-tuple-element.20.refs_7_), channel_id=1, source_target_pairs={{0,8},{8,0},{1,9},{9,1},{2,10},{10,2},{3,11},{11,3},{4,12},{12,4},... | collective-permute-start | bytes 221192 | tf_op jit(solution)/shard_map/ppermute | solution.py:228
  17.9 5.7 %collective-permute-start.7 = (bf16[2,16,1152]{2,1,0:T(8,128)(2,1)S(1)}, bf16[2,16,1152]{2,1,0:T(8,128)(2,1)S(1)}, u32[]{:S(2)}, u32[]{:S(2)}) collective-permute-start(bf16[2,16,1152]{2,1,0:T(8,128)(2,1)S(1)} %collective-permute-done.refs_0_), channel_id=1, source_target_pairs={{0,8},{8,0},{1,9},{9,1},{2,10},{10,2},{3,11},{11,3},{4,12},{12,4},... | collective-permute-start | bytes 221192 | tf_op jit(solution)/shard_map/ppermute | solution.py:228
  22.6 1.3 %collective-permute-start.8 = (bf16[2,16,1152]{2,1,0:T(8,128)(2,1)S(1)}, bf16[2,16,1152]{2,1,0:T(8,128)(2,1)S(1)}, u32[]{:S(2)}, u32[]{:S(2)}) collective-permute-start(bf16[2,16,1152]{2,1,0:T(8,128)(2,1)S(1)} %collective-permute-done.1.refs_1_), channel_id=1, source_target_pairs={{0,8},{8,0},{1,9},{9,1},{2,10},{10,2},{3,11},{11,3},{4,12},{12,4},... | collective-permute-start | bytes 221192 | tf_op jit(solution)/shard_map/ppermute | solution.py:228
  22.6 1.5 %collective-permute-start.9 = (bf16[2,16,1152]{2,1,0:T(8,128)(2,1)S(1)}, bf16[2,16,1152]{2,1,0:T(8,128)(2,1)S(1)}, u32[]{:S(2)}, u32[]{:S(2)}) collective-permute-start(bf16[2,16,1152]{2,1,0:T(8,128)(2,1)S(1)} %collective-permute-done.2.refs_2_), channel_id=1, source_target_pairs={{0,8},{8,0},{1,9},{9,1},{2,10},{10,2},{3,11},{11,3},{4,12},{12,4},... | collective-permute-start | bytes 221192 | tf_op jit(solution)/shard_map/ppermute | solution.py:228
  23.2 1.3 %collective-permute-start.10 = (bf16[2,16,1152]{2,1,0:T(8,128)(2,1)S(1)}, bf16[2,16,1152]{2,1,0:T(8,128)(2,1)S(1)}, u32[]{:S(2)}, u32[]{:S(2)}) collective-permute-start(bf16[2,16,1152]{2,1,0:T(8,128)(2,1)S(1)} %collective-permute-done.3.refs_3_), channel_id=1, source_target_pairs={{0,8},{8,0},{1,9},{9,1},{2,10},{10,2},{3,11},{11,3},{4,12},{12,4},... | collective-permute-start | bytes 221192 | tf_op jit(solution)/shard_map/ppermute | solution.py:228
  23.2 1.4 %collective-permute-start.11 = (bf16[2,16,1152]{2,1,0:T(8,128)(2,1)S(1)}, bf16[2,16,1152]{2,1,0:T(8,128)(2,1)S(1)}, u32[]{:S(2)}, u32[]{:S(2)}) collective-permute-start(bf16[2,16,1152]{2,1,0:T(8,128)(2,1)S(1)} %collective-permute-done.4.refs_4_), channel_id=1, source_target_pairs={{0,8},{8,0},{1,9},{9,1},{2,10},{10,2},{3,11},{11,3},{4,12},{12,4},... | collective-permute-start | bytes 221192 | tf_op jit(solution)/shard_map/ppermute | solution.py:228
  23.7 1.3 %collective-permute-start.12 = (bf16[2,16,1152]{2,1,0:T(8,128)(2,1)S(1)}, bf16[2,16,1152]{2,1,0:T(8,128)(2,1)S(1)}, u32[]{:S(2)}, u32[]{:S(2)}) collective-permute-start(bf16[2,16,1152]{2,1,0:T(8,128)(2,1)S(1)} %collective-permute-done.5.refs_5_), channel_id=1, source_target_pairs={{0,8},{8,0},{1,9},{9,1},{2,10},{10,2},{3,11},{11,3},{4,12},{12,4},... | collective-permute-start | bytes 221192 | tf_op jit(solution)/shard_map/ppermute | solution.py:228
  23.9 1.3 %collective-permute-start.13 = (bf16[2,16,1152]{2,1,0:T(8,128)(2,1)S(1)}, bf16[2,16,1152]{2,1,0:T(8,128)(2,1)S(1)}, u32[]{:S(2)}, u32[]{:S(2)}) collective-permute-start(bf16[2,16,1152]{2,1,0:T(8,128)(2,1)S(1)} %collective-permute-done.6.refs_6_), channel_id=1, source_target_pairs={{0,8},{8,0},{1,9},{9,1},{2,10},{10,2},{3,11},{11,3},{4,12},{12,4},... | collective-permute-start | bytes 221192 | tf_op jit(solution)/shard_map/ppermute | solution.py:228

commit v16 on v15

--- a/solution.py
+++ b/solution.py
@@ -241,7 +241,8 @@
     lanes = local_windows * local_channels
     vmem = pl.BlockSpec(memory_space=pltpu.VMEM)
     memory = pl.BlockSpec(memory_space=pl.ANY)
-    masks = [devices - 1, 1, 2, *range(devices - 2, 2, -1), 0] if aligned else [0]
+    masks = [*range(devices - 1, devices - 3, -1), 1, 2, *range(devices - 3, 2, -1), 0]
+    masks = masks if aligned else [0]
     pieces = len(masks)
     rows = (devices, groups, 2 * bins, lanes) if aligned else (2 * BINS, lanes)
     piece = rows[1:] if aligned else rows

time: 40.4 us -> 40 us (0.990)
  starting transfers between devices: 16.4 us -> 15.1 us
  waiting for transfers between devices: 5.36 us -> 6.25 us
    ppermute x7, waiting for transfers between devices: 4.22 us -> 5.33 us  [exchange(): return lax.ppermute(value, 'freq', pairs) if mask else value]
    ppermute x7, starting transfers between devices: 14.5 us -> 13.6 us  [exchange(): return lax.ppermute(value, 'freq', pairs) if mask else value]
  transfers between devices with their start and end apart: 15 -> 15, of which waited for: 6 -> 8; matrix products, arithmetic and copies ran while one was open for 0% -> 0% of each run, Pallas kernels for 0% -> 0%
where the time goes in v16:
time: 40 us; the launch traced here: 39.9 us
  Pallas kernels  15.9 us (40%)
  starting transfers between devices  15.1 us (38%)
  waiting for transfers between devices  6.25 us (16%)
  local copies, waits for them, and re-layouts  1.78 us (4%)
  matrix products  0.79 us (2%)
    pallas_call x1, Pallas kernels, local(): pl.pallas_call(functools.partial(outer_kernel, bins, sets, 1.0 / windows)...  15.1 us
    ppermute x7, starting transfers between devices, exchange(): return lax.ppermute(value, 'freq', pairs) if mask else value  13.6 us
    ppermute x7, waiting for transfers between devices, exchange(): return lax.ppermute(value, 'freq', pairs) if mask else value  5.33 us
    unnamed x4, local copies, waits for them, and re-layouts  1.78 us
    ppermute x8, starting transfers between devices, swap(): return lax.ppermute(value, 'chan', [(0, 1), (1, 0)])  1.54 us
    ppermute x8, waiting for transfers between devices, swap(): return lax.ppermute(value, 'chan', [(0, 1), (1, 0)])  0.92 us
  transfers between devices with their start and end apart: 15, of which 8 were waited for; matrix products, arithmetic and copies ran while one was open for 0% of the time, Pallas kernels for 0%

profile of v16, /device:TPU:0, one launch (start us, length us, event | category | flops | bytes accessed | tf_op | source)
XLA Modules:
  0.0 39.9 jit_solution(10811767863665207720)
XLA Ops:
  0.0 1.2 %copy-done.1 = bf16[1024,256]{1,0:T(8,128)(2,1)S(1)} copy-done((bf16[1024,256]{1,0:T(8,128)(2,1)S(1)}, bf16[1024,256]{1,0:T(8,128)(2,1)}, u32[]{:S(2)}) %copy-start.1) | copy-done | bytes 524312
  1.2 0.6 %copy-done = bf16[576,2,1024]{2,1,0:T(2,128)(2,1)S(1)} copy-done((bf16[576,2,1024]{2,1,0:T(2,128)(2,1)S(1)}, bf16[576,2,1024]{2,1,0:T(2,128)(2,1)}, u32[]{:S(2)}) %copy-start) | copy-done | bytes 2359320
  1.8 0.8 %fusion.5.spectrum_ref = bf16[2,576,256]{2,1,0:T(8,128)(2,1)S(1)} fusion(bf16[576,2,1024]{2,1,0:T(2,128)(2,1)S(1)} %copy-done, bf16[1024,256]{1,0:T(8,128)(2,1)S(1)} %table.1), kind=kOutput, calls=%fused_computation.3 | convolution fusion | flops 604274688 | bytes 3473408 | tf_op jit(solution)/shard_map/cws,sj->wcj/dot_general | solution.py:257
  2.6 0.8 %whiten.1 = (bf16[2,16,1152]{2,1,0:T(8,128)(2,1)S(1)}, bf16[2,16,1152]{2,1,0:T(8,128)(2,1)S(1)}, bf16[2,16,1152]{2,1,0:T(8,128)(2,1)S(1)}, bf16[2,16,1152]{2,1,0...) custom-call(bf16[2,576,256]{2,1,0:T(8,128)(2,1)S(1)} %fusion.5.spect, ...), custom_call_target="tpu_custom_call" | custom-call | flops 5898240 | bytes 1769472 | tf_op jit(solution)/shard_map/whiten/pallas_call | solution.py:260
  3.4 6.1 %collective-permute-start = (bf16[2,16,1152]{2,1,0:T(8,128)(2,1)S(1)}, bf16[2,16,1152]{2,1,0:T(8,128)(2,1)S(1)}, u32[]{:S(2)}, u32[]{:S(2)}) collective-permute-start(bf16[2,16,1152]{2,1,0:T(8,128)(2,1)S(1)} %get-tuple-element.13), channel_id=1, source_target_pairs={{0,7},{1,6},{2,5},{3,4},{4,3},{5,2},{6,1},{7,0},{8,15},{9,14},{10,... | collective-permute-start | bytes 221192 | tf_op jit(solution)/shard_map/ppermute | solution.py:224
  9.4 0.2 collective-permute-start.1
  9.7 0.4 %collective-permute-start.2 = (bf16[2,16,1152]{2,1,0:T(8,128)(2,1)S(1)}, bf16[2,16,1152]{2,1,0:T(8,128)(2,1)S(1)}, u32[]{:S(2)}, u32[]{:S(2)}) collective-permute-start(bf16[2,16,1152]{2,1,0:T(8,128)(2,1)S(1)} %get-tuple-element.15), channel_id=1, source_target_pairs={{0,1},{1,0},{2,3},{3,2},{4,5},{5,4},{6,7},{7,6},{8,9},{9,8},{10,11... | collective-permute-start | bytes 221192 | tf_op jit(solution)/shard_map/ppermute | solution.py:224
  10.1 0.0 collective-permute-start.3
  10.1 5.2 %collective-permute-start.4 = (bf16[2,16,1152]{2,1,0:T(8,128)(2,1)S(1)}, bf16[2,16,1152]{2,1,0:T(8,128)(2,1)S(1)}, u32[]{:S(2)}, u32[]{:S(2)}) collective-permute-start(bf16[2,16,1152]{2,1,0:T(8,128)(2,1)S(1)} %get-tuple-element.17), channel_id=1, source_target_pairs={{0,5},{1,4},{2,7},{3,6},{4,1},{5,0},{6,3},{7,2},{8,13},{9,12},{10,... | collective-permute-start | bytes 221192 | tf_op jit(solution)/shard_map/ppermute | solution.py:224
  15.3 0.0 collective-permute-done.refs_0_
  15.3 0.3 collective-permute-start.5
  15.6 0.9 %collective-permute-done.1.refs_1_ = bf16[2,16,1152]{2,1,0:T(8,128)(2,1)S(1)} collective-permute-done((bf16[2,16,1152]{2,1,0:T(8,128)(2,1)S(1)}, bf16[2,16,1152]{2,1,0:T(8,128)(2,1)S(1)}, u32[]{:S(2)}, u32[]{:S(2)}) %collective-permute-start.1) | collective-permute-done | bytes 73760 | tf_op jit(solution)/shard_map/ppermute | solution.py:224
  16.5 1.3 %collective-permute-start.6 = (bf16[2,16,1152]{2,1,0:T(8,128)(2,1)S(1)}, bf16[2,16,1152]{2,1,0:T(8,128)(2,1)S(1)}, u32[]{:S(2)}, u32[]{:S(2)}) collective-permute-start(bf16[2,16,1152]{2,1,0:T(8,128)(2,1)S(1)} %get-tuple-element.19), channel_id=1, source_target_pairs={{0,3},{1,2},{2,1},{3,0},{4,7},{5,6},{6,5},{7,4},{8,11},{9,10},{10,... | collective-permute-start | bytes 221192 | tf_op jit(solution)/shard_map/ppermute | solution.py:224
  17.9 0.5 %collective-permute-start.7 = (bf16[2,16,1152]{2,1,0:T(8,128)(2,1)S(1)}, bf16[2,16,1152]{2,1,0:T(8,128)(2,1)S(1)}, u32[]{:S(2)}, u32[]{:S(2)}) collective-permute-start(bf16[2,16,1152]{2,1,0:T(8,128)(2,1)S(1)} %collective-permute-done.refs_0_), channel_id=1, source_target_pairs={{0,8},{8,0},{1,9},{9,1},{2,10},{10,2},{3,11},{11,3},{4,12},{12,4},... | collective-permute-start | bytes 221192 | tf_op jit(solution)/shard_map/ppermute | solution.py:228
  18.4 2.8 %collective-permute-done.4.refs_4_ = bf16[2,16,1152]{2,1,0:T(8,128)(2,1)S(1)} collective-permute-done((bf16[2,16,1152]{2,1,0:T(8,128)(2,1)S(1)}, bf16[2,16,1152]{2,1,0:T(8,128)(2,1)S(1)}, u32[]{:S(2)}, u32[]{:S(2)}) %collective-permute-start.4) | collective-permute-done | bytes 73760 | tf_op jit(solution)/shard_map/ppermute | solution.py:224
  21.2 0.0 collective-permute-start.8
  21.2 0.8 %collective-permute-done.5.refs_5_ = bf16[2,16,1152]{2,1,0:T(8,128)(2,1)S(1)} collective-permute-done((bf16[2,16,1152]{2,1,0:T(8,128)(2,1)S(1)}, bf16[2,16,1152]{2,1,0:T(8,128)(2,1)S(1)}, u32[]{:S(2)}, u32[]{:S(2)}) %collective-permute-start.5) | collective-permute-done | bytes 73760 | tf_op jit(solution)/shard_map/ppermute | solution.py:224
  22.0 0.0 collective-permute-start.9
  22.0 0.8 %collective-permute-done.6.refs_6_ = bf16[2,16,1152]{2,1,0:T(8,128)(2,1)S(1)} collective-permute-done((bf16[2,16,1152]{2,1,0:T(8,128)(2,1)S(1)}, bf16[2,16,1152]{2,1,0:T(8,128)(2,1)S(1)}, u32[]{:S(2)}, u32[]{:S(2)}) %collective-permute-start.6) | collective-permute-done | bytes 73760 | tf_op jit(solution)/shard_map/ppermute | solution.py:224
  22.8 0.0 collective-permute-start.10
  22.8 0.0 collective-permute-done.14.refs_15_
  22.8 0.5 %collective-permute-start.11 = (bf16[2,16,1152]{2,1,0:T(8,128)(2,1)S(1)}, bf16[2,16,1152]{2,1,0:T(8,128)(2,1)S(1)}, u32[]{:S(2)}, u32[]{:S(2)}) collective-permute-start(bf16[2,16,1152]{2,1,0:T(8,128)(2,1)S(1)} %collective-permute-done.4.refs_4_), channel_id=1, source_target_pairs={{0,8},{8,0},{1,9},{9,1},{2,10},{10,2},{3,11},{11,3},{4,12},{12,4},... | collective-permute-start | bytes 221192 | tf_op jit(solution)/shard_map/ppermute | solution.py:228
  23.3 0.0 collective-permute-done.7.refs_8_
  23.3 0.1 collective-permute-start.12
  23.4 0.0 collective-permute-done.8.refs_9_
  23.4 0.4 %collective-permute-start.13 = (bf16[2,16,1152]{2,1,0:T(8,128)(2,1)S(1)}, bf16[2,16,1152]{2,1,0:T(8,128)(2,1)S(1)}, u32[]{:S(2)}, u32[]{:S(2)}) collective-permute-start(bf16[2,16,1152]{2,1,0:T(8,128)(2,1)S(1)} %collective-permute-done.6.refs_6_), channel_id=1, source_target_pairs={{0,8},{8,0},{1,9},{9,1},{2,10},{10,2},{3,11},{11,3},{4,12},{12,4},... | collective-permute-start | bytes 221192 | tf_op jit(solution)/shard_map/ppermute | solution.py:228
  23.9 0.0 collective-permute-done.9.refs_10_
  23.9 0.2 collective-permute-done.10.refs_11_
  24.1 0.2 collective-permute-done.11.refs_12_
  24.2 0.4 collective-permute-done.12.refs_13_
  24.6 0.2 collective-permute-done.13.refs_14_
  24.8 15.1 %outer_products.1 = bf16[2,16,576,1152]{3,2,1,0:T(8,128)(2,1)} custom-call(bf16[2,16,1152]{2,1,0:T(8,128)(2,1)S(1)} %collective-permute-done.refs_0_, bf16[2,16,1152]{2,1,0:T(8,128)(2,1)S(1)} %collective-permute-done.1.refs_1_, bf16[2,16,1152]{2,1,0:T(8,128)(2,1)S(1)} %collective-permute-done.2.refs_2_, ...), custom_call_target="tpu_custom_call" | custom-call | flops 5435817984 | bytes 42467328 | tf_op jit(solution)/shard_map/outer_products/pallas_call | solution.py:282
  (6 shorter events, 0.0 us)
Async XLA Ops:
  0.0 1.8 %copy-start = (bf16[576,2,1024]{2,1,0:T(2,128)(2,1)S(1)}, bf16[576,2,1024]{2,1,0:T(2,128)(2,1)}, u32[]{:S(2)}) copy-start(bf16[576,2,1024]{2,1,0:T(2,128)(2,1)} %param.2) | copy-start | bytes 7077892
  0.0 1.2 %copy-start.1 = (bf16[1024,256]{1,0:T(8,128)(2,1)S(1)}, bf16[1024,256]{1,0:T(8,128)(2,1)}, u32[]{:S(2)}) copy-start(bf16[1024,256]{1,0:T(8,128)(2,1)} %constant.2.clone.in_ref) | copy-start | bytes 1572868
  3.4 11.9 %collective-permute-start = (bf16[2,16,1152]{2,1,0:T(8,128)(2,1)S(1)}, bf16[2,16,1152]{2,1,0:T(8,128)(2,1)S(1)}, u32[]{:S(2)}, u32[]{:S(2)}) collective-permute-start(bf16[2,16,1152]{2,1,0:T(8,128)(2,1)S(1)} %get-tuple-element.13), channel_id=1, source_target_pairs={{0,7},{1,6},{2,5},{3,4},{4,3},{5,2},{6,1},{7,0},{8,15},{9,14},{10,... | collective-permute-start | bytes 221192 | tf_op jit(solution)/shard_map/ppermute | solution.py:224
  9.4 7.1 %collective-permute-start.1 = (bf16[2,16,1152]{2,1,0:T(8,128)(2,1)S(1)}, bf16[2,16,1152]{2,1,0:T(8,128)(2,1)S(1)}, u32[]{:S(2)}, u32[]{:S(2)}) collective-permute-start(bf16[2,16,1152]{2,1,0:T(8,128)(2,1)S(1)} %get-tuple-element.14), channel_id=1, source_target_pairs={{0,6},{1,7},{2,4},{3,5},{4,2},{5,3},{6,0},{7,1},{8,14},{9,15},{10,... | collective-permute-start | bytes 221192 | tf_op jit(solution)/shard_map/ppermute | solution.py:224
  9.7 8.2 %collective-permute-start.2 = (bf16[2,16,1152]{2,1,0:T(8,128)(2,1)S(1)}, bf16[2,16,1152]{2,1,0:T(8,128)(2,1)S(1)}, u32[]{:S(2)}, u32[]{:S(2)}) collective-permute-start(bf16[2,16,1152]{2,1,0:T(8,128)(2,1)S(1)} %get-tuple-element.15), channel_id=1, source_target_pairs={{0,1},{1,0},{2,3},{3,2},{4,5},{5,4},{6,7},{7,6},{8,9},{9,8},{10,11... | collective-permute-start | bytes 221192 | tf_op jit(solution)/shard_map/ppermute | solution.py:224
  10.1 7.8 %collective-permute-start.3 = (bf16[2,16,1152]{2,1,0:T(8,128)(2,1)S(1)}, bf16[2,16,1152]{2,1,0:T(8,128)(2,1)S(1)}, u32[]{:S(2)}, u32[]{:S(2)}) collective-permute-start(bf16[2,16,1152]{2,1,0:T(8,128)(2,1)S(1)} %get-tuple-element.16), channel_id=1, source_target_pairs={{0,2},{1,3},{2,0},{3,1},{4,6},{5,7},{6,4},{7,5},{8,10},{9,11},{10,... | collective-permute-start | bytes 221192 | tf_op jit(solution)/shard_map/ppermute | solution.py:224
  10.1 11.1 %collective-permute-start.4 = (bf16[2,16,1152]{2,1,0:T(8,128)(2,1)S(1)}, bf16[2,16,1152]{2,1,0:T(8,128)(2,1)S(1)}, u32[]{:S(2)}, u32[]{:S(2)}) collective-permute-start(bf16[2,16,1152]{2,1,0:T(8,128)(2,1)S(1)} %get-tuple-element.17), channel_id=1, source_target_pairs={{0,5},{1,4},{2,7},{3,6},{4,1},{5,0},{6,3},{7,2},{8,13},{9,12},{10,... | collective-permute-start | bytes 221192 | tf_op jit(solution)/shard_map/ppermute | solution.py:224
  15.3 6.7 %collective-permute-start.5 = (bf16[2,16,1152]{2,1,0:T(8,128)(2,1)S(1)}, bf16[2,16,1152]{2,1,0:T(8,128)(2,1)S(1)}, u32[]{:S(2)}, u32[]{:S(2)}) collective-permute-start(bf16[2,16,1152]{2,1,0:T(8,128)(2,1)S(1)} %get-tuple-element.18), channel_id=1, source_target_pairs={{0,4},{1,5},{2,6},{3,7},{4,0},{5,1},{6,2},{7,3},{8,12},{9,13},{10,... | collective-permute-start | bytes 221192 | tf_op jit(solution)/shard_map/ppermute | solution.py:224
  16.5 6.3 %collective-permute-start.6 = (bf16[2,16,1152]{2,1,0:T(8,128)(2,1)S(1)}, bf16[2,16,1152]{2,1,0:T(8,128)(2,1)S(1)}, u32[]{:S(2)}, u32[]{:S(2)}) collective-permute-start(bf16[2,16,1152]{2,1,0:T(8,128)(2,1)S(1)} %get-tuple-element.19), channel_id=1, source_target_pairs={{0,3},{1,2},{2,1},{3,0},{4,7},{5,6},{6,5},{7,4},{8,11},{9,10},{10,... | collective-permute-start | bytes 221192 | tf_op jit(solution)/shard_map/ppermute | solution.py:224
  17.9 5.0 %collective-permute-start.14 = (bf16[2,16,1152]{2,1,0:T(8,128)(2,1)S(1)}, bf16[2,16,1152]{2,1,0:T(8,128)(2,1)S(1)}, u32[]{:S(2)}, u32[]{:S(2)}) collective-permute-start(bf16[2,16,1152]{2,1,0:T(8,128)(2,1)S(1)} %get-tuple-element.20.refs_7_), channel_id=1, source_target_pairs={{0,8},{8,0},{1,9},{9,1},{2,10},{10,2},{3,11},{11,3},{4,12},{12,4},... | collective-permute-start | bytes 221192 | tf_op jit(solution)/shard_map/ppermute | solution.py:228
  17.9 5.5 %collective-permute-start.7 = (bf16[2,16,1152]{2,1,0:T(8,128)(2,1)S(1)}, bf16[2,16,1152]{2,1,0:T(8,128)(2,1)S(1)}, u32[]{:S(2)}, u32[]{:S(2)}) collective-permute-start(bf16[2,16,1152]{2,1,0:T(8,128)(2,1)S(1)} %collective-permute-done.refs_0_), channel_id=1, source_target_pairs={{0,8},{8,0},{1,9},{9,1},{2,10},{10,2},{3,11},{11,3},{4,12},{12,4},... | collective-permute-start | bytes 221192 | tf_op jit(solution)/shard_map/ppermute | solution.py:228
  21.2 2.2 %collective-permute-start.8 = (bf16[2,16,1152]{2,1,0:T(8,128)(2,1)S(1)}, bf16[2,16,1152]{2,1,0:T(8,128)(2,1)S(1)}, u32[]{:S(2)}, u32[]{:S(2)}) collective-permute-start(bf16[2,16,1152]{2,1,0:T(8,128)(2,1)S(1)} %collective-permute-done.1.refs_1_), channel_id=1, source_target_pairs={{0,8},{8,0},{1,9},{9,1},{2,10},{10,2},{3,11},{11,3},{4,12},{12,4},... | collective-permute-start | bytes 221192 | tf_op jit(solution)/shard_map/ppermute | solution.py:228
  22.0 1.8 %collective-permute-start.9 = (bf16[2,16,1152]{2,1,0:T(8,128)(2,1)S(1)}, bf16[2,16,1152]{2,1,0:T(8,128)(2,1)S(1)}, u32[]{:S(2)}, u32[]{:S(2)}) collective-permute-start(bf16[2,16,1152]{2,1,0:T(8,128)(2,1)S(1)} %collective-permute-done.2.refs_2_), channel_id=1, source_target_pairs={{0,8},{8,0},{1,9},{9,1},{2,10},{10,2},{3,11},{11,3},{4,12},{12,4},... | collective-permute-start | bytes 221192 | tf_op jit(solution)/shard_map/ppermute | solution.py:228
  22.8 1.3 %collective-permute-start.10 = (bf16[2,16,1152]{2,1,0:T(8,128)(2,1)S(1)}, bf16[2,16,1152]{2,1,0:T(8,128)(2,1)S(1)}, u32[]{:S(2)}, u32[]{:S(2)}) collective-permute-start(bf16[2,16,1152]{2,1,0:T(8,128)(2,1)S(1)} %collective-permute-done.3.refs_3_), channel_id=1, source_target_pairs={{0,8},{8,0},{1,9},{9,1},{2,10},{10,2},{3,11},{11,3},{4,12},{12,4},... | collective-permute-start | bytes 221192 | tf_op jit(solution)/shard_map/ppermute | solution.py:228
  22.8 1.4 %collective-permute-start.11 = (bf16[2,16,1152]{2,1,0:T(8,128)(2,1)S(1)}, bf16[2,16,1152]{2,1,0:T(8,128)(2,1)S(1)}, u32[]{:S(2)}, u32[]{:S(2)}) collective-permute-start(bf16[2,16,1152]{2,1,0:T(8,128)(2,1)S(1)} %collective-permute-done.4.refs_4_), channel_id=1, source_target_pairs={{0,8},{8,0},{1,9},{9,1},{2,10},{10,2},{3,11},{11,3},{4,12},{12,4},... | collective-permute-start | bytes 221192 | tf_op jit(solution)/shard_map/ppermute | solution.py:228
  23.3 1.3 %collective-permute-start.12 = (bf16[2,16,1152]{2,1,0:T(8,128)(2,1)S(1)}, bf16[2,16,1152]{2,1,0:T(8,128)(2,1)S(1)}, u32[]{:S(2)}, u32[]{:S(2)}) collective-permute-start(bf16[2,16,1152]{2,1,0:T(8,128)(2,1)S(1)} %collective-permute-done.5.refs_5_), channel_id=1, source_target_pairs={{0,8},{8,0},{1,9},{9,1},{2,10},{10,2},{3,11},{11,3},{4,12},{12,4},... | collective-permute-start | bytes 221192 | tf_op jit(solution)/shard_map/ppermute | solution.py:228
  23.4 1.4 %collective-permute-start.13 = (bf16[2,16,1152]{2,1,0:T(8,128)(2,1)S(1)}, bf16[2,16,1152]{2,1,0:T(8,128)(2,1)S(1)}, u32[]{:S(2)}, u32[]{:S(2)}) collective-permute-start(bf16[2,16,1152]{2,1,0:T(8,128)(2,1)S(1)} %collective-permute-done.6.refs_6_), channel_id=1, source_target_pairs={{0,8},{8,0},{1,9},{9,1},{2,10},{10,2},{3,11},{11,3},{4,12},{12,4},... | collective-permute-start | bytes 221192 | tf_op jit(solution)/shard_map/ppermute | solution.py:228

commit v17 on v16

--- a/solution.py
+++ b/solution.py
@@ -241,7 +241,8 @@
     lanes = local_windows * local_channels
     vmem = pl.BlockSpec(memory_space=pltpu.VMEM)
     memory = pl.BlockSpec(memory_space=pl.ANY)
-    masks = [*range(devices - 1, devices - 3, -1), 1, 2, *range(devices - 3, 2, -1), 0]
+    masks = [*range(devices - 1, devices - 3, -1), 1, 2, devices - 3, 3]
+    masks = [*masks, *(mask for mask in range(devices - 4, 3, -1)), 0]
     masks = masks if aligned else [0]
     pieces = len(masks)
     rows = (devices, groups, 2 * bins, lanes) if aligned else (2 * BINS, lanes)

time: 40 us -> 39.7 us (level)
  transfers between devices with their start and end apart: 15 -> 15, of which waited for: 8 -> 7; matrix products, arithmetic and copies ran while one was open for 0% -> 0% of each run, Pallas kernels for 0% -> 0%
where the time goes in v17:
time: 39.7 us; the launch traced here: 39.6 us
  Pallas kernels  15.9 us (40%)
  starting transfers between devices  14.9 us (38%)
  waiting for transfers between devices  6.28 us (16%)
  local copies, waits for them, and re-layouts  1.78 us (4%)
  matrix products  0.79 us (2%)
    pallas_call x1, Pallas kernels, local(): pl.pallas_call(functools.partial(outer_kernel, bins, sets, 1.0 / windows)...  15.1 us
    ppermute x7, starting transfers between devices, exchange(): return lax.ppermute(value, 'freq', pairs) if mask else value  13.2 us
    ppermute x7, waiting for transfers between devices, exchange(): return lax.ppermute(value, 'freq', pairs) if mask else value  5.36 us
    unnamed x4, local copies, waits for them, and re-layouts  1.78 us
    ppermute x8, starting transfers between devices, swap(): return lax.ppermute(value, 'chan', [(0, 1), (1, 0)])  1.6 us
    ppermute x8, waiting for transfers between devices, swap(): return lax.ppermute(value, 'chan', [(0, 1), (1, 0)])  0.92 us
  transfers between devices with their start and end apart: 15, of which 7 were waited for; matrix products, arithmetic and copies ran while one was open for 0% of the time, Pallas kernels for 0%

profile of v17, /device:TPU:0, one launch (start us, length us, event | category | flops | bytes accessed | tf_op | source)
XLA Modules:
  0.0 39.6 jit_solution(14222578765184045625)
XLA Ops:
  0.0 1.2 %copy-done.1 = bf16[1024,256]{1,0:T(8,128)(2,1)S(1)} copy-done((bf16[1024,256]{1,0:T(8,128)(2,1)S(1)}, bf16[1024,256]{1,0:T(8,128)(2,1)}, u32[]{:S(2)}) %copy-start.1) | copy-done | bytes 524312
  1.2 0.6 %copy-done = bf16[576,2,1024]{2,1,0:T(2,128)(2,1)S(1)} copy-done((bf16[576,2,1024]{2,1,0:T(2,128)(2,1)S(1)}, bf16[576,2,1024]{2,1,0:T(2,128)(2,1)}, u32[]{:S(2)}) %copy-start) | copy-done | bytes 2359320
  1.8 0.8 %fusion.5.spectrum_ref = bf16[2,576,256]{2,1,0:T(8,128)(2,1)S(1)} fusion(bf16[576,2,1024]{2,1,0:T(2,128)(2,1)S(1)} %copy-done, bf16[1024,256]{1,0:T(8,128)(2,1)S(1)} %table.1), kind=kOutput, calls=%fused_computation.3 | convolution fusion | flops 604274688 | bytes 3473408 | tf_op jit(solution)/shard_map/cws,sj->wcj/dot_general | solution.py:258
  2.6 0.8 %whiten.1 = (bf16[2,16,1152]{2,1,0:T(8,128)(2,1)S(1)}, bf16[2,16,1152]{2,1,0:T(8,128)(2,1)S(1)}, bf16[2,16,1152]{2,1,0:T(8,128)(2,1)S(1)}, bf16[2,16,1152]{2,1,0...) custom-call(bf16[2,576,256]{2,1,0:T(8,128)(2,1)S(1)} %fusion.5.spect, ...), custom_call_target="tpu_custom_call" | custom-call | flops 5898240 | bytes 1769472 | tf_op jit(solution)/shard_map/whiten/pallas_call | solution.py:261
  3.4 6.1 %collective-permute-start = (bf16[2,16,1152]{2,1,0:T(8,128)(2,1)S(1)}, bf16[2,16,1152]{2,1,0:T(8,128)(2,1)S(1)}, u32[]{:S(2)}, u32[]{:S(2)}) collective-permute-start(bf16[2,16,1152]{2,1,0:T(8,128)(2,1)S(1)} %get-tuple-element.13), channel_id=1, source_target_pairs={{0,7},{1,6},{2,5},{3,4},{4,3},{5,2},{6,1},{7,0},{8,15},{9,14},{10,... | collective-permute-start | bytes 221192 | tf_op jit(solution)/shard_map/ppermute | solution.py:224
  9.4 0.2 collective-permute-start.1
  9.7 0.4 %collective-permute-start.2 = (bf16[2,16,1152]{2,1,0:T(8,128)(2,1)S(1)}, bf16[2,16,1152]{2,1,0:T(8,128)(2,1)S(1)}, u32[]{:S(2)}, u32[]{:S(2)}) collective-permute-start(bf16[2,16,1152]{2,1,0:T(8,128)(2,1)S(1)} %get-tuple-element.15), channel_id=1, source_target_pairs={{0,1},{1,0},{2,3},{3,2},{4,5},{5,4},{6,7},{7,6},{8,9},{9,8},{10,11... | collective-permute-start | bytes 221192 | tf_op jit(solution)/shard_map/ppermute | solution.py:224
  10.1 0.0 collective-permute-start.3
  10.1 5.2 %collective-permute-start.4 = (bf16[2,16,1152]{2,1,0:T(8,128)(2,1)S(1)}, bf16[2,16,1152]{2,1,0:T(8,128)(2,1)S(1)}, u32[]{:S(2)}, u32[]{:S(2)}) collective-permute-start(bf16[2,16,1152]{2,1,0:T(8,128)(2,1)S(1)} %get-tuple-element.17), channel_id=1, source_target_pairs={{0,5},{1,4},{2,7},{3,6},{4,1},{5,0},{6,3},{7,2},{8,13},{9,12},{10,... | collective-permute-start | bytes 221192 | tf_op jit(solution)/shard_map/ppermute | solution.py:224
  15.3 0.0 collective-permute-done.refs_0_
  15.3 0.0 collective-permute-start.5
  15.3 1.2 %collective-permute-done.1.refs_1_ = bf16[2,16,1152]{2,1,0:T(8,128)(2,1)S(1)} collective-permute-done((bf16[2,16,1152]{2,1,0:T(8,128)(2,1)S(1)}, bf16[2,16,1152]{2,1,0:T(8,128)(2,1)S(1)}, u32[]{:S(2)}, u32[]{:S(2)}) %collective-permute-start.1) | collective-permute-done | bytes 73760 | tf_op jit(solution)/shard_map/ppermute | solution.py:224
  16.5 1.3 %collective-permute-start.6 = (bf16[2,16,1152]{2,1,0:T(8,128)(2,1)S(1)}, bf16[2,16,1152]{2,1,0:T(8,128)(2,1)S(1)}, u32[]{:S(2)}, u32[]{:S(2)}) collective-permute-start(bf16[2,16,1152]{2,1,0:T(8,128)(2,1)S(1)} %get-tuple-element.19), channel_id=1, source_target_pairs={{0,4},{1,5},{2,6},{3,7},{4,0},{5,1},{6,2},{7,3},{8,12},{9,13},{10,... | collective-permute-start | bytes 221192 | tf_op jit(solution)/shard_map/ppermute | solution.py:224
  17.9 0.0 collective-permute-done.2.refs_2_
  17.9 0.0 collective-permute-start.14
  17.9 0.0 collective-permute-done.3.refs_3_
  17.9 0.5 %collective-permute-start.7 = (bf16[2,16,1152]{2,1,0:T(8,128)(2,1)S(1)}, bf16[2,16,1152]{2,1,0:T(8,128)(2,1)S(1)}, u32[]{:S(2)}, u32[]{:S(2)}) collective-permute-start(bf16[2,16,1152]{2,1,0:T(8,128)(2,1)S(1)} %collective-permute-done.refs_0_), channel_id=1, source_target_pairs={{0,8},{8,0},{1,9},{9,1},{2,10},{10,2},{3,11},{11,3},{4,12},{12,4},... | collective-permute-start | bytes 221192 | tf_op jit(solution)/shard_map/ppermute | solution.py:228
  18.4 0.0 collective-permute-done.4.refs_4_
  18.4 0.1 collective-permute-start.8
  18.5 2.3 %collective-permute-done.5.refs_5_ = bf16[2,16,1152]{2,1,0:T(8,128)(2,1)S(1)} collective-permute-done((bf16[2,16,1152]{2,1,0:T(8,128)(2,1)S(1)}, bf16[2,16,1152]{2,1,0:T(8,128)(2,1)S(1)}, u32[]{:S(2)}, u32[]{:S(2)}) %collective-permute-start.5) | collective-permute-done | bytes 73760 | tf_op jit(solution)/shard_map/ppermute | solution.py:224
  20.8 0.0 collective-permute-start.9
  20.8 1.8 %collective-permute-done.6.refs_6_ = bf16[2,16,1152]{2,1,0:T(8,128)(2,1)S(1)} collective-permute-done((bf16[2,16,1152]{2,1,0:T(8,128)(2,1)S(1)}, bf16[2,16,1152]{2,1,0:T(8,128)(2,1)S(1)}, u32[]{:S(2)}, u32[]{:S(2)}) %collective-permute-start.6) | collective-permute-done | bytes 73760 | tf_op jit(solution)/shard_map/ppermute | solution.py:224
  22.6 0.0 collective-permute-start.10
  22.6 0.5 %collective-permute-start.11 = (bf16[2,16,1152]{2,1,0:T(8,128)(2,1)S(1)}, bf16[2,16,1152]{2,1,0:T(8,128)(2,1)S(1)}, u32[]{:S(2)}, u32[]{:S(2)}) collective-permute-start(bf16[2,16,1152]{2,1,0:T(8,128)(2,1)S(1)} %collective-permute-done.4.refs_4_), channel_id=1, source_target_pairs={{0,8},{8,0},{1,9},{9,1},{2,10},{10,2},{3,11},{11,3},{4,12},{12,4},... | collective-permute-start | bytes 221192 | tf_op jit(solution)/shard_map/ppermute | solution.py:228
  23.1 0.1 collective-permute-start.12
  23.2 0.0 collective-permute-done.8.refs_9_
  23.2 0.4 %collective-permute-start.13 = (bf16[2,16,1152]{2,1,0:T(8,128)(2,1)S(1)}, bf16[2,16,1152]{2,1,0:T(8,128)(2,1)S(1)}, u32[]{:S(2)}, u32[]{:S(2)}) collective-permute-start(bf16[2,16,1152]{2,1,0:T(8,128)(2,1)S(1)} %collective-permute-done.6.refs_6_), channel_id=1, source_target_pairs={{0,8},{8,0},{1,9},{9,1},{2,10},{10,2},{3,11},{11,3},{4,12},{12,4},... | collective-permute-start | bytes 221192 | tf_op jit(solution)/shard_map/ppermute | solution.py:228
  23.6 0.2 collective-permute-done.10.refs_11_
  23.8 0.2 collective-permute-done.11.refs_12_
  24.0 0.4 collective-permute-done.12.refs_13_
  24.4 0.2 collective-permute-done.13.refs_14_
  24.5 15.1 %outer_products.1 = bf16[2,16,576,1152]{3,2,1,0:T(8,128)(2,1)} custom-call(bf16[2,16,1152]{2,1,0:T(8,128)(2,1)S(1)} %collective-permute-done.refs_0_, bf16[2,16,1152]{2,1,0:T(8,128)(2,1)S(1)} %collective-permute-done.1.refs_1_, bf16[2,16,1152]{2,1,0:T(8,128)(2,1)S(1)} %collective-permute-done.2.refs_2_, ...), custom_call_target="tpu_custom_call" | custom-call | flops 5435817984 | bytes 42467328 | tf_op jit(solution)/shard_map/outer_products/pallas_call | solution.py:283
  (6 shorter events, 0.0 us)
Async XLA Ops:
  0.0 1.8 %copy-start = (bf16[576,2,1024]{2,1,0:T(2,128)(2,1)S(1)}, bf16[576,2,1024]{2,1,0:T(2,128)(2,1)}, u32[]{:S(2)}) copy-start(bf16[576,2,1024]{2,1,0:T(2,128)(2,1)} %param.2) | copy-start | bytes 7077892
  0.0 1.2 %copy-start.1 = (bf16[1024,256]{1,0:T(8,128)(2,1)S(1)}, bf16[1024,256]{1,0:T(8,128)(2,1)}, u32[]{:S(2)}) copy-start(bf16[1024,256]{1,0:T(8,128)(2,1)} %constant.2.clone.in_ref) | copy-start | bytes 1572868
  3.4 11.9 %collective-permute-start = (bf16[2,16,1152]{2,1,0:T(8,128)(2,1)S(1)}, bf16[2,16,1152]{2,1,0:T(8,128)(2,1)S(1)}, u32[]{:S(2)}, u32[]{:S(2)}) collective-permute-start(bf16[2,16,1152]{2,1,0:T(8,128)(2,1)S(1)} %get-tuple-element.13), channel_id=1, source_target_pairs={{0,7},{1,6},{2,5},{3,4},{4,3},{5,2},{6,1},{7,0},{8,15},{9,14},{10,... | collective-permute-start | bytes 221192 | tf_op jit(solution)/shard_map/ppermute | solution.py:224
  9.4 7.1 %collective-permute-start.1 = (bf16[2,16,1152]{2,1,0:T(8,128)(2,1)S(1)}, bf16[2,16,1152]{2,1,0:T(8,128)(2,1)S(1)}, u32[]{:S(2)}, u32[]{:S(2)}) collective-permute-start(bf16[2,16,1152]{2,1,0:T(8,128)(2,1)S(1)} %get-tuple-element.14), channel_id=1, source_target_pairs={{0,6},{1,7},{2,4},{3,5},{4,2},{5,3},{6,0},{7,1},{8,14},{9,15},{10,... | collective-permute-start | bytes 221192 | tf_op jit(solution)/shard_map/ppermute | solution.py:224
  9.7 8.2 %collective-permute-start.2 = (bf16[2,16,1152]{2,1,0:T(8,128)(2,1)S(1)}, bf16[2,16,1152]{2,1,0:T(8,128)(2,1)S(1)}, u32[]{:S(2)}, u32[]{:S(2)}) collective-permute-start(bf16[2,16,1152]{2,1,0:T(8,128)(2,1)S(1)} %get-tuple-element.15), channel_id=1, source_target_pairs={{0,1},{1,0},{2,3},{3,2},{4,5},{5,4},{6,7},{7,6},{8,9},{9,8},{10,11... | collective-permute-start | bytes 221192 | tf_op jit(solution)/shard_map/ppermute | solution.py:224
  10.1 7.8 %collective-permute-start.3 = (bf16[2,16,1152]{2,1,0:T(8,128)(2,1)S(1)}, bf16[2,16,1152]{2,1,0:T(8,128)(2,1)S(1)}, u32[]{:S(2)}, u32[]{:S(2)}) collective-permute-start(bf16[2,16,1152]{2,1,0:T(8,128)(2,1)S(1)} %get-tuple-element.16), channel_id=1, source_target_pairs={{0,2},{1,3},{2,0},{3,1},{4,6},{5,7},{6,4},{7,5},{8,10},{9,11},{10,... | collective-permute-start | bytes 221192 | tf_op jit(solution)/shard_map/ppermute | solution.py:224
  10.1 8.3 %collective-permute-start.4 = (bf16[2,16,1152]{2,1,0:T(8,128)(2,1)S(1)}, bf16[2,16,1152]{2,1,0:T(8,128)(2,1)S(1)}, u32[]{:S(2)}, u32[]{:S(2)}) collective-permute-start(bf16[2,16,1152]{2,1,0:T(8,128)(2,1)S(1)} %get-tuple-element.17), channel_id=1, source_target_pairs={{0,5},{1,4},{2,7},{3,6},{4,1},{5,0},{6,3},{7,2},{8,13},{9,12},{10,... | collective-permute-start | bytes 221192 | tf_op jit(solution)/shard_map/ppermute | solution.py:224
  15.3 5.5 %collective-permute-start.5 = (bf16[2,16,1152]{2,1,0:T(8,128)(2,1)S(1)}, bf16[2,16,1152]{2,1,0:T(8,128)(2,1)S(1)}, u32[]{:S(2)}, u32[]{:S(2)}) collective-permute-start(bf16[2,16,1152]{2,1,0:T(8,128)(2,1)S(1)} %get-tuple-element.18), channel_id=1, source_target_pairs={{0,3},{1,2},{2,1},{3,0},{4,7},{5,6},{6,5},{7,4},{8,11},{9,10},{10,... | collective-permute-start | bytes 221192 | tf_op jit(solution)/shard_map/ppermute | solution.py:224
  16.5 6.0 %collective-permute-start.6 = (bf16[2,16,1152]{2,1,0:T(8,128)(2,1)S(1)}, bf16[2,16,1152]{2,1,0:T(8,128)(2,1)S(1)}, u32[]{:S(2)}, u32[]{:S(2)}) collective-permute-start(bf16[2,16,1152]{2,1,0:T(8,128)(2,1)S(1)} %get-tuple-element.19), channel_id=1, source_target_pairs={{0,4},{1,5},{2,6},{3,7},{4,0},{5,1},{6,2},{7,3},{8,12},{9,13},{10,... | collective-permute-start | bytes 221192 | tf_op jit(solution)/shard_map/ppermute | solution.py:224
  17.9 4.7 %collective-permute-start.14 = (bf16[2,16,1152]{2,1,0:T(8,128)(2,1)S(1)}, bf16[2,16,1152]{2,1,0:T(8,128)(2,1)S(1)}, u32[]{:S(2)}, u32[]{:S(2)}) collective-permute-start(bf16[2,16,1152]{2,1,0:T(8,128)(2,1)S(1)} %get-tuple-element.20.refs_7_), channel_id=1, source_target_pairs={{0,8},{8,0},{1,9},{9,1},{2,10},{10,2},{3,11},{11,3},{4,12},{12,4},... | collective-permute-start | bytes 221192 | tf_op jit(solution)/shard_map/ppermute | solution.py:228
  17.9 5.2 %collective-permute-start.7 = (bf16[2,16,1152]{2,1,0:T(8,128)(2,1)S(1)}, bf16[2,16,1152]{2,1,0:T(8,128)(2,1)S(1)}, u32[]{:S(2)}, u32[]{:S(2)}) collective-permute-start(bf16[2,16,1152]{2,1,0:T(8,128)(2,1)S(1)} %collective-permute-done.refs_0_), channel_id=1, source_target_pairs={{0,8},{8,0},{1,9},{9,1},{2,10},{10,2},{3,11},{11,3},{4,12},{12,4},... | collective-permute-start | bytes 221192 | tf_op jit(solution)/shard_map/ppermute | solution.py:228
  18.4 4.8 %collective-permute-start.8 = (bf16[2,16,1152]{2,1,0:T(8,128)(2,1)S(1)}, bf16[2,16,1152]{2,1,0:T(8,128)(2,1)S(1)}, u32[]{:S(2)}, u32[]{:S(2)}) collective-permute-start(bf16[2,16,1152]{2,1,0:T(8,128)(2,1)S(1)} %collective-permute-done.1.refs_1_), channel_id=1, source_target_pairs={{0,8},{8,0},{1,9},{9,1},{2,10},{10,2},{3,11},{11,3},{4,12},{12,4},... | collective-permute-start | bytes 221192 | tf_op jit(solution)/shard_map/ppermute | solution.py:228
  20.8 2.8 %collective-permute-start.9 = (bf16[2,16,1152]{2,1,0:T(8,128)(2,1)S(1)}, bf16[2,16,1152]{2,1,0:T(8,128)(2,1)S(1)}, u32[]{:S(2)}, u32[]{:S(2)}) collective-permute-start(bf16[2,16,1152]{2,1,0:T(8,128)(2,1)S(1)} %collective-permute-done.2.refs_2_), channel_id=1, source_target_pairs={{0,8},{8,0},{1,9},{9,1},{2,10},{10,2},{3,11},{11,3},{4,12},{12,4},... | collective-permute-start | bytes 221192 | tf_op jit(solution)/shard_map/ppermute | solution.py:228
  22.6 1.3 %collective-permute-start.10 = (bf16[2,16,1152]{2,1,0:T(8,128)(2,1)S(1)}, bf16[2,16,1152]{2,1,0:T(8,128)(2,1)S(1)}, u32[]{:S(2)}, u32[]{:S(2)}) collective-permute-start(bf16[2,16,1152]{2,1,0:T(8,128)(2,1)S(1)} %collective-permute-done.3.refs_3_), channel_id=1, source_target_pairs={{0,8},{8,0},{1,9},{9,1},{2,10},{10,2},{3,11},{11,3},{4,12},{12,4},... | collective-permute-start | bytes 221192 | tf_op jit(solution)/shard_map/ppermute | solution.py:228
  22.6 1.4 %collective-permute-start.11 = (bf16[2,16,1152]{2,1,0:T(8,128)(2,1)S(1)}, bf16[2,16,1152]{2,1,0:T(8,128)(2,1)S(1)}, u32[]{:S(2)}, u32[]{:S(2)}) collective-permute-start(bf16[2,16,1152]{2,1,0:T(8,128)(2,1)S(1)} %collective-permute-done.4.refs_4_), channel_id=1, source_target_pairs={{0,8},{8,0},{1,9},{9,1},{2,10},{10,2},{3,11},{11,3},{4,12},{12,4},... | collective-permute-start | bytes 221192 | tf_op jit(solution)/shard_map/ppermute | solution.py:228
  23.1 1.3 %collective-permute-start.12 = (bf16[2,16,1152]{2,1,0:T(8,128)(2,1)S(1)}, bf16[2,16,1152]{2,1,0:T(8,128)(2,1)S(1)}, u32[]{:S(2)}, u32[]{:S(2)}) collective-permute-start(bf16[2,16,1152]{2,1,0:T(8,128)(2,1)S(1)} %collective-permute-done.5.refs_5_), channel_id=1, source_target_pairs={{0,8},{8,0},{1,9},{9,1},{2,10},{10,2},{3,11},{11,3},{4,12},{12,4},... | collective-permute-start | bytes 221192 | tf_op jit(solution)/shard_map/ppermute | solution.py:228
  23.2 1.4 %collective-permute-start.13 = (bf16[2,16,1152]{2,1,0:T(8,128)(2,1)S(1)}, bf16[2,16,1152]{2,1,0:T(8,128)(2,1)S(1)}, u32[]{:S(2)}, u32[]{:S(2)}) collective-permute-start(bf16[2,16,1152]{2,1,0:T(8,128)(2,1)S(1)} %collective-permute-done.6.refs_6_), channel_id=1, source_target_pairs={{0,8},{8,0},{1,9},{9,1},{2,10},{10,2},{3,11},{11,3},{4,12},{12,4},... | collective-permute-start | bytes 221192 | tf_op jit(solution)/shard_map/ppermute | solution.py:228

commit v18 on v17

--- a/solution.py
+++ b/solution.py
@@ -241,7 +241,7 @@
     lanes = local_windows * local_channels
     vmem = pl.BlockSpec(memory_space=pltpu.VMEM)
     memory = pl.BlockSpec(memory_space=pl.ANY)
-    masks = [*range(devices - 1, devices - 3, -1), 1, 2, devices - 3, 3]
+    masks = [*range(devices - 1, devices - 3, -1), 2, 3, devices - 3, 1]
     masks = [*masks, *(mask for mask in range(devices - 4, 3, -1)), 0]
     masks = masks if aligned else [0]
     pieces = len(masks)

time: 39.7 us -> 39.7 us (level)
  starting transfers between devices: 14.9 us -> 13.6 us
  waiting for transfers between devices: 6.28 us -> 7.46 us
    ppermute x7, waiting for transfers between devices: 5.36 us -> 6.54 us  [exchange(): return lax.ppermute(value, 'freq', pairs) if mask else value]
    ppermute x7, starting transfers between devices: 13.2 us -> 12.6 us  [exchange(): return lax.ppermute(value, 'freq', pairs) if mask else value]
    ppermute x8, starting transfers between devices: 1.6 us -> 1.03 us  [swap(): return lax.ppermute(value, 'chan', [(0, 1), (1, 0)])]
  transfers between devices with their start and end apart: 15 -> 15, of which waited for: 7 -> 9; matrix products, arithmetic and copies ran while one was open for 0% -> 0% of each run, Pallas kernels for 0% -> 0%
where the time goes in v18:
time: 39.7 us; the launch traced here: 39.5 us
  Pallas kernels  15.8 us (40%)
  starting transfers between devices  13.6 us (34%)
  waiting for transfers between devices  7.46 us (19%)
  local copies, waits for them, and re-layouts  1.78 us (4%)
  matrix products  0.79 us (2%)
    pallas_call x1, Pallas kernels, local(): pl.pallas_call(functools.partial(outer_kernel, bins, sets, 1.0 / windows)...  15.1 us
    ppermute x7, starting transfers between devices, exchange(): return lax.ppermute(value, 'freq', pairs) if mask else value  12.6 us
    ppermute x7, waiting for transfers between devices, exchange(): return lax.ppermute(value, 'freq', pairs) if mask else value  6.54 us
    unnamed x4, local copies, waits for them, and re-layouts  1.78 us
    ppermute x8, starting transfers between devices, swap(): return lax.ppermute(value, 'chan', [(0, 1), (1, 0)])  1.03 us
    ppermute x8, waiting for transfers between devices, swap(): return lax.ppermute(value, 'chan', [(0, 1), (1, 0)])  0.92 us
  transfers between devices with their start and end apart: 15, of which 9 were waited for; matrix products, arithmetic and copies ran while one was open for 0% of the time, Pallas kernels for 0%

profile of v18, /device:TPU:0, one launch (start us, length us, event | category | flops | bytes accessed | tf_op | source)
XLA Modules:
  0.0 39.5 jit_solution(5728991759373425588)
XLA Ops:
  0.0 1.2 %copy-done.1 = bf16[1024,256]{1,0:T(8,128)(2,1)S(1)} copy-done((bf16[1024,256]{1,0:T(8,128)(2,1)S(1)}, bf16[1024,256]{1,0:T(8,128)(2,1)}, u32[]{:S(2)}) %copy-start.1) | copy-done | bytes 524312
  1.2 0.6 %copy-done = bf16[576,2,1024]{2,1,0:T(2,128)(2,1)S(1)} copy-done((bf16[576,2,1024]{2,1,0:T(2,128)(2,1)S(1)}, bf16[576,2,1024]{2,1,0:T(2,128)(2,1)}, u32[]{:S(2)}) %copy-start) | copy-done | bytes 2359320
  1.8 0.8 %fusion.5.spectrum_ref = bf16[2,576,256]{2,1,0:T(8,128)(2,1)S(1)} fusion(bf16[576,2,1024]{2,1,0:T(2,128)(2,1)S(1)} %copy-done, bf16[1024,256]{1,0:T(8,128)(2,1)S(1)} %table.1), kind=kOutput, calls=%fused_computation.3 | convolution fusion | flops 604274688 | bytes 3473408 | tf_op jit(solution)/shard_map/cws,sj->wcj/dot_general | solution.py:258
  2.6 0.8 %whiten.1 = (bf16[2,16,1152]{2,1,0:T(8,128)(2,1)S(1)}, bf16[2,16,1152]{2,1,0:T(8,128)(2,1)S(1)}, bf16[2,16,1152]{2,1,0:T(8,128)(2,1)S(1)}, bf16[2,16,1152]{2,1,0...) custom-call(bf16[2,576,256]{2,1,0:T(8,128)(2,1)S(1)} %fusion.5.spect, ...), custom_call_target="tpu_custom_call" | custom-call | flops 5898240 | bytes 1769472 | tf_op jit(solution)/shard_map/whiten/pallas_call | solution.py:261
  3.4 6.1 %collective-permute-start = (bf16[2,16,1152]{2,1,0:T(8,128)(2,1)S(1)}, bf16[2,16,1152]{2,1,0:T(8,128)(2,1)S(1)}, u32[]{:S(2)}, u32[]{:S(2)}) collective-permute-start(bf16[2,16,1152]{2,1,0:T(8,128)(2,1)S(1)} %get-tuple-element.13), channel_id=1, source_target_pairs={{0,7},{1,6},{2,5},{3,4},{4,3},{5,2},{6,1},{7,0},{8,15},{9,14},{10,... | collective-permute-start | bytes 221192 | tf_op jit(solution)/shard_map/ppermute | solution.py:224
  9.4 0.2 collective-permute-start.1
  9.7 0.0 collective-permute-start.2
  9.7 1.9 %collective-permute-start.3 = (bf16[2,16,1152]{2,1,0:T(8,128)(2,1)S(1)}, bf16[2,16,1152]{2,1,0:T(8,128)(2,1)S(1)}, u32[]{:S(2)}, u32[]{:S(2)}) collective-permute-start(bf16[2,16,1152]{2,1,0:T(8,128)(2,1)S(1)} %get-tuple-element.16), channel_id=1, source_target_pairs={{0,3},{1,2},{2,1},{3,0},{4,7},{5,6},{6,5},{7,4},{8,11},{9,10},{10,... | collective-permute-start | bytes 221192 | tf_op jit(solution)/shard_map/ppermute | solution.py:224
  11.6 3.2 %collective-permute-start.4 = (bf16[2,16,1152]{2,1,0:T(8,128)(2,1)S(1)}, bf16[2,16,1152]{2,1,0:T(8,128)(2,1)S(1)}, u32[]{:S(2)}, u32[]{:S(2)}) collective-permute-start(bf16[2,16,1152]{2,1,0:T(8,128)(2,1)S(1)} %get-tuple-element.17), channel_id=1, source_target_pairs={{0,5},{1,4},{2,7},{3,6},{4,1},{5,0},{6,3},{7,2},{8,13},{9,12},{10,... | collective-permute-start | bytes 221192 | tf_op jit(solution)/shard_map/ppermute | solution.py:224
  14.7 0.0 collective-permute-done.refs_0_
  14.7 0.6 %collective-permute-start.5 = (bf16[2,16,1152]{2,1,0:T(8,128)(2,1)S(1)}, bf16[2,16,1152]{2,1,0:T(8,128)(2,1)S(1)}, u32[]{:S(2)}, u32[]{:S(2)}) collective-permute-start(bf16[2,16,1152]{2,1,0:T(8,128)(2,1)S(1)} %get-tuple-element.18), channel_id=1, source_target_pairs={{0,1},{1,0},{2,3},{3,2},{4,5},{5,4},{6,7},{7,6},{8,9},{9,8},{10,11... | collective-permute-start | bytes 221192 | tf_op jit(solution)/shard_map/ppermute | solution.py:224
  15.3 1.2 %collective-permute-done.1.refs_1_ = bf16[2,16,1152]{2,1,0:T(8,128)(2,1)S(1)} collective-permute-done((bf16[2,16,1152]{2,1,0:T(8,128)(2,1)S(1)}, bf16[2,16,1152]{2,1,0:T(8,128)(2,1)S(1)}, u32[]{:S(2)}, u32[]{:S(2)}) %collective-permute-start.1) | collective-permute-done | bytes 73760 | tf_op jit(solution)/shard_map/ppermute | solution.py:224
  16.5 0.7 %collective-permute-start.6 = (bf16[2,16,1152]{2,1,0:T(8,128)(2,1)S(1)}, bf16[2,16,1152]{2,1,0:T(8,128)(2,1)S(1)}, u32[]{:S(2)}, u32[]{:S(2)}) collective-permute-start(bf16[2,16,1152]{2,1,0:T(8,128)(2,1)S(1)} %get-tuple-element.19), channel_id=1, source_target_pairs={{0,4},{1,5},{2,6},{3,7},{4,0},{5,1},{6,2},{7,3},{8,12},{9,13},{10,... | collective-permute-start | bytes 221192 | tf_op jit(solution)/shard_map/ppermute | solution.py:224
  17.2 0.0 collective-permute-done.2.refs_2_
  17.2 0.0 collective-permute-start.14
  17.2 0.7 %collective-permute-done.3.refs_3_ = bf16[2,16,1152]{2,1,0:T(8,128)(2,1)S(1)} collective-permute-done((bf16[2,16,1152]{2,1,0:T(8,128)(2,1)S(1)}, bf16[2,16,1152]{2,1,0:T(8,128)(2,1)S(1)}, u32[]{:S(2)}, u32[]{:S(2)}) %collective-permute-start.3) | collective-permute-done | bytes 73760 | tf_op jit(solution)/shard_map/ppermute | solution.py:224
  17.9 0.0 collective-permute-start.7
  17.9 0.8 %collective-permute-done.4.refs_4_ = bf16[2,16,1152]{2,1,0:T(8,128)(2,1)S(1)} collective-permute-done((bf16[2,16,1152]{2,1,0:T(8,128)(2,1)S(1)}, bf16[2,16,1152]{2,1,0:T(8,128)(2,1)S(1)}, u32[]{:S(2)}, u32[]{:S(2)}) %collective-permute-start.4) | collective-permute-done | bytes 73760 | tf_op jit(solution)/shard_map/ppermute | solution.py:224
  18.7 0.0 collective-permute-start.8
  18.7 1.0 %collective-permute-done.5.refs_5_ = bf16[2,16,1152]{2,1,0:T(8,128)(2,1)S(1)} collective-permute-done((bf16[2,16,1152]{2,1,0:T(8,128)(2,1)S(1)}, bf16[2,16,1152]{2,1,0:T(8,128)(2,1)S(1)}, u32[]{:S(2)}, u32[]{:S(2)}) %collective-permute-start.5) | collective-permute-done | bytes 73760 | tf_op jit(solution)/shard_map/ppermute | solution.py:224
  19.7 0.0 collective-permute-start.9
  19.7 2.8 %collective-permute-done.6.refs_6_ = bf16[2,16,1152]{2,1,0:T(8,128)(2,1)S(1)} collective-permute-done((bf16[2,16,1152]{2,1,0:T(8,128)(2,1)S(1)}, bf16[2,16,1152]{2,1,0:T(8,128)(2,1)S(1)}, u32[]{:S(2)}, u32[]{:S(2)}) %collective-permute-start.6) | collective-permute-done | bytes 73760 | tf_op jit(solution)/shard_map/ppermute | solution.py:224
  22.5 0.0 collective-permute-start.10
  22.5 0.5 %collective-permute-start.11 = (bf16[2,16,1152]{2,1,0:T(8,128)(2,1)S(1)}, bf16[2,16,1152]{2,1,0:T(8,128)(2,1)S(1)}, u32[]{:S(2)}, u32[]{:S(2)}) collective-permute-start(bf16[2,16,1152]{2,1,0:T(8,128)(2,1)S(1)} %collective-permute-done.4.refs_4_), channel_id=1, source_target_pairs={{0,8},{8,0},{1,9},{9,1},{2,10},{10,2},{3,11},{11,3},{4,12},{12,4},... | collective-permute-start | bytes 221192 | tf_op jit(solution)/shard_map/ppermute | solution.py:228
  23.1 0.0 collective-permute-done.7.refs_8_
  23.1 0.1 collective-permute-start.12
  23.1 0.4 %collective-permute-start.13 = (bf16[2,16,1152]{2,1,0:T(8,128)(2,1)S(1)}, bf16[2,16,1152]{2,1,0:T(8,128)(2,1)S(1)}, u32[]{:S(2)}, u32[]{:S(2)}) collective-permute-start(bf16[2,16,1152]{2,1,0:T(8,128)(2,1)S(1)} %collective-permute-done.6.refs_6_), channel_id=1, source_target_pairs={{0,8},{8,0},{1,9},{9,1},{2,10},{10,2},{3,11},{11,3},{4,12},{12,4},... | collective-permute-start | bytes 221192 | tf_op jit(solution)/shard_map/ppermute | solution.py:228
  23.6 0.2 collective-permute-done.10.refs_11_
  23.8 0.2 collective-permute-done.11.refs_12_
  24.0 0.4 collective-permute-done.12.refs_13_
  24.3 0.2 collective-permute-done.13.refs_14_
  24.5 15.1 %outer_products.1 = bf16[2,16,576,1152]{3,2,1,0:T(8,128)(2,1)} custom-call(bf16[2,16,1152]{2,1,0:T(8,128)(2,1)S(1)} %collective-permute-done.refs_0_, bf16[2,16,1152]{2,1,0:T(8,128)(2,1)S(1)} %collective-permute-done.1.refs_1_, bf16[2,16,1152]{2,1,0:T(8,128)(2,1)S(1)} %collective-permute-done.2.refs_2_, ...), custom_call_target="tpu_custom_call" | custom-call | flops 5435817984 | bytes 42467328 | tf_op jit(solution)/shard_map/outer_products/pallas_call | solution.py:283
  (6 shorter events, 0.0 us)
Async XLA Ops:
  0.0 1.8 %copy-start = (bf16[576,2,1024]{2,1,0:T(2,128)(2,1)S(1)}, bf16[576,2,1024]{2,1,0:T(2,128)(2,1)}, u32[]{:S(2)}) copy-start(bf16[576,2,1024]{2,1,0:T(2,128)(2,1)} %param.2) | copy-start | bytes 7077892
  0.0 1.2 %copy-start.1 = (bf16[1024,256]{1,0:T(8,128)(2,1)S(1)}, bf16[1024,256]{1,0:T(8,128)(2,1)}, u32[]{:S(2)}) copy-start(bf16[1024,256]{1,0:T(8,128)(2,1)} %constant.2.clone.in_ref) | copy-start | bytes 1572868
  3.4 11.4 %collective-permute-start = (bf16[2,16,1152]{2,1,0:T(8,128)(2,1)S(1)}, bf16[2,16,1152]{2,1,0:T(8,128)(2,1)S(1)}, u32[]{:S(2)}, u32[]{:S(2)}) collective-permute-start(bf16[2,16,1152]{2,1,0:T(8,128)(2,1)S(1)} %get-tuple-element.13), channel_id=1, source_target_pairs={{0,7},{1,6},{2,5},{3,4},{4,3},{5,2},{6,1},{7,0},{8,15},{9,14},{10,... | collective-permute-start | bytes 221192 | tf_op jit(solution)/shard_map/ppermute | solution.py:224
  9.4 7.1 %collective-permute-start.1 = (bf16[2,16,1152]{2,1,0:T(8,128)(2,1)S(1)}, bf16[2,16,1152]{2,1,0:T(8,128)(2,1)S(1)}, u32[]{:S(2)}, u32[]{:S(2)}) collective-permute-start(bf16[2,16,1152]{2,1,0:T(8,128)(2,1)S(1)} %get-tuple-element.14), channel_id=1, source_target_pairs={{0,6},{1,7},{2,4},{3,5},{4,2},{5,3},{6,0},{7,1},{8,14},{9,15},{10,... | collective-permute-start | bytes 221192 | tf_op jit(solution)/shard_map/ppermute | solution.py:224
  9.7 7.5 %collective-permute-start.2 = (bf16[2,16,1152]{2,1,0:T(8,128)(2,1)S(1)}, bf16[2,16,1152]{2,1,0:T(8,128)(2,1)S(1)}, u32[]{:S(2)}, u32[]{:S(2)}) collective-permute-start(bf16[2,16,1152]{2,1,0:T(8,128)(2,1)S(1)} %get-tuple-element.15), channel_id=1, source_target_pairs={{0,2},{1,3},{2,0},{3,1},{4,6},{5,7},{6,4},{7,5},{8,10},{9,11},{10,... | collective-permute-start | bytes 221192 | tf_op jit(solution)/shard_map/ppermute | solution.py:224
  9.7 8.2 %collective-permute-start.3 = (bf16[2,16,1152]{2,1,0:T(8,128)(2,1)S(1)}, bf16[2,16,1152]{2,1,0:T(8,128)(2,1)S(1)}, u32[]{:S(2)}, u32[]{:S(2)}) collective-permute-start(bf16[2,16,1152]{2,1,0:T(8,128)(2,1)S(1)} %get-tuple-element.16), channel_id=1, source_target_pairs={{0,3},{1,2},{2,1},{3,0},{4,7},{5,6},{6,5},{7,4},{8,11},{9,10},{10,... | collective-permute-start | bytes 221192 | tf_op jit(solution)/shard_map/ppermute | solution.py:224
  11.6 7.2 %collective-permute-start.4 = (bf16[2,16,1152]{2,1,0:T(8,128)(2,1)S(1)}, bf16[2,16,1152]{2,1,0:T(8,128)(2,1)S(1)}, u32[]{:S(2)}, u32[]{:S(2)}) collective-permute-start(bf16[2,16,1152]{2,1,0:T(8,128)(2,1)S(1)} %get-tuple-element.17), channel_id=1, source_target_pairs={{0,5},{1,4},{2,7},{3,6},{4,1},{5,0},{6,3},{7,2},{8,13},{9,12},{10,... | collective-permute-start | bytes 221192 | tf_op jit(solution)/shard_map/ppermute | solution.py:224
  14.7 5.0 %collective-permute-start.5 = (bf16[2,16,1152]{2,1,0:T(8,128)(2,1)S(1)}, bf16[2,16,1152]{2,1,0:T(8,128)(2,1)S(1)}, u32[]{:S(2)}, u32[]{:S(2)}) collective-permute-start(bf16[2,16,1152]{2,1,0:T(8,128)(2,1)S(1)} %get-tuple-element.18), channel_id=1, source_target_pairs={{0,1},{1,0},{2,3},{3,2},{4,5},{5,4},{6,7},{7,6},{8,9},{9,8},{10,11... | collective-permute-start | bytes 221192 | tf_op jit(solution)/shard_map/ppermute | solution.py:224
  16.5 6.0 %collective-permute-start.6 = (bf16[2,16,1152]{2,1,0:T(8,128)(2,1)S(1)}, bf16[2,16,1152]{2,1,0:T(8,128)(2,1)S(1)}, u32[]{:S(2)}, u32[]{:S(2)}) collective-permute-start(bf16[2,16,1152]{2,1,0:T(8,128)(2,1)S(1)} %get-tuple-element.19), channel_id=1, source_target_pairs={{0,4},{1,5},{2,6},{3,7},{4,0},{5,1},{6,2},{7,3},{8,12},{9,13},{10,... | collective-permute-start | bytes 221192 | tf_op jit(solution)/shard_map/ppermute | solution.py:224
  17.2 5.4 %collective-permute-start.14 = (bf16[2,16,1152]{2,1,0:T(8,128)(2,1)S(1)}, bf16[2,16,1152]{2,1,0:T(8,128)(2,1)S(1)}, u32[]{:S(2)}, u32[]{:S(2)}) collective-permute-start(bf16[2,16,1152]{2,1,0:T(8,128)(2,1)S(1)} %get-tuple-element.20.refs_7_), channel_id=1, source_target_pairs={{0,8},{8,0},{1,9},{9,1},{2,10},{10,2},{3,11},{11,3},{4,12},{12,4},... | collective-permute-start | bytes 221192 | tf_op jit(solution)/shard_map/ppermute | solution.py:228
  17.9 5.1 %collective-permute-start.7 = (bf16[2,16,1152]{2,1,0:T(8,128)(2,1)S(1)}, bf16[2,16,1152]{2,1,0:T(8,128)(2,1)S(1)}, u32[]{:S(2)}, u32[]{:S(2)}) collective-permute-start(bf16[2,16,1152]{2,1,0:T(8,128)(2,1)S(1)} %collective-permute-done.refs_0_), channel_id=1, source_target_pairs={{0,8},{8,0},{1,9},{9,1},{2,10},{10,2},{3,11},{11,3},{4,12},{12,4},... | collective-permute-start | bytes 221192 | tf_op jit(solution)/shard_map/ppermute | solution.py:228
  18.7 4.4 %collective-permute-start.8 = (bf16[2,16,1152]{2,1,0:T(8,128)(2,1)S(1)}, bf16[2,16,1152]{2,1,0:T(8,128)(2,1)S(1)}, u32[]{:S(2)}, u32[]{:S(2)}) collective-permute-start(bf16[2,16,1152]{2,1,0:T(8,128)(2,1)S(1)} %collective-permute-done.1.refs_1_), channel_id=1, source_target_pairs={{0,8},{8,0},{1,9},{9,1},{2,10},{10,2},{3,11},{11,3},{4,12},{12,4},... | collective-permute-start | bytes 221192 | tf_op jit(solution)/shard_map/ppermute | solution.py:228
  19.7 3.9 %collective-permute-start.9 = (bf16[2,16,1152]{2,1,0:T(8,128)(2,1)S(1)}, bf16[2,16,1152]{2,1,0:T(8,128)(2,1)S(1)}, u32[]{:S(2)}, u32[]{:S(2)}) collective-permute-start(bf16[2,16,1152]{2,1,0:T(8,128)(2,1)S(1)} %collective-permute-done.2.refs_2_), channel_id=1, source_target_pairs={{0,8},{8,0},{1,9},{9,1},{2,10},{10,2},{3,11},{11,3},{4,12},{12,4},... | collective-permute-start | bytes 221192 | tf_op jit(solution)/shard_map/ppermute | solution.py:228
  22.5 1.3 %collective-permute-start.10 = (bf16[2,16,1152]{2,1,0:T(8,128)(2,1)S(1)}, bf16[2,16,1152]{2,1,0:T(8,128)(2,1)S(1)}, u32[]{:S(2)}, u32[]{:S(2)}) collective-permute-start(bf16[2,16,1152]{2,1,0:T(8,128)(2,1)S(1)} %collective-permute-done.3.refs_3_), channel_id=1, source_target_pairs={{0,8},{8,0},{1,9},{9,1},{2,10},{10,2},{3,11},{11,3},{4,12},{12,4},... | collective-permute-start | bytes 221192 | tf_op jit(solution)/shard_map/ppermute | solution.py:228
  22.5 1.4 %collective-permute-start.11 = (bf16[2,16,1152]{2,1,0:T(8,128)(2,1)S(1)}, bf16[2,16,1152]{2,1,0:T(8,128)(2,1)S(1)}, u32[]{:S(2)}, u32[]{:S(2)}) collective-permute-start(bf16[2,16,1152]{2,1,0:T(8,128)(2,1)S(1)} %collective-permute-done.4.refs_4_), channel_id=1, source_target_pairs={{0,8},{8,0},{1,9},{9,1},{2,10},{10,2},{3,11},{11,3},{4,12},{12,4},... | collective-permute-start | bytes 221192 | tf_op jit(solution)/shard_map/ppermute | solution.py:228
  23.1 1.3 %collective-permute-start.12 = (bf16[2,16,1152]{2,1,0:T(8,128)(2,1)S(1)}, bf16[2,16,1152]{2,1,0:T(8,128)(2,1)S(1)}, u32[]{:S(2)}, u32[]{:S(2)}) collective-permute-start(bf16[2,16,1152]{2,1,0:T(8,128)(2,1)S(1)} %collective-permute-done.5.refs_5_), channel_id=1, source_target_pairs={{0,8},{8,0},{1,9},{9,1},{2,10},{10,2},{3,11},{11,3},{4,12},{12,4},... | collective-permute-start | bytes 221192 | tf_op jit(solution)/shard_map/ppermute | solution.py:228
  23.1 1.4 %collective-permute-start.13 = (bf16[2,16,1152]{2,1,0:T(8,128)(2,1)S(1)}, bf16[2,16,1152]{2,1,0:T(8,128)(2,1)S(1)}, u32[]{:S(2)}, u32[]{:S(2)}) collective-permute-start(bf16[2,16,1152]{2,1,0:T(8,128)(2,1)S(1)} %collective-permute-done.6.refs_6_), channel_id=1, source_target_pairs={{0,8},{8,0},{1,9},{9,1},{2,10},{10,2},{3,11},{11,3},{4,12},{12,4},... | collective-permute-start | bytes 221192 | tf_op jit(solution)/shard_map/ppermute | solution.py:228
